TPU v7x, 512 devices: a whole 4x4x16 slice. The times are simulated.
512 devices in a mesh: seq: 16 (over x, y_lo, core), mp: 32 (over y_hi, z).
Axes of the slice: x: 4, y: 4 (y_hi: 2, y_lo: 2; y = y_hi * 2 + y_lo), z: 16, core: 2. Of those that a mesh axis runs over, the one named last changes fastest.
Arguments:
- tokens: bfloat16 [2048, 8192], P('seq', 'mp'), may hold values from -6 to 6
- block_values: bfloat16 [256, 16, 128, 128], P('mp', 'seq'), may hold values from -0.125 to 0.125
- block_rows: int32 [256, 16], P('mp', 'seq'), may hold values from 0 to 63, as said below
- grad_act: bfloat16 [2048, 32768], P('seq', 'mp'), may hold values from -1.5 to 1.5
Outputs:
- activated: bfloat16 [2048, 32768], P('seq', 'mp')
- grad_tokens: bfloat16 [2048, 8192], P('seq', 'mp')
- grad_values: bfloat16 [256, 16, 128, 128], P('mp', 'seq')
Inputs may be any that keep to these rules, and one draw needn't show every extreme that they name: `block_rows`: each block column names 16 different block rows.
All inputs are finite; a program needn't handle non-finite values.
Results may differ from a plain program's by a relative error of at most 0.023.
Values may be sent and summed in bfloat16 or wider, within the bound.
No kernel may reach another device: no remote copies, remote signals or barrier semaphores. Data moves between devices by JAX's collectives and lax.ppermute only.
A program may use at most 64 MiB of HBM per device.

v0:
```python
import jax
import jax.numpy as jnp
from jax import lax
from jax.sharding import PartitionSpec as P

SQRT_TWO_PI = 0.7978845608028654
CUBIC = 0.044715


def gelu_parts(hidden):
    inner_arg = SQRT_TWO_PI * (hidden + CUBIC * hidden * hidden * hidden)
    tanh_inner = jnp.tanh(inner_arg)
    gelu_value = 0.5 * hidden * (1.0 + tanh_inner)
    gelu_slope = 0.5 * (1.0 + tanh_inner) + 0.5 * hidden * (
        1.0 - tanh_inner * tanh_inner
    ) * SQRT_TWO_PI * (1.0 + 3.0 * CUBIC * hidden * hidden)
    return (gelu_value, gelu_slope)


def shards(tokens, block_values, block_rows, grad_act):
    tok_dev = tokens.shape[0]
    cols_dev = block_values.shape[0]
    block_size = block_values.shape[2]
    whole_rows = lax.all_gather(tokens, "mp", axis=1, tiled=True)
    row_blocks = whole_rows.reshape(tok_dev, -1, block_size)
    row_count = row_blocks.shape[1]
    panel_values, panel_rows = (
        lax.all_gather(block_values, "seq", axis=1, tiled=True),
        lax.all_gather(block_rows, "seq", axis=1, tiled=True),
    )
    kept_count = panel_rows.shape[1]
    picked = jnp.take(row_blocks, panel_rows, axis=1)
    hidden = jnp.einsum("tckp,ckpq->tcq", picked, panel_values, preferred_element_type=jnp.float32)
    gelu_value, gelu_slope = gelu_parts(hidden)
    activated = gelu_value.astype(jnp.bfloat16).reshape(tok_dev, cols_dev * block_size)
    grad_piece = grad_act.reshape(tok_dev, cols_dev, block_size).astype(jnp.float32)
    grad_hidden = (grad_piece * gelu_slope).astype(jnp.bfloat16)
    group_term = jnp.zeros((tok_dev, row_count, block_size), jnp.float32)
    for kept_index in range(kept_count):
        slot_part = jnp.einsum(
            "tcq,cpq->tcp",
            grad_hidden,
            panel_values[:, kept_index],
            preferred_element_type=jnp.float32,
        )
        group_term = group_term.at[:, panel_rows[:, kept_index]].add(slot_part)
    summed = lax.psum_scatter(
        group_term.reshape(tok_dev, row_count * block_size).astype(jnp.bfloat16),
        "mp",
        scatter_dimension=1,
        tiled=True,
    )
    full_grad = lax.all_gather(grad_hidden, "seq", axis=0, tiled=True)
    slot_tokens = lax.all_to_all(picked, "seq", split_axis=2, concat_axis=0, tiled=True)
    grad_values = jnp.einsum(
        "tckp,tcq->ckpq", slot_tokens, full_grad, preferred_element_type=jnp.float32
    ).astype(jnp.bfloat16)
    return (activated, summed, grad_values)


def solution(mesh):
    in_specs = (P("seq", "mp"), P("mp", "seq", None, None), P("mp", "seq"), P("seq", "mp"))
    out_specs = (P("seq", "mp"), P("seq", "mp"), P("mp", "seq", None, None))
    return jax.shard_map(shards, mesh=mesh, in_specs=in_specs, out_specs=out_specs, check_vma=False)
```

profile of v0, /device:TPU:24, one launch (start us, length us, event | category | flops | bytes accessed | tf_op | source)
XLA Modules:
  0.0 1009.2 jit_solution(14303631701199941003)
XLA Ops:
  7.2 1.6 copy.133
  8.9 1.8 copy.136
  10.7 16.8 %all-gather = s32[16,1,8]{2,1,0:T(1,128)S(1)} all-gather(s32[1,1,8]{2,1,0:T(1,128)} %bitcast.102), channel_id=1, replica_groups=mesh['seq'=16,'mp'=32] {'seq'}, dimensions={0}, use_global_device_ids=true | all-gather | bytes 544 | tf_op jit(solution)/shard_map/all_gather | solution.py:29
  29.3 135.2 %all-gather.5.cloned.1.call-done = bf16[128,8192]{0,1:T(8,128)(2,1)} async-done(((bf16[128,256]{0,1:T(8,128)(2,1)}), bf16[128,8192]{0,1:T(8,128)(2,1)}) %all-gather.5.cloned.1.call-update) | async-done | bytes 2097168 | tf_op jit(solution)/shard_map/all_gather | solution.py:24
  164.5 3.2 copy.134
  167.7 3.1 gather_fusion
  170.8 3.8 fusion.2
  174.6 33.3 %all-gather.7.cloned.1.call-done = bf16[8,16,128,128]{2,3,1,0:T(8,128)(2,1)} async-done(((bf16[8,1,128,128]{2,3,1,0:T(8,128)(2,1)}), bf16[8,16,128,128]{2,3,1,0:T(8,128)(2,1)}) %all-gather.7.cloned.1.call-update) | async-done | bytes 4194320 | tf_op jit(solution)/shard_map/all_gather | solution.py:28
  207.8 4.9 fusion.13
  212.7 1.3 fusion.29
  214.0 2.5 broadcast_in_dim.17
  216.5 2.7 scatter_fusion
  219.2 1.2 fusion.28
  220.5 2.7 scatter_fusion.1
  223.2 1.2 fusion.27
  224.4 2.7 scatter_fusion.2
  227.1 1.2 fusion.26
  228.3 2.7 scatter_fusion.3
  231.0 1.2 fusion.25
  232.2 2.7 scatter_fusion.4
  234.9 1.2 fusion.24
  236.1 2.7 scatter_fusion.5
  238.9 1.2 fusion.23
  240.1 2.7 scatter_fusion.6
  242.8 1.2 fusion.22
  244.0 2.7 scatter_fusion.7
  247.9 2.6 scatter_fusion.8
  251.8 2.7 scatter_fusion.9
  254.5 1.2 fusion.19
  255.7 2.7 scatter_fusion.10
  258.4 1.2 fusion.18
  259.7 2.7 scatter_fusion.11
  262.4 1.2 fusion.17
  263.6 2.7 scatter_fusion.12
  267.6 2.7 scatter_fusion.13
  271.5 2.7 scatter_fusion.14
  274.2 1.2 fusion.14
  275.5 2.9 scatter_fusion.15
  278.3 2.6 convert_element_type.28
  280.9 2.9 copy.171
  284.4 5.1 all-to-all-start
  290.4 56.7 %all-to-all-done = bf16[128,8,16,128]{3,0,1,2:T(8,128)(2,1)} async-done(((bf16[128,8,16,128]{3,0,1,2:T(8,128)(2,1)}), bf16[128,8,16,128]{3,0,1,2:T(8,128)(2,1)}, u32[]{:S(2)}, u32[]{:S(2)}) %all-to-all-start) | async-done | bytes 4194336 | tf_op jit(solution)/shard_map/all_to_all | solution.py:54
  347.1 6.8 copy.172
  353.9 7.3 reshape.30
  361.2 582.6 %reduce-scatter.2.cloned.1.call-done = bf16[128,256]{0,1:T(8,128)(2,1)} async-done(((bf16[128,8192]{0,1:T(8,128)(2,1)}), bf16[128,256]{0,1:T(8,128)(2,1)}) %reduce-scatter.2.cloned.1.call-update) | async-done | bytes 65552 | tf_op jit(solution)/shard_map/reduce_scatter | solution.py:47
  943.9 1.6 copy.175
  945.5 51.8 %all-gather.9.cloned.1.call-done = bf16[2048,8,128]{0,2,1:T(8,128)(2,1)} async-done(((bf16[128,8,128]{0,2,1:T(8,128)(2,1)}), bf16[2048,8,128]{0,2,1:T(8,128)(2,1)}) %all-gather.9.cloned.1.call-update) | async-done | bytes 4194320 | tf_op jit(solution)/shard_map/all_gather | solution.py:53
  997.2 5.4 fusion.6
  (23 shorter events, 8.3 us)
Async XLA Ops:
  7.2 157.3 %all-gather.5.cloned.1.call-start = ((), (), s32[]{:S(2)}) async-start(), calls=%async_computation.2 | async-start | bytes 2162688 | tf_op jit(solution)/shard_map/all_gather | solution.py:24
  8.8 199.0 %all-gather.7.cloned.1.call-start = ((), (), s32[]{:S(2)}) async-start(), calls=%async_computation.3 | async-start | bytes 4456448 | tf_op jit(solution)/shard_map/all_gather | solution.py:28
  10.7 933.2 %reduce-scatter.2.cloned.1.call-start = ((), (), s32[]{:S(2)}) async-start(), calls=%async_computation.4 | async-start | bytes 2162688 | tf_op jit(solution)/shard_map/reduce_scatter | solution.py:47
  212.7 61.5 %copy-start = (bf16[128,8,128]{0,2,1:T(8,128)(2,1)}, bf16[128,8,128]{0,2,1:T(8,128)(2,1)S(1)}, u32[]{:S(2)}) copy-start(bf16[128,8,128]{0,2,1:T(8,128)(2,1)S(1)} %get-tuple-element.31) | copy-start | bytes 786436
  283.8 713.4 %all-gather.9.cloned.1.call-start = ((), (), s32[]{:S(2)}) async-start(), calls=%async_computation.5 | async-start | bytes 4456448 | tf_op jit(solution)/shard_map/all_gather | solution.py:53
  284.4 62.6 %all-to-all-start = ((bf16[128,8,16,128]{3,0,1,2:T(8,128)(2,1)}), bf16[128,8,16,128]{3,0,1,2:T(8,128)(2,1)}, u32[]{:S(2)}, u32[]{:S(2)}) async-start(bf16[128,8,16,128]{3,0,1,2:T(8,128)(2,1)} %fusion.2), calls=%async_computation.1 | async-start | bytes 8388608 | tf_op jit(solution)/shard_map/all_to_all | solution.py:54
Sparse Core Ops, SparseCore 0:
  11.7 152.7 all-gather.4
  167.2 40.6 all-gather.6
  284.0 659.8 reduce-scatter.1
  946.4 50.8 all-gather.8
where the time goes:
time: 1010 us
  waiting for transfers between devices  860 us (85%)
  other arithmetic  50.1 us (5%)
  local copies, waits for them, and re-layouts  33 us (3%)
  matrix products  29.9 us (3%)
  blocking collectives  16.8 us (2%)
  between operations  13.9 us (1%)
    reduce_scatter x1, waiting for transfers between devices, shards(): lax.psum_scatter(group_term.reshape(tok_dev, row_count * block_size).asty...  583 us
    all_gather x1, waiting for transfers between devices, shards(): whole_rows = lax.all_gather(tokens, 'mp', axis=1, tiled=True)  135 us
    all_to_all x1, waiting for transfers between devices, shards(): lax.all_to_all(picked, 'seq', split_axis=2, concat_axis=0, tiled=True)  56.7 us
    all_gather x1, waiting for transfers between devices, shards(): full_grad = lax.all_gather(grad_hidden, 'seq', axis=0, tiled=True)  51.8 us
    scatter-add x16, other arithmetic, shards(): group_term = group_term.at[:, panel_rows[:, kept_index]].add(slot_part)  43.3 us
    all_gather x1, waiting for transfers between devices, shards(): lax.all_gather(block_values, 'seq', axis=1, tiled=True)  33.3 us
  transfers between devices with their start and end apart: 5, of which 5 were waited for; matrix products, arithmetic and copies ran while one was open for 3% of the time, Pallas kernels for 0%

commit v1 on v0

v1 whole, which is shorter than its diff:
```python
import jax
import jax.numpy as jnp
from jax import lax
from jax.experimental import pallas as pl
from jax.experimental.pallas import tpu as pltpu
from jax.sharding import Mesh
from jax.sharding import PartitionSpec as P

SQRT_TWO_PI = 0.7978845608028654
CUBIC = 0.044715
AXES = ("x", "yl", "core", "yh", "z")
SIZES = (4, 2, 2, 2, 16)
SEQ = ("x", "yl", "core")
MP = ("yh", "z")


def gelu_parts(hidden):
    inner_arg = SQRT_TWO_PI * (hidden + CUBIC * hidden * hidden * hidden)
    tanh_inner = jnp.tanh(inner_arg)
    gelu_value = 0.5 * hidden * (1.0 + tanh_inner)
    gelu_slope = 0.5 * (1.0 + tanh_inner) + 0.5 * hidden * (
        1.0 - tanh_inner * tanh_inner
    ) * SQRT_TWO_PI * (1.0 + 3.0 * CUBIC * hidden * hidden)
    return gelu_value, gelu_slope


def column_kernel(rows_ref, tok_ref, w_ref, gact_ref, act_ref, term_ref, gv_ref, acc, tok_t):
    c = pl.program_id(0)
    kept = w_ref.shape[0]

    @pl.when(c == 0)
    def _():
        acc[...] = jnp.zeros_like(acc)

        @pl.loop(0, tok_ref.shape[0])
        def _(r):
            tok_t[r] = tok_ref[r].T

    rows = [rows_ref[k, c] for k in range(kept)]
    weights = w_ref[...].reshape(kept * 128, 128)
    picked = jnp.concatenate([tok_ref[r] for r in rows], axis=1)
    hidden = jnp.dot(picked, weights, preferred_element_type=jnp.float32)
    value, slope = gelu_parts(hidden)
    act_ref[...] = value.astype(jnp.bfloat16)
    grad_hidden = (gact_ref[...].astype(jnp.float32) * slope).astype(jnp.bfloat16)
    for k in range(kept):
        acc[rows[k]] += lax.dot_general(
            grad_hidden, w_ref[k, 0], (((1,), (1,)), ((), ())), preferred_element_type=jnp.float32
        )
        gv_ref[k, 0] = jnp.dot(
            tok_t[rows[k]], grad_hidden, preferred_element_type=jnp.float32
        ).astype(jnp.bfloat16)

    @pl.when(c == pl.num_programs(0) - 1)
    def _():
        term_ref[...] = acc[...].astype(jnp.bfloat16)


def columns(rows, tok, weights, grad_act):
    n_rows, n_tok, block = tok.shape
    kept, cols = weights.shape[:2]
    return pl.pallas_call(
        column_kernel,
        grid_spec=pltpu.PrefetchScalarGridSpec(
            num_scalar_prefetch=1,
            grid=(cols,),
            in_specs=[
                pl.BlockSpec((n_rows, n_tok, block), lambda c, rows: (0, 0, 0)),
                pl.BlockSpec((kept, 1, block, block), lambda c, rows: (0, c, 0, 0)),
                pl.BlockSpec((n_tok, block), lambda c, rows: (0, c)),
            ],
            out_specs=[
                pl.BlockSpec((n_tok, block), lambda c, rows: (0, c)),
                pl.BlockSpec((n_rows, n_tok, block), lambda c, rows: (0, 0, 0)),
                pl.BlockSpec((kept, 1, block, block), lambda c, rows: (0, c, 0, 0)),
            ],
            scratch_shapes=[
                pltpu.VMEM((n_rows, n_tok, block), jnp.float32),
                pltpu.VMEM((n_rows, block, n_tok), jnp.bfloat16),
            ],
        ),
        out_shape=[
            jax.ShapeDtypeStruct((n_tok, cols * block), jnp.bfloat16),
            jax.ShapeDtypeStruct((n_rows, n_tok, block), jnp.bfloat16),
            jax.ShapeDtypeStruct((kept, cols, block, block), jnp.bfloat16),
        ],
        compiler_params=pltpu.CompilerParams(vmem_limit_bytes=40 * 2**20),
        cost_estimate=pl.CostEstimate(flops=1_610_612_736, bytes_accessed=13_000_000, transcendentals=131072),
    )(rows, tok, weights, grad_act)


def shards(tokens, block_values, block_rows, grad_act):
    n_tok = tokens.shape[0]
    cols, _, block, _ = block_values.shape
    mine = tokens.reshape(n_tok, 2, block).transpose(1, 0, 2)
    pair = lax.all_gather(mine, "yh", axis=0)
    tok = lax.all_gather(pair, "z", axis=0).reshape(64, n_tok, block)
    rows = lax.all_gather(block_rows.reshape(cols), SEQ, axis=0)
    weights = lax.all_gather(block_values.reshape(cols, block, block), SEQ, axis=0)
    rows = (rows % 32) // 2 * 4 + rows // 32 * 2 + rows % 2
    activated, term, gv = columns(rows, tok, weights, grad_act)
    gv = lax.all_to_all(gv, SEQ, 0, 0)
    gv = gv.astype(jnp.float32).sum(0).astype(jnp.bfloat16)
    part = lax.psum_scatter(term.reshape(16, 2, 2, n_tok, block), "z", scatter_dimension=0)
    yh = lax.axis_index("yh")
    keep = lax.dynamic_index_in_dim(part, yh, 0, keepdims=False)
    give = lax.dynamic_index_in_dim(part, 1 - yh, 0, keepdims=False)
    got = lax.ppermute(give, "yh", [(0, 1), (1, 0)])
    summed = (keep.astype(jnp.float32) + got.astype(jnp.float32)).astype(jnp.bfloat16)
    summed = summed.transpose(1, 0, 2).reshape(n_tok, 2 * block)
    return activated, summed, gv.reshape(cols, 1, block, block)


def solution(mesh):
    fine = Mesh(mesh.devices.reshape(SIZES), AXES)
    in_specs = (P(SEQ, MP), P(MP, SEQ, None, None), P(MP, SEQ), P(SEQ, MP))
    out_specs = (P(SEQ, MP), P(SEQ, MP), P(MP, SEQ, None, None))
    return jax.shard_map(shards, mesh=fine, in_specs=in_specs, out_specs=out_specs, check_vma=False)
```

time: 1010 us -> 250 us (0.25)
  waiting for transfers between devices: 860 us -> 176 us
  other arithmetic: 50.1 us -> 4.41 us
  matrix products: 29.9 us -> 0 us
  local copies, waits for them, and re-layouts: 33 us -> 10.8 us
  Pallas kernels: 0 us -> 15.8 us
    reduce_scatter x1, waiting for transfers between devices: 583 us -> 68.4 us  [shards(): lax.psum_scatter(term.reshape(16, 2, 2, n_tok, block), 'z', scatter_dimen...]
    all_gather x3 -> x2, waiting for transfers between devices: 220 us -> 106 us  [the longest x1 62.2 us: shards(): tok = lax.all_gather(pair, 'z', axis=0).reshape(64, n_tok, block)]
    all_to_all x1, waiting for transfers between devices: 56.7 us -> 0.01 us  [shards(): gv = lax.all_to_all(gv, SEQ, 0, 0)]
    scatter-add x16 -> x0, other arithmetic: 43.3 us -> none  [shards(): group_term = group_term.at[:, panel_rows[:, kept_index]].add(slot_part)]
    dot_general x18 -> x0, matrix products: 29.9 us -> none  [the longest x16 19.7 us: shards(): jnp.einsum('tcq,cpq->tcp', grad_hidden, panel_values[:, kept_index], pref...]
    pallas_call x0 -> x1, Pallas kernels: none -> 15.8 us  [columns(): pl.pallas_call(column_kernel, grid_spec=pltpu.PrefetchScalarGridSpec(num_...]
    unnamed x0 -> x1, blocking collectives: none -> 11.7 us
    all_gather x1, blocking collectives: 16.8 us -> 6.55 us  [shards(): pair = lax.all_gather(mine, 'yh', axis=0)]
  transfers between devices with their start and end apart: 5 -> 5, of which waited for: 5 -> 4; matrix products, arithmetic and copies ran while one was open for 3% -> 3% of each run, Pallas kernels for 0% -> 0%
where the time goes in v1:
time: 250 us; the launch traced here: 248 us
  waiting for transfers between devices  176 us (70%)
  blocking collectives  18.2 us (7%)
  Pallas kernels  15.8 us (6%)
  between operations  14.5 us (6%)
  local copies, waits for them, and re-layouts  10.8 us (4%)
  starting transfers between devices  8.42 us (3%)
  other arithmetic  4.41 us (2%)
    reduce_scatter x1, waiting for transfers between devices, shards(): lax.psum_scatter(term.reshape(16, 2, 2, n_tok, block), 'z', scatter_dimen...  68.4 us
    all_gather x1, waiting for transfers between devices, shards(): tok = lax.all_gather(pair, 'z', axis=0).reshape(64, n_tok, block)  62.2 us
    all_gather x1, waiting for transfers between devices, shards(): lax.all_gather(block_values.reshape(cols, block, block), SEQ, axis=0)  44 us
    pallas_call x1, Pallas kernels, columns(): pl.pallas_call(column_kernel, grid_spec=pltpu.PrefetchScalarGridSpec(num_...  15.8 us
    unnamed x1, blocking collectives  11.7 us
    unnamed x14, local copies, waits for them, and re-layouts  9.65 us
    all_gather x1, blocking collectives, shards(): pair = lax.all_gather(mine, 'yh', axis=0)  6.55 us
    all_to_all x1, starting transfers between devices, shards(): gv = lax.all_to_all(gv, SEQ, 0, 0)  5 us
  transfers between devices with their start and end apart: 5, of which 4 were waited for; matrix products, arithmetic and copies ran while one was open for 3% of the time, Pallas kernels for 0%

profile of v1, /device:TPU:24, one launch (start us, length us, event | category | flops | bytes accessed | tf_op | source)
XLA Modules:
  0.0 247.9 jit_solution(9659982512813304280)
XLA Ops:
  7.2 0.0 all-gather.7.cloned.1.call-start
  7.2 0.9 copy.12
  8.2 0.1 copy.13
  8.3 6.6 %all-gather.1 = bf16[4,128,128]{2,1,0:T(8,128)(2,1)} all-gather(bf16[2,128,128]{2,1,0:T(8,128)(2,1)S(1)} %copy.13), channel_id=3, replica_groups=mesh['x'=4,'yl'=2,'core'=2,'yh'=2,'z'=16] {'yh'}, dimensions={0}, use_global_device_ids=true | all-gather | bytes 196608 | tf_op jit(solution)/shard_map/all_gather | solution.py:96
  14.9 0.0 all-gather.7.cloned.1.call-update
  14.9 0.0 all-gather.9.cloned.1.call-start
  14.9 0.7 all-gather.9.cloned.1.call-update
  15.6 0.0 reduce-scatter.2.cloned.1.call-start
  15.7 1.3 dynamic-slice.2
  17.6 0.8 bitcast_dynamic-update-slice_fusion
  18.4 11.7 %all-reduce = s32[128]{0:T(128)S(1)} all-reduce(s32[128]{0:T(128)S(1)} %bitcast_dynamic-update-slice_fusion), channel_id=2, replica_groups=mesh['x'=4,'yl'=2,'core'=2,'yh'=2,'z'=16] {'x','yl','core'}, use_global_device_ids=true, to_apply=%add | all-reduce | flops 128 | bytes 1024
  30.0 0.1 reshape.33
  30.2 62.2 %all-gather.7.cloned.1.call-done = bf16[32,2,128,128]{3,2,1,0:T(8,128)(2,1)} async-done(((bf16[2,2,128,128]{3,2,1,0:T(8,128)(2,1)}), bf16[32,2,128,128]{3,2,1,0:T(8,128)(2,1)}) %all-gather.7.cloned.1.call-update) | async-done | bytes 2097168 | tf_op jit(solution)/shard_map/all_gather | solution.py:97
  92.3 44.0 %all-gather.9.cloned.1.call-done = bf16[128,1,128,128]{3,2,1,0:T(8,128)(2,1)} async-done(((bf16[8,1,128,128]{3,2,1,0:T(8,128)(2,1)}), bf16[128,1,128,128]{3,2,1,0:T(8,128)(2,1)}) %all-gather.9.cloned.1.call-update) | async-done | bytes 4194320 | tf_op jit(solution)/shard_map/all_gather | solution.py:99
  136.3 0.0 copy-start
  136.3 2.2 copy-done
  138.5 0.0 copy-start.2
  138.5 1.6 copy-done.2
  140.1 0.0 copy-start.3
  140.1 0.9 copy-done.3
  141.0 15.8 %shard_map.67 = (bf16[128,1024]{1,0:T(8,128)(2,1)}, bf16[64,128,128]{2,1,0:T(8,128)(2,1)}, bf16[16,8,128,128]{3,2,1,0:T(8,128)(2,1)S(1)}) custom-call(s32[16,8]{1,0:T(8,128)S(1)} %fusion.5.rows_ref, bf16[64,128,128]{2,1,0:T(8,128)(2,1)S(1)} %bitcast.24, bf16[16,8,128,128]{3,2,1,0:T(8,128)(2,1)S(1)} %bitcast.23, bf16[128,1024]{1,0:T(8,128)(2,1)S(1)} %copy-done.3), custom_call_target="tpu_custom_call" | custom-call | flops 1610612736 | bytes 13000000 | tf_op jit(solution)/shard_map/pallas_call | solution.py:62
  156.8 0.0 copy-start.1
  156.8 1.9 copy-done.1
  158.8 0.0 reduce-scatter.2.cloned.1.call-update
  158.8 5.0 %all-to-all-start = ((bf16[16,8,128,128]{3,2,1,0:T(8,128)(2,1)}), bf16[16,8,128,128]{3,2,1,0:T(8,128)(2,1)}, u32[]{:S(2)}, u32[]{:S(2)}) async-start(bf16[16,8,128,128]{3,2,1,0:T(8,128)(2,1)} %copy-done.1), calls=%async_computation.1 | async-start | bytes 8388608 | tf_op jit(solution)/shard_map/all_to_all | solution.py:102
  163.8 68.4 %reduce-scatter.2.cloned.1.call-done = bf16[1,2,2,128,128]{4,3,2,1,0:T(8,128)(2,1)} async-done(((bf16[16,2,2,128,128]{4,3,2,1,0:T(8,128)(2,1)}), bf16[1,2,2,128,128]{4,3,2,1,0:T(8,128)(2,1)}) %reduce-scatter.2.cloned.1.call-update) | async-done | bytes 131088 | tf_op jit(solution)/shard_map/reduce_scatter | solution.py:104
  232.2 0.0 copy-start.4
  232.2 0.9 dynamic-slice_bitcast_fusion
  233.1 3.3 %collective-permute-start = (bf16[2,128,128]{2,1,0:T(8,128)(2,1)S(1)}, bf16[2,128,128]{2,1,0:T(8,128)(2,1)S(1)}, u32[]{:S(2)}, u32[]{:S(2)}) collective-permute-start(bf16[2,128,128]{2,1,0:T(8,128)(2,1)S(1)} %dynamic-slice_bitcast_fusion), channel_id=1, source_target_pairs={{0,16},{16,0},{1,17},{17,1},{2,18},{18,2},{3,19},{19,3},{4,20},{20... | collective-permute-start | bytes 196616 | tf_op jit(solution)/shard_map/ppermute | solution.py:108
  236.4 0.0 all-to-all-done
  236.4 3.7 %reduce_sum.12 = bf16[8,128,128]{2,1,0:T(8,128)(2,1)} reduce(bf16[16,8,128,128]{3,2,1,0:T(8,128)(2,1)} %all-to-all-done, bf16[]{:T(256)} %constant.68.clone.1), dimensions={0}, to_apply=%region_1.2 | reduce | flops 1966080 | bytes 4456450 | tf_op jit(solution)/shard_map/reduce_sum | solution.py:103
  240.2 0.6 collective-permute-done
  240.8 0.0 copy-done.4
  240.8 0.6 copy_bitcast_fusion
  (2 shorter events, 0.0 us)
Async XLA Ops:
  7.2 85.2 %all-gather.7.cloned.1.call-start = ((), (), s32[]{:S(2)}) async-start(), calls=%async_computation.3 | async-start | bytes 2228224 | tf_op jit(solution)/shard_map/all_gather | solution.py:97
  14.9 121.4 %all-gather.9.cloned.1.call-start = ((), (), s32[]{:S(2)}) async-start(), calls=%async_computation.4 | async-start | bytes 4456448 | tf_op jit(solution)/shard_map/all_gather | solution.py:99
  15.6 216.6 %reduce-scatter.2.cloned.1.call-start = ((), (), s32[]{:S(2)}) async-start(), calls=%async_computation.2 | async-start | bytes 2228224 | tf_op jit(solution)/shard_map/reduce_scatter | solution.py:104
  136.3 2.2 copy-start
  138.5 1.6 copy-start.2
  140.1 0.9 copy-start.3
  156.8 1.9 copy-start.1
  158.8 77.6 %all-to-all-start = ((bf16[16,8,128,128]{3,2,1,0:T(8,128)(2,1)}), bf16[16,8,128,128]{3,2,1,0:T(8,128)(2,1)}, u32[]{:S(2)}, u32[]{:S(2)}) async-start(bf16[16,8,128,128]{3,2,1,0:T(8,128)(2,1)} %copy-done.1), calls=%async_computation.1 | async-start | bytes 8388608 | tf_op jit(solution)/shard_map/all_to_all | solution.py:102
  232.2 8.6 %copy-start.4 = (bf16[1,2,2,128,128]{4,3,2,1,0:T(8,128)(2,1)S(1)}, bf16[1,2,2,128,128]{4,3,2,1,0:T(8,128)(2,1)}, u32[]{:S(2)}) copy-start(bf16[1,2,2,128,128]{4,3,2,1,0:T(8,128)(2,1)} %reduce-scatter.2.cloned.1.call-done) | copy-start | bytes 393220
  233.1 7.7 %collective-permute-start = (bf16[2,128,128]{2,1,0:T(8,128)(2,1)S(1)}, bf16[2,128,128]{2,1,0:T(8,128)(2,1)S(1)}, u32[]{:S(2)}, u32[]{:S(2)}) collective-permute-start(bf16[2,128,128]{2,1,0:T(8,128)(2,1)S(1)} %dynamic-slice_bitcast_fusion), channel_id=1, source_target_pairs={{0,16},{16,0},{1,17},{17,1},{2,18},{18,2},{3,19},{19,3},{4,20},{20... | collective-permute-start | bytes 196616 | tf_op jit(solution)/shard_map/ppermute | solution.py:108
Sparse Core Ops, SparseCore 0:
  15.0 77.2 all-gather.6
  94.5 41.7 all-gather.8
  158.9 73.2 reduce-scatter.1

commit v2 on v1

v2 whole, which is shorter than its diff:
```python
import jax
import jax.numpy as jnp
from jax import lax
from jax.experimental import pallas as pl
from jax.experimental.pallas import tpu as pltpu
from jax.sharding import Mesh
from jax.sharding import PartitionSpec as P

SQRT_TWO_PI = 0.7978845608028654
CUBIC = 0.044715
AXES = ("x", "yl", "core", "yh", "z")
SIZES = (4, 2, 2, 2, 16)
SEQ = ("x", "yl", "core")
MP = ("yh", "z")
BF16, F32 = jnp.bfloat16, jnp.float32
OWN, LEFT, RIGHT = (0, 4, 8, 12), (1, 5, 9, 13), (15, 3, 7, 11)
FAR_LEFT, FAR_RIGHT = (6, 10), (14, 2)
PARTS = (OWN, LEFT, RIGHT, FAR_LEFT, FAR_RIGHT)


def gelu_parts(hidden):
    inner_arg = SQRT_TWO_PI * (hidden + CUBIC * hidden * hidden * hidden)
    tanh_inner = jnp.tanh(inner_arg)
    gelu_value = 0.5 * hidden * (1.0 + tanh_inner)
    gelu_slope = 0.5 * (1.0 + tanh_inner) + 0.5 * hidden * (
        1.0 - tanh_inner * tanh_inner
    ) * SQRT_TWO_PI * (1.0 + 3.0 * CUBIC * hidden * hidden)
    return gelu_value, gelu_slope


def hidden_kernel(
    rows_ref, own, left, right, far_left, far_right, w_ref, gact_ref, act_ref, gh_ref, gv_ref, tok, sem
):
    c = pl.program_id(0)
    kept = gv_ref.shape[0]

    @pl.when(c == 0)
    def _():
        copies = [
            pltpu.make_async_copy(ref.at[i], tok.at[pl.ds(4 * d, 4)], sem.at[d])
            for ref, part in zip((own, left, right, far_left, far_right), PARTS)
            for i, d in enumerate(part)
        ]
        for copy in copies:
            copy.start()
        for copy in copies:
            copy.wait()

    rows = [rows_ref[k, c] for k in range(kept)]
    weights = w_ref[...].reshape(kept * 128, 128)
    picked = jnp.concatenate([tok[r] for r in rows], axis=1)
    hidden = jnp.dot(picked, weights, preferred_element_type=F32)
    value, slope = gelu_parts(hidden)
    act_ref[...] = value.astype(BF16)
    grad_hidden = (gact_ref[...].astype(F32) * slope).astype(BF16)
    gh_ref[...] = grad_hidden
    grads = lax.dot_general(
        grad_hidden, picked, (((0,), (0,)), ((), ())), preferred_element_type=F32
    ).astype(BF16)
    for k in range(kept):
        gv_ref[k, 0] = grads[:, k * 128 : (k + 1) * 128]


def term_kernel(rows_ref, gh_ref, w_ref, own, left, right, far_left, far_right, acc):
    c = pl.program_id(0)
    kept = w_ref.shape[0]

    @pl.when(c == 0)
    def _():
        acc[...] = jnp.zeros_like(acc)

    weights = w_ref[...].reshape(kept * 128, 128)
    part = lax.dot_general(
        gh_ref[...], weights, (((1,), (1,)), ((), ())), preferred_element_type=F32
    )
    for k in range(kept):
        acc[rows_ref[k, c]] += part[:, k * 128 : (k + 1) * 128]

    @pl.when(c == pl.num_programs(0) - 1)
    def _():
        for ref, places in zip((own, left, right, far_left, far_right), PARTS):
            for i, d in enumerate(places):
                ref[i] = acc[4 * d : 4 * d + 4].astype(BF16)


def hidden_call(rows, parts, weights, grad_act):
    kept, cols = rows.shape
    n_tok = grad_act.shape[0]
    column = pl.BlockSpec((n_tok, 128), lambda c, rows: (0, c))
    return pl.pallas_call(
        hidden_kernel,
        grid_spec=pltpu.PrefetchScalarGridSpec(
            num_scalar_prefetch=1,
            grid=(cols,),
            in_specs=[pl.BlockSpec(memory_space=pl.ANY)] * 5
            + [pl.BlockSpec((kept, 128, 128), lambda c, rows: (0, c, 0)), column],
            out_specs=[
                column,
                column,
                pl.BlockSpec((kept, 1, 128, 128), lambda c, rows: (0, c, 0, 0)),
            ],
            scratch_shapes=[pltpu.VMEM((64, n_tok, 128), BF16), pltpu.SemaphoreType.DMA((16,))],
        ),
        out_shape=[
            jax.ShapeDtypeStruct((n_tok, cols * 128), BF16),
            jax.ShapeDtypeStruct((n_tok, cols * 128), BF16),
            jax.ShapeDtypeStruct((kept, cols, 128, 128), BF16),
        ],
        compiler_params=pltpu.CompilerParams(vmem_limit_bytes=40 * 2**20),
        cost_estimate=pl.CostEstimate(flops=1_073_741_824, bytes_accessed=11_000_000, transcendentals=131072),
    )(rows, *parts, weights, grad_act)


def term_call(rows, grad_hidden, weights):
    kept, cols = rows.shape
    n_tok = grad_hidden.shape[0]
    return pl.pallas_call(
        term_kernel,
        grid_spec=pltpu.PrefetchScalarGridSpec(
            num_scalar_prefetch=1,
            grid=(cols,),
            in_specs=[
                pl.BlockSpec((n_tok, 128), lambda c, rows: (0, c)),
                pl.BlockSpec((kept, 128, 128), lambda c, rows: (0, c, 0)),
            ],
            out_specs=[
                pl.BlockSpec((len(p), 4, n_tok, 128), lambda c, rows: (0, 0, 0, 0)) for p in PARTS
            ],
            scratch_shapes=[pltpu.VMEM((64, n_tok, 128), F32)],
        ),
        out_shape=[jax.ShapeDtypeStruct((len(p), 4, n_tok, 128), BF16) for p in PARTS],
        compiler_params=pltpu.CompilerParams(vmem_limit_bytes=40 * 2**20),
        cost_estimate=pl.CostEstimate(flops=536_870_912, bytes_accessed=7_000_000, transcendentals=0),
    )(rows, grad_hidden, weights)


def shift(a, by):
    return lax.ppermute(a, "z", [(i, (i + by) % 16) for i in range(16)])


def swap(a, axis):
    return lax.ppermute(a, axis, [(0, 1), (1, 0)])


def total(*arrays):
    return sum(a.astype(F32) for a in arrays)


def gather_tokens(mine):
    quad = jnp.stack([mine, shift(mine, 4), shift(mine, 8), shift(mine, -4)])
    own = jnp.concatenate([quad, swap(quad, "yh")], axis=1)
    left, right = shift(own, 1), shift(own, -1)
    return own, left, right, shift(left[1:3], 1), shift(right[0:2], -1)


def reduce_terms(own, left, right, far_left, far_right):
    from_right, from_left = shift(far_left, -1), shift(far_right, 1)
    left = jnp.concatenate([left[:1], total(left[1:3], from_right).astype(BF16), left[3:]])
    right = jnp.concatenate([total(right[:2], from_left).astype(BF16), right[2:]])
    own = total(own, shift(left, -1), shift(right, 1)).astype(BF16)
    own = total(own[:, :2], swap(own[:, 2:], "yh")).astype(BF16)
    return total(own[0], shift(own[1], -4), shift(own[2], 8), shift(own[3], 4)).astype(BF16)


def shards(tokens, block_values, block_rows, grad_act):
    n_tok = tokens.shape[0]
    cols = block_values.shape[0]
    row_tile = jnp.zeros((16, 128), BF16).at[0, :cols].set(block_rows[:, 0].astype(BF16))
    sent = jnp.concatenate([block_values.reshape(cols * 128, 128), row_tile])
    weights = lax.all_gather(sent, SEQ, axis=0)
    parts = gather_tokens(tokens.reshape(n_tok, 2, 128).transpose(1, 0, 2))
    rows = weights[:, cols * 128, :cols].astype(jnp.int32)
    away = (lax.axis_index("z") - rows % 32 // 2) % 16
    rows = away * 4 + (rows // 32 + lax.axis_index("yh")) % 2 * 2 + rows % 2
    activated, grad_hidden, grads = hidden_call(rows, parts, weights, grad_act)
    grads = lax.all_to_all(grads, SEQ, 0, 0)
    summed = reduce_terms(*term_call(rows, grad_hidden, weights))
    summed = summed.transpose(1, 0, 2).reshape(n_tok, 256)
    grads = total(*grads).astype(BF16).transpose(0, 2, 1)
    return activated, summed, grads[:, None]


def solution(mesh):
    fine = Mesh(mesh.devices.reshape(SIZES), AXES)
    in_specs = (P(SEQ, MP), P(MP, SEQ, None, None), P(MP, SEQ), P(SEQ, MP))
    out_specs = (P(SEQ, MP), P(SEQ, MP), P(MP, SEQ, None, None))
    return jax.shard_map(shards, mesh=fine, in_specs=in_specs, out_specs=out_specs, check_vma=False)
```

time: 250 us -> 206 us (0.82)
  waiting for transfers between devices: 176 us -> 73 us
  starting transfers between devices: 8.42 us -> 82.4 us
  blocking collectives: 18.2 us -> 0 us
    all_gather x2 -> x1, waiting for transfers between devices: 106 us -> 0.02 us  [shards(): weights = lax.all_gather(sent, SEQ, axis=0)]
    ppermute x1 -> x16, starting transfers between devices: 3.3 us -> 76.5 us  [the longest x14 70.5 us: shift(): return lax.ppermute(a, 'z', [(i, (i + by) % 16) for i in range(16)])]
    ppermute x1 -> x16, waiting for transfers between devices: 0.6 us -> 73 us  [the longest x14 44.3 us: shift(): return lax.ppermute(a, 'z', [(i, (i + by) % 16) for i in range(16)])]
    reduce_scatter x1 -> x0, waiting for transfers between devices: 68.4 us -> none  [shards(): lax.psum_scatter(term.reshape(16, 2, 2, n_tok, block), 'z', scatter_dimen...]
    unnamed x1 -> x0, blocking collectives: 11.7 us -> none
    all_gather x1 -> x0, blocking collectives: 6.55 us -> none  [shards(): pair = lax.all_gather(mine, 'yh', axis=0)]
    reduce_sum x1 -> x0, other arithmetic: 3.74 us -> none  [shards(): gv = gv.astype(jnp.float32).sum(0).astype(jnp.bfloat16)]
    broadcast_in_dim x0 -> x1, other arithmetic: none -> 2.77 us  [shards(): return (activated, summed, grads[:, None])]
  transfers between devices with their start and end apart: 5 -> 18, of which waited for: 4 -> 11; matrix products, arithmetic and copies ran while one was open for 3% -> 2% of each run, Pallas kernels for 0% -> 2%
where the time goes in v2:
time: 206 us; the launch traced here: 203 us
  starting transfers between devices  82.4 us (40%)
  waiting for transfers between devices  73 us (35%)
  Pallas kernels  15.9 us (8%)
  between operations  14.4 us (7%)
  local copies, waits for them, and re-layouts  10.3 us (5%)
  other arithmetic  6.59 us (3%)
    ppermute x14, starting transfers between devices, shift(): return lax.ppermute(a, 'z', [(i, (i + by) % 16) for i in range(16)])  70.5 us
    ppermute x14, waiting for transfers between devices, shift(): return lax.ppermute(a, 'z', [(i, (i + by) % 16) for i in range(16)])  44.3 us
    ppermute x2, waiting for transfers between devices, swap(): return lax.ppermute(a, axis, [(0, 1), (1, 0)])  28.6 us
    pallas_call x1, Pallas kernels, hidden_call(): pl.pallas_call(hidden_kernel, grid_spec=pltpu.PrefetchScalarGridSpec(num_...  11 us
    unnamed x11, local copies, waits for them, and re-layouts  9.91 us
    ppermute x2, starting transfers between devices, swap(): return lax.ppermute(a, axis, [(0, 1), (1, 0)])  6 us
    all_to_all x1, starting transfers between devices, shards(): grads = lax.all_to_all(grads, SEQ, 0, 0)  5.86 us
    pallas_call x1, Pallas kernels, term_call(): pl.pallas_call(term_kernel, grid_spec=pltpu.PrefetchScalarGridSpec(num_sc...  4.87 us
  transfers between devices with their start and end apart: 18, of which 11 were waited for; matrix products, arithmetic and copies ran while one was open for 2% of the time, Pallas kernels for 2%

profile of v2, /device:TPU:24, one launch (start us, length us, event | category | flops | bytes accessed | tf_op | source)
XLA Modules:
  0.0 202.5 jit_solution(18362468842151172899)
XLA Ops:
  7.2 0.7 convert_bitcast_fusion
  7.9 1.7 fusion.2
  9.6 1.0 copy.28
  10.5 0.1 copy.29
  10.7 15.7 %collective-permute-start.1 = (bf16[2,128,128]{2,1,0:T(8,128)(2,1)S(1)}, bf16[2,128,128]{2,1,0:T(8,128)(2,1)S(1)}, u32[]{:S(2)}, u32[]{:S(2)}) collective-permute-start(bf16[2,128,128]{2,1,0:T(8,128)(2,1)S(1)} %bitcast.44), channel_id=1, source_target_pairs={{0,8},{1,9},{2,10},{3,11},{4,12},{5,13},{6,14},{7,15},{8,0},{9,1},... | collective-permute-start | bytes 196616 | tf_op jit(solution)/shard_map/ppermute | solution.py:138
  26.4 4.3 %collective-permute-start = (bf16[2,128,128]{2,1,0:T(8,128)(2,1)S(1)}, bf16[2,128,128]{2,1,0:T(8,128)(2,1)S(1)}, u32[]{:S(2)}, u32[]{:S(2)}) collective-permute-start(bf16[2,128,128]{2,1,0:T(8,128)(2,1)S(1)} %bitcast.45), channel_id=1, source_target_pairs={{0,4},{1,5},{2,6},{3,7},{4,8},{5,9},{6,10},{7,11},{8,12},{9,13},{1... | collective-permute-start | bytes 196616 | tf_op jit(solution)/shard_map/ppermute | solution.py:138
  30.7 5.5 %collective-permute-start.2 = (bf16[2,128,128]{2,1,0:T(8,128)(2,1)S(1)}, bf16[2,128,128]{2,1,0:T(8,128)(2,1)S(1)}, u32[]{:S(2)}, u32[]{:S(2)}) collective-permute-start(bf16[2,128,128]{2,1,0:T(8,128)(2,1)S(1)} %bitcast.46), channel_id=1, source_target_pairs={{0,12},{1,13},{2,14},{3,15},{4,0},{5,1},{6,2},{7,3},{8,4},{9,5},{1... | collective-permute-start | bytes 196616 | tf_op jit(solution)/shard_map/ppermute | solution.py:138
  36.2 1.0 collective-permute-done
  37.2 6.7 %collective-permute-done.2 = bf16[2,128,128]{2,1,0:T(8,128)(2,1)S(1)} collective-permute-done((bf16[2,128,128]{2,1,0:T(8,128)(2,1)S(1)}, bf16[2,128,128]{2,1,0:T(8,128)(2,1)S(1)}, u32[]{:S(2)}, u32[]{:S(2)}) %collective-permute-start.2) | collective-permute-done | bytes 65568 | tf_op jit(solution)/shard_map/ppermute | solution.py:138
  43.9 3.1 %collective-permute-start.3 = (bf16[4,2,128,128]{3,2,1,0:T(8,128)(2,1)S(1)}, bf16[4,2,128,128]{3,2,1,0:T(8,128)(2,1)S(1)}, u32[]{:S(2)}, u32[]{:S(2)}) collective-permute-start(bf16[4,2,128,128]{3,2,1,0:T(8,128)(2,1)S(1)} %pad_maximum_fusion.3), channel_id=1, source_target_pairs={{0,16},{16,0},{1,17},{17,1},{2,18},{18,2},{3,19},{19,3},{4,20},{20... | collective-permute-start | bytes 786440 | tf_op jit(solution)/shard_map/ppermute | solution.py:142
  47.0 13.3 %collective-permute-done.3 = bf16[4,2,128,128]{3,2,1,0:T(8,128)(2,1)S(1)} collective-permute-done((bf16[4,2,128,128]{3,2,1,0:T(8,128)(2,1)S(1)}, bf16[4,2,128,128]{3,2,1,0:T(8,128)(2,1)S(1)}, u32[]{:S(2)}, u32[]{:S(2)}) %collective-permute-start.3) | collective-permute-done | bytes 262176 | tf_op jit(solution)/shard_map/ppermute | solution.py:142
  60.4 4.4 %collective-permute-start.5 = (bf16[4,4,128,128]{3,2,1,0:T(8,128)(2,1)S(1)}, bf16[4,4,128,128]{3,2,1,0:T(8,128)(2,1)S(1)}, u32[]{:S(2)}, u32[]{:S(2)}) collective-permute-start(bf16[4,4,128,128]{3,2,1,0:T(8,128)(2,1)S(1)} %pad_maximum_fusion.own), channel_id=1, source_target_pairs={{0,15},{1,0},{2,1},{3,2},{4,3},{5,4},{6,5},{7,6},{8,7},{9,8},{10,9... | collective-permute-start | bytes 1572872 | tf_op jit(solution)/shard_map/ppermute | solution.py:138
  64.8 1.9 collective-permute-start.4
  66.7 6.0 %collective-permute-done.5.right = bf16[4,4,128,128]{3,2,1,0:T(8,128)(2,1)S(1)} collective-permute-done((bf16[4,4,128,128]{3,2,1,0:T(8,128)(2,1)S(1)}, bf16[4,4,128,128]{3,2,1,0:T(8,128)(2,1)S(1)}, u32[]{:S(2)}, u32[]{:S(2)}) %collective-permute-start.5) | collective-permute-done | bytes 524320 | tf_op jit(solution)/shard_map/ppermute | solution.py:138
  72.8 5.1 %collective-permute-start.7 = (bf16[2,4,128,128]{3,2,1,0:T(8,128)(2,1)S(1)}, bf16[2,4,128,128]{3,2,1,0:T(8,128)(2,1)S(1)}, u32[]{:S(2)}, u32[]{:S(2)}) collective-permute-start(bf16[2,4,128,128]{3,2,1,0:T(8,128)(2,1)S(1)} %slice.74), channel_id=1, source_target_pairs={{0,15},{1,0},{2,1},{3,2},{4,3},{5,4},{6,5},{7,6},{8,7},{9,8},{10,9... | collective-permute-start | bytes 786440 | tf_op jit(solution)/shard_map/ppermute | solution.py:138
  77.9 1.9 collective-permute-start.6
  79.9 0.8 slice_convert_fusion
  80.7 1.1 collective-permute-done.7.far_right
  81.7 5.6 %collective-permute-done.6.far_left = bf16[2,4,128,128]{3,2,1,0:T(8,128)(2,1)S(1)} collective-permute-done((bf16[2,4,128,128]{3,2,1,0:T(8,128)(2,1)S(1)}, bf16[2,4,128,128]{3,2,1,0:T(8,128)(2,1)S(1)}, u32[]{:S(2)}, u32[]{:S(2)}) %collective-permute-start.6) | collective-permute-done | bytes 262176 | tf_op jit(solution)/shard_map/ppermute | solution.py:138
  87.4 2.2 %copy-done = bf16[16640,128]{1,0:T(8,128)(2,1)S(1)} copy-done((bf16[16640,128]{1,0:T(8,128)(2,1)S(1)}, bf16[16640,128]{1,0:T(8,128)(2,1)}, u32[]{:S(2)}) %copy-start) | copy-done | bytes 4259864
  89.6 0.9 copy-done.3
  90.5 11.0 %shard_map.67 = (bf16[128,1024]{1,0:T(8,128)(2,1)}, bf16[128,1024]{1,0:T(8,128)(2,1)S(1)}, bf16[16,8,128,128]{3,2,1,0:T(8,128)(2,1)S(1)}) custom-call(s32[16,8]{1,0:T(8,128)S(1)} %fusion.13.rows_ref, bf16[4,4,128,128]{3,2,1,0:T(8,128)(2,1)S(1)} %pad_maximum_fusion.own, bf16[4,4,128,128]{3,2,1,0:T(8,128)(2,1)S(1)} %collective-permute-done.4.left, ...), custom_call_target="tpu_custom_call" | custom-call | flops 1073741824 | bytes 11000000 | tf_op jit(solution)/shard_map/pallas_call | solution.py:90
  101.6 2.0 copy-done.2
  103.6 5.9 %all-to-all-start = ((bf16[16,8,128,128]{3,2,1,0:T(8,128)(2,1)}), bf16[16,8,128,128]{3,2,1,0:T(8,128)(2,1)}, u32[]{:S(2)}, u32[]{:S(2)}) async-start(bf16[16,8,128,128]{3,2,1,0:T(8,128)(2,1)} %copy-done.2), calls=%async_computation | async-start | bytes 8388608 | tf_op jit(solution)/shard_map/all_to_all | solution.py:176
  109.4 2.2 %copy-done.1 = bf16[16640,128]{1,0:T(8,128)(2,1)S(1)} copy-done((bf16[16640,128]{1,0:T(8,128)(2,1)S(1)}, bf16[16640,128]{1,0:T(8,128)(2,1)}, u32[]{:S(2)}) %copy-start.1) | copy-done | bytes 4259864
  111.6 4.9 %shard_map.68 = (bf16[4,4,128,128]{3,2,1,0:T(8,128)(2,1)S(1)}, bf16[4,4,128,128]{3,2,1,0:T(8,128)(2,1)S(1)}, bf16[4,4,128,128]{3,2,1,0:T(8,128)(2,1)S(1)}, bf16[...) custom-call(s32[16,8]{1,0:T(8,128)S(1)} %fusion.13.rows_ref, bf16[128,1024]{1,0:T(8,128)(2,1)S(1)} %get-tuple-element.24.gh_ref, ...), custom_call_target="tpu_custom_call" | custom-call | flops 536870912 | bytes 7000000 | tf_op jit(solution)/shard_map/pallas_call | solution.py:117
  116.5 1.9 collective-permute-start.10
  118.5 5.1 %collective-permute-start.8 = (bf16[2,4,128,128]{3,2,1,0:T(8,128)(2,1)S(1)}, bf16[2,4,128,128]{3,2,1,0:T(8,128)(2,1)S(1)}, u32[]{:S(2)}, u32[]{:S(2)}) collective-permute-start(bf16[2,4,128,128]{3,2,1,0:T(8,128)(2,1)S(1)} %get-tuple-element.27), channel_id=1, source_target_pairs={{0,15},{1,0},{2,1},{3,2},{4,3},{5,4},{6,5},{7,6},{8,7},{9,8},{10,9... | collective-permute-start | bytes 786440 | tf_op jit(solution)/shard_map/ppermute | solution.py:138
  123.6 4.3 %collective-permute-done.10 = bf16[2,4,128,128]{3,2,1,0:T(8,128)(2,1)S(1)} collective-permute-done((bf16[2,4,128,128]{3,2,1,0:T(8,128)(2,1)S(1)}, bf16[2,4,128,128]{3,2,1,0:T(8,128)(2,1)S(1)}, u32[]{:S(2)}, u32[]{:S(2)}) %collective-permute-start.10) | collective-permute-done | bytes 262176 | tf_op jit(solution)/shard_map/ppermute | solution.py:138
  128.0 0.1 add_convert_fusion.2
  128.1 1.9 collective-permute-start.11
  130.0 0.1 add_convert_fusion.3
  130.1 0.1 pad_maximum_fusion.1
  130.2 5.1 %collective-permute-start.9 = (bf16[4,4,128,128]{3,2,1,0:T(8,128)(2,1)S(1)}, bf16[4,4,128,128]{3,2,1,0:T(8,128)(2,1)S(1)}, u32[]{:S(2)}, u32[]{:S(2)}) collective-permute-start(bf16[4,4,128,128]{3,2,1,0:T(8,128)(2,1)S(1)} %pad_maximum_fusion.1), channel_id=1, source_target_pairs={{0,15},{1,0},{2,1},{3,2},{4,3},{5,4},{6,5},{7,6},{8,7},{9,8},{10,9... | collective-permute-start | bytes 1572872 | tf_op jit(solution)/shard_map/ppermute | solution.py:138
  135.3 9.1 %collective-permute-done.11 = bf16[4,4,128,128]{3,2,1,0:T(8,128)(2,1)S(1)} collective-permute-done((bf16[4,4,128,128]{3,2,1,0:T(8,128)(2,1)S(1)}, bf16[4,4,128,128]{3,2,1,0:T(8,128)(2,1)S(1)}, u32[]{:S(2)}, u32[]{:S(2)}) %collective-permute-start.11) | collective-permute-done | bytes 524320 | tf_op jit(solution)/shard_map/ppermute | solution.py:138
  144.5 1.3 collective-permute-done.9
  145.8 0.2 add_convert_fusion
  146.1 2.9 %collective-permute-start.12 = (bf16[4,2,128,128]{3,2,1,0:T(8,128)(2,1)S(1)}, bf16[4,2,128,128]{3,2,1,0:T(8,128)(2,1)S(1)}, u32[]{:S(2)}, u32[]{:S(2)}) collective-permute-start(bf16[4,2,128,128]{3,2,1,0:T(8,128)(2,1)S(1)} %slice.76), channel_id=1, source_target_pairs={{0,16},{16,0},{1,17},{17,1},{2,18},{18,2},{3,19},{19,3},{4,20},{20... | collective-permute-start | bytes 786440 | tf_op jit(solution)/shard_map/ppermute | solution.py:142
  148.9 15.4 %collective-permute-done.12 = bf16[4,2,128,128]{3,2,1,0:T(8,128)(2,1)S(1)} collective-permute-done((bf16[4,2,128,128]{3,2,1,0:T(8,128)(2,1)S(1)}, bf16[4,2,128,128]{3,2,1,0:T(8,128)(2,1)S(1)}, u32[]{:S(2)}, u32[]{:S(2)}) %collective-permute-start.12) | collective-permute-done | bytes 262176 | tf_op jit(solution)/shard_map/ppermute | solution.py:142
  164.3 0.1 add_convert_fusion.1
  164.4 5.5 %collective-permute-start.13 = (bf16[2,128,128]{2,1,0:T(8,128)(2,1)S(1)}, bf16[2,128,128]{2,1,0:T(8,128)(2,1)S(1)}, u32[]{:S(2)}, u32[]{:S(2)}) collective-permute-start(bf16[2,128,128]{2,1,0:T(8,128)(2,1)S(1)} %get-tuple-element.42), channel_id=1, source_target_pairs={{0,12},{1,13},{2,14},{3,15},{4,0},{5,1},{6,2},{7,3},{8,4},{9,5},{1... | collective-permute-start | bytes 196616 | tf_op jit(solution)/shard_map/ppermute | solution.py:138
  169.9 4.2 %collective-permute-start.15 = (bf16[2,128,128]{2,1,0:T(8,128)(2,1)S(1)}, bf16[2,128,128]{2,1,0:T(8,128)(2,1)S(1)}, u32[]{:S(2)}, u32[]{:S(2)}) collective-permute-start(bf16[2,128,128]{2,1,0:T(8,128)(2,1)S(1)} %get-tuple-element.43), channel_id=1, source_target_pairs={{0,4},{1,5},{2,6},{3,7},{4,8},{5,9},{6,10},{7,11},{8,12},{9,13},{1... | collective-permute-start | bytes 196616 | tf_op jit(solution)/shard_map/ppermute | solution.py:138
  174.2 7.9 %collective-permute-start.14 = (bf16[2,128,128]{2,1,0:T(8,128)(2,1)S(1)}, bf16[2,128,128]{2,1,0:T(8,128)(2,1)S(1)}, u32[]{:S(2)}, u32[]{:S(2)}) collective-permute-start(bf16[2,128,128]{2,1,0:T(8,128)(2,1)S(1)} %get-tuple-element.44), channel_id=1, source_target_pairs={{0,8},{1,9},{2,10},{3,11},{4,12},{5,13},{6,14},{7,15},{8,0},{9,1},... | collective-permute-start | bytes 196616 | tf_op jit(solution)/shard_map/ppermute | solution.py:138
  182.1 9.1 %collective-permute-done.14 = bf16[2,128,128]{2,1,0:T(8,128)(2,1)S(1)} collective-permute-done((bf16[2,128,128]{2,1,0:T(8,128)(2,1)S(1)}, bf16[2,128,128]{2,1,0:T(8,128)(2,1)S(1)}, u32[]{:S(2)}, u32[]{:S(2)}) %collective-permute-start.14) | collective-permute-done | bytes 65568 | tf_op jit(solution)/shard_map/ppermute | solution.py:138
  191.2 0.1 copy.30
  191.3 0.7 copy.31
  192.1 2.8 %fusion.3 = bf16[8,1,128,128]{2,3,0,1:T(8,128)(2,1)S(1)} fusion(bf16[16,8,128,128]{3,2,1,0:T(8,128)(2,1)} %all-to-all-done), kind=kLoop, calls=%fused_computation.14 | loop fusion | flops 4194304 | bytes 4456448 | tf_op jit(solution)/shard_map/broadcast_in_dim | solution.py:180
  194.8 0.9 copy.32
  (24 shorter events, 0.4 us)
Async XLA Ops:
  7.2 72.7 %all-gather.3.cloned.1.call-start = ((), (), s32[]{:S(2)}) async-start(), calls=%async_computation.1 | async-start | bytes 4526080 | tf_op jit(solution)/shard_map/all_gather | solution.py:170
  10.7 25.5 %collective-permute-start.1 = (bf16[2,128,128]{2,1,0:T(8,128)(2,1)S(1)}, bf16[2,128,128]{2,1,0:T(8,128)(2,1)S(1)}, u32[]{:S(2)}, u32[]{:S(2)}) collective-permute-start(bf16[2,128,128]{2,1,0:T(8,128)(2,1)S(1)} %bitcast.44), channel_id=1, source_target_pairs={{0,8},{1,9},{2,10},{3,11},{4,12},{5,13},{6,14},{7,15},{8,0},{9,1},... | collective-permute-start | bytes 196616 | tf_op jit(solution)/shard_map/ppermute | solution.py:138
  26.4 10.8 %collective-permute-start = (bf16[2,128,128]{2,1,0:T(8,128)(2,1)S(1)}, bf16[2,128,128]{2,1,0:T(8,128)(2,1)S(1)}, u32[]{:S(2)}, u32[]{:S(2)}) collective-permute-start(bf16[2,128,128]{2,1,0:T(8,128)(2,1)S(1)} %bitcast.45), channel_id=1, source_target_pairs={{0,4},{1,5},{2,6},{3,7},{4,8},{5,9},{6,10},{7,11},{8,12},{9,13},{1... | collective-permute-start | bytes 196616 | tf_op jit(solution)/shard_map/ppermute | solution.py:138
  30.7 13.2 %collective-permute-start.2 = (bf16[2,128,128]{2,1,0:T(8,128)(2,1)S(1)}, bf16[2,128,128]{2,1,0:T(8,128)(2,1)S(1)}, u32[]{:S(2)}, u32[]{:S(2)}) collective-permute-start(bf16[2,128,128]{2,1,0:T(8,128)(2,1)S(1)} %bitcast.46), channel_id=1, source_target_pairs={{0,12},{1,13},{2,14},{3,15},{4,0},{5,1},{6,2},{7,3},{8,4},{9,5},{1... | collective-permute-start | bytes 196616 | tf_op jit(solution)/shard_map/ppermute | solution.py:138
  43.9 16.4 %collective-permute-start.3 = (bf16[4,2,128,128]{3,2,1,0:T(8,128)(2,1)S(1)}, bf16[4,2,128,128]{3,2,1,0:T(8,128)(2,1)S(1)}, u32[]{:S(2)}, u32[]{:S(2)}) collective-permute-start(bf16[4,2,128,128]{3,2,1,0:T(8,128)(2,1)S(1)} %pad_maximum_fusion.3), channel_id=1, source_target_pairs={{0,16},{16,0},{1,17},{17,1},{2,18},{18,2},{3,19},{19,3},{4,20},{20... | collective-permute-start | bytes 786440 | tf_op jit(solution)/shard_map/ppermute | solution.py:142
  60.4 12.4 %collective-permute-start.5 = (bf16[4,4,128,128]{3,2,1,0:T(8,128)(2,1)S(1)}, bf16[4,4,128,128]{3,2,1,0:T(8,128)(2,1)S(1)}, u32[]{:S(2)}, u32[]{:S(2)}) collective-permute-start(bf16[4,4,128,128]{3,2,1,0:T(8,128)(2,1)S(1)} %pad_maximum_fusion.own), channel_id=1, source_target_pairs={{0,15},{1,0},{2,1},{3,2},{4,3},{5,4},{6,5},{7,6},{8,7},{9,8},{10,9... | collective-permute-start | bytes 1572872 | tf_op jit(solution)/shard_map/ppermute | solution.py:138
  64.8 13.1 %collective-permute-start.4 = (bf16[4,4,128,128]{3,2,1,0:T(8,128)(2,1)S(1)}, bf16[4,4,128,128]{3,2,1,0:T(8,128)(2,1)S(1)}, u32[]{:S(2)}, u32[]{:S(2)}) collective-permute-start(bf16[4,4,128,128]{3,2,1,0:T(8,128)(2,1)S(1)} %pad_maximum_fusion.own), channel_id=1, source_target_pairs={{0,1},{1,2},{2,3},{3,4},{4,5},{5,6},{6,7},{7,8},{8,9},{9,10},{10,1... | collective-permute-start | bytes 1572872 | tf_op jit(solution)/shard_map/ppermute | solution.py:138
  72.8 9.0 %collective-permute-start.7 = (bf16[2,4,128,128]{3,2,1,0:T(8,128)(2,1)S(1)}, bf16[2,4,128,128]{3,2,1,0:T(8,128)(2,1)S(1)}, u32[]{:S(2)}, u32[]{:S(2)}) collective-permute-start(bf16[2,4,128,128]{3,2,1,0:T(8,128)(2,1)S(1)} %slice.74), channel_id=1, source_target_pairs={{0,15},{1,0},{2,1},{3,2},{4,3},{5,4},{6,5},{7,6},{8,7},{9,8},{10,9... | collective-permute-start | bytes 786440 | tf_op jit(solution)/shard_map/ppermute | solution.py:138
  77.9 9.5 %collective-permute-start.6 = (bf16[2,4,128,128]{3,2,1,0:T(8,128)(2,1)S(1)}, bf16[2,4,128,128]{3,2,1,0:T(8,128)(2,1)S(1)}, u32[]{:S(2)}, u32[]{:S(2)}) collective-permute-start(bf16[2,4,128,128]{3,2,1,0:T(8,128)(2,1)S(1)} %slice.73), channel_id=1, source_target_pairs={{0,1},{1,2},{2,3},{3,4},{4,5},{5,6},{6,7},{7,8},{8,9},{9,10},{10,1... | collective-permute-start | bytes 786440 | tf_op jit(solution)/shard_map/ppermute | solution.py:138
  87.4 2.2 %copy-start = (bf16[16640,128]{1,0:T(8,128)(2,1)S(1)}, bf16[16640,128]{1,0:T(8,128)(2,1)}, u32[]{:S(2)}) copy-start(bf16[16640,128]{1,0:T(8,128)(2,1)} %all-gather.3.cloned.1.call-done) | copy-start | bytes 12779524
  89.6 0.9 copy-start.3
  101.6 2.0 copy-start.2
  103.6 88.5 %all-to-all-start = ((bf16[16,8,128,128]{3,2,1,0:T(8,128)(2,1)}), bf16[16,8,128,128]{3,2,1,0:T(8,128)(2,1)}, u32[]{:S(2)}, u32[]{:S(2)}) async-start(bf16[16,8,128,128]{3,2,1,0:T(8,128)(2,1)} %copy-done.2), calls=%async_computation | async-start | bytes 8388608 | tf_op jit(solution)/shard_map/all_to_all | solution.py:176
  109.4 2.2 %copy-start.1 = (bf16[16640,128]{1,0:T(8,128)(2,1)S(1)}, bf16[16640,128]{1,0:T(8,128)(2,1)}, u32[]{:S(2)}) copy-start(bf16[16640,128]{1,0:T(8,128)(2,1)} %all-gather.3.cloned.1.call-done) | copy-start | bytes 12779524
  116.5 11.5 %collective-permute-start.10 = (bf16[2,4,128,128]{3,2,1,0:T(8,128)(2,1)S(1)}, bf16[2,4,128,128]{3,2,1,0:T(8,128)(2,1)S(1)}, u32[]{:S(2)}, u32[]{:S(2)}) collective-permute-start(bf16[2,4,128,128]{3,2,1,0:T(8,128)(2,1)S(1)} %get-tuple-element.29), channel_id=1, source_target_pairs={{0,1},{1,2},{2,3},{3,4},{4,5},{5,6},{6,7},{7,8},{8,9},{9,10},{10,1... | collective-permute-start | bytes 786440 | tf_op jit(solution)/shard_map/ppermute | solution.py:138
  118.5 11.6 %collective-permute-start.8 = (bf16[2,4,128,128]{3,2,1,0:T(8,128)(2,1)S(1)}, bf16[2,4,128,128]{3,2,1,0:T(8,128)(2,1)S(1)}, u32[]{:S(2)}, u32[]{:S(2)}) collective-permute-start(bf16[2,4,128,128]{3,2,1,0:T(8,128)(2,1)S(1)} %get-tuple-element.27), channel_id=1, source_target_pairs={{0,15},{1,0},{2,1},{3,2},{4,3},{5,4},{6,5},{7,6},{8,7},{9,8},{10,9... | collective-permute-start | bytes 786440 | tf_op jit(solution)/shard_map/ppermute | solution.py:138
  128.1 16.4 %collective-permute-start.11 = (bf16[4,4,128,128]{3,2,1,0:T(8,128)(2,1)S(1)}, bf16[4,4,128,128]{3,2,1,0:T(8,128)(2,1)S(1)}, u32[]{:S(2)}, u32[]{:S(2)}) collective-permute-start(bf16[4,4,128,128]{3,2,1,0:T(8,128)(2,1)S(1)} %pad_maximum_fusion.2), channel_id=1, source_target_pairs={{0,1},{1,2},{2,3},{3,4},{4,5},{5,6},{6,7},{7,8},{8,9},{9,10},{10,1... | collective-permute-start | bytes 1572872 | tf_op jit(solution)/shard_map/ppermute | solution.py:138
  130.2 15.6 %collective-permute-start.9 = (bf16[4,4,128,128]{3,2,1,0:T(8,128)(2,1)S(1)}, bf16[4,4,128,128]{3,2,1,0:T(8,128)(2,1)S(1)}, u32[]{:S(2)}, u32[]{:S(2)}) collective-permute-start(bf16[4,4,128,128]{3,2,1,0:T(8,128)(2,1)S(1)} %pad_maximum_fusion.1), channel_id=1, source_target_pairs={{0,15},{1,0},{2,1},{3,2},{4,3},{5,4},{6,5},{7,6},{8,7},{9,8},{10,9... | collective-permute-start | bytes 1572872 | tf_op jit(solution)/shard_map/ppermute | solution.py:138
  146.1 18.2 %collective-permute-start.12 = (bf16[4,2,128,128]{3,2,1,0:T(8,128)(2,1)S(1)}, bf16[4,2,128,128]{3,2,1,0:T(8,128)(2,1)S(1)}, u32[]{:S(2)}, u32[]{:S(2)}) collective-permute-start(bf16[4,2,128,128]{3,2,1,0:T(8,128)(2,1)S(1)} %slice.76), channel_id=1, source_target_pairs={{0,16},{16,0},{1,17},{17,1},{2,18},{18,2},{3,19},{19,3},{4,20},{20... | collective-permute-start | bytes 786440 | tf_op jit(solution)/shard_map/ppermute | solution.py:142
  164.4 17.7 %collective-permute-start.13 = (bf16[2,128,128]{2,1,0:T(8,128)(2,1)S(1)}, bf16[2,128,128]{2,1,0:T(8,128)(2,1)S(1)}, u32[]{:S(2)}, u32[]{:S(2)}) collective-permute-start(bf16[2,128,128]{2,1,0:T(8,128)(2,1)S(1)} %get-tuple-element.42), channel_id=1, source_target_pairs={{0,12},{1,13},{2,14},{3,15},{4,0},{5,1},{6,2},{7,3},{8,4},{9,5},{1... | collective-permute-start | bytes 196616 | tf_op jit(solution)/shard_map/ppermute | solution.py:138
  169.9 12.1 %collective-permute-start.15 = (bf16[2,128,128]{2,1,0:T(8,128)(2,1)S(1)}, bf16[2,128,128]{2,1,0:T(8,128)(2,1)S(1)}, u32[]{:S(2)}, u32[]{:S(2)}) collective-permute-start(bf16[2,128,128]{2,1,0:T(8,128)(2,1)S(1)} %get-tuple-element.43), channel_id=1, source_target_pairs={{0,4},{1,5},{2,6},{3,7},{4,8},{5,9},{6,10},{7,11},{8,12},{9,13},{1... | collective-permute-start | bytes 196616 | tf_op jit(solution)/shard_map/ppermute | solution.py:138
  174.2 17.0 %collective-permute-start.14 = (bf16[2,128,128]{2,1,0:T(8,128)(2,1)S(1)}, bf16[2,128,128]{2,1,0:T(8,128)(2,1)S(1)}, u32[]{:S(2)}, u32[]{:S(2)}) collective-permute-start(bf16[2,128,128]{2,1,0:T(8,128)(2,1)S(1)} %get-tuple-element.44), channel_id=1, source_target_pairs={{0,8},{1,9},{2,10},{3,11},{4,12},{5,13},{6,14},{7,15},{8,0},{9,1},... | collective-permute-start | bytes 196616 | tf_op jit(solution)/shard_map/ppermute | solution.py:138
Sparse Core Ops, SparseCore 0:
  10.1 52.9 all-gather.2

commit v3 on v2

v3 whole, which is shorter than its diff:
```python
import jax
import jax.numpy as jnp
from jax import lax
from jax.experimental import pallas as pl
from jax.experimental.pallas import tpu as pltpu
from jax.sharding import Mesh
from jax.sharding import PartitionSpec as P

SQRT_TWO_PI = 0.7978845608028654
CUBIC = 0.044715
AXES = ("x", "yl", "core", "yh", "zh", "zl")
SIZES = (4, 2, 2, 2, 4, 4)
SEQ = ("x", "yl", "core")
FAR = ("yh", "zh")
MP = ("yh", "zh", "zl")
Z = ("zh", "zl")
BF16, F32 = jnp.bfloat16, jnp.float32
OWN, RIGHT, FAR_LEFT, FAR_RIGHT, LEFT = (0, 16), (16, 16), (32, 8), (40, 8), (48, 16)
PARTS = (OWN, LEFT, RIGHT, FAR_LEFT, FAR_RIGHT)


def gelu_parts(hidden):
    inner_arg = SQRT_TWO_PI * (hidden + CUBIC * hidden * hidden * hidden)
    tanh_inner = jnp.tanh(inner_arg)
    gelu_value = 0.5 * hidden * (1.0 + tanh_inner)
    gelu_slope = 0.5 * (1.0 + tanh_inner) + 0.5 * hidden * (
        1.0 - tanh_inner * tanh_inner
    ) * SQRT_TWO_PI * (1.0 + 3.0 * CUBIC * hidden * hidden)
    return gelu_value, gelu_slope


def fetch_columns(w_ref, w_all, w_sem):
    for c in range(w_ref.shape[1] // 128):
        own = (slice(None), slice(c * 128, (c + 1) * 128))
        pltpu.make_async_copy(w_ref.at[own], w_all.at[:, c], w_sem.at[c]).start()


def await_column(w_ref, w_all, w_sem, c):
    pltpu.make_async_copy(w_ref.at[:, pl.ds(0, 128)], w_all.at[:, c], w_sem.at[c]).wait()


def hidden_kernel(
    rows_ref, core_ref, own, left, right, far_left, far_right, w_ref, gact_ref, act_ref, gh_ref, keep_ref, give_ref, tok, w_all, sem, w_sem
):
    c = pl.program_id(0)
    half = keep_ref.shape[0]

    @pl.when(c == 0)
    def _():
        copies = [
            pltpu.make_async_copy(ref, tok.at[pl.ds(start, size)], sem.at[i])
            for i, (ref, (start, size)) in enumerate(zip((own, left, right, far_left, far_right), PARTS))
        ]
        for copy in copies:
            copy.start()
        fetch_columns(w_ref, w_all, w_sem)
        for copy in copies:
            copy.wait()

    await_column(w_ref, w_all, w_sem, c)
    core = core_ref[0]
    slots = [2 * j + core for j in range(half)] + [2 * j + 1 - core for j in range(half)]
    weights = jnp.concatenate([w_all[k, c] for k in slots], axis=0)
    picked = jnp.concatenate([tok[rows_ref[k, c]] for k in slots], axis=1)
    hidden = jnp.dot(picked, weights, preferred_element_type=F32)
    value, slope = gelu_parts(hidden)
    act_ref[...] = value.astype(BF16)
    grad_hidden = (gact_ref[...].astype(F32) * slope).astype(BF16)
    gh_ref[...] = grad_hidden
    grads = lax.dot_general(
        grad_hidden, picked, (((0,), (0,)), ((), ())), preferred_element_type=F32
    ).astype(BF16)
    for j in range(half):
        keep_ref[j, 0] = grads[:, j * 128 : (j + 1) * 128]
        give_ref[j, 0] = grads[:, (half + j) * 128 : (half + j + 1) * 128]


def term_kernel(rows_ref, gh_ref, w_ref, own, left, right, far_left, far_right, acc, w_all, w_sem):
    c = pl.program_id(0)
    kept = w_ref.shape[0]

    @pl.when(c == 0)
    def _():
        fetch_columns(w_ref, w_all, w_sem)
        acc[...] = jnp.zeros_like(acc)

    await_column(w_ref, w_all, w_sem, c)
    weights = jnp.concatenate([w_all[k, c] for k in range(kept)], axis=0)
    part = lax.dot_general(
        gh_ref[...], weights, (((1,), (1,)), ((), ())), preferred_element_type=F32
    )
    for k in range(kept):
        acc[rows_ref[k, c]] += part[:, k * 128 : (k + 1) * 128]

    @pl.when(c == pl.num_programs(0) - 1)
    def _():
        for ref, (start, size) in zip((own, left, right, far_left, far_right), PARTS):
            ref[...] = acc[start : start + size].astype(BF16)


def hidden_call(rows, core, parts, weights, grad_act):
    kept, cols = rows.shape
    n_tok = grad_act.shape[0]
    column = pl.BlockSpec((n_tok, 128), lambda c, *_: (0, c))
    half = pl.BlockSpec((kept // 2, 1, 128, 128), lambda c, *_: (0, c, 0, 0))
    wide = jax.ShapeDtypeStruct((n_tok, cols * 128), BF16)
    grads = jax.ShapeDtypeStruct((kept // 2, cols, 128, 128), BF16)
    return pl.pallas_call(
        hidden_kernel,
        grid_spec=pltpu.PrefetchScalarGridSpec(
            num_scalar_prefetch=2,
            grid=(cols,),
            in_specs=[pl.BlockSpec(memory_space=pl.ANY)] * 5
            + [pl.BlockSpec(memory_space=pltpu.HBM), column],
            out_specs=[column, column, half, half],
            scratch_shapes=[
                pltpu.VMEM((64, n_tok, 128), BF16),
                pltpu.VMEM((kept, cols, 128, 128), BF16),
                pltpu.SemaphoreType.DMA((5,)),
                pltpu.SemaphoreType.DMA((cols,)),
            ],
        ),
        out_shape=[wide, wide, grads, grads],
        compiler_params=pltpu.CompilerParams(vmem_limit_bytes=18 * 2**20),
        cost_estimate=pl.CostEstimate(flops=1_073_741_824, bytes_accessed=11_000_000, transcendentals=131072),
    )(rows, core, *parts, weights, grad_act)


def term_call(rows, grad_hidden, weights):
    kept, cols = rows.shape
    n_tok = grad_hidden.shape[0]
    return pl.pallas_call(
        term_kernel,
        grid_spec=pltpu.PrefetchScalarGridSpec(
            num_scalar_prefetch=1,
            grid=(cols,),
            in_specs=[
                pl.BlockSpec((n_tok, 128), lambda c, rows: (0, c)),
                pl.BlockSpec(memory_space=pltpu.HBM),
            ],
            out_specs=[pl.BlockSpec((n, n_tok, 128), lambda c, rows: (0, 0, 0)) for _, n in PARTS],
            scratch_shapes=[
                pltpu.VMEM((64, n_tok, 128), F32),
                pltpu.VMEM((kept, cols, 128, 128), BF16),
                pltpu.SemaphoreType.DMA((cols,)),
            ],
        ),
        out_shape=[jax.ShapeDtypeStruct((n, n_tok, 128), BF16) for _, n in PARTS],
        compiler_params=pltpu.CompilerParams(vmem_limit_bytes=20 * 2**20),
        cost_estimate=pl.CostEstimate(flops=536_870_912, bytes_accessed=7_000_000, transcendentals=0),
    )(rows, grad_hidden, weights)


def shift(a, by):
    return lax.ppermute(a, Z, [(i, (i + by) % 16) for i in range(16)])


def total(*arrays):
    return sum(a.astype(F32) for a in arrays)


def gather_tokens(mine):
    own = lax.all_to_all(jnp.broadcast_to(mine, (8,) + mine.shape), FAR, 0, 0)
    own = own.reshape((16,) + mine.shape[1:])
    left, right = shift(own, 1), shift(own, -1)
    return own, left, right, shift(left[:8], 1), shift(right[8:], -1)


def combine_kernel(own_ref, left_ref, right_ref, grads_ref, own_out, grads_out):
    own_out[...] = total(own_ref[...], left_ref[...], right_ref[...]).astype(BF16)
    for c in range(grads_ref.shape[1]):
        summed = sum(grads_ref[i, c].astype(F32) for i in range(grads_ref.shape[0]))
        grads_out[c] = summed.T.astype(BF16)


def add_kernel(keep_ref, got_ref, after_ref, both_ref):
    both_ref[...] = total(keep_ref[...], got_ref[...]).astype(BF16)


def add_after(keep, got, after):
    block = pl.BlockSpec((2,) + keep.shape[1:], lambda i: (i, 0, 0, 0))
    return pl.pallas_call(
        add_kernel,
        grid=(keep.shape[0] // 2,),
        in_specs=[block, block, pl.BlockSpec(memory_space=pl.ANY)],
        out_specs=block,
        out_shape=jax.ShapeDtypeStruct(keep.shape, BF16),
        compiler_params=pltpu.CompilerParams(vmem_limit_bytes=8 * 2**20),
        cost_estimate=pl.CostEstimate(flops=1_000_000, bytes_accessed=6_300_000, transcendentals=0),
    )(keep, got, after)


def reduce_all(keep, give, own, left, right, far_left, far_right):
    from_right, from_left = shift(far_left, -1), shift(far_right, 1)
    both = add_after(keep, lax.ppermute(give, "core", [(0, 1), (1, 0)]), own)
    grads = lax.all_to_all(both, ("x", "yl"), 0, 0)
    left = jnp.concatenate([total(left[:8], from_right).astype(BF16), left[8:]])
    right = jnp.concatenate([right[:8], total(right[8:], from_left).astype(BF16)])
    own, grads = pl.pallas_call(
        combine_kernel,
        out_shape=[
            jax.ShapeDtypeStruct(own.shape, BF16),
            jax.ShapeDtypeStruct(grads.shape[1:], BF16),
        ],
        compiler_params=pltpu.CompilerParams(vmem_limit_bytes=12 * 2**20),
        cost_estimate=pl.CostEstimate(flops=2_000_000, bytes_accessed=4_500_000, transcendentals=0),
    )(own, shift(left, -1), shift(right, 1), grads)
    own = lax.all_to_all(own.reshape((8, 2) + own.shape[1:]), FAR, 0, 0)
    return total(*own).astype(BF16), grads[:, None]


def shards(tokens, block_values, block_rows, grad_act):
    n_tok = tokens.shape[0]
    cols = block_values.shape[0]
    parts = gather_tokens(tokens.reshape(n_tok, 2, 128).transpose(1, 0, 2))
    row_tile = jnp.zeros((16, 128), BF16).at[0, :cols].set(block_rows[:, 0].astype(BF16))
    sent = jnp.concatenate([block_values.reshape(cols * 128, 128), row_tile])
    weights = lax.all_gather(sent, SEQ, axis=0)
    rows = weights[:, cols * 128, :cols].astype(jnp.int32)
    rows = (rows // 2 - lax.axis_index("zl")) % 4 * 16 + rows // 32 * 8 + rows % 32 // 8 * 2 + rows % 2
    core = lax.axis_index("core").reshape(1)
    activated, grad_hidden, keep, give = hidden_call(rows, core, parts, weights, grad_act)
    terms = term_call(rows, grad_hidden, weights)
    summed, grads = reduce_all(keep, give, *terms)
    return activated, summed.transpose(1, 0, 2).reshape(n_tok, 256), grads


def solution(mesh):
    fine = Mesh(mesh.devices.reshape(SIZES), AXES)
    in_specs = (P(SEQ, MP), P(MP, SEQ, None, None), P(MP, SEQ), P(SEQ, MP))
    out_specs = (P(SEQ, MP), P(SEQ, MP), P(MP, SEQ, None, None))
    return jax.shard_map(shards, mesh=fine, in_specs=in_specs, out_specs=out_specs, check_vma=False)
```

time: 206 us -> 190 us (0.922)
  the two profiles are of different devices: /device:TPU:24 before, /device:TPU:1 now
where the time goes in v3:
time: 190 us; the launch traced here: 189 us
  blocking collectives  82.5 us (43%)
  starting transfers between devices  37.9 us (20%)
  waiting for transfers between devices  27 us (14%)
  between operations  14.3 us (8%)
  Pallas kernels  13.2 us (7%)
  local copies, waits for them, and re-layouts  8.93 us (5%)
  other arithmetic  5.07 us (3%)
    all_to_all x1, blocking collectives, gather_tokens(): own = lax.all_to_all(jnp.broadcast_to(mine, (8,) + mine.shape), FAR, 0, 0)  46.5 us
    all_to_all x1, blocking collectives, reduce_all(): own = lax.all_to_all(own.reshape((8, 2) + own.shape[1:]), FAR, 0, 0)  35.9 us
    ppermute x8, starting transfers between devices, shift(): return lax.ppermute(a, Z, [(i, (i + by) % 16) for i in range(16)])  27.3 us
    ppermute x8, waiting for transfers between devices, shift(): return lax.ppermute(a, Z, [(i, (i + by) % 16) for i in range(16)])  25 us
    pallas_call x1, Pallas kernels, hidden_call(): pl.pallas_call(hidden_kernel, grid_spec=pltpu.PrefetchScalarGridSpec(num_...  7.32 us
    unnamed x20, local copies, waits for them, and re-layouts  6.88 us
    ppermute x1, starting transfers between devices, reduce_all(): both = add_after(keep, lax.ppermute(give, 'core', [(0, 1), (1, 0)]), own)  6.35 us
    pallas_call x1, Pallas kernels, term_call(): pl.pallas_call(term_kernel, grid_spec=pltpu.PrefetchScalarGridSpec(num_sc...  4.28 us
  transfers between devices with their start and end apart: 11, of which 7 were waited for; matrix products, arithmetic and copies ran while one was open for 2% of the time, Pallas kernels for 2%

profile of v3, /device:TPU:1, one launch (start us, length us, event | category | flops | bytes accessed | tf_op | source)
XLA Modules:
  0.0 188.8 jit_solution(5839513241795144732)
XLA Ops:
  7.2 0.0 all-gather.3.cloned.1.call-start
  7.2 0.7 convert_bitcast_fusion
  7.9 1.7 fusion.1
  9.6 0.0 all-gather.3.cloned.1.call-update
  9.6 0.9 reshape.79
  10.5 0.1 broadcast_in_dim.7
  10.6 46.5 %all_to_all.15 = bf16[8,2,128,128]{3,2,1,0:T(8,128)(2,1)S(1)} all-to-all(bf16[8,2,128,128]{3,2,1,0:T(8,128)(2,1)S(1)} %broadcast_in_dim.7), channel_id=1, replica_groups=mesh['x'=4,'yl'=2,'core'=2,'yh'=2,'zh'=4,'zl'=4] {'yh','zh'}, dimensions={0} | all-to-all | bytes 1048576 | tf_op jit(solution)/shard_map/all_to_all | solution.py:163
  57.1 4.2 %collective-permute-start.1 = (bf16[16,128,128]{2,1,0:T(8,128)(2,1)S(1)}, bf16[16,128,128]{2,1,0:T(8,128)(2,1)S(1)}, u32[]{:S(2)}, u32[]{:S(2)}) collective-permute-start(bf16[16,128,128]{2,1,0:T(8,128)(2,1)S(1)} %bitcast.23), channel_id=1, source_target_pairs={{0,15},{1,0},{2,1},{3,2},{4,3},{5,4},{6,5},{7,6},{8,7},{9,8},{10,9... | collective-permute-start | bytes 1572872 | tf_op jit(solution)/shard_map/ppermute | solution.py:155
  61.4 4.8 %collective-permute-start = (bf16[16,128,128]{2,1,0:T(8,128)(2,1)S(1)}, bf16[16,128,128]{2,1,0:T(8,128)(2,1)S(1)}, u32[]{:S(2)}, u32[]{:S(2)}) collective-permute-start(bf16[16,128,128]{2,1,0:T(8,128)(2,1)S(1)} %bitcast.24), channel_id=1, source_target_pairs={{0,1},{1,2},{2,3},{3,4},{4,5},{5,6},{6,7},{7,8},{8,9},{9,10},{10,1... | collective-permute-start | bytes 1572872 | tf_op jit(solution)/shard_map/ppermute | solution.py:155
  66.2 7.7 %collective-permute-done.1.right = bf16[16,128,128]{2,1,0:T(8,128)(2,1)S(1)} collective-permute-done((bf16[16,128,128]{2,1,0:T(8,128)(2,1)S(1)}, bf16[16,128,128]{2,1,0:T(8,128)(2,1)S(1)}, u32[]{:S(2)}, u32[]{:S(2)}) %collective-permute-start.1) | collective-permute-done | bytes 524320 | tf_op jit(solution)/shard_map/ppermute | solution.py:155
  73.9 1.9 %collective-permute-start.3 = (bf16[8,128,128]{2,1,0:T(8,128)(2,1)S(1)}, bf16[8,128,128]{2,1,0:T(8,128)(2,1)S(1)}, u32[]{:S(2)}, u32[]{:S(2)}) collective-permute-start(bf16[8,128,128]{2,1,0:T(8,128)(2,1)S(1)} %slice.46), channel_id=1, source_target_pairs={{0,15},{1,0},{2,1},{3,2},{4,3},{5,4},{6,5},{7,6},{8,7},{9,8},{10,9... | collective-permute-start | bytes 786440 | tf_op jit(solution)/shard_map/ppermute | solution.py:155
  75.9 0.0 collective-permute-done.left
  75.9 3.4 %collective-permute-start.2 = (bf16[8,128,128]{2,1,0:T(8,128)(2,1)S(1)}, bf16[8,128,128]{2,1,0:T(8,128)(2,1)S(1)}, u32[]{:S(2)}, u32[]{:S(2)}) collective-permute-start(bf16[8,128,128]{2,1,0:T(8,128)(2,1)S(1)} %slice.45), channel_id=1, source_target_pairs={{0,1},{1,2},{2,3},{3,4},{4,5},{5,6},{6,7},{7,8},{8,9},{9,10},{10,1... | collective-permute-start | bytes 786440 | tf_op jit(solution)/shard_map/ppermute | solution.py:155
  79.3 0.0 all-gather.3.cloned.1.call-done
  79.3 0.8 slice_convert_fusion
  80.1 1.0 collective-permute-done.3.far_right
  81.1 3.2 %collective-permute-done.2.far_left = bf16[8,128,128]{2,1,0:T(8,128)(2,1)S(1)} collective-permute-done((bf16[8,128,128]{2,1,0:T(8,128)(2,1)S(1)}, bf16[8,128,128]{2,1,0:T(8,128)(2,1)S(1)}, u32[]{:S(2)}, u32[]{:S(2)}) %collective-permute-start.2) | collective-permute-done | bytes 262176 | tf_op jit(solution)/shard_map/ppermute | solution.py:155
  84.2 0.0 copy-done.8
  84.2 2.2 %copy-done = bf16[16640,128]{1,0:T(8,128)(2,1)S(1)} copy-done((bf16[16640,128]{1,0:T(8,128)(2,1)S(1)}, bf16[16640,128]{1,0:T(8,128)(2,1)}, u32[]{:S(2)}) %copy-start) | copy-done | bytes 4259864
  86.4 7.3 %shard_map.67 = (bf16[128,1024]{1,0:T(8,128)(2,1)}, bf16[128,1024]{1,0:T(8,128)(2,1)S(1)}, bf16[8,8,128,128]{3,2,1,0:T(8,128)(2,1)S(1)}, bf16[8,8,128,128]{3,2,1,0:T(8,128)(2,1)S(1)}) custom-call(s32[16,8]{1,0:T(8,128)S(1)} %fusion.8.rows_ref, s32[1]{0:T(128)} %bitcast.4.core_ref, bf16[16,128,128]{2,1,0:T(8,128)(2,1)S(1)} %bitcast.25, ...), custom_call_target="tpu_custom_call" | custom-call | flops 1073741824 | bytes 11000000 | tf_op jit(solution)/shard_map/pallas_call | solution.py:108
  93.8 6.3 %collective-permute-start.8 = (bf16[8,8,128,128]{3,2,1,0:T(8,128)(2,1)S(1)}, bf16[8,8,128,128]{3,2,1,0:T(8,128)(2,1)S(1)}, u32[]{:S(2)}, u32[]{:S(2)}) collective-permute-start(bf16[8,8,128,128]{3,2,1,0:T(8,128)(2,1)S(1)} %get-tuple-element.34), channel_id=1, source_target_pairs={{0,32},{32,0},{1,33},{33,1},{2,34},{34,2},{3,35},{35,3},{4,36},{36... | collective-permute-start | bytes 6291464 | tf_op jit(solution)/shard_map/ppermute | solution.py:195
  100.1 4.3 %shard_map.68 = (bf16[16,128,128]{2,1,0:T(8,128)(2,1)S(1)}, bf16[16,128,128]{2,1,0:T(8,128)(2,1)S(1)}, bf16[16,128,128]{2,1,0:T(8,128)(2,1)S(1)}, bf16[8,128,128...) custom-call(s32[16,8]{1,0:T(8,128)S(1)} %fusion.8.rows_ref, bf16[128,1024]{1,0:T(8,128)(2,1)S(1)} %get-tuple-element.27.gh_ref, ...), custom_call_target="tpu_custom_call" | custom-call | flops 536870912 | bytes 7000000 | tf_op jit(solution)/shard_map/pallas_call | solution.py:132
  104.4 0.8 copy-done.7
  105.2 0.7 copy-done.9
  105.9 0.0 collective-permute-done.8.got_ref
  105.9 0.5 shard_map.69
  106.5 0.0 copy-start.2
  106.5 1.3 copy-done.2
  107.8 4.2 %all-to-all-start.1 = ((bf16[8,8,128,128]{3,2,1,0:T(8,128)(2,1)}), bf16[8,8,128,128]{3,2,1,0:T(8,128)(2,1)S(1)}, u32[]{:S(2)}, u32[]{:S(2)}) async-start(bf16[8,8,128,128]{3,2,1,0:T(8,128)(2,1)} %copy-done.2), calls=%async_computation.1 | async-start | bytes 4194304 | tf_op jit(solution)/shard_map/all_to_all | solution.py:196
  112.0 2.4 %collective-permute-start.6 = (bf16[8,128,128]{2,1,0:T(8,128)(2,1)}, bf16[8,128,128]{2,1,0:T(8,128)(2,1)S(1)}, u32[]{:S(2)}, u32[]{:S(2)}) collective-permute-start(bf16[8,128,128]{2,1,0:T(8,128)(2,1)} %copy-done.9), channel_id=1, source_target_pairs={{0,1},{1,2},{2,3},{3,4},{4,5},{5,6},{6,7},{7,8},{8,9},{9,10},{10,1... | collective-permute-start | bytes 786440 | tf_op jit(solution)/shard_map/ppermute | solution.py:155
  114.3 0.0 copy-done.5
  114.4 1.0 slice.42
  115.4 4.1 %collective-permute-start.4 = (bf16[8,128,128]{2,1,0:T(8,128)(2,1)S(1)}, bf16[8,128,128]{2,1,0:T(8,128)(2,1)S(1)}, u32[]{:S(2)}, u32[]{:S(2)}) collective-permute-start(bf16[8,128,128]{2,1,0:T(8,128)(2,1)S(1)} %get-tuple-element.30), channel_id=1, source_target_pairs={{0,15},{1,0},{2,1},{3,2},{4,3},{5,4},{6,5},{7,6},{8,7},{9,8},{10,9... | collective-permute-start | bytes 786440 | tf_op jit(solution)/shard_map/ppermute | solution.py:155
  119.5 3.3 %collective-permute-done.6 = bf16[8,128,128]{2,1,0:T(8,128)(2,1)S(1)} collective-permute-done((bf16[8,128,128]{2,1,0:T(8,128)(2,1)}, bf16[8,128,128]{2,1,0:T(8,128)(2,1)S(1)}, u32[]{:S(2)}, u32[]{:S(2)}) %collective-permute-start.6) | collective-permute-done | bytes 262176 | tf_op jit(solution)/shard_map/ppermute | solution.py:155
  122.9 1.0 add_convert_fusion
  123.9 1.9 %collective-permute-start.7 = (bf16[16,128,128]{2,1,0:T(8,128)(2,1)S(1)}, bf16[16,128,128]{2,1,0:T(8,128)(2,1)S(1)}, u32[]{:S(2)}, u32[]{:S(2)}) collective-permute-start(bf16[16,128,128]{2,1,0:T(8,128)(2,1)S(1)} %pad_maximum_fusion.1), channel_id=1, source_target_pairs={{0,1},{1,2},{2,3},{3,4},{4,5},{5,6},{6,7},{7,8},{8,9},{9,10},{10,1... | collective-permute-start | bytes 1572872 | tf_op jit(solution)/shard_map/ppermute | solution.py:155
  125.9 0.0 collective-permute-done.4
  125.9 0.0 copy-done.6
  125.9 0.1 add_convert_fusion.1
  126.0 4.6 %collective-permute-start.5 = (bf16[16,128,128]{2,1,0:T(8,128)(2,1)S(1)}, bf16[16,128,128]{2,1,0:T(8,128)(2,1)S(1)}, u32[]{:S(2)}, u32[]{:S(2)}) collective-permute-start(bf16[16,128,128]{2,1,0:T(8,128)(2,1)S(1)} %pad_maximum_fusion), channel_id=1, source_target_pairs={{0,15},{1,0},{2,1},{3,2},{4,3},{5,4},{6,5},{7,6},{8,7},{9,8},{10,9... | collective-permute-start | bytes 1572872 | tf_op jit(solution)/shard_map/ppermute | solution.py:155
  130.6 8.7 %collective-permute-done.7.right_ref = bf16[16,128,128]{2,1,0:T(8,128)(2,1)S(1)} collective-permute-done((bf16[16,128,128]{2,1,0:T(8,128)(2,1)S(1)}, bf16[16,128,128]{2,1,0:T(8,128)(2,1)S(1)}, u32[]{:S(2)}, u32[]{:S(2)}) %collective-permute-start.7) | collective-permute-done | bytes 524320 | tf_op jit(solution)/shard_map/ppermute | solution.py:155
  139.4 1.1 collective-permute-done.5.left_ref
  140.4 0.8 copy-done.3
  141.2 2.0 %all-to-all-done.1.grads_ref = bf16[8,8,128,128]{3,2,1,0:T(8,128)(2,1)S(1)} async-done(((bf16[8,8,128,128]{3,2,1,0:T(8,128)(2,1)}), bf16[8,8,128,128]{3,2,1,0:T(8,128)(2,1)S(1)}, u32[]{:S(2)}, u32[]{:S(2)}) %all-to-all-start.1) | async-done | bytes 2097184 | tf_op jit(solution)/shard_map/all_to_all | solution.py:196
  143.2 1.0 copy-done.4
  144.3 1.1 shard_map.70
  145.3 35.9 %all_to_all.16 = bf16[8,2,128,128]{3,2,1,0:T(8,128)(2,1)S(1)} all-to-all(bf16[8,2,128,128]{3,2,1,0:T(8,128)(2,1)S(1)} %bitcast.26), channel_id=1, replica_groups=mesh['x'=4,'yl'=2,'core'=2,'yh'=2,'zh'=4,'zl'=4] {'yh','zh'}, dimensions={0} | all-to-all | bytes 1048576 | tf_op jit(solution)/shard_map/all_to_all | solution.py:208
  181.3 0.7 copy_bitcast_fusion
  (17 shorter events, 0.2 us)
Async XLA Ops:
  7.2 77.1 %copy-start.8 = (bf16[128,1024]{1,0:T(8,128)(2,1)S(1)}, bf16[128,1024]{1,0:T(8,128)(2,1)}, u32[]{:S(2)}) copy-start(bf16[128,1024]{1,0:T(8,128)(2,1)} %gact_ref.1) | copy-start | bytes 786436
  7.2 72.1 %all-gather.3.cloned.1.call-start = ((), (), s32[]{:S(2)}) async-start(), calls=%async_computation.3 | async-start | bytes 4526080 | tf_op jit(solution)/shard_map/all_gather | solution.py:218
  57.1 16.8 %collective-permute-start.1 = (bf16[16,128,128]{2,1,0:T(8,128)(2,1)S(1)}, bf16[16,128,128]{2,1,0:T(8,128)(2,1)S(1)}, u32[]{:S(2)}, u32[]{:S(2)}) collective-permute-start(bf16[16,128,128]{2,1,0:T(8,128)(2,1)S(1)} %bitcast.23), channel_id=1, source_target_pairs={{0,15},{1,0},{2,1},{3,2},{4,3},{5,4},{6,5},{7,6},{8,7},{9,8},{10,9... | collective-permute-start | bytes 1572872 | tf_op jit(solution)/shard_map/ppermute | solution.py:155
  61.4 14.5 %collective-permute-start = (bf16[16,128,128]{2,1,0:T(8,128)(2,1)S(1)}, bf16[16,128,128]{2,1,0:T(8,128)(2,1)S(1)}, u32[]{:S(2)}, u32[]{:S(2)}) collective-permute-start(bf16[16,128,128]{2,1,0:T(8,128)(2,1)S(1)} %bitcast.24), channel_id=1, source_target_pairs={{0,1},{1,2},{2,3},{3,4},{4,5},{5,6},{6,7},{7,8},{8,9},{9,10},{10,1... | collective-permute-start | bytes 1572872 | tf_op jit(solution)/shard_map/ppermute | solution.py:155
  73.9 7.1 %collective-permute-start.3 = (bf16[8,128,128]{2,1,0:T(8,128)(2,1)S(1)}, bf16[8,128,128]{2,1,0:T(8,128)(2,1)S(1)}, u32[]{:S(2)}, u32[]{:S(2)}) collective-permute-start(bf16[8,128,128]{2,1,0:T(8,128)(2,1)S(1)} %slice.46), channel_id=1, source_target_pairs={{0,15},{1,0},{2,1},{3,2},{4,3},{5,4},{6,5},{7,6},{8,7},{9,8},{10,9... | collective-permute-start | bytes 786440 | tf_op jit(solution)/shard_map/ppermute | solution.py:155
  75.9 8.3 %collective-permute-start.2 = (bf16[8,128,128]{2,1,0:T(8,128)(2,1)S(1)}, bf16[8,128,128]{2,1,0:T(8,128)(2,1)S(1)}, u32[]{:S(2)}, u32[]{:S(2)}) collective-permute-start(bf16[8,128,128]{2,1,0:T(8,128)(2,1)S(1)} %slice.45), channel_id=1, source_target_pairs={{0,1},{1,2},{2,3},{3,4},{4,5},{5,6},{6,7},{7,8},{8,9},{9,10},{10,1... | collective-permute-start | bytes 786440 | tf_op jit(solution)/shard_map/ppermute | solution.py:155
  84.2 2.2 %copy-start = (bf16[16640,128]{1,0:T(8,128)(2,1)S(1)}, bf16[16640,128]{1,0:T(8,128)(2,1)}, u32[]{:S(2)}) copy-start(bf16[16640,128]{1,0:T(8,128)(2,1)} %all-gather.3.cloned.1.call-done) | copy-start | bytes 12779524
  86.4 13.7 %copy-start.1 = (bf16[16640,128]{1,0:T(8,128)(2,1)S(1)}, bf16[16640,128]{1,0:T(8,128)(2,1)}, u32[]{:S(2)}) copy-start(bf16[16640,128]{1,0:T(8,128)(2,1)} %all-gather.3.cloned.1.call-done) | copy-start | bytes 12779524
  93.8 12.2 %collective-permute-start.8 = (bf16[8,8,128,128]{3,2,1,0:T(8,128)(2,1)S(1)}, bf16[8,8,128,128]{3,2,1,0:T(8,128)(2,1)S(1)}, u32[]{:S(2)}, u32[]{:S(2)}) collective-permute-start(bf16[8,8,128,128]{3,2,1,0:T(8,128)(2,1)S(1)} %get-tuple-element.34), channel_id=1, source_target_pairs={{0,32},{32,0},{1,33},{33,1},{2,34},{34,2},{3,35},{35,3},{4,36},{36... | collective-permute-start | bytes 6291464 | tf_op jit(solution)/shard_map/ppermute | solution.py:195
  104.4 0.8 copy-start.7
  105.2 0.7 copy-start.9
  105.9 8.4 %copy-start.5 = (bf16[16,128,128]{2,1,0:T(8,128)(2,1)}, bf16[16,128,128]{2,1,0:T(8,128)(2,1)S(1)}, u32[]{:S(2)}) copy-start(bf16[16,128,128]{2,1,0:T(8,128)(2,1)S(1)} %get-tuple-element.29) | copy-start | bytes 1572868
  106.5 1.3 copy-start.2
  107.8 35.4 %all-to-all-start.1 = ((bf16[8,8,128,128]{3,2,1,0:T(8,128)(2,1)}), bf16[8,8,128,128]{3,2,1,0:T(8,128)(2,1)S(1)}, u32[]{:S(2)}, u32[]{:S(2)}) async-start(bf16[8,8,128,128]{3,2,1,0:T(8,128)(2,1)} %copy-done.2), calls=%async_computation.1 | async-start | bytes 4194304 | tf_op jit(solution)/shard_map/all_to_all | solution.py:196
  112.0 10.9 %collective-permute-start.6 = (bf16[8,128,128]{2,1,0:T(8,128)(2,1)}, bf16[8,128,128]{2,1,0:T(8,128)(2,1)S(1)}, u32[]{:S(2)}, u32[]{:S(2)}) collective-permute-start(bf16[8,128,128]{2,1,0:T(8,128)(2,1)} %copy-done.9), channel_id=1, source_target_pairs={{0,1},{1,2},{2,3},{3,4},{4,5},{5,6},{6,7},{7,8},{8,9},{9,10},{10,1... | collective-permute-start | bytes 786440 | tf_op jit(solution)/shard_map/ppermute | solution.py:155
  114.4 11.5 %copy-start.6 = (bf16[16,128,128]{2,1,0:T(8,128)(2,1)S(1)}, bf16[16,128,128]{2,1,0:T(8,128)(2,1)}, u32[]{:S(2)}) copy-start(bf16[16,128,128]{2,1,0:T(8,128)(2,1)} %copy-done.5) | copy-start | bytes 1572868
  115.4 10.5 %collective-permute-start.4 = (bf16[8,128,128]{2,1,0:T(8,128)(2,1)S(1)}, bf16[8,128,128]{2,1,0:T(8,128)(2,1)S(1)}, u32[]{:S(2)}, u32[]{:S(2)}) collective-permute-start(bf16[8,128,128]{2,1,0:T(8,128)(2,1)S(1)} %get-tuple-element.30), channel_id=1, source_target_pairs={{0,15},{1,0},{2,1},{3,2},{4,3},{5,4},{6,5},{7,6},{8,7},{9,8},{10,9... | collective-permute-start | bytes 786440 | tf_op jit(solution)/shard_map/ppermute | solution.py:155
  123.9 15.4 %collective-permute-start.7 = (bf16[16,128,128]{2,1,0:T(8,128)(2,1)S(1)}, bf16[16,128,128]{2,1,0:T(8,128)(2,1)S(1)}, u32[]{:S(2)}, u32[]{:S(2)}) collective-permute-start(bf16[16,128,128]{2,1,0:T(8,128)(2,1)S(1)} %pad_maximum_fusion.1), channel_id=1, source_target_pairs={{0,1},{1,2},{2,3},{3,4},{4,5},{5,6},{6,7},{7,8},{8,9},{9,10},{10,1... | collective-permute-start | bytes 1572872 | tf_op jit(solution)/shard_map/ppermute | solution.py:155
  126.0 14.4 %collective-permute-start.5 = (bf16[16,128,128]{2,1,0:T(8,128)(2,1)S(1)}, bf16[16,128,128]{2,1,0:T(8,128)(2,1)S(1)}, u32[]{:S(2)}, u32[]{:S(2)}) collective-permute-start(bf16[16,128,128]{2,1,0:T(8,128)(2,1)S(1)} %pad_maximum_fusion), channel_id=1, source_target_pairs={{0,15},{1,0},{2,1},{3,2},{4,3},{5,4},{6,5},{7,6},{8,7},{9,8},{10,9... | collective-permute-start | bytes 1572872 | tf_op jit(solution)/shard_map/ppermute | solution.py:155
  140.4 0.8 copy-start.3
  143.2 1.0 copy-start.4
Sparse Core Ops, SparseCore 0:
  10.1 52.3 all-gather.2

commit v4 on v3

--- a/solution.py
+++ b/solution.py
@@ -8,14 +8,13 @@
 
 SQRT_TWO_PI = 0.7978845608028654
 CUBIC = 0.044715
-AXES = ("x", "yl", "core", "yh", "zh", "zl")
-SIZES = (4, 2, 2, 2, 4, 4)
+AXES = ("x", "yl", "core", "yh", "z")
+SIZES = (4, 2, 2, 2, 16)
 SEQ = ("x", "yl", "core")
-FAR = ("yh", "zh")
-MP = ("yh", "zh", "zl")
-Z = ("zh", "zl")
+MP = ("yh", "z")
 BF16, F32 = jnp.bfloat16, jnp.float32
-OWN, RIGHT, FAR_LEFT, FAR_RIGHT, LEFT = (0, 16), (16, 16), (32, 8), (40, 8), (48, 16)
+OWN, LEFT, RIGHT = (0, 4, 8, 12), (1, 5, 9, 13), (15, 3, 7, 11)
+FAR_LEFT, FAR_RIGHT = (6, 10), (14, 2)
 PARTS = (OWN, LEFT, RIGHT, FAR_LEFT, FAR_RIGHT)
 
 
@@ -48,8 +47,9 @@
     @pl.when(c == 0)
     def _():
         copies = [
-            pltpu.make_async_copy(ref, tok.at[pl.ds(start, size)], sem.at[i])
-            for i, (ref, (start, size)) in enumerate(zip((own, left, right, far_left, far_right), PARTS))
+            pltpu.make_async_copy(ref.at[pl.ds(4 * i, 4)], tok.at[pl.ds(4 * d, 4)], sem.at[d])
+            for ref, part in zip((own, left, right, far_left, far_right), PARTS)
+            for i, d in enumerate(part)
         ]
         for copy in copies:
             copy.start()
@@ -94,8 +94,9 @@
 
     @pl.when(c == pl.num_programs(0) - 1)
     def _():
-        for ref, (start, size) in zip((own, left, right, far_left, far_right), PARTS):
-            ref[...] = acc[start : start + size].astype(BF16)
+        for ref, part in zip((own, left, right, far_left, far_right), PARTS):
+            for i, d in enumerate(part):
+                ref[4 * i : 4 * i + 4] = acc[4 * d : 4 * d + 4].astype(BF16)
 
 
 def hidden_call(rows, core, parts, weights, grad_act):
@@ -116,7 +117,7 @@
             scratch_shapes=[
                 pltpu.VMEM((64, n_tok, 128), BF16),
                 pltpu.VMEM((kept, cols, 128, 128), BF16),
-                pltpu.SemaphoreType.DMA((5,)),
+                pltpu.SemaphoreType.DMA((16,)),
                 pltpu.SemaphoreType.DMA((cols,)),
             ],
         ),
@@ -138,21 +139,25 @@
                 pl.BlockSpec((n_tok, 128), lambda c, rows: (0, c)),
                 pl.BlockSpec(memory_space=pltpu.HBM),
             ],
-            out_specs=[pl.BlockSpec((n, n_tok, 128), lambda c, rows: (0, 0, 0)) for _, n in PARTS],
+            out_specs=[pl.BlockSpec((4 * len(p), n_tok, 128), lambda c, rows: (0, 0, 0)) for p in PARTS],
             scratch_shapes=[
                 pltpu.VMEM((64, n_tok, 128), F32),
                 pltpu.VMEM((kept, cols, 128, 128), BF16),
                 pltpu.SemaphoreType.DMA((cols,)),
             ],
         ),
-        out_shape=[jax.ShapeDtypeStruct((n, n_tok, 128), BF16) for _, n in PARTS],
+        out_shape=[jax.ShapeDtypeStruct((4 * len(p), n_tok, 128), BF16) for p in PARTS],
         compiler_params=pltpu.CompilerParams(vmem_limit_bytes=20 * 2**20),
         cost_estimate=pl.CostEstimate(flops=536_870_912, bytes_accessed=7_000_000, transcendentals=0),
     )(rows, grad_hidden, weights)
 
 
 def shift(a, by):
-    return lax.ppermute(a, Z, [(i, (i + by) % 16) for i in range(16)])
+    return lax.ppermute(a, "z", [(i, (i + by) % 16) for i in range(16)])
+
+
+def swap(a, axis):
+    return lax.ppermute(a, axis, [(0, 1), (1, 0)])
 
 
 def total(*arrays):
@@ -160,17 +165,23 @@
 
 
 def gather_tokens(mine):
-    own = lax.all_to_all(jnp.broadcast_to(mine, (8,) + mine.shape), FAR, 0, 0)
-    own = own.reshape((16,) + mine.shape[1:])
+    pair = jnp.concatenate([mine, swap(mine, "yh")])
+    left, right = shift(pair, 4), shift(pair, -4)
+    own = jnp.concatenate([pair, left, shift(left[:2], 4), shift(right[2:], -4), right])
     left, right = shift(own, 1), shift(own, -1)
-    return own, left, right, shift(left[:8], 1), shift(right[8:], -1)
-
-
-def combine_kernel(own_ref, left_ref, right_ref, grads_ref, own_out, grads_out):
-    own_out[...] = total(own_ref[...], left_ref[...], right_ref[...]).astype(BF16)
-    for c in range(grads_ref.shape[1]):
-        summed = sum(grads_ref[i, c].astype(F32) for i in range(grads_ref.shape[0]))
-        grads_out[c] = summed.T.astype(BF16)
+    return own, left, right, shift(left[4:12], 1), shift(right[:8], -1)
+
+
+def reduce_terms(own, left, right, far_left, far_right):
+    from_right, from_left = shift(far_left, -1), shift(far_right, 1)
+    left = jnp.concatenate([left[:4], total(left[4:12], from_right).astype(BF16), left[12:]])
+    right = jnp.concatenate([total(right[:8], from_left).astype(BF16), right[8:]])
+    own = total(own, shift(left, -1), shift(right, 1)).astype(BF16)
+    from_right, from_left = shift(own[8:10], -4), shift(own[10:12], 4)
+    left = jnp.concatenate([total(own[4:6], from_right).astype(BF16), own[6:8]])
+    right = jnp.concatenate([own[12:14], total(own[14:16], from_left).astype(BF16)])
+    pair = total(own[:4], shift(left, -4), shift(right, 4)).astype(BF16)
+    return total(pair[:2], swap(pair[2:], "yh")).astype(BF16)
 
 
 def add_kernel(keep_ref, got_ref, after_ref, both_ref):
@@ -190,23 +201,21 @@
     )(keep, got, after)
 
 
-def reduce_all(keep, give, own, left, right, far_left, far_right):
-    from_right, from_left = shift(far_left, -1), shift(far_right, 1)
-    both = add_after(keep, lax.ppermute(give, "core", [(0, 1), (1, 0)]), own)
+def sum_kernel(grads_ref, out_ref):
+    for c in range(grads_ref.shape[1]):
+        summed = sum(grads_ref[i, c].astype(F32) for i in range(grads_ref.shape[0]))
+        out_ref[c] = summed.T.astype(BF16)
+
+
+def reduce_grads(keep, give, after):
+    both = add_after(keep, swap(give, "core"), after)
     grads = lax.all_to_all(both, ("x", "yl"), 0, 0)
-    left = jnp.concatenate([total(left[:8], from_right).astype(BF16), left[8:]])
-    right = jnp.concatenate([right[:8], total(right[8:], from_left).astype(BF16)])
-    own, grads = pl.pallas_call(
-        combine_kernel,
-        out_shape=[
-            jax.ShapeDtypeStruct(own.shape, BF16),
-            jax.ShapeDtypeStruct(grads.shape[1:], BF16),
-        ],
-        compiler_params=pltpu.CompilerParams(vmem_limit_bytes=12 * 2**20),
-        cost_estimate=pl.CostEstimate(flops=2_000_000, bytes_accessed=4_500_000, transcendentals=0),
-    )(own, shift(left, -1), shift(right, 1), grads)
-    own = lax.all_to_all(own.reshape((8, 2) + own.shape[1:]), FAR, 0, 0)
-    return total(*own).astype(BF16), grads[:, None]
+    return pl.pallas_call(
+        sum_kernel,
+        out_shape=jax.ShapeDtypeStruct(grads.shape[1:], BF16),
+        compiler_params=pltpu.CompilerParams(vmem_limit_bytes=8 * 2**20),
+        cost_estimate=pl.CostEstimate(flops=2_000_000, bytes_accessed=2_500_000, transcendentals=0),
+    )(grads)[:, None]
 
 
 def shards(tokens, block_values, block_rows, grad_act):
@@ -217,11 +226,13 @@
     sent = jnp.concatenate([block_values.reshape(cols * 128, 128), row_tile])
     weights = lax.all_gather(sent, SEQ, axis=0)
     rows = weights[:, cols * 128, :cols].astype(jnp.int32)
-    rows = (rows // 2 - lax.axis_index("zl")) % 4 * 16 + rows // 32 * 8 + rows % 32 // 8 * 2 + rows % 2
+    away = (lax.axis_index("z") - rows % 32 // 2) % 16
+    rows = away * 4 + (rows // 32 + lax.axis_index("yh")) % 2 * 2 + rows % 2
     core = lax.axis_index("core").reshape(1)
     activated, grad_hidden, keep, give = hidden_call(rows, core, parts, weights, grad_act)
     terms = term_call(rows, grad_hidden, weights)
-    summed, grads = reduce_all(keep, give, *terms)
+    grads = reduce_grads(keep, give, terms[0])
+    summed = reduce_terms(*terms)
     return activated, summed.transpose(1, 0, 2).reshape(n_tok, 256), grads
 
 

time: 190 us -> 193 us (1.016)
  the two profiles are of different devices: /device:TPU:1 before, /device:TPU:24 now
where the time goes in v4:
time: 193 us; the launch traced here: 191 us
  starting transfers between devices  84.7 us (44%)
  waiting for transfers between devices  64.3 us (33%)
  Pallas kernels  16.4 us (8%)
  between operations  14.5 us (8%)
  other arithmetic  5.82 us (3%)
  local copies, waits for them, and re-layouts  5.71 us (3%)
    ppermute x16, starting transfers between devices, shift(): return lax.ppermute(a, 'z', [(i, (i + by) % 16) for i in range(16)])  70.7 us
    ppermute x16, waiting for transfers between devices, shift(): return lax.ppermute(a, 'z', [(i, (i + by) % 16) for i in range(16)])  55.2 us
    pallas_call x1, Pallas kernels, hidden_call(): pl.pallas_call(hidden_kernel, grid_spec=pltpu.PrefetchScalarGridSpec(num_...  10.5 us
    ppermute x3, waiting for transfers between devices, swap(): return lax.ppermute(a, axis, [(0, 1), (1, 0)])  9 us
    ppermute x3, starting transfers between devices, swap(): return lax.ppermute(a, axis, [(0, 1), (1, 0)])  8.24 us
    all_to_all x1, starting transfers between devices, reduce_grads(): grads = lax.all_to_all(both, ('x', 'yl'), 0, 0)  5.75 us
    unnamed x15, local copies, waits for them, and re-layouts  5.34 us
    pallas_call x1, Pallas kernels, term_call(): pl.pallas_call(term_kernel, grid_spec=pltpu.PrefetchScalarGridSpec(num_sc...  4.28 us
  transfers between devices with their start and end apart: 21, of which 14 were waited for; matrix products, arithmetic and copies ran while one was open for 3% of the time, Pallas kernels for 3%

profile of v4, /device:TPU:24, one launch (start us, length us, event | category | flops | bytes accessed | tf_op | source)
XLA Modules:
  0.0 191.4 jit_solution(12887849798595489277)
XLA Ops:
  7.2 0.7 convert_bitcast_fusion
  7.9 1.7 fusion.1
  9.6 1.0 copy.28
  10.6 0.1 copy.29
  10.7 3.1 %collective-permute-start = (bf16[2,128,128]{2,1,0:T(8,128)(2,1)S(1)}, bf16[2,128,128]{2,1,0:T(8,128)(2,1)S(1)}, u32[]{:S(2)}, u32[]{:S(2)}) collective-permute-start(bf16[2,128,128]{2,1,0:T(8,128)(2,1)S(1)} %bitcast.18), channel_id=1, source_target_pairs={{0,16},{16,0},{1,17},{17,1},{2,18},{18,2},{3,19},{19,3},{4,20},{20... | collective-permute-start | bytes 196616 | tf_op jit(solution)/shard_map/ppermute | solution.py:160
  13.9 4.5 %collective-permute-done = bf16[2,128,128]{2,1,0:T(8,128)(2,1)S(1)} collective-permute-done((bf16[2,128,128]{2,1,0:T(8,128)(2,1)S(1)}, bf16[2,128,128]{2,1,0:T(8,128)(2,1)S(1)}, u32[]{:S(2)}, u32[]{:S(2)}) %collective-permute-start) | collective-permute-done | bytes 65568 | tf_op jit(solution)/shard_map/ppermute | solution.py:160
  18.4 12.7 %collective-permute-start.3 = (bf16[4,128,128]{2,1,0:T(8,128)(2,1)S(1)}, bf16[4,128,128]{2,1,0:T(8,128)(2,1)S(1)}, u32[]{:S(2)}, u32[]{:S(2)}) collective-permute-start(bf16[4,128,128]{2,1,0:T(8,128)(2,1)S(1)} %pad_maximum_fusion.2), channel_id=1, source_target_pairs={{0,12},{1,13},{2,14},{3,15},{4,0},{5,1},{6,2},{7,3},{8,4},{9,5},{1... | collective-permute-start | bytes 393224 | tf_op jit(solution)/shard_map/ppermute | solution.py:156
  31.1 1.9 %collective-permute-start.1 = (bf16[4,128,128]{2,1,0:T(8,128)(2,1)S(1)}, bf16[4,128,128]{2,1,0:T(8,128)(2,1)S(1)}, u32[]{:S(2)}, u32[]{:S(2)}) collective-permute-start(bf16[4,128,128]{2,1,0:T(8,128)(2,1)S(1)} %pad_maximum_fusion.2), channel_id=1, source_target_pairs={{0,4},{1,5},{2,6},{3,7},{4,8},{5,9},{6,10},{7,11},{8,12},{9,13},{1... | collective-permute-start | bytes 393224 | tf_op jit(solution)/shard_map/ppermute | solution.py:156
  33.1 8.1 %collective-permute-done.3 = bf16[4,128,128]{2,1,0:T(8,128)(2,1)S(1)} collective-permute-done((bf16[4,128,128]{2,1,0:T(8,128)(2,1)S(1)}, bf16[4,128,128]{2,1,0:T(8,128)(2,1)S(1)}, u32[]{:S(2)}, u32[]{:S(2)}) %collective-permute-start.3) | collective-permute-done | bytes 131104 | tf_op jit(solution)/shard_map/ppermute | solution.py:156
  41.2 8.3 %collective-permute-start.4 = (bf16[2,128,128]{2,1,0:T(8,128)(2,1)S(1)}, bf16[2,128,128]{2,1,0:T(8,128)(2,1)S(1)}, u32[]{:S(2)}, u32[]{:S(2)}) collective-permute-start(bf16[2,128,128]{2,1,0:T(8,128)(2,1)S(1)} %slice.94), channel_id=1, source_target_pairs={{0,12},{1,13},{2,14},{3,15},{4,0},{5,1},{6,2},{7,3},{8,4},{9,5},{1... | collective-permute-start | bytes 196616 | tf_op jit(solution)/shard_map/ppermute | solution.py:156
  49.5 1.9 %collective-permute-start.2 = (bf16[2,128,128]{2,1,0:T(8,128)(2,1)S(1)}, bf16[2,128,128]{2,1,0:T(8,128)(2,1)S(1)}, u32[]{:S(2)}, u32[]{:S(2)}) collective-permute-start(bf16[2,128,128]{2,1,0:T(8,128)(2,1)S(1)} %slice.93), channel_id=1, source_target_pairs={{0,4},{1,5},{2,6},{3,7},{4,8},{5,9},{6,10},{7,11},{8,12},{9,13},{1... | collective-permute-start | bytes 196616 | tf_op jit(solution)/shard_map/ppermute | solution.py:156
  51.5 10.0 %collective-permute-done.2 = bf16[2,128,128]{2,1,0:T(8,128)(2,1)S(1)} collective-permute-done((bf16[2,128,128]{2,1,0:T(8,128)(2,1)S(1)}, bf16[2,128,128]{2,1,0:T(8,128)(2,1)S(1)}, u32[]{:S(2)}, u32[]{:S(2)}) %collective-permute-start.2) | collective-permute-done | bytes 65568 | tf_op jit(solution)/shard_map/ppermute | solution.py:156
  61.5 2.3 %collective-permute-start.6 = (bf16[16,128,128]{2,1,0:T(8,128)(2,1)S(1)}, bf16[16,128,128]{2,1,0:T(8,128)(2,1)S(1)}, u32[]{:S(2)}, u32[]{:S(2)}) collective-permute-start(bf16[16,128,128]{2,1,0:T(8,128)(2,1)S(1)} %constant_dynamic-update-slice_fusion.own), channel_id=1, source_target_pairs={{0,15},{1,0},{2,1},{3,2},{4,3},{5,4},{6,5},{7,6},{8,7},{9,8},{10,9... | collective-permute-start | bytes 1572872 | tf_op jit(solution)/shard_map/ppermute | solution.py:156
  63.8 3.6 %collective-permute-start.5 = (bf16[16,128,128]{2,1,0:T(8,128)(2,1)S(1)}, bf16[16,128,128]{2,1,0:T(8,128)(2,1)S(1)}, u32[]{:S(2)}, u32[]{:S(2)}) collective-permute-start(bf16[16,128,128]{2,1,0:T(8,128)(2,1)S(1)} %constant_dynamic-update-slice_fusion.own), channel_id=1, source_target_pairs={{0,1},{1,2},{2,3},{3,4},{4,5},{5,6},{6,7},{7,8},{8,9},{9,10},{10,1... | collective-permute-start | bytes 1572872 | tf_op jit(solution)/shard_map/ppermute | solution.py:156
  67.4 7.4 %collective-permute-done.6.right = bf16[16,128,128]{2,1,0:T(8,128)(2,1)S(1)} collective-permute-done((bf16[16,128,128]{2,1,0:T(8,128)(2,1)S(1)}, bf16[16,128,128]{2,1,0:T(8,128)(2,1)S(1)}, u32[]{:S(2)}, u32[]{:S(2)}) %collective-permute-start.6) | collective-permute-done | bytes 524320 | tf_op jit(solution)/shard_map/ppermute | solution.py:156
  74.8 4.0 %collective-permute-start.8 = (bf16[8,128,128]{2,1,0:T(8,128)(2,1)S(1)}, bf16[8,128,128]{2,1,0:T(8,128)(2,1)S(1)}, u32[]{:S(2)}, u32[]{:S(2)}) collective-permute-start(bf16[8,128,128]{2,1,0:T(8,128)(2,1)S(1)} %slice.96), channel_id=1, source_target_pairs={{0,15},{1,0},{2,1},{3,2},{4,3},{5,4},{6,5},{7,6},{8,7},{9,8},{10,9... | collective-permute-start | bytes 786440 | tf_op jit(solution)/shard_map/ppermute | solution.py:156
  78.8 1.9 %collective-permute-start.7 = (bf16[8,128,128]{2,1,0:T(8,128)(2,1)S(1)}, bf16[8,128,128]{2,1,0:T(8,128)(2,1)S(1)}, u32[]{:S(2)}, u32[]{:S(2)}) collective-permute-start(bf16[8,128,128]{2,1,0:T(8,128)(2,1)S(1)} %slice.95), channel_id=1, source_target_pairs={{0,1},{1,2},{2,3},{3,4},{4,5},{5,6},{6,7},{7,8},{8,9},{9,10},{10,1... | collective-permute-start | bytes 786440 | tf_op jit(solution)/shard_map/ppermute | solution.py:156
  80.8 0.8 slice_convert_fusion
  81.6 1.5 collective-permute-done.8.far_right
  83.1 5.2 %collective-permute-done.7.far_left = bf16[8,128,128]{2,1,0:T(8,128)(2,1)S(1)} collective-permute-done((bf16[8,128,128]{2,1,0:T(8,128)(2,1)S(1)}, bf16[8,128,128]{2,1,0:T(8,128)(2,1)S(1)}, u32[]{:S(2)}, u32[]{:S(2)}) %collective-permute-start.7) | collective-permute-done | bytes 262176 | tf_op jit(solution)/shard_map/ppermute | solution.py:156
  88.3 2.2 %copy-done = bf16[16640,128]{1,0:T(8,128)(2,1)S(1)} copy-done((bf16[16640,128]{1,0:T(8,128)(2,1)S(1)}, bf16[16640,128]{1,0:T(8,128)(2,1)}, u32[]{:S(2)}) %copy-start) | copy-done | bytes 4259864
  90.5 10.5 %shard_map.67 = (bf16[128,1024]{1,0:T(8,128)(2,1)}, bf16[128,1024]{1,0:T(8,128)(2,1)S(1)}, bf16[8,8,128,128]{3,2,1,0:T(8,128)(2,1)S(1)}, bf16[8,8,128,128]{3,2,1,0:T(8,128)(2,1)S(1)}) custom-call(s32[16,8]{1,0:T(8,128)S(1)} %fusion.8.rows_ref, s32[1]{0:T(128)} %bitcast.4.core_ref, bf16[16,128,128]{2,1,0:T(8,128)(2,1)S(1)} %constant_dynamic-update-slice_fusion.own, ...), custom_call_target="tpu_custom_call" | custom-call | flops 1073741824 | bytes 11000000 | tf_op jit(solution)/shard_map/pallas_call | solution.py:109
  101.1 1.9 %collective-permute-start.18 = (bf16[8,8,128,128]{3,2,1,0:T(8,128)(2,1)S(1)}, bf16[8,8,128,128]{3,2,1,0:T(8,128)(2,1)S(1)}, u32[]{:S(2)}, u32[]{:S(2)}) collective-permute-start(bf16[8,8,128,128]{3,2,1,0:T(8,128)(2,1)S(1)} %get-tuple-element.32), channel_id=1, source_target_pairs={{0,32},{32,0},{1,33},{33,1},{2,34},{34,2},{3,35},{35,3},{4,36},{36... | collective-permute-start | bytes 6291464 | tf_op jit(solution)/shard_map/ppermute | solution.py:160
  103.0 4.3 %shard_map.68 = (bf16[16,128,128]{2,1,0:T(8,128)(2,1)S(1)}, bf16[16,128,128]{2,1,0:T(8,128)(2,1)S(1)}, bf16[16,128,128]{2,1,0:T(8,128)(2,1)S(1)}, bf16[8,128,128...) custom-call(s32[16,8]{1,0:T(8,128)S(1)} %fusion.8.rows_ref, bf16[128,1024]{1,0:T(8,128)(2,1)S(1)} %get-tuple-element.25.gh_ref, ...), custom_call_target="tpu_custom_call" | custom-call | flops 536870912 | bytes 7000000 | tf_op jit(solution)/shard_map/pallas_call | solution.py:133
  107.3 1.9 %collective-permute-start.11 = (bf16[8,128,128]{2,1,0:T(8,128)(2,1)S(1)}, bf16[8,128,128]{2,1,0:T(8,128)(2,1)S(1)}, u32[]{:S(2)}, u32[]{:S(2)}) collective-permute-start(bf16[8,128,128]{2,1,0:T(8,128)(2,1)S(1)} %get-tuple-element.30), channel_id=1, source_target_pairs={{0,1},{1,2},{2,3},{3,4},{4,5},{5,6},{6,7},{7,8},{8,9},{9,10},{10,1... | collective-permute-start | bytes 786440 | tf_op jit(solution)/shard_map/ppermute | solution.py:156
  109.2 5.1 %collective-permute-start.9 = (bf16[8,128,128]{2,1,0:T(8,128)(2,1)S(1)}, bf16[8,128,128]{2,1,0:T(8,128)(2,1)S(1)}, u32[]{:S(2)}, u32[]{:S(2)}) collective-permute-start(bf16[8,128,128]{2,1,0:T(8,128)(2,1)S(1)} %get-tuple-element.28), channel_id=1, source_target_pairs={{0,15},{1,0},{2,1},{3,2},{4,3},{5,4},{6,5},{7,6},{8,7},{9,8},{10,9... | collective-permute-start | bytes 786440 | tf_op jit(solution)/shard_map/ppermute | solution.py:156
  114.4 4.7 %collective-permute-done.11 = bf16[8,128,128]{2,1,0:T(8,128)(2,1)S(1)} collective-permute-done((bf16[8,128,128]{2,1,0:T(8,128)(2,1)S(1)}, bf16[8,128,128]{2,1,0:T(8,128)(2,1)S(1)}, u32[]{:S(2)}, u32[]{:S(2)}) %collective-permute-start.11) | collective-permute-done | bytes 262176 | tf_op jit(solution)/shard_map/ppermute | solution.py:156
  119.2 1.9 %collective-permute-start.12 = (bf16[16,128,128]{2,1,0:T(8,128)(2,1)S(1)}, bf16[16,128,128]{2,1,0:T(8,128)(2,1)}, u32[]{:S(2)}, u32[]{:S(2)}) collective-permute-start(bf16[16,128,128]{2,1,0:T(8,128)(2,1)S(1)} %pad_maximum_fusion.1), channel_id=1, source_target_pairs={{0,1},{1,2},{2,3},{3,4},{4,5},{5,6},{6,7},{7,8},{8,9},{9,10},{10,1... | collective-permute-start | bytes 1572872 | tf_op jit(solution)/shard_map/ppermute | solution.py:156
  121.3 0.9 pad_maximum_fusion
  122.1 5.1 %collective-permute-start.10 = (bf16[16,128,128]{2,1,0:T(8,128)(2,1)}, bf16[16,128,128]{2,1,0:T(8,128)(2,1)}, u32[]{:S(2)}, u32[]{:S(2)}) collective-permute-start(bf16[16,128,128]{2,1,0:T(8,128)(2,1)} %pad_maximum_fusion), channel_id=1, source_target_pairs={{0,15},{1,0},{2,1},{3,2},{4,3},{5,4},{6,5},{7,6},{8,7},{9,8},{10,9... | collective-permute-start | bytes 1572872 | tf_op jit(solution)/shard_map/ppermute | solution.py:156
  127.3 0.5 shard_map.69
  127.8 1.4 copy-done.2
  129.2 5.8 %all-to-all-start = ((bf16[8,8,128,128]{3,2,1,0:T(8,128)(2,1)}), bf16[8,8,128,128]{3,2,1,0:T(8,128)(2,1)S(1)}, u32[]{:S(2)}, u32[]{:S(2)}) async-start(bf16[8,8,128,128]{3,2,1,0:T(8,128)(2,1)} %copy-done.2), calls=%async_computation | async-start | bytes 4194304 | tf_op jit(solution)/shard_map/all_to_all | solution.py:212
  134.9 1.0 collective-permute-done.12
  136.0 2.3 %collective-permute-done.10 = bf16[16,128,128]{2,1,0:T(8,128)(2,1)} collective-permute-done((bf16[16,128,128]{2,1,0:T(8,128)(2,1)}, bf16[16,128,128]{2,1,0:T(8,128)(2,1)}, u32[]{:S(2)}, u32[]{:S(2)}) %collective-permute-start.10) | collective-permute-done | bytes 524320 | tf_op jit(solution)/shard_map/ppermute | solution.py:156
  138.3 1.4 add_convert_fusion
  139.8 5.7 %collective-permute-start.13 = (bf16[2,128,128]{2,1,0:T(8,128)(2,1)S(1)}, bf16[2,128,128]{2,1,0:T(8,128)(2,1)S(1)}, u32[]{:S(2)}, u32[]{:S(2)}) collective-permute-start(bf16[2,128,128]{2,1,0:T(8,128)(2,1)S(1)} %get-tuple-element.44), channel_id=1, source_target_pairs={{0,12},{1,13},{2,14},{3,15},{4,0},{5,1},{6,2},{7,3},{8,4},{9,5},{1... | collective-permute-start | bytes 196616 | tf_op jit(solution)/shard_map/ppermute | solution.py:156
  145.5 4.0 %collective-permute-start.15 = (bf16[2,128,128]{2,1,0:T(8,128)(2,1)S(1)}, bf16[2,128,128]{2,1,0:T(8,128)(2,1)S(1)}, u32[]{:S(2)}, u32[]{:S(2)}) collective-permute-start(bf16[2,128,128]{2,1,0:T(8,128)(2,1)S(1)} %get-tuple-element.45), channel_id=1, source_target_pairs={{0,4},{1,5},{2,6},{3,7},{4,8},{5,9},{6,10},{7,11},{8,12},{9,13},{1... | collective-permute-start | bytes 196616 | tf_op jit(solution)/shard_map/ppermute | solution.py:156
  149.5 1.3 collective-permute-done.13
  150.9 4.8 %collective-permute-done.15 = bf16[2,128,128]{2,1,0:T(8,128)(2,1)S(1)} collective-permute-done((bf16[2,128,128]{2,1,0:T(8,128)(2,1)S(1)}, bf16[2,128,128]{2,1,0:T(8,128)(2,1)S(1)}, u32[]{:S(2)}, u32[]{:S(2)}) %collective-permute-start.15) | collective-permute-done | bytes 65568 | tf_op jit(solution)/shard_map/ppermute | solution.py:156
  155.7 4.3 %collective-permute-start.16 = (bf16[4,128,128]{2,1,0:T(8,128)(2,1)S(1)}, bf16[4,128,128]{2,1,0:T(8,128)(2,1)S(1)}, u32[]{:S(2)}, u32[]{:S(2)}) collective-permute-start(bf16[4,128,128]{2,1,0:T(8,128)(2,1)S(1)} %pad_maximum_fusion.4), channel_id=1, source_target_pairs={{0,4},{1,5},{2,6},{3,7},{4,8},{5,9},{6,10},{7,11},{8,12},{9,13},{1... | collective-permute-start | bytes 393224 | tf_op jit(solution)/shard_map/ppermute | solution.py:156
  160.0 6.0 %collective-permute-start.14 = (bf16[4,128,128]{2,1,0:T(8,128)(2,1)S(1)}, bf16[4,128,128]{2,1,0:T(8,128)(2,1)S(1)}, u32[]{:S(2)}, u32[]{:S(2)}) collective-permute-start(bf16[4,128,128]{2,1,0:T(8,128)(2,1)S(1)} %pad_maximum_fusion.3), channel_id=1, source_target_pairs={{0,12},{1,13},{2,14},{3,15},{4,0},{5,1},{6,2},{7,3},{8,4},{9,5},{1... | collective-permute-start | bytes 393224 | tf_op jit(solution)/shard_map/ppermute | solution.py:156
  166.1 6.6 %collective-permute-done.16 = bf16[4,128,128]{2,1,0:T(8,128)(2,1)S(1)} collective-permute-done((bf16[4,128,128]{2,1,0:T(8,128)(2,1)S(1)}, bf16[4,128,128]{2,1,0:T(8,128)(2,1)S(1)}, u32[]{:S(2)}, u32[]{:S(2)}) %collective-permute-start.16) | collective-permute-done | bytes 131104 | tf_op jit(solution)/shard_map/ppermute | solution.py:156
  172.7 2.2 %collective-permute-done.14 = bf16[4,128,128]{2,1,0:T(8,128)(2,1)S(1)} collective-permute-done((bf16[4,128,128]{2,1,0:T(8,128)(2,1)S(1)}, bf16[4,128,128]{2,1,0:T(8,128)(2,1)S(1)}, u32[]{:S(2)}, u32[]{:S(2)}) %collective-permute-start.14) | collective-permute-done | bytes 131104 | tf_op jit(solution)/shard_map/ppermute | solution.py:156
  174.9 3.2 %collective-permute-start.17 = (bf16[2,128,128]{2,1,0:T(8,128)(2,1)S(1)}, bf16[2,128,128]{2,1,0:T(8,128)(2,1)S(1)}, u32[]{:S(2)}, u32[]{:S(2)}) collective-permute-start(bf16[2,128,128]{2,1,0:T(8,128)(2,1)S(1)} %slice.105), channel_id=1, source_target_pairs={{0,16},{16,0},{1,17},{17,1},{2,18},{18,2},{3,19},{19,3},{4,20},{20... | collective-permute-start | bytes 196616 | tf_op jit(solution)/shard_map/ppermute | solution.py:160
  178.1 4.5 %collective-permute-done.17 = bf16[2,128,128]{2,1,0:T(8,128)(2,1)S(1)} collective-permute-done((bf16[2,128,128]{2,1,0:T(8,128)(2,1)S(1)}, bf16[2,128,128]{2,1,0:T(8,128)(2,1)S(1)}, u32[]{:S(2)}, u32[]{:S(2)}) %collective-permute-start.17) | collective-permute-done | bytes 65568 | tf_op jit(solution)/shard_map/ppermute | solution.py:160
  182.7 0.7 copy.31
  183.5 1.1 shard_map.70
  (40 shorter events, 0.8 us)
Async XLA Ops:
  7.2 81.1 %copy-start.3 = (bf16[128,1024]{1,0:T(8,128)(2,1)S(1)}, bf16[128,1024]{1,0:T(8,128)(2,1)}, u32[]{:S(2)}) copy-start(bf16[128,1024]{1,0:T(8,128)(2,1)} %gact_ref.1) | copy-start | bytes 786436
  7.2 73.6 %all-gather.3.cloned.1.call-start = ((), (), s32[]{:S(2)}) async-start(), calls=%async_computation.1 | async-start | bytes 4526080 | tf_op jit(solution)/shard_map/all_gather | solution.py:227
  10.7 7.7 %collective-permute-start = (bf16[2,128,128]{2,1,0:T(8,128)(2,1)S(1)}, bf16[2,128,128]{2,1,0:T(8,128)(2,1)S(1)}, u32[]{:S(2)}, u32[]{:S(2)}) collective-permute-start(bf16[2,128,128]{2,1,0:T(8,128)(2,1)S(1)} %bitcast.18), channel_id=1, source_target_pairs={{0,16},{16,0},{1,17},{17,1},{2,18},{18,2},{3,19},{19,3},{4,20},{20... | collective-permute-start | bytes 196616 | tf_op jit(solution)/shard_map/ppermute | solution.py:160
  18.4 22.8 %collective-permute-start.3 = (bf16[4,128,128]{2,1,0:T(8,128)(2,1)S(1)}, bf16[4,128,128]{2,1,0:T(8,128)(2,1)S(1)}, u32[]{:S(2)}, u32[]{:S(2)}) collective-permute-start(bf16[4,128,128]{2,1,0:T(8,128)(2,1)S(1)} %pad_maximum_fusion.2), channel_id=1, source_target_pairs={{0,12},{1,13},{2,14},{3,15},{4,0},{5,1},{6,2},{7,3},{8,4},{9,5},{1... | collective-permute-start | bytes 393224 | tf_op jit(solution)/shard_map/ppermute | solution.py:156
  31.1 18.4 %collective-permute-start.1 = (bf16[4,128,128]{2,1,0:T(8,128)(2,1)S(1)}, bf16[4,128,128]{2,1,0:T(8,128)(2,1)S(1)}, u32[]{:S(2)}, u32[]{:S(2)}) collective-permute-start(bf16[4,128,128]{2,1,0:T(8,128)(2,1)S(1)} %pad_maximum_fusion.2), channel_id=1, source_target_pairs={{0,4},{1,5},{2,6},{3,7},{4,8},{5,9},{6,10},{7,11},{8,12},{9,13},{1... | collective-permute-start | bytes 393224 | tf_op jit(solution)/shard_map/ppermute | solution.py:156
  41.2 20.2 %collective-permute-start.4 = (bf16[2,128,128]{2,1,0:T(8,128)(2,1)S(1)}, bf16[2,128,128]{2,1,0:T(8,128)(2,1)S(1)}, u32[]{:S(2)}, u32[]{:S(2)}) collective-permute-start(bf16[2,128,128]{2,1,0:T(8,128)(2,1)S(1)} %slice.94), channel_id=1, source_target_pairs={{0,12},{1,13},{2,14},{3,15},{4,0},{5,1},{6,2},{7,3},{8,4},{9,5},{1... | collective-permute-start | bytes 196616 | tf_op jit(solution)/shard_map/ppermute | solution.py:156
  49.5 11.9 %collective-permute-start.2 = (bf16[2,128,128]{2,1,0:T(8,128)(2,1)S(1)}, bf16[2,128,128]{2,1,0:T(8,128)(2,1)S(1)}, u32[]{:S(2)}, u32[]{:S(2)}) collective-permute-start(bf16[2,128,128]{2,1,0:T(8,128)(2,1)S(1)} %slice.93), channel_id=1, source_target_pairs={{0,4},{1,5},{2,6},{3,7},{4,8},{5,9},{6,10},{7,11},{8,12},{9,13},{1... | collective-permute-start | bytes 196616 | tf_op jit(solution)/shard_map/ppermute | solution.py:156
  61.5 13.3 %collective-permute-start.6 = (bf16[16,128,128]{2,1,0:T(8,128)(2,1)S(1)}, bf16[16,128,128]{2,1,0:T(8,128)(2,1)S(1)}, u32[]{:S(2)}, u32[]{:S(2)}) collective-permute-start(bf16[16,128,128]{2,1,0:T(8,128)(2,1)S(1)} %constant_dynamic-update-slice_fusion.own), channel_id=1, source_target_pairs={{0,15},{1,0},{2,1},{3,2},{4,3},{5,4},{6,5},{7,6},{8,7},{9,8},{10,9... | collective-permute-start | bytes 1572872 | tf_op jit(solution)/shard_map/ppermute | solution.py:156
  63.8 15.0 %collective-permute-start.5 = (bf16[16,128,128]{2,1,0:T(8,128)(2,1)S(1)}, bf16[16,128,128]{2,1,0:T(8,128)(2,1)S(1)}, u32[]{:S(2)}, u32[]{:S(2)}) collective-permute-start(bf16[16,128,128]{2,1,0:T(8,128)(2,1)S(1)} %constant_dynamic-update-slice_fusion.own), channel_id=1, source_target_pairs={{0,1},{1,2},{2,3},{3,4},{4,5},{5,6},{6,7},{7,8},{8,9},{9,10},{10,1... | collective-permute-start | bytes 1572872 | tf_op jit(solution)/shard_map/ppermute | solution.py:156
  74.8 8.3 %collective-permute-start.8 = (bf16[8,128,128]{2,1,0:T(8,128)(2,1)S(1)}, bf16[8,128,128]{2,1,0:T(8,128)(2,1)S(1)}, u32[]{:S(2)}, u32[]{:S(2)}) collective-permute-start(bf16[8,128,128]{2,1,0:T(8,128)(2,1)S(1)} %slice.96), channel_id=1, source_target_pairs={{0,15},{1,0},{2,1},{3,2},{4,3},{5,4},{6,5},{7,6},{8,7},{9,8},{10,9... | collective-permute-start | bytes 786440 | tf_op jit(solution)/shard_map/ppermute | solution.py:156
  78.8 9.5 %collective-permute-start.7 = (bf16[8,128,128]{2,1,0:T(8,128)(2,1)S(1)}, bf16[8,128,128]{2,1,0:T(8,128)(2,1)S(1)}, u32[]{:S(2)}, u32[]{:S(2)}) collective-permute-start(bf16[8,128,128]{2,1,0:T(8,128)(2,1)S(1)} %slice.95), channel_id=1, source_target_pairs={{0,1},{1,2},{2,3},{3,4},{4,5},{5,6},{6,7},{7,8},{8,9},{9,10},{10,1... | collective-permute-start | bytes 786440 | tf_op jit(solution)/shard_map/ppermute | solution.py:156
  88.3 2.2 %copy-start = (bf16[16640,128]{1,0:T(8,128)(2,1)S(1)}, bf16[16640,128]{1,0:T(8,128)(2,1)}, u32[]{:S(2)}) copy-start(bf16[16640,128]{1,0:T(8,128)(2,1)} %all-gather.3.cloned.1.call-done) | copy-start | bytes 12779524
  90.5 12.5 %copy-start.1 = (bf16[16640,128]{1,0:T(8,128)(2,1)S(1)}, bf16[16640,128]{1,0:T(8,128)(2,1)}, u32[]{:S(2)}) copy-start(bf16[16640,128]{1,0:T(8,128)(2,1)} %all-gather.3.cloned.1.call-done) | copy-start | bytes 12779524
  101.1 26.2 %collective-permute-start.18 = (bf16[8,8,128,128]{3,2,1,0:T(8,128)(2,1)S(1)}, bf16[8,8,128,128]{3,2,1,0:T(8,128)(2,1)S(1)}, u32[]{:S(2)}, u32[]{:S(2)}) collective-permute-start(bf16[8,8,128,128]{3,2,1,0:T(8,128)(2,1)S(1)} %get-tuple-element.32), channel_id=1, source_target_pairs={{0,32},{32,0},{1,33},{33,1},{2,34},{34,2},{3,35},{35,3},{4,36},{36... | collective-permute-start | bytes 6291464 | tf_op jit(solution)/shard_map/ppermute | solution.py:160
  107.3 11.8 %collective-permute-start.11 = (bf16[8,128,128]{2,1,0:T(8,128)(2,1)S(1)}, bf16[8,128,128]{2,1,0:T(8,128)(2,1)S(1)}, u32[]{:S(2)}, u32[]{:S(2)}) collective-permute-start(bf16[8,128,128]{2,1,0:T(8,128)(2,1)S(1)} %get-tuple-element.30), channel_id=1, source_target_pairs={{0,1},{1,2},{2,3},{3,4},{4,5},{5,6},{6,7},{7,8},{8,9},{9,10},{10,1... | collective-permute-start | bytes 786440 | tf_op jit(solution)/shard_map/ppermute | solution.py:156
  109.2 11.9 %collective-permute-start.9 = (bf16[8,128,128]{2,1,0:T(8,128)(2,1)S(1)}, bf16[8,128,128]{2,1,0:T(8,128)(2,1)S(1)}, u32[]{:S(2)}, u32[]{:S(2)}) collective-permute-start(bf16[8,128,128]{2,1,0:T(8,128)(2,1)S(1)} %get-tuple-element.28), channel_id=1, source_target_pairs={{0,15},{1,0},{2,1},{3,2},{4,3},{5,4},{6,5},{7,6},{8,7},{9,8},{10,9... | collective-permute-start | bytes 786440 | tf_op jit(solution)/shard_map/ppermute | solution.py:156
  119.2 16.8 %collective-permute-start.12 = (bf16[16,128,128]{2,1,0:T(8,128)(2,1)S(1)}, bf16[16,128,128]{2,1,0:T(8,128)(2,1)}, u32[]{:S(2)}, u32[]{:S(2)}) collective-permute-start(bf16[16,128,128]{2,1,0:T(8,128)(2,1)S(1)} %pad_maximum_fusion.1), channel_id=1, source_target_pairs={{0,1},{1,2},{2,3},{3,4},{4,5},{5,6},{6,7},{7,8},{8,9},{9,10},{10,1... | collective-permute-start | bytes 1572872 | tf_op jit(solution)/shard_map/ppermute | solution.py:156
  122.1 16.2 %collective-permute-start.10 = (bf16[16,128,128]{2,1,0:T(8,128)(2,1)}, bf16[16,128,128]{2,1,0:T(8,128)(2,1)}, u32[]{:S(2)}, u32[]{:S(2)}) collective-permute-start(bf16[16,128,128]{2,1,0:T(8,128)(2,1)} %pad_maximum_fusion), channel_id=1, source_target_pairs={{0,15},{1,0},{2,1},{3,2},{4,3},{5,4},{6,5},{7,6},{8,7},{9,8},{10,9... | collective-permute-start | bytes 1572872 | tf_op jit(solution)/shard_map/ppermute | solution.py:156
  127.8 1.4 copy-start.2
  129.2 54.3 %all-to-all-start = ((bf16[8,8,128,128]{3,2,1,0:T(8,128)(2,1)}), bf16[8,8,128,128]{3,2,1,0:T(8,128)(2,1)S(1)}, u32[]{:S(2)}, u32[]{:S(2)}) async-start(bf16[8,8,128,128]{3,2,1,0:T(8,128)(2,1)} %copy-done.2), calls=%async_computation | async-start | bytes 4194304 | tf_op jit(solution)/shard_map/all_to_all | solution.py:212
  139.8 11.1 %collective-permute-start.13 = (bf16[2,128,128]{2,1,0:T(8,128)(2,1)S(1)}, bf16[2,128,128]{2,1,0:T(8,128)(2,1)S(1)}, u32[]{:S(2)}, u32[]{:S(2)}) collective-permute-start(bf16[2,128,128]{2,1,0:T(8,128)(2,1)S(1)} %get-tuple-element.44), channel_id=1, source_target_pairs={{0,12},{1,13},{2,14},{3,15},{4,0},{5,1},{6,2},{7,3},{8,4},{9,5},{1... | collective-permute-start | bytes 196616 | tf_op jit(solution)/shard_map/ppermute | solution.py:156
  145.5 10.1 %collective-permute-start.15 = (bf16[2,128,128]{2,1,0:T(8,128)(2,1)S(1)}, bf16[2,128,128]{2,1,0:T(8,128)(2,1)S(1)}, u32[]{:S(2)}, u32[]{:S(2)}) collective-permute-start(bf16[2,128,128]{2,1,0:T(8,128)(2,1)S(1)} %get-tuple-element.45), channel_id=1, source_target_pairs={{0,4},{1,5},{2,6},{3,7},{4,8},{5,9},{6,10},{7,11},{8,12},{9,13},{1... | collective-permute-start | bytes 196616 | tf_op jit(solution)/shard_map/ppermute | solution.py:156
  155.7 16.9 %collective-permute-start.16 = (bf16[4,128,128]{2,1,0:T(8,128)(2,1)S(1)}, bf16[4,128,128]{2,1,0:T(8,128)(2,1)S(1)}, u32[]{:S(2)}, u32[]{:S(2)}) collective-permute-start(bf16[4,128,128]{2,1,0:T(8,128)(2,1)S(1)} %pad_maximum_fusion.4), channel_id=1, source_target_pairs={{0,4},{1,5},{2,6},{3,7},{4,8},{5,9},{6,10},{7,11},{8,12},{9,13},{1... | collective-permute-start | bytes 393224 | tf_op jit(solution)/shard_map/ppermute | solution.py:156
  160.0 14.8 %collective-permute-start.14 = (bf16[4,128,128]{2,1,0:T(8,128)(2,1)S(1)}, bf16[4,128,128]{2,1,0:T(8,128)(2,1)S(1)}, u32[]{:S(2)}, u32[]{:S(2)}) collective-permute-start(bf16[4,128,128]{2,1,0:T(8,128)(2,1)S(1)} %pad_maximum_fusion.3), channel_id=1, source_target_pairs={{0,12},{1,13},{2,14},{3,15},{4,0},{5,1},{6,2},{7,3},{8,4},{9,5},{1... | collective-permute-start | bytes 393224 | tf_op jit(solution)/shard_map/ppermute | solution.py:156
  174.9 7.7 %collective-permute-start.17 = (bf16[2,128,128]{2,1,0:T(8,128)(2,1)S(1)}, bf16[2,128,128]{2,1,0:T(8,128)(2,1)S(1)}, u32[]{:S(2)}, u32[]{:S(2)}) collective-permute-start(bf16[2,128,128]{2,1,0:T(8,128)(2,1)S(1)} %slice.105), channel_id=1, source_target_pairs={{0,16},{16,0},{1,17},{17,1},{2,18},{18,2},{3,19},{19,3},{4,20},{20... | collective-permute-start | bytes 196616 | tf_op jit(solution)/shard_map/ppermute | solution.py:160
Sparse Core Ops, SparseCore 0:
  10.1 48.9 all-gather.2

commit v5 on v3

v5 whole, which is shorter than its diff:
```python
import jax
import jax.numpy as jnp
from jax import lax
from jax.experimental import pallas as pl
from jax.experimental.pallas import tpu as pltpu
from jax.sharding import Mesh
from jax.sharding import PartitionSpec as P

SQRT_TWO_PI = 0.7978845608028654
CUBIC = 0.044715
AXES = ("x", "yl", "core", "yh", "zh", "zl")
SIZES = (4, 2, 2, 2, 4, 4)
SEQ = ("x", "yl", "core")
MP = ("yh", "zh", "zl")
FAR = ("yh", "zh")
Z = ("zh", "zl")
BF16, F32 = jnp.bfloat16, jnp.float32
OWN, RIGHT, FAR_LEFT, FAR_RIGHT, LEFT = (0, 16), (16, 16), (32, 8), (40, 8), (48, 16)
PARTS = (OWN, LEFT, RIGHT, FAR_LEFT, FAR_RIGHT)


def gelu_parts(hidden):
    inner_arg = SQRT_TWO_PI * (hidden + CUBIC * hidden * hidden * hidden)
    tanh_inner = jnp.tanh(inner_arg)
    gelu_value = 0.5 * hidden * (1.0 + tanh_inner)
    gelu_slope = 0.5 * (1.0 + tanh_inner) + 0.5 * hidden * (
        1.0 - tanh_inner * tanh_inner
    ) * SQRT_TWO_PI * (1.0 + 3.0 * CUBIC * hidden * hidden)
    return gelu_value, gelu_slope


def fetch_columns(halves, w_all, w_sem):
    kept = halves[0].shape[0]
    for c in range(w_all.shape[1]):
        for h, w_ref in enumerate(halves):
            pltpu.make_async_copy(
                w_ref.at[:, pl.ds(c * 128, 128)], w_all.at[pl.ds(h * kept, kept), c], w_sem.at[c, h]
            ).start()


def await_column(halves, w_all, w_sem, c):
    kept = halves[0].shape[0]
    for h, w_ref in enumerate(halves):
        pltpu.make_async_copy(
            w_ref.at[:, pl.ds(0, 128)], w_all.at[pl.ds(h * kept, kept), c], w_sem.at[c, h]
        ).wait()


def hidden_kernel(
    rows_ref, own, left, right, far_left, far_right, mine, other, gact_ref, act_ref, gh_ref, keep_ref, give_ref, tok, w_all, sem, w_sem
):
    c = pl.program_id(0)
    half = keep_ref.shape[0]

    @pl.when(c == 0)
    def _():
        copies = [
            pltpu.make_async_copy(ref, tok.at[pl.ds(start, size)], sem.at[i])
            for i, (ref, (start, size)) in enumerate(zip((own, left, right, far_left, far_right), PARTS))
        ]
        for copy in copies:
            copy.start()
        fetch_columns((mine, other), w_all, w_sem)
        for copy in copies:
            copy.wait()

    await_column((mine, other), w_all, w_sem, c)
    weights = jnp.concatenate([w_all[k, c] for k in range(2 * half)], axis=0)
    picked = jnp.concatenate([tok[rows_ref[k, c]] for k in range(2 * half)], axis=1)
    hidden = jnp.dot(picked, weights, preferred_element_type=F32)
    value, slope = gelu_parts(hidden)
    act_ref[...] = value.astype(BF16)
    grad_hidden = (gact_ref[...].astype(F32) * slope).astype(BF16)
    gh_ref[...] = grad_hidden
    grads = lax.dot_general(
        grad_hidden, picked, (((0,), (0,)), ((), ())), preferred_element_type=F32
    ).astype(BF16)
    for j in range(half):
        keep_ref[j, 0] = grads[:, j * 128 : (j + 1) * 128]
        give_ref[j, 0] = grads[:, (half + j) * 128 : (half + j + 1) * 128]


def term_kernel(rows_ref, gh_ref, mine, other, own, left, right, far_left, far_right, acc, w_all, w_sem):
    c = pl.program_id(0)
    kept = w_all.shape[0]

    @pl.when(c == 0)
    def _():
        fetch_columns((mine, other), w_all, w_sem)
        acc[...] = jnp.zeros_like(acc)

    await_column((mine, other), w_all, w_sem, c)
    weights = jnp.concatenate([w_all[k, c] for k in range(kept)], axis=0)
    part = lax.dot_general(
        gh_ref[...], weights, (((1,), (1,)), ((), ())), preferred_element_type=F32
    )
    for k in range(kept):
        acc[rows_ref[k, c]] += part[:, k * 128 : (k + 1) * 128]

    @pl.when(c == pl.num_programs(0) - 1)
    def _():
        for ref, (start, size) in zip((own, left, right, far_left, far_right), PARTS):
            ref[...] = acc[start : start + size].astype(BF16)


def hidden_call(rows, parts, mine, other, grad_act):
    kept, cols = rows.shape
    n_tok = grad_act.shape[0]
    column = pl.BlockSpec((n_tok, 128), lambda c, *_: (0, c))
    half = pl.BlockSpec((kept // 2, 1, 128, 128), lambda c, *_: (0, c, 0, 0))
    wide = jax.ShapeDtypeStruct((n_tok, cols * 128), BF16)
    grads = jax.ShapeDtypeStruct((kept // 2, cols, 128, 128), BF16)
    return pl.pallas_call(
        hidden_kernel,
        grid_spec=pltpu.PrefetchScalarGridSpec(
            num_scalar_prefetch=1,
            grid=(cols,),
            in_specs=[pl.BlockSpec(memory_space=pl.ANY)] * 7 + [column],
            out_specs=[column, column, half, half],
            scratch_shapes=[
                pltpu.VMEM((64, n_tok, 128), BF16),
                pltpu.VMEM((kept, cols, 128, 128), BF16),
                pltpu.SemaphoreType.DMA((5,)),
                pltpu.SemaphoreType.DMA((cols, 2)),
            ],
        ),
        out_shape=[wide, wide, grads, grads],
        compiler_params=pltpu.CompilerParams(vmem_limit_bytes=18 * 2**20),
        cost_estimate=pl.CostEstimate(flops=1_073_741_824, bytes_accessed=11_000_000, transcendentals=131072),
    )(rows, *parts, mine, other, grad_act)


def term_call(rows, grad_hidden, mine, other):
    kept, cols = rows.shape
    n_tok = grad_hidden.shape[0]
    return pl.pallas_call(
        term_kernel,
        grid_spec=pltpu.PrefetchScalarGridSpec(
            num_scalar_prefetch=1,
            grid=(cols,),
            in_specs=[pl.BlockSpec((n_tok, 128), lambda c, rows: (0, c))]
            + [pl.BlockSpec(memory_space=pl.ANY)] * 2,
            out_specs=[pl.BlockSpec((n, n_tok, 128), lambda c, rows: (0, 0, 0)) for _, n in PARTS],
            scratch_shapes=[
                pltpu.VMEM((64, n_tok, 128), F32),
                pltpu.VMEM((kept, cols, 128, 128), BF16),
                pltpu.SemaphoreType.DMA((cols, 2)),
            ],
        ),
        out_shape=[jax.ShapeDtypeStruct((n, n_tok, 128), BF16) for _, n in PARTS],
        compiler_params=pltpu.CompilerParams(vmem_limit_bytes=20 * 2**20),
        cost_estimate=pl.CostEstimate(flops=536_870_912, bytes_accessed=7_000_000, transcendentals=0),
    )(rows, grad_hidden, mine, other)


def shift(a, by):
    return lax.ppermute(a, Z, [(i, (i + by) % 16) for i in range(16)])


def swap(a, axis):
    return lax.ppermute(a, axis, [(0, 1), (1, 0)])


def total(*arrays):
    return sum(a.astype(F32) for a in arrays)


def order_kernel(*refs):
    pass


def held_until(x, *after):
    anywhere = pl.BlockSpec(memory_space=pl.ANY)
    return pl.pallas_call(
        order_kernel,
        in_specs=[anywhere] * (1 + len(after)),
        out_specs=anywhere,
        out_shape=jax.ShapeDtypeStruct(x.shape, x.dtype),
        input_output_aliases={0: 0},
        compiler_params=pltpu.CompilerParams(vmem_limit_bytes=2**20),
    )(x, *after)


def gather_far(mine):
    own = lax.all_to_all(jnp.broadcast_to(mine, (8,) + mine.shape), FAR, 0, 0)
    return own.reshape((16,) + mine.shape[1:])


def gather_near(own):
    left, right = shift(own, 1), shift(own, -1)
    return own, left, right, shift(left[:8], 1), shift(right[8:], -1)


def near_kernel(left_ref, right_ref, from_right, from_left, left_out, right_out):
    left_out[...] = total(left_ref[...], from_right[...]).astype(BF16)
    right_out[...] = total(right_ref[...], from_left[...]).astype(BF16)


def add_near(left, right, from_right, from_left):
    n, n_tok, _ = left.shape
    first = pl.BlockSpec((n // 2, n_tok, 128), lambda i: (0, 0, 0))
    second = pl.BlockSpec((n // 2, n_tok, 128), lambda i: (1, 0, 0))
    return pl.pallas_call(
        near_kernel,
        grid=(1,),
        in_specs=[first, second, first, first],
        out_specs=[first, second],
        out_shape=[jax.ShapeDtypeStruct(left.shape, BF16)] * 2,
        input_output_aliases={0: 0, 1: 1},
        compiler_params=pltpu.CompilerParams(vmem_limit_bytes=6 * 2**20),
        cost_estimate=pl.CostEstimate(flops=500_000, bytes_accessed=1_500_000, transcendentals=0),
    )(left, right, from_right, from_left)


def combine_kernel(own_ref, left_ref, right_ref, grads_ref, own_out, grads_out):
    own_out[...] = total(own_ref[...], left_ref[...], right_ref[...]).astype(BF16)
    for c in range(grads_ref.shape[1]):
        summed = sum(grads_ref[i, c].astype(F32) for i in range(grads_ref.shape[0]))
        grads_out[c] = summed.T.astype(BF16)


def finish_kernel(far_ref, out_ref):
    summed = sum(far_ref[i].astype(F32) for i in range(far_ref.shape[0])).astype(BF16)
    out_ref[...] = jnp.concatenate([summed[0], summed[1]], axis=1)


def reduce_all(keep, give, own, left, right, far_left, far_right):
    both = add_after(keep, swap(give, "core"), own)
    grads = lax.all_to_all(both, ("x", "yl"), 0, 0)
    left, right = add_near(left, right, shift(far_left, -1), shift(far_right, 1))
    own, grads = pl.pallas_call(
        combine_kernel,
        out_shape=[
            jax.ShapeDtypeStruct(own.shape, BF16),
            jax.ShapeDtypeStruct(grads.shape[1:], BF16),
        ],
        compiler_params=pltpu.CompilerParams(vmem_limit_bytes=12 * 2**20),
        cost_estimate=pl.CostEstimate(flops=2_000_000, bytes_accessed=4_500_000, transcendentals=0),
    )(own, shift(left, -1), shift(right, 1), grads)
    far = lax.all_to_all(own.reshape((8, 2) + own.shape[1:]), FAR, 0, 0)
    summed = pl.pallas_call(
        finish_kernel,
        out_shape=jax.ShapeDtypeStruct((own.shape[1], 256), BF16),
        compiler_params=pltpu.CompilerParams(vmem_limit_bytes=4 * 2**20),
        cost_estimate=pl.CostEstimate(flops=300_000, bytes_accessed=600_000, transcendentals=0),
    )(far)
    return summed, grads[:, None]


def order_kernel(*refs):
    pass


def held_until(x, *after):
    anywhere = pl.BlockSpec(memory_space=pl.ANY)
    return pl.pallas_call(
        order_kernel,
        in_specs=[anywhere] * (1 + len(after)),
        out_specs=anywhere,
        out_shape=jax.ShapeDtypeStruct(x.shape, x.dtype),
        input_output_aliases={0: 0},
        compiler_params=pltpu.CompilerParams(vmem_limit_bytes=2**20),
    )(x, *after)


def add_kernel(keep_ref, got_ref, after_ref, both_ref):
    both_ref[...] = total(keep_ref[...], got_ref[...]).astype(BF16)


def add_after(keep, got, after):
    block = pl.BlockSpec((2,) + keep.shape[1:], lambda i: (i, 0, 0, 0))
    return pl.pallas_call(
        add_kernel,
        grid=(keep.shape[0] // 2,),
        in_specs=[block, block, pl.BlockSpec(memory_space=pl.ANY)],
        out_specs=block,
        out_shape=jax.ShapeDtypeStruct(keep.shape, BF16),
        compiler_params=pltpu.CompilerParams(vmem_limit_bytes=8 * 2**20),
        cost_estimate=pl.CostEstimate(flops=1_000_000, bytes_accessed=6_300_000, transcendentals=0),
    )(keep, got, after)


def gather_weights(block_values, block_rows, after, later):
    cols = block_values.shape[0]
    row_tile = jnp.zeros((16, 128), BF16).at[0, :cols].set(block_rows[:, 0].astype(BF16))
    sent = jnp.concatenate([block_values.reshape(cols * 128, 128), row_tile])
    sent = held_until(jnp.broadcast_to(sent, (8,) + sent.shape), after)
    mine = held_until(lax.all_to_all(sent, ("x", "yl"), 0, 0), *later)
    other = swap(mine, "core")
    rows = jnp.concatenate([mine[:, cols * 128, :cols], other[:, cols * 128, :cols]])
    return mine, other, rows.astype(jnp.int32)


def place_of(rows):
    return (rows // 2 - lax.axis_index("zl")) % 4 * 16 + rows // 32 * 8 + rows % 32 // 8 * 2 + rows % 2


def shards(tokens, block_values, block_rows, grad_act):
    n_tok = tokens.shape[0]
    own = gather_far(tokens.reshape(n_tok, 2, 128).transpose(1, 0, 2))
    parts = gather_near(own)
    mine, other, rows = gather_weights(block_values, block_rows, own, parts[3:])
    rows = place_of(rows)
    activated, grad_hidden, keep, give = hidden_call(rows, parts, mine, other, grad_act)
    terms = term_call(rows, grad_hidden, mine, other)
    summed, grads = reduce_all(keep, give, *terms)
    return activated, summed, grads


def solution(mesh):
    fine = Mesh(mesh.devices.reshape(SIZES), AXES)
    in_specs = (P(SEQ, MP), P(MP, SEQ, None, None), P(MP, SEQ), P(SEQ, MP))
    out_specs = (P(SEQ, MP), P(SEQ, MP), P(MP, SEQ, None, None))
    return jax.shard_map(shards, mesh=fine, in_specs=in_specs, out_specs=out_specs, check_vma=False)
```

time: 190 us -> 200 us (1.053)
  blocking collectives: 82.5 us -> 41.1 us
  waiting for transfers between devices: 27 us -> 64.7 us
  starting transfers between devices: 37.9 us -> 58.8 us
  between operations: 14.3 us -> 0.86 us
  local copies, waits for them, and re-layouts: 8.93 us -> 16.3 us
  other arithmetic: 5.07 us -> 1.66 us
  Pallas kernels: 13.2 us -> 15.4 us
    all_to_all x2 -> x1, blocking collectives: 82.5 us -> 41.1 us  [reduce_all(): far = lax.all_to_all(own.reshape((8, 2) + own.shape[1:]), FAR, 0, 0)]
    all_to_all x0 -> x2, waiting for transfers between devices: none -> 28.8 us  [the longest x1 26.6 us: gather_far(): own = lax.all_to_all(jnp.broadcast_to(mine, (8,) + mine.shape), FAR, 0, 0)]
    all_to_all x0 -> x2, starting transfers between devices: none -> 22.4 us  [the longest x1 18.3 us: gather_far(): own = lax.all_to_all(jnp.broadcast_to(mine, (8,) + mine.shape), FAR, 0, 0)]
    ppermute x8, waiting for transfers between devices: 25 us -> 32 us  [shift(): return lax.ppermute(a, Z, [(i, (i + by) % 16) for i in range(16)])]
    unnamed x20 -> x32, local copies, waits for them, and re-layouts: 6.88 us -> 13.5 us
    ppermute x1 -> x2, waiting for transfers between devices: 0.01 us -> 3.92 us  [swap(): return lax.ppermute(a, axis, [(0, 1), (1, 0)])]
    ppermute x8, starting transfers between devices: 27.3 us -> 24.7 us  [shift(): return lax.ppermute(a, Z, [(i, (i + by) % 16) for i in range(16)])]
    ppermute x1 -> x2, starting transfers between devices: 6.35 us -> 6.51 us  [swap(): return lax.ppermute(a, axis, [(0, 1), (1, 0)])]
  transfers between devices with their start and end apart: 11 -> 13, of which waited for: 7 -> 10; matrix products, arithmetic and copies ran while one was open for 2% -> 1% of each run, Pallas kernels for 2% -> 3%
where the time goes in v5:
time: 200 us; the launch traced here: 199 us
  waiting for transfers between devices  64.7 us (32%)
  starting transfers between devices  58.8 us (29%)
  blocking collectives  41.1 us (21%)
  local copies, waits for them, and re-layouts  16.3 us (8%)
  Pallas kernels  15.4 us (8%)
    all_to_all x1, blocking collectives, reduce_all(): far = lax.all_to_all(own.reshape((8, 2) + own.shape[1:]), FAR, 0, 0)  41.1 us
    ppermute x8, waiting for transfers between devices, shift(): return lax.ppermute(a, Z, [(i, (i + by) % 16) for i in range(16)])  32 us
    all_to_all x1, waiting for transfers between devices, gather_far(): own = lax.all_to_all(jnp.broadcast_to(mine, (8,) + mine.shape), FAR, 0, 0)  26.6 us
    ppermute x8, starting transfers between devices, shift(): return lax.ppermute(a, Z, [(i, (i + by) % 16) for i in range(16)])  24.7 us
    all_to_all x1, starting transfers between devices, gather_far(): own = lax.all_to_all(jnp.broadcast_to(mine, (8,) + mine.shape), FAR, 0, 0)  18.3 us
    unnamed x32, local copies, waits for them, and re-layouts  13.5 us
    pallas_call x1, Pallas kernels, hidden_call(): pl.pallas_call(hidden_kernel, grid_spec=pltpu.PrefetchScalarGridSpec(num_...  7.95 us
    ppermute x2, starting transfers between devices, swap(): return lax.ppermute(a, axis, [(0, 1), (1, 0)])  6.51 us
  transfers between devices with their start and end apart: 13, of which 10 were waited for; matrix products, arithmetic and copies ran while one was open for 1% of the time, Pallas kernels for 3%

profile of v5, /device:TPU:1, one launch (start us, length us, event | category | flops | bytes accessed | tf_op | source)
XLA Modules:
  0.0 198.9 jit_solution(14315717860076683488)
XLA Ops:
  0.6 0.9 reshape.55
  1.5 0.9 broadcast_in_dim.11
  2.4 18.3 %all-to-all-start = ((bf16[8,2,128,128]{3,2,1,0:T(8,128)(2,1)}), bf16[8,2,128,128]{3,2,1,0:T(8,128)(2,1)S(1)}, u32[]{:S(2)}, u32[]{:S(2)}) async-start(bf16[8,2,128,128]{3,2,1,0:T(8,128)(2,1)} %broadcast_in_dim.11), calls=%async_computation | async-start | bytes 1048576 | tf_op jit(solution)/shard_map/all_to_all | solution.py:185
  20.7 0.7 convert_bitcast_fusion
  21.3 1.0 fusion.1
  22.3 26.6 %all-to-all-done = bf16[8,2,128,128]{3,2,1,0:T(8,128)(2,1)S(1)} async-done(((bf16[8,2,128,128]{3,2,1,0:T(8,128)(2,1)}), bf16[8,2,128,128]{3,2,1,0:T(8,128)(2,1)S(1)}, u32[]{:S(2)}, u32[]{:S(2)}) %all-to-all-start) | async-done | bytes 524320 | tf_op jit(solution)/shard_map/all_to_all | solution.py:185
  49.2 1.3 copy-done
  50.6 4.1 %all-to-all-start.1 = ((bf16[8,1040,128]{2,1,0:T(8,128)(2,1)}), bf16[8,1040,128]{2,1,0:T(8,128)(2,1)S(1)}, u32[]{:S(2)}, u32[]{:S(2)}) async-start(bf16[8,1040,128]{2,1,0:T(8,128)(2,1)} %copy-done), calls=%async_computation.1 | async-start | bytes 4259840 | tf_op jit(solution)/shard_map/all_to_all | solution.py:288
  54.7 4.9 %collective-permute-start.2 = (bf16[16,128,128]{2,1,0:T(8,128)(2,1)S(1)}, bf16[16,128,128]{2,1,0:T(8,128)(2,1)S(1)}, u32[]{:S(2)}, u32[]{:S(2)}) collective-permute-start(bf16[16,128,128]{2,1,0:T(8,128)(2,1)S(1)} %bitcast.16), channel_id=1, source_target_pairs={{0,15},{1,0},{2,1},{3,2},{4,3},{5,4},{6,5},{7,6},{8,7},{9,8},{10,9... | collective-permute-start | bytes 1572872 | tf_op jit(solution)/shard_map/ppermute | solution.py:157
  59.6 3.6 %collective-permute-start = (bf16[16,128,128]{2,1,0:T(8,128)(2,1)S(1)}, bf16[16,128,128]{2,1,0:T(8,128)(2,1)S(1)}, u32[]{:S(2)}, u32[]{:S(2)}) collective-permute-start(bf16[16,128,128]{2,1,0:T(8,128)(2,1)S(1)} %bitcast.17), channel_id=1, source_target_pairs={{0,1},{1,2},{2,3},{3,4},{4,5},{5,6},{6,7},{7,8},{8,9},{9,10},{10,1... | collective-permute-start | bytes 1572872 | tf_op jit(solution)/shard_map/ppermute | solution.py:157
  63.2 8.0 %collective-permute-done.2.right = bf16[16,128,128]{2,1,0:T(8,128)(2,1)S(1)} collective-permute-done((bf16[16,128,128]{2,1,0:T(8,128)(2,1)S(1)}, bf16[16,128,128]{2,1,0:T(8,128)(2,1)S(1)}, u32[]{:S(2)}, u32[]{:S(2)}) %collective-permute-start.2) | collective-permute-done | bytes 524320 | tf_op jit(solution)/shard_map/ppermute | solution.py:157
  71.2 2.5 %collective-permute-start.3 = (bf16[8,128,128]{2,1,0:T(8,128)(2,1)S(1)}, bf16[8,128,128]{2,1,0:T(8,128)(2,1)S(1)}, u32[]{:S(2)}, u32[]{:S(2)}) collective-permute-start(bf16[8,128,128]{2,1,0:T(8,128)(2,1)S(1)} %slice.33), channel_id=1, source_target_pairs={{0,15},{1,0},{2,1},{3,2},{4,3},{5,4},{6,5},{7,6},{8,7},{9,8},{10,9... | collective-permute-start | bytes 786440 | tf_op jit(solution)/shard_map/ppermute | solution.py:157
  73.8 2.8 %collective-permute-start.1 = (bf16[8,128,128]{2,1,0:T(8,128)(2,1)S(1)}, bf16[8,128,128]{2,1,0:T(8,128)(2,1)S(1)}, u32[]{:S(2)}, u32[]{:S(2)}) collective-permute-start(bf16[8,128,128]{2,1,0:T(8,128)(2,1)S(1)} %slice.32), channel_id=1, source_target_pairs={{0,1},{1,2},{2,3},{3,4},{4,5},{5,6},{6,7},{7,8},{8,9},{9,10},{10,1... | collective-permute-start | bytes 786440 | tf_op jit(solution)/shard_map/ppermute | solution.py:157
  76.5 2.1 %collective-permute-done.3.refs_2_.far_right = bf16[8,128,128]{2,1,0:T(8,128)(2,1)S(1)} collective-permute-done((bf16[8,128,128]{2,1,0:T(8,128)(2,1)S(1)}, bf16[8,128,128]{2,1,0:T(8,128)(2,1)S(1)}, u32[]{:S(2)}, u32[]{:S(2)}) %collective-permute-start.3) | collective-permute-done | bytes 262176 | tf_op jit(solution)/shard_map/ppermute | solution.py:157
  78.6 3.8 %collective-permute-done.1.refs_1_.far_left = bf16[8,128,128]{2,1,0:T(8,128)(2,1)S(1)} collective-permute-done((bf16[8,128,128]{2,1,0:T(8,128)(2,1)S(1)}, bf16[8,128,128]{2,1,0:T(8,128)(2,1)S(1)}, u32[]{:S(2)}, u32[]{:S(2)}) %collective-permute-start.1) | collective-permute-done | bytes 262176 | tf_op jit(solution)/shard_map/ppermute | solution.py:157
  82.4 0.7 copy-done.4
  83.1 2.1 %all-to-all-done.1.refs_0_ = bf16[8,1040,128]{2,1,0:T(8,128)(2,1)S(1)} async-done(((bf16[8,1040,128]{2,1,0:T(8,128)(2,1)}), bf16[8,1040,128]{2,1,0:T(8,128)(2,1)S(1)}, u32[]{:S(2)}, u32[]{:S(2)}) %all-to-all-start.1) | async-done | bytes 2129952 | tf_op jit(solution)/shard_map/all_to_all | solution.py:288
  85.2 0.9 copy-done.5
  86.2 4.2 %collective-permute-start.4 = (bf16[8,1040,128]{2,1,0:T(8,128)(2,1)S(1)}, bf16[8,1040,128]{2,1,0:T(8,128)(2,1)}, u32[]{:S(2)}, u32[]{:S(2)}) collective-permute-start(bf16[8,1040,128]{2,1,0:T(8,128)(2,1)S(1)} %shard_map.68.mine), channel_id=1, source_target_pairs={{0,32},{32,0},{1,33},{33,1},{2,34},{34,2},{3,35},{35,3},{4,36},{36... | collective-permute-start | bytes 6389768 | tf_op jit(solution)/shard_map/ppermute | solution.py:161
  90.4 3.9 %collective-permute-done.4.other = bf16[8,1040,128]{2,1,0:T(8,128)(2,1)} collective-permute-done((bf16[8,1040,128]{2,1,0:T(8,128)(2,1)S(1)}, bf16[8,1040,128]{2,1,0:T(8,128)(2,1)}, u32[]{:S(2)}, u32[]{:S(2)}) %collective-permute-start.4) | collective-permute-done | bytes 2129952 | tf_op jit(solution)/shard_map/ppermute | solution.py:161
  94.4 0.7 slice.35
  95.1 1.0 copy-done.3
  96.2 0.9 copy-done.6
  97.1 0.9 copy-done.13
  98.1 7.9 %shard_map.69 = (bf16[128,1024]{1,0:T(8,128)(2,1)}, bf16[128,1024]{1,0:T(8,128)(2,1)S(1)}, bf16[8,8,128,128]{3,2,1,0:T(8,128)(2,1)S(1)}, bf16[8,8,128,128]{3,2,1,0:T(8,128)(2,1)S(1)}) custom-call(s32[16,8]{1,0:T(8,128)S(1)} %fusion.11.rows_ref, bf16[16,128,128]{2,1,0:T(8,128)(2,1)S(1)} %bitcast.18, bf16[16,128,128]{2,1,0:T(8,128)(2,1)S(1)} %copy-done.3, ...), custom_call_target="tpu_custom_call" | custom-call | flops 1073741824 | bytes 11000000 | tf_op jit(solution)/shard_map/pallas_call | solution.py:113
  106.0 2.3 %collective-permute-start.9 = (bf16[8,8,128,128]{3,2,1,0:T(8,128)(2,1)S(1)}, bf16[8,8,128,128]{3,2,1,0:T(8,128)(2,1)S(1)}, u32[]{:S(2)}, u32[]{:S(2)}) collective-permute-start(bf16[8,8,128,128]{3,2,1,0:T(8,128)(2,1)S(1)} %get-tuple-element.38), channel_id=1, source_target_pairs={{0,32},{32,0},{1,33},{33,1},{2,34},{34,2},{3,35},{35,3},{4,36},{36... | collective-permute-start | bytes 6291464 | tf_op jit(solution)/shard_map/ppermute | solution.py:161
  108.3 4.8 %shard_map.70 = (bf16[16,128,128]{2,1,0:T(8,128)(2,1)S(1)}, bf16[16,128,128]{2,1,0:T(8,128)(2,1)S(1)}, bf16[16,128,128]{2,1,0:T(8,128)(2,1)S(1)}, bf16[8,128,128...) custom-call(s32[16,8]{1,0:T(8,128)S(1)} %fusion.11.rows_ref, bf16[128,1024]{1,0:T(8,128)(2,1)S(1)} %get-tuple-element.29.gh_ref, ...), custom_call_target="tpu_custom_call" | custom-call | flops 536870912 | bytes 7000000 | tf_op jit(solution)/shard_map/pallas_call | solution.py:136
  113.1 0.8 copy-done.7
  113.9 0.7 copy-done.14
  114.6 0.5 shard_map.72
  115.1 1.3 copy-done.1
  116.5 5.1 %all-to-all-start.2 = ((bf16[8,8,128,128]{3,2,1,0:T(8,128)(2,1)}), bf16[8,8,128,128]{3,2,1,0:T(8,128)(2,1)S(1)}, u32[]{:S(2)}, u32[]{:S(2)}) async-start(bf16[8,8,128,128]{3,2,1,0:T(8,128)(2,1)} %copy-done.1), calls=%async_computation.2 | async-start | bytes 4194304 | tf_op jit(solution)/shard_map/all_to_all | solution.py:229
  121.6 2.1 %collective-permute-start.5 = (bf16[8,128,128]{2,1,0:T(8,128)(2,1)}, bf16[8,128,128]{2,1,0:T(8,128)(2,1)S(1)}, u32[]{:S(2)}, u32[]{:S(2)}) collective-permute-start(bf16[8,128,128]{2,1,0:T(8,128)(2,1)} %copy-done.14), channel_id=1, source_target_pairs={{0,15},{1,0},{2,1},{3,2},{4,3},{5,4},{6,5},{7,6},{8,7},{9,8},{10,9... | collective-permute-start | bytes 786440 | tf_op jit(solution)/shard_map/ppermute | solution.py:157
  123.7 3.7 %collective-permute-start.6 = (bf16[8,128,128]{2,1,0:T(8,128)(2,1)S(1)}, bf16[8,128,128]{2,1,0:T(8,128)(2,1)S(1)}, u32[]{:S(2)}, u32[]{:S(2)}) collective-permute-start(bf16[8,128,128]{2,1,0:T(8,128)(2,1)S(1)} %get-tuple-element.34), channel_id=1, source_target_pairs={{0,1},{1,2},{2,3},{3,4},{4,5},{5,6},{6,7},{7,8},{8,9},{9,10},{10,1... | collective-permute-start | bytes 786440 | tf_op jit(solution)/shard_map/ppermute | solution.py:157
  127.3 4.8 %collective-permute-done.5.from_right = bf16[8,128,128]{2,1,0:T(8,128)(2,1)S(1)} collective-permute-done((bf16[8,128,128]{2,1,0:T(8,128)(2,1)}, bf16[8,128,128]{2,1,0:T(8,128)(2,1)S(1)}, u32[]{:S(2)}, u32[]{:S(2)}) %collective-permute-start.5) | collective-permute-done | bytes 262176 | tf_op jit(solution)/shard_map/ppermute | solution.py:157
  132.1 2.1 %collective-permute-done.6.from_left = bf16[8,128,128]{2,1,0:T(8,128)(2,1)S(1)} collective-permute-done((bf16[8,128,128]{2,1,0:T(8,128)(2,1)S(1)}, bf16[8,128,128]{2,1,0:T(8,128)(2,1)S(1)}, u32[]{:S(2)}, u32[]{:S(2)}) %collective-permute-start.6) | collective-permute-done | bytes 262176 | tf_op jit(solution)/shard_map/ppermute | solution.py:157
  134.2 1.0 copy-done.8
  135.7 2.4 %collective-permute-start.7 = (bf16[16,128,128]{2,1,0:T(8,128)(2,1)S(1)}, bf16[16,128,128]{2,1,0:T(8,128)(2,1)S(1)}, u32[]{:S(2)}, u32[]{:S(2)}) collective-permute-start(bf16[16,128,128]{2,1,0:T(8,128)(2,1)S(1)} %get-tuple-element.35), channel_id=1, source_target_pairs={{0,15},{1,0},{2,1},{3,2},{4,3},{5,4},{6,5},{7,6},{8,7},{9,8},{10,9... | collective-permute-start | bytes 1572872 | tf_op jit(solution)/shard_map/ppermute | solution.py:157
  138.1 2.9 %collective-permute-start.8 = (bf16[16,128,128]{2,1,0:T(8,128)(2,1)S(1)}, bf16[16,128,128]{2,1,0:T(8,128)(2,1)S(1)}, u32[]{:S(2)}, u32[]{:S(2)}) collective-permute-start(bf16[16,128,128]{2,1,0:T(8,128)(2,1)S(1)} %get-tuple-element.36), channel_id=1, source_target_pairs={{0,1},{1,2},{2,3},{3,4},{4,5},{5,6},{6,7},{7,8},{8,9},{9,10},{10,1... | collective-permute-start | bytes 1572872 | tf_op jit(solution)/shard_map/ppermute | solution.py:157
  141.0 8.7 %collective-permute-done.7.left_ref = bf16[16,128,128]{2,1,0:T(8,128)(2,1)S(1)} collective-permute-done((bf16[16,128,128]{2,1,0:T(8,128)(2,1)S(1)}, bf16[16,128,128]{2,1,0:T(8,128)(2,1)S(1)}, u32[]{:S(2)}, u32[]{:S(2)}) %collective-permute-start.7) | collective-permute-done | bytes 524320 | tf_op jit(solution)/shard_map/ppermute | solution.py:157
  149.7 0.8 copy-done.9
  150.5 2.5 %collective-permute-done.8.right_ref = bf16[16,128,128]{2,1,0:T(8,128)(2,1)S(1)} collective-permute-done((bf16[16,128,128]{2,1,0:T(8,128)(2,1)S(1)}, bf16[16,128,128]{2,1,0:T(8,128)(2,1)S(1)}, u32[]{:S(2)}, u32[]{:S(2)}) %collective-permute-start.8) | collective-permute-done | bytes 524320 | tf_op jit(solution)/shard_map/ppermute | solution.py:157
  153.0 0.8 copy-done.11
  153.8 1.0 copy-done.10
  154.9 1.0 copy-done.12
  155.9 1.1 shard_map.73
  157.0 41.1 %all_to_all.20.far_ref = bf16[8,2,128,128]{3,2,1,0:T(8,128)(2,1)S(1)} all-to-all(bf16[8,2,128,128]{3,2,1,0:T(8,128)(2,1)S(1)} %bitcast.19), channel_id=1, replica_groups=mesh['x'=4,'yl'=2,'core'=2,'yh'=2,'zh'=4,'zl'=4] {'yh','zh'}, dimensions={0} | all-to-all | bytes 1048576 | tf_op jit(solution)/shard_map/all_to_all | solution.py:240
  198.2 0.7 shard_map.74
  (30 shorter events, 0.8 us)
Async XLA Ops:
  2.4 46.5 %all-to-all-start = ((bf16[8,2,128,128]{3,2,1,0:T(8,128)(2,1)}), bf16[8,2,128,128]{3,2,1,0:T(8,128)(2,1)S(1)}, u32[]{:S(2)}, u32[]{:S(2)}) async-start(bf16[8,2,128,128]{3,2,1,0:T(8,128)(2,1)} %broadcast_in_dim.11), calls=%async_computation | async-start | bytes 1048576 | tf_op jit(solution)/shard_map/all_to_all | solution.py:185
  49.2 1.4 copy-start
  50.6 34.6 %all-to-all-start.1 = ((bf16[8,1040,128]{2,1,0:T(8,128)(2,1)}), bf16[8,1040,128]{2,1,0:T(8,128)(2,1)S(1)}, u32[]{:S(2)}, u32[]{:S(2)}) async-start(bf16[8,1040,128]{2,1,0:T(8,128)(2,1)} %copy-done), calls=%async_computation.1 | async-start | bytes 4259840 | tf_op jit(solution)/shard_map/all_to_all | solution.py:288
  54.7 16.5 %collective-permute-start.2 = (bf16[16,128,128]{2,1,0:T(8,128)(2,1)S(1)}, bf16[16,128,128]{2,1,0:T(8,128)(2,1)S(1)}, u32[]{:S(2)}, u32[]{:S(2)}) collective-permute-start(bf16[16,128,128]{2,1,0:T(8,128)(2,1)S(1)} %bitcast.16), channel_id=1, source_target_pairs={{0,15},{1,0},{2,1},{3,2},{4,3},{5,4},{6,5},{7,6},{8,7},{9,8},{10,9... | collective-permute-start | bytes 1572872 | tf_op jit(solution)/shard_map/ppermute | solution.py:157
  59.6 14.1 %collective-permute-start = (bf16[16,128,128]{2,1,0:T(8,128)(2,1)S(1)}, bf16[16,128,128]{2,1,0:T(8,128)(2,1)S(1)}, u32[]{:S(2)}, u32[]{:S(2)}) collective-permute-start(bf16[16,128,128]{2,1,0:T(8,128)(2,1)S(1)} %bitcast.17), channel_id=1, source_target_pairs={{0,1},{1,2},{2,3},{3,4},{4,5},{5,6},{6,7},{7,8},{8,9},{9,10},{10,1... | collective-permute-start | bytes 1572872 | tf_op jit(solution)/shard_map/ppermute | solution.py:157
  71.2 7.4 %collective-permute-start.3 = (bf16[8,128,128]{2,1,0:T(8,128)(2,1)S(1)}, bf16[8,128,128]{2,1,0:T(8,128)(2,1)S(1)}, u32[]{:S(2)}, u32[]{:S(2)}) collective-permute-start(bf16[8,128,128]{2,1,0:T(8,128)(2,1)S(1)} %slice.33), channel_id=1, source_target_pairs={{0,15},{1,0},{2,1},{3,2},{4,3},{5,4},{6,5},{7,6},{8,7},{9,8},{10,9... | collective-permute-start | bytes 786440 | tf_op jit(solution)/shard_map/ppermute | solution.py:157
  73.7 4.9 %copy-start.2 = (bf16[16,128,128]{2,1,0:T(8,128)(2,1)}, bf16[16,128,128]{2,1,0:T(8,128)(2,1)S(1)}, u32[]{:S(2)}) copy-start(bf16[16,128,128]{2,1,0:T(8,128)(2,1)S(1)} %collective-permute-done.left) | copy-start | bytes 1572868
  73.8 8.6 %collective-permute-start.1 = (bf16[8,128,128]{2,1,0:T(8,128)(2,1)S(1)}, bf16[8,128,128]{2,1,0:T(8,128)(2,1)S(1)}, u32[]{:S(2)}, u32[]{:S(2)}) collective-permute-start(bf16[8,128,128]{2,1,0:T(8,128)(2,1)S(1)} %slice.32), channel_id=1, source_target_pairs={{0,1},{1,2},{2,3},{3,4},{4,5},{5,6},{6,7},{7,8},{8,9},{9,10},{10,1... | collective-permute-start | bytes 786440 | tf_op jit(solution)/shard_map/ppermute | solution.py:157
  82.4 0.7 copy-start.4
  85.2 1.0 copy-start.5
  86.2 8.2 %collective-permute-start.4 = (bf16[8,1040,128]{2,1,0:T(8,128)(2,1)S(1)}, bf16[8,1040,128]{2,1,0:T(8,128)(2,1)}, u32[]{:S(2)}, u32[]{:S(2)}) collective-permute-start(bf16[8,1040,128]{2,1,0:T(8,128)(2,1)S(1)} %shard_map.68.mine), channel_id=1, source_target_pairs={{0,32},{32,0},{1,33},{33,1},{2,34},{34,2},{3,35},{35,3},{4,36},{36... | collective-permute-start | bytes 6389768 | tf_op jit(solution)/shard_map/ppermute | solution.py:161
  95.1 1.0 copy-start.3
  96.2 0.9 copy-start.6
  97.1 0.9 copy-start.13
  106.0 8.6 %collective-permute-start.9 = (bf16[8,8,128,128]{3,2,1,0:T(8,128)(2,1)S(1)}, bf16[8,8,128,128]{3,2,1,0:T(8,128)(2,1)S(1)}, u32[]{:S(2)}, u32[]{:S(2)}) collective-permute-start(bf16[8,8,128,128]{3,2,1,0:T(8,128)(2,1)S(1)} %get-tuple-element.38), channel_id=1, source_target_pairs={{0,32},{32,0},{1,33},{33,1},{2,34},{34,2},{3,35},{35,3},{4,36},{36... | collective-permute-start | bytes 6291464 | tf_op jit(solution)/shard_map/ppermute | solution.py:161
  113.1 0.8 copy-start.7
  113.9 0.7 copy-start.14
  115.1 1.4 copy-start.1
  116.5 37.4 %all-to-all-start.2 = ((bf16[8,8,128,128]{3,2,1,0:T(8,128)(2,1)}), bf16[8,8,128,128]{3,2,1,0:T(8,128)(2,1)S(1)}, u32[]{:S(2)}, u32[]{:S(2)}) async-start(bf16[8,8,128,128]{3,2,1,0:T(8,128)(2,1)} %copy-done.1), calls=%async_computation.2 | async-start | bytes 4194304 | tf_op jit(solution)/shard_map/all_to_all | solution.py:229
  121.6 10.5 %collective-permute-start.5 = (bf16[8,128,128]{2,1,0:T(8,128)(2,1)}, bf16[8,128,128]{2,1,0:T(8,128)(2,1)S(1)}, u32[]{:S(2)}, u32[]{:S(2)}) collective-permute-start(bf16[8,128,128]{2,1,0:T(8,128)(2,1)} %copy-done.14), channel_id=1, source_target_pairs={{0,15},{1,0},{2,1},{3,2},{4,3},{5,4},{6,5},{7,6},{8,7},{9,8},{10,9... | collective-permute-start | bytes 786440 | tf_op jit(solution)/shard_map/ppermute | solution.py:157
  123.7 10.6 %collective-permute-start.6 = (bf16[8,128,128]{2,1,0:T(8,128)(2,1)S(1)}, bf16[8,128,128]{2,1,0:T(8,128)(2,1)S(1)}, u32[]{:S(2)}, u32[]{:S(2)}) collective-permute-start(bf16[8,128,128]{2,1,0:T(8,128)(2,1)S(1)} %get-tuple-element.34), channel_id=1, source_target_pairs={{0,1},{1,2},{2,3},{3,4},{4,5},{5,6},{6,7},{7,8},{8,9},{9,10},{10,1... | collective-permute-start | bytes 786440 | tf_op jit(solution)/shard_map/ppermute | solution.py:157
  134.2 1.0 copy-start.8
  135.7 14.0 %collective-permute-start.7 = (bf16[16,128,128]{2,1,0:T(8,128)(2,1)S(1)}, bf16[16,128,128]{2,1,0:T(8,128)(2,1)S(1)}, u32[]{:S(2)}, u32[]{:S(2)}) collective-permute-start(bf16[16,128,128]{2,1,0:T(8,128)(2,1)S(1)} %get-tuple-element.35), channel_id=1, source_target_pairs={{0,15},{1,0},{2,1},{3,2},{4,3},{5,4},{6,5},{7,6},{8,7},{9,8},{10,9... | collective-permute-start | bytes 1572872 | tf_op jit(solution)/shard_map/ppermute | solution.py:157
  138.1 15.0 %collective-permute-start.8 = (bf16[16,128,128]{2,1,0:T(8,128)(2,1)S(1)}, bf16[16,128,128]{2,1,0:T(8,128)(2,1)S(1)}, u32[]{:S(2)}, u32[]{:S(2)}) collective-permute-start(bf16[16,128,128]{2,1,0:T(8,128)(2,1)S(1)} %get-tuple-element.36), channel_id=1, source_target_pairs={{0,1},{1,2},{2,3},{3,4},{4,5},{5,6},{6,7},{7,8},{8,9},{9,10},{10,1... | collective-permute-start | bytes 1572872 | tf_op jit(solution)/shard_map/ppermute | solution.py:157
  149.7 0.8 copy-start.9
  153.0 0.8 copy-start.11
  153.8 1.0 copy-start.10
  154.9 1.0 copy-start.12

commit v6 on v5

--- a/solution.py
+++ b/solution.py
@@ -181,14 +181,11 @@
     )(x, *after)
 
 
-def gather_far(mine):
-    own = lax.all_to_all(jnp.broadcast_to(mine, (8,) + mine.shape), FAR, 0, 0)
-    return own.reshape((16,) + mine.shape[1:])
-
-
-def gather_near(own):
+def gather_tokens(pair):
+    left, right = shift(pair, 4), shift(pair, -4)
+    own = jnp.concatenate([pair, left, shift(left[:2], 4), shift(right[2:], -4), right])
     left, right = shift(own, 1), shift(own, -1)
-    return own, left, right, shift(left[:8], 1), shift(right[8:], -1)
+    return own, left, right, shift(left[4:12], 1), shift(right[:8], -1)
 
 
 def near_kernel(left_ref, right_ref, from_right, from_left, left_out, right_out):
@@ -224,8 +221,7 @@
     out_ref[...] = jnp.concatenate([summed[0], summed[1]], axis=1)
 
 
-def reduce_all(keep, give, own, left, right, far_left, far_right):
-    both = add_after(keep, swap(give, "core"), own)
+def reduce_all(both, own, left, right, far_left, far_right):
     grads = lax.all_to_all(both, ("x", "yl"), 0, 0)
     left, right = add_near(left, right, shift(far_left, -1), shift(far_right, 1))
     own, grads = pl.pallas_call(
@@ -263,47 +259,62 @@
     )(x, *after)
 
 
-def add_kernel(keep_ref, got_ref, after_ref, both_ref):
+def add_kernel(keep_ref, got_ref, both_ref, mark_ref):
     both_ref[...] = total(keep_ref[...], got_ref[...]).astype(BF16)
-
-
-def add_after(keep, got, after):
+    mark_ref[...] = jnp.zeros_like(mark_ref)
+
+
+def add_halves(keep, got):
     block = pl.BlockSpec((2,) + keep.shape[1:], lambda i: (i, 0, 0, 0))
     return pl.pallas_call(
         add_kernel,
         grid=(keep.shape[0] // 2,),
-        in_specs=[block, block, pl.BlockSpec(memory_space=pl.ANY)],
-        out_specs=block,
-        out_shape=jax.ShapeDtypeStruct(keep.shape, BF16),
+        in_specs=[block, block],
+        out_specs=[block, pl.BlockSpec((8, 128), lambda i: (0, 0))],
+        out_shape=[
+            jax.ShapeDtypeStruct(keep.shape, BF16),
+            jax.ShapeDtypeStruct((8, 128), F32),
+        ],
         compiler_params=pltpu.CompilerParams(vmem_limit_bytes=8 * 2**20),
         cost_estimate=pl.CostEstimate(flops=1_000_000, bytes_accessed=6_300_000, transcendentals=0),
-    )(keep, got, after)
+    )(keep, got)
 
 
 def gather_weights(block_values, block_rows, after, later):
     cols = block_values.shape[0]
     row_tile = jnp.zeros((16, 128), BF16).at[0, :cols].set(block_rows[:, 0].astype(BF16))
-    sent = jnp.concatenate([block_values.reshape(cols * 128, 128), row_tile])
-    sent = held_until(jnp.broadcast_to(sent, (8,) + sent.shape), after)
-    mine = held_until(lax.all_to_all(sent, ("x", "yl"), 0, 0), *later)
+    sent = held_until(jnp.concatenate([block_values.reshape(cols * 128, 128), row_tile]), after)
+    mine = lax.all_to_all(jnp.broadcast_to(sent, (8,) + sent.shape), ("x", "yl"), 0, 0)
+    mine = held_until(mine, later)
     other = swap(mine, "core")
     rows = jnp.concatenate([mine[:, cols * 128, :cols], other[:, cols * 128, :cols]])
     return mine, other, rows.astype(jnp.int32)
 
 
-def place_of(rows):
+def token_places(rows):
+    z = lax.axis_index("zh") * 4 + lax.axis_index("zl")
+    away = (z - rows % 32 // 2) % 16
+    kind = away % 4
+    group = jnp.where(kind == 0, 0, jnp.where(kind == 1, 48, jnp.where(kind == 2, 32, 16)))
+    ahead = jnp.where(kind == 2, 10, jnp.where(kind == 3, 1, 0))
+    other_yh = (rows // 32 + lax.axis_index("yh")) % 2
+    return group + (away + ahead) // 4 % 4 * 4 + other_yh * 2 + rows % 2
+
+
+def term_places(rows):
     return (rows // 2 - lax.axis_index("zl")) % 4 * 16 + rows // 32 * 8 + rows % 32 // 8 * 2 + rows % 2
 
 
 def shards(tokens, block_values, block_rows, grad_act):
     n_tok = tokens.shape[0]
-    own = gather_far(tokens.reshape(n_tok, 2, 128).transpose(1, 0, 2))
-    parts = gather_near(own)
-    mine, other, rows = gather_weights(block_values, block_rows, own, parts[3:])
-    rows = place_of(rows)
-    activated, grad_hidden, keep, give = hidden_call(rows, parts, mine, other, grad_act)
-    terms = term_call(rows, grad_hidden, mine, other)
-    summed, grads = reduce_all(keep, give, *terms)
+    mine = tokens.reshape(n_tok, 2, 128).transpose(1, 0, 2)
+    pair = jnp.concatenate([mine, swap(mine, "yh")])
+    parts = gather_tokens(pair)
+    mine, other, rows = gather_weights(block_values, block_rows, pair, parts[0])
+    activated, grad_hidden, keep, give = hidden_call(token_places(rows), parts, mine, other, grad_act)
+    both, mark = add_halves(keep, swap(give, "core"))
+    terms = term_call(term_places(rows), held_until(grad_hidden, mark), mine, other)
+    summed, grads = reduce_all(both, *terms)
     return activated, summed, grads
 
 

time: 200 us -> 200 us (level)
  the two profiles are of different devices: /device:TPU:1 before, /device:TPU:24 now
where the time goes in v6:
time: 200 us; the launch traced here: 196 us
  starting transfers between devices  66.6 us (33%)
  waiting for transfers between devices  59.8 us (30%)
  blocking collectives  35.4 us (18%)
  Pallas kernels  17.4 us (9%)
  local copies, waits for them, and re-layouts  14.5 us (7%)
    ppermute x12, waiting for transfers between devices, shift(): return lax.ppermute(a, Z, [(i, (i + by) % 16) for i in range(16)])  52.8 us
    ppermute x12, starting transfers between devices, shift(): return lax.ppermute(a, Z, [(i, (i + by) % 16) for i in range(16)])  47.5 us
    all_to_all x1, blocking collectives, reduce_all(): far = lax.all_to_all(own.reshape((8, 2) + own.shape[1:]), FAR, 0, 0)  35.4 us
    unnamed x28, local copies, waits for them, and re-layouts  10.5 us
    pallas_call x1, Pallas kernels, hidden_call(): pl.pallas_call(hidden_kernel, grid_spec=pltpu.PrefetchScalarGridSpec(num_...  7.97 us
    ppermute x3, waiting for transfers between devices, swap(): return lax.ppermute(a, axis, [(0, 1), (1, 0)])  7.01 us
    ppermute x3, starting transfers between devices, swap(): return lax.ppermute(a, axis, [(0, 1), (1, 0)])  6.99 us
    all_to_all x1, starting transfers between devices, gather_weights(): lax.all_to_all(jnp.broadcast_to(sent, (8,) + sent.shape), ('x', 'yl'), 0, 0)  6.44 us
  transfers between devices with their start and end apart: 17, of which 11 were waited for; matrix products, arithmetic and copies ran while one was open for 2% of the time, Pallas kernels for 3%

profile of v6, /device:TPU:24, one launch (start us, length us, event | category | flops | bytes accessed | tf_op | source)
XLA Modules:
  0.0 196.3 jit_solution(14331455367160720769)
XLA Ops:
  0.6 0.9 copy.13
  1.7 3.1 %collective-permute-start = (bf16[2,128,128]{2,1,0:T(8,128)(2,1)S(1)}, bf16[2,128,128]{2,1,0:T(8,128)(2,1)S(1)}, u32[]{:S(2)}, u32[]{:S(2)}) collective-permute-start(bf16[2,128,128]{2,1,0:T(8,128)(2,1)S(1)} %bitcast.17), channel_id=1, source_target_pairs={{0,16},{16,0},{1,17},{17,1},{2,18},{18,2},{3,19},{19,3},{4,20},{20... | collective-permute-start | bytes 196616 | tf_op jit(solution)/shard_map/ppermute | solution.py:161
  5.5 1.0 fusion.1.refs_0_
  6.5 2.9 %collective-permute-done = bf16[2,128,128]{2,1,0:T(8,128)(2,1)S(1)} collective-permute-done((bf16[2,128,128]{2,1,0:T(8,128)(2,1)S(1)}, bf16[2,128,128]{2,1,0:T(8,128)(2,1)S(1)}, u32[]{:S(2)}, u32[]{:S(2)}) %collective-permute-start) | collective-permute-done | bytes 65568 | tf_op jit(solution)/shard_map/ppermute | solution.py:161
  9.4 1.6 broadcast_in_dim.21
  11.0 6.4 %all-to-all-start = ((bf16[8,1040,128]{2,1,0:T(8,128)(2,1)}), bf16[8,1040,128]{2,1,0:T(8,128)(2,1)S(1)}, u32[]{:S(2)}, u32[]{:S(2)}) async-start(bf16[8,1040,128]{2,1,0:T(8,128)(2,1)} %broadcast_in_dim.21), calls=%async_computation | async-start | bytes 4259840 | tf_op jit(solution)/shard_map/all_to_all | solution.py:287
  17.5 12.0 %collective-permute-start.3 = (bf16[4,128,128]{2,1,0:T(8,128)(2,1)S(1)}, bf16[4,128,128]{2,1,0:T(8,128)(2,1)S(1)}, u32[]{:S(2)}, u32[]{:S(2)}) collective-permute-start(bf16[4,128,128]{2,1,0:T(8,128)(2,1)S(1)} %pad_maximum_fusion.refs_1_), channel_id=1, source_target_pairs={{0,12},{1,13},{2,14},{3,15},{4,0},{5,1},{6,2},{7,3},{8,4},{9,5},{1... | collective-permute-start | bytes 393224 | tf_op jit(solution)/shard_map/ppermute | solution.py:157
  29.5 1.9 collective-permute-start.1
  31.5 7.5 %collective-permute-done.3 = bf16[4,128,128]{2,1,0:T(8,128)(2,1)S(1)} collective-permute-done((bf16[4,128,128]{2,1,0:T(8,128)(2,1)S(1)}, bf16[4,128,128]{2,1,0:T(8,128)(2,1)S(1)}, u32[]{:S(2)}, u32[]{:S(2)}) %collective-permute-start.3) | collective-permute-done | bytes 131104 | tf_op jit(solution)/shard_map/ppermute | solution.py:157
  39.0 8.3 %collective-permute-start.4 = (bf16[2,128,128]{2,1,0:T(8,128)(2,1)S(1)}, bf16[2,128,128]{2,1,0:T(8,128)(2,1)S(1)}, u32[]{:S(2)}, u32[]{:S(2)}) collective-permute-start(bf16[2,128,128]{2,1,0:T(8,128)(2,1)S(1)} %slice.41), channel_id=1, source_target_pairs={{0,12},{1,13},{2,14},{3,15},{4,0},{5,1},{6,2},{7,3},{8,4},{9,5},{1... | collective-permute-start | bytes 196616 | tf_op jit(solution)/shard_map/ppermute | solution.py:157
  47.3 1.9 collective-permute-start.2
  49.3 9.9 %collective-permute-done.2 = bf16[2,128,128]{2,1,0:T(8,128)(2,1)S(1)} collective-permute-done((bf16[2,128,128]{2,1,0:T(8,128)(2,1)S(1)}, bf16[2,128,128]{2,1,0:T(8,128)(2,1)S(1)}, u32[]{:S(2)}, u32[]{:S(2)}) %collective-permute-start.2) | collective-permute-done | bytes 65568 | tf_op jit(solution)/shard_map/ppermute | solution.py:157
  59.3 1.9 collective-permute-start.5
  61.2 2.1 %collective-permute-start.7 = (bf16[16,128,128]{2,1,0:T(8,128)(2,1)S(1)}, bf16[16,128,128]{2,1,0:T(8,128)(2,1)S(1)}, u32[]{:S(2)}, u32[]{:S(2)}) collective-permute-start(bf16[16,128,128]{2,1,0:T(8,128)(2,1)S(1)} %constant_dynamic-update-slice_fusion.refs_1_.own), channel_id=1, source_target_pairs={{0,15},{1,0},{2,1},{3,2},{4,3},{5,4},{6,5},{7,6},{8,7},{9,8},{10,9... | collective-permute-start | bytes 1572872 | tf_op jit(solution)/shard_map/ppermute | solution.py:157
  63.3 3.8 %collective-permute-start.6 = (bf16[16,128,128]{2,1,0:T(8,128)(2,1)S(1)}, bf16[16,128,128]{2,1,0:T(8,128)(2,1)S(1)}, u32[]{:S(2)}, u32[]{:S(2)}) collective-permute-start(bf16[16,128,128]{2,1,0:T(8,128)(2,1)S(1)} %constant_dynamic-update-slice_fusion.refs_1_.own), channel_id=1, source_target_pairs={{0,1},{1,2},{2,3},{3,4},{4,5},{5,6},{6,7},{7,8},{8,9},{9,10},{10,1... | collective-permute-start | bytes 1572872 | tf_op jit(solution)/shard_map/ppermute | solution.py:157
  67.0 10.4 %collective-permute-done.7.right = bf16[16,128,128]{2,1,0:T(8,128)(2,1)S(1)} collective-permute-done((bf16[16,128,128]{2,1,0:T(8,128)(2,1)S(1)}, bf16[16,128,128]{2,1,0:T(8,128)(2,1)S(1)}, u32[]{:S(2)}, u32[]{:S(2)}) %collective-permute-start.7) | collective-permute-done | bytes 524320 | tf_op jit(solution)/shard_map/ppermute | solution.py:157
  77.4 0.7 slice.45
  78.1 3.4 %collective-permute-start.9 = (bf16[8,128,128]{2,1,0:T(8,128)(2,1)}, bf16[8,128,128]{2,1,0:T(8,128)(2,1)S(1)}, u32[]{:S(2)}, u32[]{:S(2)}) collective-permute-start(bf16[8,128,128]{2,1,0:T(8,128)(2,1)} %slice.45), channel_id=1, source_target_pairs={{0,15},{1,0},{2,1},{3,2},{4,3},{5,4},{6,5},{7,6},{8,7},{9,8},{10,9... | collective-permute-start | bytes 786440 | tf_op jit(solution)/shard_map/ppermute | solution.py:157
  81.6 0.7 slice.44
  82.3 0.8 copy-done.1
  83.1 2.4 %collective-permute-start.8 = (bf16[8,128,128]{2,1,0:T(8,128)(2,1)}, bf16[8,128,128]{2,1,0:T(8,128)(2,1)}, u32[]{:S(2)}, u32[]{:S(2)}) collective-permute-start(bf16[8,128,128]{2,1,0:T(8,128)(2,1)} %slice.44), channel_id=1, source_target_pairs={{0,1},{1,2},{2,3},{3,4},{4,5},{5,6},{6,7},{7,8},{8,9},{9,10},{10,1... | collective-permute-start | bytes 786440 | tf_op jit(solution)/shard_map/ppermute | solution.py:157
  85.5 0.7 slice.43
  86.4 1.8 collective-permute-done.9.far_right
  88.2 0.7 copy-done.8
  88.9 5.3 %collective-permute-done.8.far_left = bf16[8,128,128]{2,1,0:T(8,128)(2,1)} collective-permute-done((bf16[8,128,128]{2,1,0:T(8,128)(2,1)}, bf16[8,128,128]{2,1,0:T(8,128)(2,1)}, u32[]{:S(2)}, u32[]{:S(2)}) %collective-permute-start.8) | collective-permute-done | bytes 262176 | tf_op jit(solution)/shard_map/ppermute | solution.py:157
  94.2 1.0 copy-done.2
  95.2 0.9 copy-done.7
  96.2 0.9 copy-done.9
  97.1 8.0 %shard_map.69 = (bf16[128,1024]{1,0:T(8,128)(2,1)}, bf16[128,1024]{1,0:T(8,128)(2,1)S(1)}, bf16[8,8,128,128]{3,2,1,0:T(8,128)(2,1)S(1)}, bf16[8,8,128,128]{3,2,1,0:T(8,128)(2,1)S(1)}) custom-call(s32[16,8]{1,0:T(8,128)S(1)} %get-tuple-element.52.rows_ref, bf16[16,128,128]{2,1,0:T(8,128)(2,1)S(1)} %constant_dynamic-update-slice_fusion.refs_1_.own, ...), custom_call_target="tpu_custom_call" | custom-call | flops 1073741824 | bytes 11000000 | tf_op jit(solution)/shard_map/pallas_call | solution.py:113
  105.1 1.9 collective-permute-start.10
  107.0 4.1 %collective-permute-done.10.got_ref = bf16[8,8,128,128]{3,2,1,0:T(8,128)(2,1)S(1)} collective-permute-done((bf16[8,8,128,128]{3,2,1,0:T(8,128)(2,1)S(1)}, bf16[8,8,128,128]{3,2,1,0:T(8,128)(2,1)S(1)}, u32[]{:S(2)}, u32[]{:S(2)}) %collective-permute-start.10) | collective-permute-done | bytes 2097184 | tf_op jit(solution)/shard_map/ppermute | solution.py:161
  111.7 1.4 copy-done
  113.1 5.7 %all-to-all-start.1 = ((bf16[8,8,128,128]{3,2,1,0:T(8,128)(2,1)}), bf16[8,8,128,128]{3,2,1,0:T(8,128)(2,1)}, u32[]{:S(2)}, u32[]{:S(2)}) async-start(bf16[8,8,128,128]{3,2,1,0:T(8,128)(2,1)} %copy-done), calls=%async_computation.1 | async-start | bytes 4194304 | tf_op jit(solution)/shard_map/all_to_all | solution.py:225
  118.8 4.8 %shard_map.72 = (bf16[16,128,128]{2,1,0:T(8,128)(2,1)S(1)}, bf16[16,128,128]{2,1,0:T(8,128)(2,1)S(1)}, bf16[16,128,128]{2,1,0:T(8,128)(2,1)S(1)}, bf16[8,128,128...) custom-call(s32[16,8]{1,0:T(8,128)S(1)} %get-tuple-element.51.rows_ref, bf16[128,1024]{1,0:T(8,128)(2,1)S(1)} %shard_map.71.gh_ref, ...), custom_call_target="tpu_custom_call" | custom-call | flops 536870912 | bytes 7000000 | tf_op jit(solution)/shard_map/pallas_call | solution.py:136
  123.6 1.9 collective-permute-start.11
  125.5 3.9 %collective-permute-start.12 = (bf16[8,128,128]{2,1,0:T(8,128)(2,1)S(1)}, bf16[8,128,128]{2,1,0:T(8,128)(2,1)S(1)}, u32[]{:S(2)}, u32[]{:S(2)}) collective-permute-start(bf16[8,128,128]{2,1,0:T(8,128)(2,1)S(1)} %get-tuple-element.39), channel_id=1, source_target_pairs={{0,1},{1,2},{2,3},{3,4},{4,5},{5,6},{6,7},{7,8},{8,9},{9,10},{10,1... | collective-permute-start | bytes 786440 | tf_op jit(solution)/shard_map/ppermute | solution.py:157
  129.4 3.8 %collective-permute-done.11.from_right = bf16[8,128,128]{2,1,0:T(8,128)(2,1)S(1)} collective-permute-done((bf16[8,128,128]{2,1,0:T(8,128)(2,1)S(1)}, bf16[8,128,128]{2,1,0:T(8,128)(2,1)S(1)}, u32[]{:S(2)}, u32[]{:S(2)}) %collective-permute-start.11) | collective-permute-done | bytes 262176 | tf_op jit(solution)/shard_map/ppermute | solution.py:157
  133.3 3.1 %collective-permute-done.12.from_left = bf16[8,128,128]{2,1,0:T(8,128)(2,1)S(1)} collective-permute-done((bf16[8,128,128]{2,1,0:T(8,128)(2,1)S(1)}, bf16[8,128,128]{2,1,0:T(8,128)(2,1)S(1)}, u32[]{:S(2)}, u32[]{:S(2)}) %collective-permute-start.12) | collective-permute-done | bytes 262176 | tf_op jit(solution)/shard_map/ppermute | solution.py:157
  136.8 1.9 collective-permute-start.13
  138.7 3.9 %collective-permute-start.14 = (bf16[16,128,128]{2,1,0:T(8,128)(2,1)S(1)}, bf16[16,128,128]{2,1,0:T(8,128)(2,1)S(1)}, u32[]{:S(2)}, u32[]{:S(2)}) collective-permute-start(bf16[16,128,128]{2,1,0:T(8,128)(2,1)S(1)} %get-tuple-element.41), channel_id=1, source_target_pairs={{0,1},{1,2},{2,3},{3,4},{4,5},{5,6},{6,7},{7,8},{8,9},{9,10},{10,1... | collective-permute-start | bytes 1572872 | tf_op jit(solution)/shard_map/ppermute | solution.py:157
  142.6 8.5 %collective-permute-done.13.left_ref = bf16[16,128,128]{2,1,0:T(8,128)(2,1)S(1)} collective-permute-done((bf16[16,128,128]{2,1,0:T(8,128)(2,1)S(1)}, bf16[16,128,128]{2,1,0:T(8,128)(2,1)S(1)}, u32[]{:S(2)}, u32[]{:S(2)}) %collective-permute-start.13) | collective-permute-done | bytes 524320 | tf_op jit(solution)/shard_map/ppermute | solution.py:157
  151.2 0.8 copy-done.3
  152.0 2.3 %collective-permute-done.14.right_ref = bf16[16,128,128]{2,1,0:T(8,128)(2,1)S(1)} collective-permute-done((bf16[16,128,128]{2,1,0:T(8,128)(2,1)S(1)}, bf16[16,128,128]{2,1,0:T(8,128)(2,1)S(1)}, u32[]{:S(2)}, u32[]{:S(2)}) %collective-permute-start.14) | collective-permute-done | bytes 524320 | tf_op jit(solution)/shard_map/ppermute | solution.py:157
  154.3 0.8 copy-done.5
  155.1 1.0 copy-done.4
  156.2 1.0 copy-done.6
  157.2 3.0 %shard_map.74 = (bf16[16,128,128]{2,1,0:T(8,128)(2,1)S(1)}, bf16[8,128,128]{2,1,0:T(8,128)(2,1)}) custom-call(bf16[16,128,128]{2,1,0:T(8,128)(2,1)S(1)} %get-tuple-element.35.own_ref, bf16[16,128,128]{2,1,0:T(8,128)(2,1)S(1)} %copy-done.4, bf16[16,128,128]{2,1,0:T(8,128)(2,1)S(1)} %copy-done.6, bf16[8,8,128,128]{3,2,1,0:T(8,128)(2,1)} %all-to-all-done.1.grads_ref), custom_call_target="tpu_custom_call" | custom-call | flops 2000000 | bytes 4500000 | tf_op jit(solution)/shard_map/pallas_call | solution.py:227
  160.2 35.4 %all_to_all.15.far_ref = bf16[8,2,128,128]{3,2,1,0:T(8,128)(2,1)S(1)} all-to-all(bf16[8,2,128,128]{3,2,1,0:T(8,128)(2,1)S(1)} %bitcast.16), channel_id=1, replica_groups=mesh['x'=4,'yl'=2,'core'=2,'yh'=2,'zh'=4,'zl'=4] {'yh','zh'}, dimensions={0} | all-to-all | bytes 1048576 | tf_op jit(solution)/shard_map/all_to_all | solution.py:236
  (37 shorter events, 2.6 us)
Async XLA Ops:
  1.7 7.7 %collective-permute-start = (bf16[2,128,128]{2,1,0:T(8,128)(2,1)S(1)}, bf16[2,128,128]{2,1,0:T(8,128)(2,1)S(1)}, u32[]{:S(2)}, u32[]{:S(2)}) collective-permute-start(bf16[2,128,128]{2,1,0:T(8,128)(2,1)S(1)} %bitcast.17), channel_id=1, source_target_pairs={{0,16},{16,0},{1,17},{17,1},{2,18},{18,2},{3,19},{19,3},{4,20},{20... | collective-permute-start | bytes 196616 | tf_op jit(solution)/shard_map/ppermute | solution.py:161
  11.0 48.2 %all-to-all-start = ((bf16[8,1040,128]{2,1,0:T(8,128)(2,1)}), bf16[8,1040,128]{2,1,0:T(8,128)(2,1)S(1)}, u32[]{:S(2)}, u32[]{:S(2)}) async-start(bf16[8,1040,128]{2,1,0:T(8,128)(2,1)} %broadcast_in_dim.21), calls=%async_computation | async-start | bytes 4259840 | tf_op jit(solution)/shard_map/all_to_all | solution.py:287
  17.5 21.5 %collective-permute-start.3 = (bf16[4,128,128]{2,1,0:T(8,128)(2,1)S(1)}, bf16[4,128,128]{2,1,0:T(8,128)(2,1)S(1)}, u32[]{:S(2)}, u32[]{:S(2)}) collective-permute-start(bf16[4,128,128]{2,1,0:T(8,128)(2,1)S(1)} %pad_maximum_fusion.refs_1_), channel_id=1, source_target_pairs={{0,12},{1,13},{2,14},{3,15},{4,0},{5,1},{6,2},{7,3},{8,4},{9,5},{1... | collective-permute-start | bytes 393224 | tf_op jit(solution)/shard_map/ppermute | solution.py:157
  29.5 17.8 %collective-permute-start.1 = (bf16[4,128,128]{2,1,0:T(8,128)(2,1)S(1)}, bf16[4,128,128]{2,1,0:T(8,128)(2,1)S(1)}, u32[]{:S(2)}, u32[]{:S(2)}) collective-permute-start(bf16[4,128,128]{2,1,0:T(8,128)(2,1)S(1)} %pad_maximum_fusion.refs_1_), channel_id=1, source_target_pairs={{0,4},{1,5},{2,6},{3,7},{4,8},{5,9},{6,10},{7,11},{8,12},{9,13},{1... | collective-permute-start | bytes 393224 | tf_op jit(solution)/shard_map/ppermute | solution.py:157
  39.0 20.2 %collective-permute-start.4 = (bf16[2,128,128]{2,1,0:T(8,128)(2,1)S(1)}, bf16[2,128,128]{2,1,0:T(8,128)(2,1)S(1)}, u32[]{:S(2)}, u32[]{:S(2)}) collective-permute-start(bf16[2,128,128]{2,1,0:T(8,128)(2,1)S(1)} %slice.41), channel_id=1, source_target_pairs={{0,12},{1,13},{2,14},{3,15},{4,0},{5,1},{6,2},{7,3},{8,4},{9,5},{1... | collective-permute-start | bytes 196616 | tf_op jit(solution)/shard_map/ppermute | solution.py:157
  47.3 11.9 %collective-permute-start.2 = (bf16[2,128,128]{2,1,0:T(8,128)(2,1)S(1)}, bf16[2,128,128]{2,1,0:T(8,128)(2,1)S(1)}, u32[]{:S(2)}, u32[]{:S(2)}) collective-permute-start(bf16[2,128,128]{2,1,0:T(8,128)(2,1)S(1)} %slice.40), channel_id=1, source_target_pairs={{0,4},{1,5},{2,6},{3,7},{4,8},{5,9},{6,10},{7,11},{8,12},{9,13},{1... | collective-permute-start | bytes 196616 | tf_op jit(solution)/shard_map/ppermute | solution.py:157
  59.3 26.3 %collective-permute-start.5 = (bf16[8,1040,128]{2,1,0:T(8,128)(2,1)S(1)}, bf16[8,1040,128]{2,1,0:T(8,128)(2,1)}, u32[]{:S(2)}, u32[]{:S(2)}) collective-permute-start(bf16[8,1040,128]{2,1,0:T(8,128)(2,1)S(1)} %shard_map.68.mine), channel_id=1, source_target_pairs={{0,32},{32,0},{1,33},{33,1},{2,34},{34,2},{3,35},{35,3},{4,36},{36... | collective-permute-start | bytes 6389768 | tf_op jit(solution)/shard_map/ppermute | solution.py:161
  61.2 16.2 %collective-permute-start.7 = (bf16[16,128,128]{2,1,0:T(8,128)(2,1)S(1)}, bf16[16,128,128]{2,1,0:T(8,128)(2,1)S(1)}, u32[]{:S(2)}, u32[]{:S(2)}) collective-permute-start(bf16[16,128,128]{2,1,0:T(8,128)(2,1)S(1)} %constant_dynamic-update-slice_fusion.refs_1_.own), channel_id=1, source_target_pairs={{0,15},{1,0},{2,1},{3,2},{4,3},{5,4},{6,5},{7,6},{8,7},{9,8},{10,9... | collective-permute-start | bytes 1572872 | tf_op jit(solution)/shard_map/ppermute | solution.py:157
  63.3 18.3 %collective-permute-start.6 = (bf16[16,128,128]{2,1,0:T(8,128)(2,1)S(1)}, bf16[16,128,128]{2,1,0:T(8,128)(2,1)S(1)}, u32[]{:S(2)}, u32[]{:S(2)}) collective-permute-start(bf16[16,128,128]{2,1,0:T(8,128)(2,1)S(1)} %constant_dynamic-update-slice_fusion.refs_1_.own), channel_id=1, source_target_pairs={{0,1},{1,2},{2,3},{3,4},{4,5},{5,6},{6,7},{7,8},{8,9},{9,10},{10,1... | collective-permute-start | bytes 1572872 | tf_op jit(solution)/shard_map/ppermute | solution.py:157
  78.1 10.0 %collective-permute-start.9 = (bf16[8,128,128]{2,1,0:T(8,128)(2,1)}, bf16[8,128,128]{2,1,0:T(8,128)(2,1)S(1)}, u32[]{:S(2)}, u32[]{:S(2)}) collective-permute-start(bf16[8,128,128]{2,1,0:T(8,128)(2,1)} %slice.45), channel_id=1, source_target_pairs={{0,15},{1,0},{2,1},{3,2},{4,3},{5,4},{6,5},{7,6},{8,7},{9,8},{10,9... | collective-permute-start | bytes 786440 | tf_op jit(solution)/shard_map/ppermute | solution.py:157
  82.3 0.8 copy-start.1
  83.1 11.1 %collective-permute-start.8 = (bf16[8,128,128]{2,1,0:T(8,128)(2,1)}, bf16[8,128,128]{2,1,0:T(8,128)(2,1)}, u32[]{:S(2)}, u32[]{:S(2)}) collective-permute-start(bf16[8,128,128]{2,1,0:T(8,128)(2,1)} %slice.44), channel_id=1, source_target_pairs={{0,1},{1,2},{2,3},{3,4},{4,5},{5,6},{6,7},{7,8},{8,9},{9,10},{10,1... | collective-permute-start | bytes 786440 | tf_op jit(solution)/shard_map/ppermute | solution.py:157
  88.2 0.7 copy-start.8
  94.2 1.0 copy-start.2
  95.2 0.9 copy-start.7
  96.2 0.9 copy-start.9
  105.1 6.1 %collective-permute-start.10 = (bf16[8,8,128,128]{3,2,1,0:T(8,128)(2,1)S(1)}, bf16[8,8,128,128]{3,2,1,0:T(8,128)(2,1)S(1)}, u32[]{:S(2)}, u32[]{:S(2)}) collective-permute-start(bf16[8,8,128,128]{3,2,1,0:T(8,128)(2,1)S(1)} %get-tuple-element.33), channel_id=1, source_target_pairs={{0,32},{32,0},{1,33},{33,1},{2,34},{34,2},{3,35},{35,3},{4,36},{36... | collective-permute-start | bytes 6291464 | tf_op jit(solution)/shard_map/ppermute | solution.py:161
  111.7 1.4 copy-start
  113.1 42.0 %all-to-all-start.1 = ((bf16[8,8,128,128]{3,2,1,0:T(8,128)(2,1)}), bf16[8,8,128,128]{3,2,1,0:T(8,128)(2,1)}, u32[]{:S(2)}, u32[]{:S(2)}) async-start(bf16[8,8,128,128]{3,2,1,0:T(8,128)(2,1)} %copy-done), calls=%async_computation.1 | async-start | bytes 4194304 | tf_op jit(solution)/shard_map/all_to_all | solution.py:225
  123.6 9.7 %collective-permute-start.11 = (bf16[8,128,128]{2,1,0:T(8,128)(2,1)S(1)}, bf16[8,128,128]{2,1,0:T(8,128)(2,1)S(1)}, u32[]{:S(2)}, u32[]{:S(2)}) collective-permute-start(bf16[8,128,128]{2,1,0:T(8,128)(2,1)S(1)} %get-tuple-element.38), channel_id=1, source_target_pairs={{0,15},{1,0},{2,1},{3,2},{4,3},{5,4},{6,5},{7,6},{8,7},{9,8},{10,9... | collective-permute-start | bytes 786440 | tf_op jit(solution)/shard_map/ppermute | solution.py:157
  125.5 10.9 %collective-permute-start.12 = (bf16[8,128,128]{2,1,0:T(8,128)(2,1)S(1)}, bf16[8,128,128]{2,1,0:T(8,128)(2,1)S(1)}, u32[]{:S(2)}, u32[]{:S(2)}) collective-permute-start(bf16[8,128,128]{2,1,0:T(8,128)(2,1)S(1)} %get-tuple-element.39), channel_id=1, source_target_pairs={{0,1},{1,2},{2,3},{3,4},{4,5},{5,6},{6,7},{7,8},{8,9},{9,10},{10,1... | collective-permute-start | bytes 786440 | tf_op jit(solution)/shard_map/ppermute | solution.py:157
  136.8 14.4 %collective-permute-start.13 = (bf16[16,128,128]{2,1,0:T(8,128)(2,1)S(1)}, bf16[16,128,128]{2,1,0:T(8,128)(2,1)S(1)}, u32[]{:S(2)}, u32[]{:S(2)}) collective-permute-start(bf16[16,128,128]{2,1,0:T(8,128)(2,1)S(1)} %get-tuple-element.40), channel_id=1, source_target_pairs={{0,15},{1,0},{2,1},{3,2},{4,3},{5,4},{6,5},{7,6},{8,7},{9,8},{10,9... | collective-permute-start | bytes 1572872 | tf_op jit(solution)/shard_map/ppermute | solution.py:157
  138.7 15.6 %collective-permute-start.14 = (bf16[16,128,128]{2,1,0:T(8,128)(2,1)S(1)}, bf16[16,128,128]{2,1,0:T(8,128)(2,1)S(1)}, u32[]{:S(2)}, u32[]{:S(2)}) collective-permute-start(bf16[16,128,128]{2,1,0:T(8,128)(2,1)S(1)} %get-tuple-element.41), channel_id=1, source_target_pairs={{0,1},{1,2},{2,3},{3,4},{4,5},{5,6},{6,7},{7,8},{8,9},{9,10},{10,1... | collective-permute-start | bytes 1572872 | tf_op jit(solution)/shard_map/ppermute | solution.py:157
  151.2 0.8 copy-start.3
  154.3 0.8 copy-start.5
  155.1 1.0 copy-start.4
  156.1 1.0 copy-start.6

commit v7 on v6

v7 whole, which is shorter than its diff:
```python
import jax
import jax.numpy as jnp
from jax import lax
from jax.experimental import pallas as pl
from jax.experimental.pallas import tpu as pltpu
from jax.sharding import Mesh
from jax.sharding import PartitionSpec as P

SQRT_TWO_PI = 0.7978845608028654
CUBIC = 0.044715
AXES = ("x", "yl", "core", "yh", "z")
SIZES = (4, 2, 2, 2, 16)
SEQ = ("x", "yl", "core")
MP = ("yh", "z")
RING = 16
BF16, F32 = jnp.bfloat16, jnp.float32


def gelu_parts(hidden):
    inner_arg = SQRT_TWO_PI * (hidden + CUBIC * hidden * hidden * hidden)
    tanh_inner = jnp.tanh(inner_arg)
    gelu_value = 0.5 * hidden * (1.0 + tanh_inner)
    gelu_slope = 0.5 * (1.0 + tanh_inner) + 0.5 * hidden * (
        1.0 - tanh_inner * tanh_inner
    ) * SQRT_TWO_PI * (1.0 + 3.0 * CUBIC * hidden * hidden)
    return gelu_value, gelu_slope


def fetch_columns(halves, w_all, w_sem):
    kept = halves[0].shape[0]
    for c in range(w_all.shape[1]):
        for h, w_ref in enumerate(halves):
            pltpu.make_async_copy(
                w_ref.at[:, pl.ds(c * 128, 128)], w_all.at[pl.ds(h * kept, kept), c], w_sem.at[c, h]
            ).start()


def await_column(halves, w_all, w_sem, c):
    kept = halves[0].shape[0]
    for h, w_ref in enumerate(halves):
        pltpu.make_async_copy(
            w_ref.at[:, pl.ds(0, 128)], w_all.at[pl.ds(h * kept, kept), c], w_sem.at[c, h]
        ).wait()


def hidden_kernel(rows_ref, *refs):
    parts = refs[:RING]
    mine, other, gact_ref, act_ref, gh_ref, keep_ref, give_ref, tok, w_all, sem, w_sem = refs[RING:]
    c = pl.program_id(0)
    half = keep_ref.shape[0]

    @pl.when(c == 0)
    def _():
        copies = [
            pltpu.make_async_copy(ref, tok.at[pl.ds(4 * i, 4)], sem.at[i]) for i, ref in enumerate(parts)
        ]
        for copy in copies:
            copy.start()
        fetch_columns((mine, other), w_all, w_sem)
        for copy in copies:
            copy.wait()

    await_column((mine, other), w_all, w_sem, c)
    weights = jnp.concatenate([w_all[k, c] for k in range(2 * half)], axis=0)
    picked = jnp.concatenate([tok[rows_ref[k, c]] for k in range(2 * half)], axis=1)
    hidden = jnp.dot(picked, weights, preferred_element_type=F32)
    value, slope = gelu_parts(hidden)
    act_ref[...] = value.astype(BF16)
    grad_hidden = (gact_ref[...].astype(F32) * slope).astype(BF16)
    gh_ref[...] = grad_hidden
    grads = lax.dot_general(
        grad_hidden, picked, (((0,), (0,)), ((), ())), preferred_element_type=F32
    ).astype(BF16)
    for j in range(half):
        keep_ref[j, 0] = grads[:, j * 128 : (j + 1) * 128]
        give_ref[j, 0] = grads[:, (half + j) * 128 : (half + j + 1) * 128]


def term_kernel(rows_ref, gh_ref, mine, other, *refs):
    acc, w_all, w_sem = refs[RING:]
    c = pl.program_id(0)
    kept = w_all.shape[0]

    @pl.when(c == 0)
    def _():
        fetch_columns((mine, other), w_all, w_sem)
        acc[...] = jnp.zeros_like(acc)

    await_column((mine, other), w_all, w_sem, c)
    weights = jnp.concatenate([w_all[k, c] for k in range(kept)], axis=0)
    part = lax.dot_general(
        gh_ref[...], weights, (((1,), (1,)), ((), ())), preferred_element_type=F32
    )
    for k in range(kept):
        acc[rows_ref[k, c]] += part[:, k * 128 : (k + 1) * 128]

    @pl.when(c == pl.num_programs(0) - 1)
    def _():
        for i, ref in enumerate(refs[:RING]):
            ref[...] = acc[4 * i : 4 * i + 4].astype(BF16)


def hidden_call(rows, parts, mine, other, grad_act):
    kept, cols = rows.shape
    n_tok = grad_act.shape[0]
    column = pl.BlockSpec((n_tok, 128), lambda c, *_: (0, c))
    half = pl.BlockSpec((kept // 2, 1, 128, 128), lambda c, *_: (0, c, 0, 0))
    wide = jax.ShapeDtypeStruct((n_tok, cols * 128), BF16)
    grads = jax.ShapeDtypeStruct((kept // 2, cols, 128, 128), BF16)
    return pl.pallas_call(
        hidden_kernel,
        grid_spec=pltpu.PrefetchScalarGridSpec(
            num_scalar_prefetch=1,
            grid=(cols,),
            in_specs=[pl.BlockSpec(memory_space=pl.ANY)] * (RING + 2) + [column],
            out_specs=[column, column, half, half],
            scratch_shapes=[
                pltpu.VMEM((64, n_tok, 128), BF16),
                pltpu.VMEM((kept, cols, 128, 128), BF16),
                pltpu.SemaphoreType.DMA((RING,)),
                pltpu.SemaphoreType.DMA((cols, 2)),
            ],
        ),
        out_shape=[wide, wide, grads, grads],
        compiler_params=pltpu.CompilerParams(vmem_limit_bytes=18 * 2**20),
        cost_estimate=pl.CostEstimate(flops=1_073_741_824, bytes_accessed=11_000_000, transcendentals=131072),
    )(rows, *parts, mine, other, grad_act)


def term_call(rows, grad_hidden, mine, other):
    kept, cols = rows.shape
    n_tok = grad_hidden.shape[0]
    return pl.pallas_call(
        term_kernel,
        grid_spec=pltpu.PrefetchScalarGridSpec(
            num_scalar_prefetch=1,
            grid=(cols,),
            in_specs=[pl.BlockSpec((n_tok, 128), lambda c, rows: (0, c))]
            + [pl.BlockSpec(memory_space=pl.ANY)] * 2,
            out_specs=[pl.BlockSpec((4, n_tok, 128), lambda c, rows: (0, 0, 0))] * RING,
            scratch_shapes=[
                pltpu.VMEM((64, n_tok, 128), F32),
                pltpu.VMEM((kept, cols, 128, 128), BF16),
                pltpu.SemaphoreType.DMA((cols, 2)),
            ],
        ),
        out_shape=[jax.ShapeDtypeStruct((4, n_tok, 128), BF16)] * RING,
        compiler_params=pltpu.CompilerParams(vmem_limit_bytes=20 * 2**20),
        cost_estimate=pl.CostEstimate(flops=536_870_912, bytes_accessed=7_000_000, transcendentals=0),
    )(rows, grad_hidden, mine, other)


def shift(a, by):
    return lax.ppermute(a, "z", [(i, (i + by) % RING) for i in range(RING)])


def swap(a, axis):
    return lax.ppermute(a, axis, [(0, 1), (1, 0)])


def total(*arrays):
    return sum(a.astype(F32) for a in arrays)


def gather_tokens(pair):
    parts = [pair] * RING
    up, down = pair, pair
    for step in range(1, RING // 2 + 1):
        got_up = shift(up, 1)
        if step < RING // 2:
            got_down = shift(down, -1)
            up = held_until(got_up, down)
            down = held_until(got_down, up)
            parts[step] = down
        else:
            up = got_up
        parts[-step] = up
    return parts


def step_kernel(got_ref, own_ref, after_ref, out_ref):
    out_ref[...] = total(got_ref[...], own_ref[...]).astype(BF16)


def add_step(got, own, after):
    block = pl.BlockSpec(memory_space=pltpu.VMEM)
    return pl.pallas_call(
        step_kernel,
        in_specs=[block, block, pl.BlockSpec(memory_space=pl.ANY)],
        out_specs=block,
        out_shape=jax.ShapeDtypeStruct(own.shape, BF16),
        compiler_params=pltpu.CompilerParams(vmem_limit_bytes=2 * 2**20),
        cost_estimate=pl.CostEstimate(flops=100_000, bytes_accessed=400_000, transcendentals=0),
    )(got, own, after)


def last_kernel(up_ref, down_ref, own_ref, keep_ref, give_ref):
    summed = total(up_ref[...], down_ref[...], own_ref[...])
    keep_ref[...] = summed[:2]
    give_ref[...] = summed[2:].astype(BF16)


def finish_kernel(keep_ref, got_ref, out_ref):
    summed = (keep_ref[...] + got_ref[...].astype(F32)).astype(BF16)
    out_ref[...] = jnp.concatenate([summed[0], summed[1]], axis=1)


def reduce_terms(terms):
    n_tok = terms[0].shape[1]
    half = RING // 2
    up, down = terms[half], terms[half + 1]
    for step in range(half - 1):
        got_up, got_down = shift(up, 1), shift(down, -1)
        up = add_step(got_up, terms[half - 1 - step], down)
        down = add_step(got_down, terms[half + 2 + step], up) if step < half - 2 else got_down
    keep, give = pl.pallas_call(
        last_kernel,
        out_shape=[
            jax.ShapeDtypeStruct((2, n_tok, 128), F32),
            jax.ShapeDtypeStruct((2, n_tok, 128), BF16),
        ],
        compiler_params=pltpu.CompilerParams(vmem_limit_bytes=4 * 2**20),
        cost_estimate=pl.CostEstimate(flops=200_000, bytes_accessed=600_000, transcendentals=0),
    )(shift(up, 1), down, terms[0])
    return pl.pallas_call(
        finish_kernel,
        out_shape=jax.ShapeDtypeStruct((n_tok, 256), BF16),
        compiler_params=pltpu.CompilerParams(vmem_limit_bytes=4 * 2**20),
        cost_estimate=pl.CostEstimate(flops=100_000, bytes_accessed=300_000, transcendentals=0),
    )(keep, swap(give, "yh"))


def sum_kernel(grads_ref, out_ref):
    for c in range(grads_ref.shape[1]):
        summed = sum(grads_ref[i, c].astype(F32) for i in range(grads_ref.shape[0]))
        out_ref[c] = summed.T.astype(BF16)


def sum_grads(grads):
    return pl.pallas_call(
        sum_kernel,
        out_shape=jax.ShapeDtypeStruct(grads.shape[1:], BF16),
        compiler_params=pltpu.CompilerParams(vmem_limit_bytes=8 * 2**20),
        cost_estimate=pl.CostEstimate(flops=2_000_000, bytes_accessed=2_500_000, transcendentals=0),
    )(grads)[:, None]


def order_kernel(*refs):
    pass


def held_until(x, *after):
    anywhere = pl.BlockSpec(memory_space=pl.ANY)
    return pl.pallas_call(
        order_kernel,
        in_specs=[anywhere] * (1 + len(after)),
        out_specs=anywhere,
        out_shape=jax.ShapeDtypeStruct(x.shape, x.dtype),
        input_output_aliases={0: 0},
        compiler_params=pltpu.CompilerParams(vmem_limit_bytes=2**20),
    )(x, *after)


def add_kernel(keep_ref, got_ref, both_ref, mark_ref):
    both_ref[...] = total(keep_ref[...], got_ref[...]).astype(BF16)
    mark_ref[...] = jnp.zeros_like(mark_ref)


def add_halves(keep, got):
    block = pl.BlockSpec((2,) + keep.shape[1:], lambda i: (i, 0, 0, 0))
    return pl.pallas_call(
        add_kernel,
        grid=(keep.shape[0] // 2,),
        in_specs=[block, block],
        out_specs=[block, pl.BlockSpec((8, 128), lambda i: (0, 0))],
        out_shape=[
            jax.ShapeDtypeStruct(keep.shape, BF16),
            jax.ShapeDtypeStruct((8, 128), F32),
        ],
        compiler_params=pltpu.CompilerParams(vmem_limit_bytes=8 * 2**20),
        cost_estimate=pl.CostEstimate(flops=1_000_000, bytes_accessed=6_300_000, transcendentals=0),
    )(keep, got)


def gather_weights(block_values, block_rows, after, later):
    cols = block_values.shape[0]
    row_tile = jnp.zeros((16, 128), BF16).at[0, :cols].set(block_rows[:, 0].astype(BF16))
    sent = held_until(jnp.concatenate([block_values.reshape(cols * 128, 128), row_tile]), after)
    mine = lax.all_to_all(jnp.broadcast_to(sent, (8,) + sent.shape), ("x", "yl"), 0, 0)
    mine = held_until(mine, later)
    other = swap(mine, "core")
    rows = jnp.concatenate([mine[:, cols * 128, :cols], other[:, cols * 128, :cols]])
    return mine, other, rows.astype(jnp.int32)


def places(rows):
    ahead = (rows % 32 // 2 - lax.axis_index("z")) % RING
    return ahead * 4 + (rows // 32 + lax.axis_index("yh")) % 2 * 2 + rows % 2


def shards(tokens, block_values, block_rows, grad_act):
    n_tok = tokens.shape[0]
    mine = tokens.reshape(n_tok, 2, 128).transpose(1, 0, 2)
    pair = jnp.concatenate([mine, swap(mine, "yh")])
    parts = gather_tokens(pair)
    mine, other, rows = gather_weights(block_values, block_rows, pair, parts[5])
    rows = places(rows)
    activated, grad_hidden, keep, give = hidden_call(rows, parts, mine, other, grad_act)
    both, mark = add_halves(keep, swap(give, "core"))
    terms = term_call(rows, held_until(grad_hidden, mark), mine, other)
    grads = sum_grads(lax.all_to_all(both, ("x", "yl"), 0, 0))
    return activated, reduce_terms(terms), grads


def solution(mesh):
    fine = Mesh(mesh.devices.reshape(SIZES), AXES)
    in_specs = (P(SEQ, MP), P(MP, SEQ, None, None), P(MP, SEQ), P(SEQ, MP))
    out_specs = (P(SEQ, MP), P(SEQ, MP), P(MP, SEQ, None, None))
    return jax.shard_map(shards, mesh=fine, in_specs=in_specs, out_specs=out_specs, check_vma=False)
```

time: 200 us -> 204 us (1.020); the launches traced: 196 us -> 203 us
  starting transfers between devices: 66.6 us -> 131 us
  blocking collectives: 35.4 us -> 0 us
  waiting for transfers between devices: 59.8 us -> 41.3 us
  local copies, waits for them, and re-layouts: 14.5 us -> 8.22 us
  Pallas kernels: 17.4 us -> 19.5 us
    ppermute x12 -> x30, starting transfers between devices: 47.5 us -> 109 us  [shift(): return lax.ppermute(a, 'z', [(i, (i + by) % RING) for i in range(RING)])]
    all_to_all x1 -> x0, blocking collectives: 35.4 us -> none  [reduce_all(): far = lax.all_to_all(own.reshape((8, 2) + own.shape[1:]), FAR, 0, 0)]
    ppermute x12 -> x30, waiting for transfers between devices: 52.8 us -> 29.6 us  [shift(): return lax.ppermute(a, 'z', [(i, (i + by) % RING) for i in range(RING)])]
    unnamed x28 -> x19, local copies, waits for them, and re-layouts: 10.5 us -> 5.74 us
    ppermute x3 -> x4, waiting for transfers between devices: 7.01 us -> 11.7 us  [swap(): return lax.ppermute(a, axis, [(0, 1), (1, 0)])]
    ppermute x3 -> x4, starting transfers between devices: 6.99 us -> 9.97 us  [swap(): return lax.ppermute(a, axis, [(0, 1), (1, 0)])]
    pallas_call x1, Pallas kernels: 7.97 us -> 10.3 us  [hidden_call(): pl.pallas_call(hidden_kernel, grid_spec=pltpu.PrefetchScalarGridSpec(num_...]
    pallas_call x3 -> x16, Pallas kernels: 4.12 us -> 3.77 us  [the longest x1 2.64 us: sum_grads(): pl.pallas_call(sum_kernel, out_shape=jax.ShapeDtypeStruct(grads.shape[1:]...]
  transfers between devices with their start and end apart: 17 -> 36, of which waited for: 11 -> 21; matrix products, arithmetic and copies ran while one was open for 2% -> 1% of each run, Pallas kernels for 3% -> 3%
where the time goes in v7:
time: 204 us; the launch traced here: 203 us
  starting transfers between devices  131 us (64%)
  waiting for transfers between devices  41.3 us (20%)
  Pallas kernels  19.5 us (10%)
  local copies, waits for them, and re-layouts  8.22 us (4%)
    ppermute x30, starting transfers between devices, shift(): return lax.ppermute(a, 'z', [(i, (i + by) % RING) for i in range(RING)])  109 us
    ppermute x30, waiting for transfers between devices, shift(): return lax.ppermute(a, 'z', [(i, (i + by) % RING) for i in range(RING)])  29.6 us
    ppermute x4, waiting for transfers between devices, swap(): return lax.ppermute(a, axis, [(0, 1), (1, 0)])  11.7 us
    pallas_call x1, Pallas kernels, hidden_call(): pl.pallas_call(hidden_kernel, grid_spec=pltpu.PrefetchScalarGridSpec(num_...  10.3 us
    ppermute x4, starting transfers between devices, swap(): return lax.ppermute(a, axis, [(0, 1), (1, 0)])  9.97 us
    all_to_all x1, starting transfers between devices, gather_weights(): lax.all_to_all(jnp.broadcast_to(sent, (8,) + sent.shape), ('x', 'yl'), 0, 0)  6.44 us
    all_to_all x1, starting transfers between devices, shards(): grads = sum_grads(lax.all_to_all(both, ('x', 'yl'), 0, 0))  5.99 us
    unnamed x19, local copies, waits for them, and re-layouts  5.74 us
  transfers between devices with their start and end apart: 36, of which 21 were waited for; matrix products, arithmetic and copies ran while one was open for 1% of the time, Pallas kernels for 3%

profile of v7, /device:TPU:24, one launch (start us, length us, event | category | flops | bytes accessed | tf_op | source)
XLA Modules:
  0.0 203.0 jit_solution(14022475938214591883)
XLA Ops:
  1.7 3.1 %collective-permute-start = (bf16[2,128,128]{2,1,0:T(8,128)(2,1)S(1)}, bf16[2,128,128]{2,1,0:T(8,128)(2,1)S(1)}, u32[]{:S(2)}, u32[]{:S(2)}) collective-permute-start(bf16[2,128,128]{2,1,0:T(8,128)(2,1)S(1)} %bitcast.17), channel_id=1, source_target_pairs={{0,16},{16,0},{1,17},{17,1},{2,18},{18,2},{3,19},{19,3},{4,20},{20... | collective-permute-start | bytes 196616 | tf_op jit(solution)/shard_map/ppermute | solution.py:158
  6.5 2.9 %collective-permute-done = bf16[2,128,128]{2,1,0:T(8,128)(2,1)S(1)} collective-permute-done((bf16[2,128,128]{2,1,0:T(8,128)(2,1)S(1)}, bf16[2,128,128]{2,1,0:T(8,128)(2,1)S(1)}, u32[]{:S(2)}, u32[]{:S(2)}) %collective-permute-start) | collective-permute-done | bytes 65568 | tf_op jit(solution)/shard_map/ppermute | solution.py:158
  9.4 1.6 broadcast_in_dim.7
  11.0 6.4 %all-to-all-start = ((bf16[8,1040,128]{2,1,0:T(8,128)(2,1)}), bf16[8,1040,128]{2,1,0:T(8,128)(2,1)S(1)}, u32[]{:S(2)}, u32[]{:S(2)}) async-start(bf16[8,1040,128]{2,1,0:T(8,128)(2,1)} %broadcast_in_dim.7), calls=%async_computation | async-start | bytes 4259840 | tf_op jit(solution)/shard_map/all_to_all | solution.py:289
  17.5 3.1 %collective-permute-start.2 = (bf16[4,128,128]{2,1,0:T(8,128)(2,1)S(1)}, bf16[4,128,128]{2,1,0:T(8,128)(2,1)S(1)}, u32[]{:S(2)}, u32[]{:S(2)}) collective-permute-start(bf16[4,128,128]{2,1,0:T(8,128)(2,1)S(1)} %pad_maximum_fusion.refs_1_.refs_0_), channel_id=1, source_target_pairs={{0,1},{1,2},{2,3},{3,4},{4,5},{5,6},{6,7},{7,8},{8,9},{9,10},{10,1... | collective-permute-start | bytes 393224 | tf_op jit(solution)/shard_map/ppermute | solution.py:154
  20.6 9.5 %collective-permute-start.1 = (bf16[4,128,128]{2,1,0:T(8,128)(2,1)S(1)}, bf16[4,128,128]{2,1,0:T(8,128)(2,1)S(1)}, u32[]{:S(2)}, u32[]{:S(2)}) collective-permute-start(bf16[4,128,128]{2,1,0:T(8,128)(2,1)S(1)} %pad_maximum_fusion.refs_1_.refs_0_), channel_id=1, source_target_pairs={{0,15},{1,0},{2,1},{3,2},{4,3},{5,4},{6,5},{7,6},{8,7},{9,8},{10,9... | collective-permute-start | bytes 393224 | tf_op jit(solution)/shard_map/ppermute | solution.py:154
  31.1 1.9 collective-permute-start.4
  33.1 5.1 %collective-permute-start.3 = (bf16[4,128,128]{2,1,0:T(8,128)(2,1)S(1)}, bf16[4,128,128]{2,1,0:T(8,128)(2,1)S(1)}, u32[]{:S(2)}, u32[]{:S(2)}) collective-permute-start(bf16[4,128,128]{2,1,0:T(8,128)(2,1)S(1)} %shard_map.69.refs_1_), channel_id=1, source_target_pairs={{0,15},{1,0},{2,1},{3,2},{4,3},{5,4},{6,5},{7,6},{8,7},{9,8},{10,9... | collective-permute-start | bytes 393224 | tf_op jit(solution)/shard_map/ppermute | solution.py:154
  39.2 1.9 collective-permute-start.6
  41.1 5.1 %collective-permute-start.5 = (bf16[4,128,128]{2,1,0:T(8,128)(2,1)S(1)}, bf16[4,128,128]{2,1,0:T(8,128)(2,1)S(1)}, u32[]{:S(2)}, u32[]{:S(2)}) collective-permute-start(bf16[4,128,128]{2,1,0:T(8,128)(2,1)S(1)} %shard_map.71.refs_1_.refs_2_), channel_id=1, source_target_pairs={{0,15},{1,0},{2,1},{3,2},{4,3},{5,4},{6,5},{7,6},{8,7},{9,8},{10,9... | collective-permute-start | bytes 393224 | tf_op jit(solution)/shard_map/ppermute | solution.py:154
  47.2 1.9 collective-permute-start.8
  49.2 5.1 %collective-permute-start.7 = (bf16[4,128,128]{2,1,0:T(8,128)(2,1)S(1)}, bf16[4,128,128]{2,1,0:T(8,128)(2,1)S(1)}, u32[]{:S(2)}, u32[]{:S(2)}) collective-permute-start(bf16[4,128,128]{2,1,0:T(8,128)(2,1)S(1)} %shard_map.73.refs_1_.refs_3_), channel_id=1, source_target_pairs={{0,15},{1,0},{2,1},{3,2},{4,3},{5,4},{6,5},{7,6},{8,7},{9,8},{10,9... | collective-permute-start | bytes 393224 | tf_op jit(solution)/shard_map/ppermute | solution.py:154
  55.5 1.9 collective-permute-start.10
  57.4 5.1 %collective-permute-start.9 = (bf16[4,128,128]{2,1,0:T(8,128)(2,1)S(1)}, bf16[4,128,128]{2,1,0:T(8,128)(2,1)S(1)}, u32[]{:S(2)}, u32[]{:S(2)}) collective-permute-start(bf16[4,128,128]{2,1,0:T(8,128)(2,1)S(1)} %shard_map.75.refs_1_.refs_4_), channel_id=1, source_target_pairs={{0,15},{1,0},{2,1},{3,2},{4,3},{5,4},{6,5},{7,6},{8,7},{9,8},{10,9... | collective-permute-start | bytes 393224 | tf_op jit(solution)/shard_map/ppermute | solution.py:154
  65.1 1.9 collective-permute-start.11
  67.0 1.9 collective-permute-start.13
  68.9 5.6 %collective-permute-start.12 = (bf16[4,128,128]{2,1,0:T(8,128)(2,1)S(1)}, bf16[4,128,128]{2,1,0:T(8,128)(2,1)}, u32[]{:S(2)}, u32[]{:S(2)}) collective-permute-start(bf16[4,128,128]{2,1,0:T(8,128)(2,1)S(1)} %shard_map.77.refs_1_.refs_5_), channel_id=1, source_target_pairs={{0,15},{1,0},{2,1},{3,2},{4,3},{5,4},{6,5},{7,6},{8,7},{9,8},{10,9... | collective-permute-start | bytes 393224 | tf_op jit(solution)/shard_map/ppermute | solution.py:154
  74.5 2.2 %collective-permute-done.13.refs_0_ = bf16[4,128,128]{2,1,0:T(8,128)(2,1)S(1)} collective-permute-done((bf16[4,128,128]{2,1,0:T(8,128)(2,1)S(1)}, bf16[4,128,128]{2,1,0:T(8,128)(2,1)S(1)}, u32[]{:S(2)}, u32[]{:S(2)}) %collective-permute-start.13) | collective-permute-done | bytes 131104 | tf_op jit(solution)/shard_map/ppermute | solution.py:154
  76.7 1.9 collective-permute-start.15
  79.3 5.1 %collective-permute-start.14 = (bf16[4,128,128]{2,1,0:T(8,128)(2,1)}, bf16[4,128,128]{2,1,0:T(8,128)(2,1)}, u32[]{:S(2)}, u32[]{:S(2)}) collective-permute-start(bf16[4,128,128]{2,1,0:T(8,128)(2,1)} %shard_map.80.refs_1_.refs_6_), channel_id=1, source_target_pairs={{0,15},{1,0},{2,1},{3,2},{4,3},{5,4},{6,5},{7,6},{8,7},{9,8},{10,9... | collective-permute-start | bytes 393224 | tf_op jit(solution)/shard_map/ppermute | solution.py:154
  85.2 1.9 collective-permute-start.16
  88.1 5.5 %collective-permute-done.16.refs_8_ = bf16[4,128,128]{2,1,0:T(8,128)(2,1)} collective-permute-done((bf16[4,128,128]{2,1,0:T(8,128)(2,1)}, bf16[4,128,128]{2,1,0:T(8,128)(2,1)}, u32[]{:S(2)}, u32[]{:S(2)}) %collective-permute-start.16) | collective-permute-done | bytes 131104 | tf_op jit(solution)/shard_map/ppermute | solution.py:154
  96.4 10.3 %shard_map.83 = (bf16[128,1024]{1,0:T(8,128)(2,1)}, bf16[128,1024]{1,0:T(8,128)(2,1)S(1)}, bf16[8,8,128,128]{3,2,1,0:T(8,128)(2,1)S(1)}, bf16[8,8,128,128]{3,2,1,0:T(8,128)(2,1)S(1)}) custom-call(s32[16,8]{1,0:T(8,128)S(1)} %fusion.10.rows_ref, bf16[4,128,128]{2,1,0:T(8,128)(2,1)S(1)} %pad_maximum_fusion.refs_1_.refs_0_, ...), custom_call_target="tpu_custom_call" | custom-call | flops 1073741824 | bytes 11000000 | tf_op jit(solution)/shard_map/pallas_call | solution.py:110
  106.7 1.9 collective-permute-start.17
  108.6 4.1 %collective-permute-done.17.got_ref = bf16[8,8,128,128]{3,2,1,0:T(8,128)(2,1)S(1)} collective-permute-done((bf16[8,8,128,128]{3,2,1,0:T(8,128)(2,1)S(1)}, bf16[8,8,128,128]{3,2,1,0:T(8,128)(2,1)S(1)}, u32[]{:S(2)}, u32[]{:S(2)}) %collective-permute-start.17) | collective-permute-done | bytes 2097184 | tf_op jit(solution)/shard_map/ppermute | solution.py:158
  114.7 6.0 %all-to-all-start.1 = ((bf16[8,8,128,128]{3,2,1,0:T(8,128)(2,1)}), bf16[8,8,128,128]{3,2,1,0:T(8,128)(2,1)}, u32[]{:S(2)}, u32[]{:S(2)}) async-start(bf16[8,8,128,128]{3,2,1,0:T(8,128)(2,1)} %copy-done), calls=%async_computation.1 | async-start | bytes 4194304 | tf_op jit(solution)/shard_map/all_to_all | solution.py:311
  120.7 4.8 %shard_map.86 = (bf16[4,128,128]{2,1,0:T(8,128)(2,1)S(1)}, bf16[4,128,128]{2,1,0:T(8,128)(2,1)S(1)}, bf16[4,128,128]{2,1,0:T(8,128)(2,1)S(1)}, bf16[4,128,128]{2...) custom-call(s32[16,8]{1,0:T(8,128)S(1)} %fusion.10.rows_ref, ...), custom_call_target="tpu_custom_call" | custom-call | flops 536870912 | bytes 7000000 | tf_op jit(solution)/shard_map/pallas_call | solution.py:133
  125.5 1.9 collective-permute-start.18
  127.4 5.1 %collective-permute-start.20 = (bf16[4,128,128]{2,1,0:T(8,128)(2,1)S(1)}, bf16[4,128,128]{2,1,0:T(8,128)(2,1)S(1)}, u32[]{:S(2)}, u32[]{:S(2)}) collective-permute-start(bf16[4,128,128]{2,1,0:T(8,128)(2,1)S(1)} %get-tuple-element.46.after_ref), channel_id=1, source_target_pairs={{0,15},{1,0},{2,1},{3,2},{4,3},{5,4},{6,5},{7,6},{8,7},{9,8},{10,9... | collective-permute-start | bytes 393224 | tf_op jit(solution)/shard_map/ppermute | solution.py:154
  133.6 1.9 collective-permute-start.19
  135.6 5.1 %collective-permute-start.22 = (bf16[4,128,128]{2,1,0:T(8,128)(2,1)S(1)}, bf16[4,128,128]{2,1,0:T(8,128)(2,1)S(1)}, u32[]{:S(2)}, u32[]{:S(2)}) collective-permute-start(bf16[4,128,128]{2,1,0:T(8,128)(2,1)S(1)} %shard_map.88.after_ref), channel_id=1, source_target_pairs={{0,15},{1,0},{2,1},{3,2},{4,3},{5,4},{6,5},{7,6},{8,7},{9,8},{10,9... | collective-permute-start | bytes 393224 | tf_op jit(solution)/shard_map/ppermute | solution.py:154
  141.7 1.9 collective-permute-start.21
  143.7 5.1 %collective-permute-start.24 = (bf16[4,128,128]{2,1,0:T(8,128)(2,1)S(1)}, bf16[4,128,128]{2,1,0:T(8,128)(2,1)S(1)}, u32[]{:S(2)}, u32[]{:S(2)}) collective-permute-start(bf16[4,128,128]{2,1,0:T(8,128)(2,1)S(1)} %shard_map.90.after_ref), channel_id=1, source_target_pairs={{0,15},{1,0},{2,1},{3,2},{4,3},{5,4},{6,5},{7,6},{8,7},{9,8},{10,9... | collective-permute-start | bytes 393224 | tf_op jit(solution)/shard_map/ppermute | solution.py:154
  149.8 1.9 collective-permute-start.23
  151.8 5.1 %collective-permute-start.26 = (bf16[4,128,128]{2,1,0:T(8,128)(2,1)S(1)}, bf16[4,128,128]{2,1,0:T(8,128)(2,1)S(1)}, u32[]{:S(2)}, u32[]{:S(2)}) collective-permute-start(bf16[4,128,128]{2,1,0:T(8,128)(2,1)S(1)} %shard_map.92.after_ref), channel_id=1, source_target_pairs={{0,15},{1,0},{2,1},{3,2},{4,3},{5,4},{6,5},{7,6},{8,7},{9,8},{10,9... | collective-permute-start | bytes 393224 | tf_op jit(solution)/shard_map/ppermute | solution.py:154
  158.0 1.9 collective-permute-start.25
  159.9 5.1 %collective-permute-start.28 = (bf16[4,128,128]{2,1,0:T(8,128)(2,1)S(1)}, bf16[4,128,128]{2,1,0:T(8,128)(2,1)S(1)}, u32[]{:S(2)}, u32[]{:S(2)}) collective-permute-start(bf16[4,128,128]{2,1,0:T(8,128)(2,1)S(1)} %shard_map.94.after_ref), channel_id=1, source_target_pairs={{0,15},{1,0},{2,1},{3,2},{4,3},{5,4},{6,5},{7,6},{8,7},{9,8},{10,9... | collective-permute-start | bytes 393224 | tf_op jit(solution)/shard_map/ppermute | solution.py:154
  166.1 1.9 collective-permute-start.27
  168.0 5.1 %collective-permute-start.30 = (bf16[4,128,128]{2,1,0:T(8,128)(2,1)S(1)}, bf16[4,128,128]{2,1,0:T(8,128)(2,1)S(1)}, u32[]{:S(2)}, u32[]{:S(2)}) collective-permute-start(bf16[4,128,128]{2,1,0:T(8,128)(2,1)S(1)} %shard_map.96.after_ref), channel_id=1, source_target_pairs={{0,15},{1,0},{2,1},{3,2},{4,3},{5,4},{6,5},{7,6},{8,7},{9,8},{10,9... | collective-permute-start | bytes 393224 | tf_op jit(solution)/shard_map/ppermute | solution.py:154
  173.2 1.8 collective-permute-done.27.got_ref
  175.0 1.9 collective-permute-start.29
  177.0 5.4 %collective-permute-start.32 = (bf16[4,128,128]{2,1,0:T(8,128)(2,1)S(1)}, bf16[4,128,128]{2,1,0:T(8,128)(2,1)S(1)}, u32[]{:S(2)}, u32[]{:S(2)}) collective-permute-start(bf16[4,128,128]{2,1,0:T(8,128)(2,1)S(1)} %shard_map.98.after_ref), channel_id=1, source_target_pairs={{0,15},{1,0},{2,1},{3,2},{4,3},{5,4},{6,5},{7,6},{8,7},{9,8},{10,9... | collective-permute-start | bytes 393224 | tf_op jit(solution)/shard_map/ppermute | solution.py:154
  182.4 1.5 collective-permute-done.29.got_ref
  183.9 1.9 collective-permute-start.31
  185.9 6.1 %collective-permute-done.31.up_ref = bf16[4,128,128]{2,1,0:T(8,128)(2,1)S(1)} collective-permute-done((bf16[4,128,128]{2,1,0:T(8,128)(2,1)S(1)}, bf16[4,128,128]{2,1,0:T(8,128)(2,1)S(1)}, u32[]{:S(2)}, u32[]{:S(2)}) %collective-permute-start.31) | collective-permute-done | bytes 131104 | tf_op jit(solution)/shard_map/ppermute | solution.py:154
  192.1 3.0 %collective-permute-start.33 = (bf16[2,128,128]{2,1,0:T(8,128)(2,1)S(1)}, bf16[2,128,128]{2,1,0:T(8,128)(2,1)S(1)}, u32[]{:S(2)}, u32[]{:S(2)}) collective-permute-start(bf16[2,128,128]{2,1,0:T(8,128)(2,1)S(1)} %get-tuple-element.61), channel_id=1, source_target_pairs={{0,16},{16,0},{1,17},{17,1},{2,18},{18,2},{3,19},{19,3},{4,20},{20... | collective-permute-start | bytes 196616 | tf_op jit(solution)/shard_map/ppermute | solution.py:158
  195.1 4.7 %collective-permute-done.33.got_ref = bf16[2,128,128]{2,1,0:T(8,128)(2,1)S(1)} collective-permute-done((bf16[2,128,128]{2,1,0:T(8,128)(2,1)S(1)}, bf16[2,128,128]{2,1,0:T(8,128)(2,1)S(1)}, u32[]{:S(2)}, u32[]{:S(2)}) %collective-permute-start.33) | collective-permute-done | bytes 65568 | tf_op jit(solution)/shard_map/ppermute | solution.py:158
  200.4 2.6 %shard_map.102 = bf16[8,128,128]{2,1,0:T(8,128)(2,1)} custom-call(bf16[8,8,128,128]{3,2,1,0:T(8,128)(2,1)} %all-to-all-done.1.grads_ref), custom_call_target="tpu_custom_call" | custom-call | flops 2000000 | bytes 2500000 | tf_op jit(solution)/shard_map/pallas_call | solution.py:240
  (87 shorter events, 22.4 us)
Async XLA Ops:
  1.7 7.7 %collective-permute-start = (bf16[2,128,128]{2,1,0:T(8,128)(2,1)S(1)}, bf16[2,128,128]{2,1,0:T(8,128)(2,1)S(1)}, u32[]{:S(2)}, u32[]{:S(2)}) collective-permute-start(bf16[2,128,128]{2,1,0:T(8,128)(2,1)S(1)} %bitcast.17), channel_id=1, source_target_pairs={{0,16},{16,0},{1,17},{17,1},{2,18},{18,2},{3,19},{19,3},{4,20},{20... | collective-permute-start | bytes 196616 | tf_op jit(solution)/shard_map/ppermute | solution.py:158
  11.0 54.1 %all-to-all-start = ((bf16[8,1040,128]{2,1,0:T(8,128)(2,1)}), bf16[8,1040,128]{2,1,0:T(8,128)(2,1)S(1)}, u32[]{:S(2)}, u32[]{:S(2)}) async-start(bf16[8,1040,128]{2,1,0:T(8,128)(2,1)} %broadcast_in_dim.7), calls=%async_computation | async-start | bytes 4259840 | tf_op jit(solution)/shard_map/all_to_all | solution.py:289
  17.5 13.6 %collective-permute-start.2 = (bf16[4,128,128]{2,1,0:T(8,128)(2,1)S(1)}, bf16[4,128,128]{2,1,0:T(8,128)(2,1)S(1)}, u32[]{:S(2)}, u32[]{:S(2)}) collective-permute-start(bf16[4,128,128]{2,1,0:T(8,128)(2,1)S(1)} %pad_maximum_fusion.refs_1_.refs_0_), channel_id=1, source_target_pairs={{0,1},{1,2},{2,3},{3,4},{4,5},{5,6},{6,7},{7,8},{8,9},{9,10},{10,1... | collective-permute-start | bytes 393224 | tf_op jit(solution)/shard_map/ppermute | solution.py:154
  20.6 12.4 %collective-permute-start.1 = (bf16[4,128,128]{2,1,0:T(8,128)(2,1)S(1)}, bf16[4,128,128]{2,1,0:T(8,128)(2,1)S(1)}, u32[]{:S(2)}, u32[]{:S(2)}) collective-permute-start(bf16[4,128,128]{2,1,0:T(8,128)(2,1)S(1)} %pad_maximum_fusion.refs_1_.refs_0_), channel_id=1, source_target_pairs={{0,15},{1,0},{2,1},{3,2},{4,3},{5,4},{6,5},{7,6},{8,7},{9,8},{10,9... | collective-permute-start | bytes 393224 | tf_op jit(solution)/shard_map/ppermute | solution.py:154
  31.1 26.3 %copy-start.1 = (bf16[4,128,128]{2,1,0:T(8,128)(2,1)}, bf16[4,128,128]{2,1,0:T(8,128)(2,1)S(1)}, u32[]{:S(2)}) copy-start(bf16[4,128,128]{2,1,0:T(8,128)(2,1)S(1)} %shard_map.68.refs_1_.refs_15_) | copy-start | bytes 393220
  31.1 8.1 %collective-permute-start.4 = (bf16[4,128,128]{2,1,0:T(8,128)(2,1)S(1)}, bf16[4,128,128]{2,1,0:T(8,128)(2,1)S(1)}, u32[]{:S(2)}, u32[]{:S(2)}) collective-permute-start(bf16[4,128,128]{2,1,0:T(8,128)(2,1)S(1)} %shard_map.68.refs_1_.refs_15_), channel_id=1, source_target_pairs={{0,1},{1,2},{2,3},{3,4},{4,5},{5,6},{6,7},{7,8},{8,9},{9,10},{10,1... | collective-permute-start | bytes 393224 | tf_op jit(solution)/shard_map/ppermute | solution.py:154
  33.1 8.0 %collective-permute-start.3 = (bf16[4,128,128]{2,1,0:T(8,128)(2,1)S(1)}, bf16[4,128,128]{2,1,0:T(8,128)(2,1)S(1)}, u32[]{:S(2)}, u32[]{:S(2)}) collective-permute-start(bf16[4,128,128]{2,1,0:T(8,128)(2,1)S(1)} %shard_map.69.refs_1_), channel_id=1, source_target_pairs={{0,15},{1,0},{2,1},{3,2},{4,3},{5,4},{6,5},{7,6},{8,7},{9,8},{10,9... | collective-permute-start | bytes 393224 | tf_op jit(solution)/shard_map/ppermute | solution.py:154
  39.2 8.1 %collective-permute-start.6 = (bf16[4,128,128]{2,1,0:T(8,128)(2,1)S(1)}, bf16[4,128,128]{2,1,0:T(8,128)(2,1)S(1)}, u32[]{:S(2)}, u32[]{:S(2)}) collective-permute-start(bf16[4,128,128]{2,1,0:T(8,128)(2,1)S(1)} %shard_map.70.refs_1_.refs_14_), channel_id=1, source_target_pairs={{0,1},{1,2},{2,3},{3,4},{4,5},{5,6},{6,7},{7,8},{8,9},{9,10},{10,1... | collective-permute-start | bytes 393224 | tf_op jit(solution)/shard_map/ppermute | solution.py:154
  41.1 8.0 %collective-permute-start.5 = (bf16[4,128,128]{2,1,0:T(8,128)(2,1)S(1)}, bf16[4,128,128]{2,1,0:T(8,128)(2,1)S(1)}, u32[]{:S(2)}, u32[]{:S(2)}) collective-permute-start(bf16[4,128,128]{2,1,0:T(8,128)(2,1)S(1)} %shard_map.71.refs_1_.refs_2_), channel_id=1, source_target_pairs={{0,15},{1,0},{2,1},{3,2},{4,3},{5,4},{6,5},{7,6},{8,7},{9,8},{10,9... | collective-permute-start | bytes 393224 | tf_op jit(solution)/shard_map/ppermute | solution.py:154
  47.2 8.2 %collective-permute-start.8 = (bf16[4,128,128]{2,1,0:T(8,128)(2,1)S(1)}, bf16[4,128,128]{2,1,0:T(8,128)(2,1)S(1)}, u32[]{:S(2)}, u32[]{:S(2)}) collective-permute-start(bf16[4,128,128]{2,1,0:T(8,128)(2,1)S(1)} %shard_map.72.refs_1_.refs_13_), channel_id=1, source_target_pairs={{0,1},{1,2},{2,3},{3,4},{4,5},{5,6},{6,7},{7,8},{8,9},{9,10},{10,1... | collective-permute-start | bytes 393224 | tf_op jit(solution)/shard_map/ppermute | solution.py:154
  49.2 8.2 %collective-permute-start.7 = (bf16[4,128,128]{2,1,0:T(8,128)(2,1)S(1)}, bf16[4,128,128]{2,1,0:T(8,128)(2,1)S(1)}, u32[]{:S(2)}, u32[]{:S(2)}) collective-permute-start(bf16[4,128,128]{2,1,0:T(8,128)(2,1)S(1)} %shard_map.73.refs_1_.refs_3_), channel_id=1, source_target_pairs={{0,15},{1,0},{2,1},{3,2},{4,3},{5,4},{6,5},{7,6},{8,7},{9,8},{10,9... | collective-permute-start | bytes 393224 | tf_op jit(solution)/shard_map/ppermute | solution.py:154
  55.5 8.1 %collective-permute-start.10 = (bf16[4,128,128]{2,1,0:T(8,128)(2,1)S(1)}, bf16[4,128,128]{2,1,0:T(8,128)(2,1)S(1)}, u32[]{:S(2)}, u32[]{:S(2)}) collective-permute-start(bf16[4,128,128]{2,1,0:T(8,128)(2,1)S(1)} %shard_map.74.refs_1_.refs_12_), channel_id=1, source_target_pairs={{0,1},{1,2},{2,3},{3,4},{4,5},{5,6},{6,7},{7,8},{8,9},{9,10},{10,1... | collective-permute-start | bytes 393224 | tf_op jit(solution)/shard_map/ppermute | solution.py:154
  57.4 7.6 %collective-permute-start.9 = (bf16[4,128,128]{2,1,0:T(8,128)(2,1)S(1)}, bf16[4,128,128]{2,1,0:T(8,128)(2,1)S(1)}, u32[]{:S(2)}, u32[]{:S(2)}) collective-permute-start(bf16[4,128,128]{2,1,0:T(8,128)(2,1)S(1)} %shard_map.75.refs_1_.refs_4_), channel_id=1, source_target_pairs={{0,15},{1,0},{2,1},{3,2},{4,3},{5,4},{6,5},{7,6},{8,7},{9,8},{10,9... | collective-permute-start | bytes 393224 | tf_op jit(solution)/shard_map/ppermute | solution.py:154
  65.1 22.2 %collective-permute-start.11 = (bf16[8,1040,128]{2,1,0:T(8,128)(2,1)S(1)}, bf16[8,1040,128]{2,1,0:T(8,128)(2,1)}, u32[]{:S(2)}, u32[]{:S(2)}) collective-permute-start(bf16[8,1040,128]{2,1,0:T(8,128)(2,1)S(1)} %shard_map.78.refs_16_.mine), channel_id=1, source_target_pairs={{0,32},{32,0},{1,33},{33,1},{2,34},{34,2},{3,35},{35,3},{4,36},{36... | collective-permute-start | bytes 6389768 | tf_op jit(solution)/shard_map/ppermute | solution.py:158
  67.0 9.7 %collective-permute-start.13 = (bf16[4,128,128]{2,1,0:T(8,128)(2,1)S(1)}, bf16[4,128,128]{2,1,0:T(8,128)(2,1)S(1)}, u32[]{:S(2)}, u32[]{:S(2)}) collective-permute-start(bf16[4,128,128]{2,1,0:T(8,128)(2,1)S(1)} %shard_map.76.refs_1_.refs_11_), channel_id=1, source_target_pairs={{0,1},{1,2},{2,3},{3,4},{4,5},{5,6},{6,7},{7,8},{8,9},{9,10},{10,1... | collective-permute-start | bytes 393224 | tf_op jit(solution)/shard_map/ppermute | solution.py:154
  68.9 9.7 %collective-permute-start.12 = (bf16[4,128,128]{2,1,0:T(8,128)(2,1)S(1)}, bf16[4,128,128]{2,1,0:T(8,128)(2,1)}, u32[]{:S(2)}, u32[]{:S(2)}) collective-permute-start(bf16[4,128,128]{2,1,0:T(8,128)(2,1)S(1)} %shard_map.77.refs_1_.refs_5_), channel_id=1, source_target_pairs={{0,15},{1,0},{2,1},{3,2},{4,3},{5,4},{6,5},{7,6},{8,7},{9,8},{10,9... | collective-permute-start | bytes 393224 | tf_op jit(solution)/shard_map/ppermute | solution.py:154
  76.7 8.5 %collective-permute-start.15 = (bf16[4,128,128]{2,1,0:T(8,128)(2,1)S(1)}, bf16[4,128,128]{2,1,0:T(8,128)(2,1)}, u32[]{:S(2)}, u32[]{:S(2)}) collective-permute-start(bf16[4,128,128]{2,1,0:T(8,128)(2,1)S(1)} %shard_map.79.refs_1_.refs_10_), channel_id=1, source_target_pairs={{0,1},{1,2},{2,3},{3,4},{4,5},{5,6},{6,7},{7,8},{8,9},{9,10},{10,1... | collective-permute-start | bytes 393224 | tf_op jit(solution)/shard_map/ppermute | solution.py:154
  78.7 0.7 copy-start.3
  79.3 8.0 %collective-permute-start.14 = (bf16[4,128,128]{2,1,0:T(8,128)(2,1)}, bf16[4,128,128]{2,1,0:T(8,128)(2,1)}, u32[]{:S(2)}, u32[]{:S(2)}) collective-permute-start(bf16[4,128,128]{2,1,0:T(8,128)(2,1)} %shard_map.80.refs_1_.refs_6_), channel_id=1, source_target_pairs={{0,15},{1,0},{2,1},{3,2},{4,3},{5,4},{6,5},{7,6},{8,7},{9,8},{10,9... | collective-permute-start | bytes 393224 | tf_op jit(solution)/shard_map/ppermute | solution.py:154
  85.2 8.4 %collective-permute-start.16 = (bf16[4,128,128]{2,1,0:T(8,128)(2,1)}, bf16[4,128,128]{2,1,0:T(8,128)(2,1)}, u32[]{:S(2)}, u32[]{:S(2)}) collective-permute-start(bf16[4,128,128]{2,1,0:T(8,128)(2,1)} %shard_map.81.refs_1_.refs_9_), channel_id=1, source_target_pairs={{0,1},{1,2},{2,3},{3,4},{4,5},{5,6},{6,7},{7,8},{8,9},{9,10},{10,1... | collective-permute-start | bytes 393224 | tf_op jit(solution)/shard_map/ppermute | solution.py:154
  93.6 0.9 copy-start.2
  94.5 0.9 copy-start.4
  95.4 0.9 copy-start.7
  106.7 6.6 %copy-start.5 = (bf16[128,1024]{1,0:T(8,128)(2,1)}, bf16[128,1024]{1,0:T(8,128)(2,1)S(1)}, u32[]{:S(2)}) copy-start(bf16[128,1024]{1,0:T(8,128)(2,1)S(1)} %get-tuple-element.40.refs_0_) | copy-start | bytes 786436
  106.7 6.1 %collective-permute-start.17 = (bf16[8,8,128,128]{3,2,1,0:T(8,128)(2,1)S(1)}, bf16[8,8,128,128]{3,2,1,0:T(8,128)(2,1)S(1)}, u32[]{:S(2)}, u32[]{:S(2)}) collective-permute-start(bf16[8,8,128,128]{3,2,1,0:T(8,128)(2,1)S(1)} %get-tuple-element.42), channel_id=1, source_target_pairs={{0,32},{32,0},{1,33},{33,1},{2,34},{34,2},{3,35},{35,3},{4,36},{36... | collective-permute-start | bytes 6291464 | tf_op jit(solution)/shard_map/ppermute | solution.py:158
  113.3 1.4 copy-start
  114.7 6.0 %copy-start.6 = (bf16[128,1024]{1,0:T(8,128)(2,1)S(1)}, bf16[128,1024]{1,0:T(8,128)(2,1)}, u32[]{:S(2)}) copy-start(bf16[128,1024]{1,0:T(8,128)(2,1)} %copy-done.5) | copy-start | bytes 786436
  114.7 85.7 %all-to-all-start.1 = ((bf16[8,8,128,128]{3,2,1,0:T(8,128)(2,1)}), bf16[8,8,128,128]{3,2,1,0:T(8,128)(2,1)}, u32[]{:S(2)}, u32[]{:S(2)}) async-start(bf16[8,8,128,128]{3,2,1,0:T(8,128)(2,1)} %copy-done), calls=%async_computation.1 | async-start | bytes 4194304 | tf_op jit(solution)/shard_map/all_to_all | solution.py:311
  125.5 8.1 %collective-permute-start.18 = (bf16[4,128,128]{2,1,0:T(8,128)(2,1)S(1)}, bf16[4,128,128]{2,1,0:T(8,128)(2,1)S(1)}, u32[]{:S(2)}, u32[]{:S(2)}) collective-permute-start(bf16[4,128,128]{2,1,0:T(8,128)(2,1)S(1)} %get-tuple-element.44), channel_id=1, source_target_pairs={{0,1},{1,2},{2,3},{3,4},{4,5},{5,6},{6,7},{7,8},{8,9},{9,10},{10,1... | collective-permute-start | bytes 393224 | tf_op jit(solution)/shard_map/ppermute | solution.py:154
  127.4 8.1 %collective-permute-start.20 = (bf16[4,128,128]{2,1,0:T(8,128)(2,1)S(1)}, bf16[4,128,128]{2,1,0:T(8,128)(2,1)S(1)}, u32[]{:S(2)}, u32[]{:S(2)}) collective-permute-start(bf16[4,128,128]{2,1,0:T(8,128)(2,1)S(1)} %get-tuple-element.46.after_ref), channel_id=1, source_target_pairs={{0,15},{1,0},{2,1},{3,2},{4,3},{5,4},{6,5},{7,6},{8,7},{9,8},{10,9... | collective-permute-start | bytes 393224 | tf_op jit(solution)/shard_map/ppermute | solution.py:154
  133.6 8.1 %collective-permute-start.19 = (bf16[4,128,128]{2,1,0:T(8,128)(2,1)S(1)}, bf16[4,128,128]{2,1,0:T(8,128)(2,1)S(1)}, u32[]{:S(2)}, u32[]{:S(2)}) collective-permute-start(bf16[4,128,128]{2,1,0:T(8,128)(2,1)S(1)} %shard_map.87.after_ref), channel_id=1, source_target_pairs={{0,1},{1,2},{2,3},{3,4},{4,5},{5,6},{6,7},{7,8},{8,9},{9,10},{10,1... | collective-permute-start | bytes 393224 | tf_op jit(solution)/shard_map/ppermute | solution.py:154
  135.6 8.1 %collective-permute-start.22 = (bf16[4,128,128]{2,1,0:T(8,128)(2,1)S(1)}, bf16[4,128,128]{2,1,0:T(8,128)(2,1)S(1)}, u32[]{:S(2)}, u32[]{:S(2)}) collective-permute-start(bf16[4,128,128]{2,1,0:T(8,128)(2,1)S(1)} %shard_map.88.after_ref), channel_id=1, source_target_pairs={{0,15},{1,0},{2,1},{3,2},{4,3},{5,4},{6,5},{7,6},{8,7},{9,8},{10,9... | collective-permute-start | bytes 393224 | tf_op jit(solution)/shard_map/ppermute | solution.py:154
  141.7 8.1 %collective-permute-start.21 = (bf16[4,128,128]{2,1,0:T(8,128)(2,1)S(1)}, bf16[4,128,128]{2,1,0:T(8,128)(2,1)S(1)}, u32[]{:S(2)}, u32[]{:S(2)}) collective-permute-start(bf16[4,128,128]{2,1,0:T(8,128)(2,1)S(1)} %shard_map.89.after_ref), channel_id=1, source_target_pairs={{0,1},{1,2},{2,3},{3,4},{4,5},{5,6},{6,7},{7,8},{8,9},{9,10},{10,1... | collective-permute-start | bytes 393224 | tf_op jit(solution)/shard_map/ppermute | solution.py:154
  143.7 8.1 %collective-permute-start.24 = (bf16[4,128,128]{2,1,0:T(8,128)(2,1)S(1)}, bf16[4,128,128]{2,1,0:T(8,128)(2,1)S(1)}, u32[]{:S(2)}, u32[]{:S(2)}) collective-permute-start(bf16[4,128,128]{2,1,0:T(8,128)(2,1)S(1)} %shard_map.90.after_ref), channel_id=1, source_target_pairs={{0,15},{1,0},{2,1},{3,2},{4,3},{5,4},{6,5},{7,6},{8,7},{9,8},{10,9... | collective-permute-start | bytes 393224 | tf_op jit(solution)/shard_map/ppermute | solution.py:154
  149.8 8.1 %collective-permute-start.23 = (bf16[4,128,128]{2,1,0:T(8,128)(2,1)S(1)}, bf16[4,128,128]{2,1,0:T(8,128)(2,1)S(1)}, u32[]{:S(2)}, u32[]{:S(2)}) collective-permute-start(bf16[4,128,128]{2,1,0:T(8,128)(2,1)S(1)} %shard_map.91.after_ref), channel_id=1, source_target_pairs={{0,1},{1,2},{2,3},{3,4},{4,5},{5,6},{6,7},{7,8},{8,9},{9,10},{10,1... | collective-permute-start | bytes 393224 | tf_op jit(solution)/shard_map/ppermute | solution.py:154
  151.8 8.1 %collective-permute-start.26 = (bf16[4,128,128]{2,1,0:T(8,128)(2,1)S(1)}, bf16[4,128,128]{2,1,0:T(8,128)(2,1)S(1)}, u32[]{:S(2)}, u32[]{:S(2)}) collective-permute-start(bf16[4,128,128]{2,1,0:T(8,128)(2,1)S(1)} %shard_map.92.after_ref), channel_id=1, source_target_pairs={{0,15},{1,0},{2,1},{3,2},{4,3},{5,4},{6,5},{7,6},{8,7},{9,8},{10,9... | collective-permute-start | bytes 393224 | tf_op jit(solution)/shard_map/ppermute | solution.py:154
  158.0 8.1 %collective-permute-start.25 = (bf16[4,128,128]{2,1,0:T(8,128)(2,1)S(1)}, bf16[4,128,128]{2,1,0:T(8,128)(2,1)S(1)}, u32[]{:S(2)}, u32[]{:S(2)}) collective-permute-start(bf16[4,128,128]{2,1,0:T(8,128)(2,1)S(1)} %shard_map.93.after_ref), channel_id=1, source_target_pairs={{0,1},{1,2},{2,3},{3,4},{4,5},{5,6},{6,7},{7,8},{8,9},{9,10},{10,1... | collective-permute-start | bytes 393224 | tf_op jit(solution)/shard_map/ppermute | solution.py:154
  159.9 8.1 %collective-permute-start.28 = (bf16[4,128,128]{2,1,0:T(8,128)(2,1)S(1)}, bf16[4,128,128]{2,1,0:T(8,128)(2,1)S(1)}, u32[]{:S(2)}, u32[]{:S(2)}) collective-permute-start(bf16[4,128,128]{2,1,0:T(8,128)(2,1)S(1)} %shard_map.94.after_ref), channel_id=1, source_target_pairs={{0,15},{1,0},{2,1},{3,2},{4,3},{5,4},{6,5},{7,6},{8,7},{9,8},{10,9... | collective-permute-start | bytes 393224 | tf_op jit(solution)/shard_map/ppermute | solution.py:154
  166.1 8.9 %collective-permute-start.27 = (bf16[4,128,128]{2,1,0:T(8,128)(2,1)S(1)}, bf16[4,128,128]{2,1,0:T(8,128)(2,1)S(1)}, u32[]{:S(2)}, u32[]{:S(2)}) collective-permute-start(bf16[4,128,128]{2,1,0:T(8,128)(2,1)S(1)} %shard_map.95.after_ref), channel_id=1, source_target_pairs={{0,1},{1,2},{2,3},{3,4},{4,5},{5,6},{6,7},{7,8},{8,9},{9,10},{10,1... | collective-permute-start | bytes 393224 | tf_op jit(solution)/shard_map/ppermute | solution.py:154
  168.0 8.9 %collective-permute-start.30 = (bf16[4,128,128]{2,1,0:T(8,128)(2,1)S(1)}, bf16[4,128,128]{2,1,0:T(8,128)(2,1)S(1)}, u32[]{:S(2)}, u32[]{:S(2)}) collective-permute-start(bf16[4,128,128]{2,1,0:T(8,128)(2,1)S(1)} %shard_map.96.after_ref), channel_id=1, source_target_pairs={{0,15},{1,0},{2,1},{3,2},{4,3},{5,4},{6,5},{7,6},{8,7},{9,8},{10,9... | collective-permute-start | bytes 393224 | tf_op jit(solution)/shard_map/ppermute | solution.py:154
  175.0 8.9 %collective-permute-start.29 = (bf16[4,128,128]{2,1,0:T(8,128)(2,1)S(1)}, bf16[4,128,128]{2,1,0:T(8,128)(2,1)S(1)}, u32[]{:S(2)}, u32[]{:S(2)}) collective-permute-start(bf16[4,128,128]{2,1,0:T(8,128)(2,1)S(1)} %shard_map.97.after_ref), channel_id=1, source_target_pairs={{0,1},{1,2},{2,3},{3,4},{4,5},{5,6},{6,7},{7,8},{8,9},{9,10},{10,1... | collective-permute-start | bytes 393224 | tf_op jit(solution)/shard_map/ppermute | solution.py:154
  177.0 8.9 %collective-permute-start.32 = (bf16[4,128,128]{2,1,0:T(8,128)(2,1)S(1)}, bf16[4,128,128]{2,1,0:T(8,128)(2,1)S(1)}, u32[]{:S(2)}, u32[]{:S(2)}) collective-permute-start(bf16[4,128,128]{2,1,0:T(8,128)(2,1)S(1)} %shard_map.98.after_ref), channel_id=1, source_target_pairs={{0,15},{1,0},{2,1},{3,2},{4,3},{5,4},{6,5},{7,6},{8,7},{9,8},{10,9... | collective-permute-start | bytes 393224 | tf_op jit(solution)/shard_map/ppermute | solution.py:154
  183.9 8.1 %collective-permute-start.31 = (bf16[4,128,128]{2,1,0:T(8,128)(2,1)S(1)}, bf16[4,128,128]{2,1,0:T(8,128)(2,1)S(1)}, u32[]{:S(2)}, u32[]{:S(2)}) collective-permute-start(bf16[4,128,128]{2,1,0:T(8,128)(2,1)S(1)} %shard_map.99), channel_id=1, source_target_pairs={{0,1},{1,2},{2,3},{3,4},{4,5},{5,6},{6,7},{7,8},{8,9},{9,10},{10,1... | collective-permute-start | bytes 393224 | tf_op jit(solution)/shard_map/ppermute | solution.py:154
  192.1 7.7 %collective-permute-start.33 = (bf16[2,128,128]{2,1,0:T(8,128)(2,1)S(1)}, bf16[2,128,128]{2,1,0:T(8,128)(2,1)S(1)}, u32[]{:S(2)}, u32[]{:S(2)}) collective-permute-start(bf16[2,128,128]{2,1,0:T(8,128)(2,1)S(1)} %get-tuple-element.61), channel_id=1, source_target_pairs={{0,16},{16,0},{1,17},{17,1},{2,18},{18,2},{3,19},{19,3},{4,20},{20... | collective-permute-start | bytes 196616 | tf_op jit(solution)/shard_map/ppermute | solution.py:158

commit v8 on v7

--- a/solution.py
+++ b/solution.py
@@ -13,6 +13,7 @@
 SEQ = ("x", "yl", "core")
 MP = ("yh", "z")
 RING = 16
+HALF = RING // 2 + 1
 BF16, F32 = jnp.bfloat16, jnp.float32
 
 
@@ -44,16 +45,18 @@
 
 
 def hidden_kernel(rows_ref, *refs):
-    parts = refs[:RING]
-    mine, other, gact_ref, act_ref, gh_ref, keep_ref, give_ref, tok, w_all, sem, w_sem = refs[RING:]
+    parts, rest = refs[:HALF], refs[HALF]
+    mine, other, gact_ref, act_ref, gh_ref, keep_ref, give_ref, tok, w_all, sem, w_sem = refs[HALF + 1 :]
     c = pl.program_id(0)
     half = keep_ref.shape[0]
 
     @pl.when(c == 0)
     def _():
         copies = [
-            pltpu.make_async_copy(ref, tok.at[pl.ds(4 * i, 4)], sem.at[i]) for i, ref in enumerate(parts)
+            pltpu.make_async_copy(ref.at[0], tok.at[pl.ds(4 * i, 4)], sem.at[i])
+            for i, ref in enumerate(parts)
         ]
+        copies.append(pltpu.make_async_copy(rest, tok.at[pl.ds(4 * HALF, rest.shape[0])], sem.at[HALF]))
         for copy in copies:
             copy.start()
         fetch_columns((mine, other), w_all, w_sem)
@@ -77,7 +80,7 @@
 
 
 def term_kernel(rows_ref, gh_ref, mine, other, *refs):
-    acc, w_all, w_sem = refs[RING:]
+    acc, w_all, w_sem = refs[HALF + 1 :]
     c = pl.program_id(0)
     kept = w_all.shape[0]
 
@@ -96,8 +99,9 @@
 
     @pl.when(c == pl.num_programs(0) - 1)
     def _():
-        for i, ref in enumerate(refs[:RING]):
+        for i, ref in enumerate(refs[:HALF]):
             ref[...] = acc[4 * i : 4 * i + 4].astype(BF16)
+        refs[HALF][...] = acc[4 * HALF :].astype(BF16)
 
 
 def hidden_call(rows, parts, mine, other, grad_act):
@@ -112,12 +116,12 @@
         grid_spec=pltpu.PrefetchScalarGridSpec(
             num_scalar_prefetch=1,
             grid=(cols,),
-            in_specs=[pl.BlockSpec(memory_space=pl.ANY)] * (RING + 2) + [column],
+            in_specs=[pl.BlockSpec(memory_space=pl.ANY)] * (HALF + 3) + [column],
             out_specs=[column, column, half, half],
             scratch_shapes=[
                 pltpu.VMEM((64, n_tok, 128), BF16),
                 pltpu.VMEM((kept, cols, 128, 128), BF16),
-                pltpu.SemaphoreType.DMA((RING,)),
+                pltpu.SemaphoreType.DMA((HALF + 1,)),
                 pltpu.SemaphoreType.DMA((cols, 2)),
             ],
         ),
@@ -137,21 +141,23 @@
             grid=(cols,),
             in_specs=[pl.BlockSpec((n_tok, 128), lambda c, rows: (0, c))]
             + [pl.BlockSpec(memory_space=pl.ANY)] * 2,
-            out_specs=[pl.BlockSpec((4, n_tok, 128), lambda c, rows: (0, 0, 0))] * RING,
+            out_specs=[pl.BlockSpec((n, n_tok, 128), lambda c, rows: (0, 0, 0)) for n in [4] * HALF + [4 * (RING - HALF)]],
             scratch_shapes=[
                 pltpu.VMEM((64, n_tok, 128), F32),
                 pltpu.VMEM((kept, cols, 128, 128), BF16),
                 pltpu.SemaphoreType.DMA((cols, 2)),
             ],
         ),
-        out_shape=[jax.ShapeDtypeStruct((4, n_tok, 128), BF16)] * RING,
+        out_shape=[jax.ShapeDtypeStruct((n, n_tok, 128), BF16) for n in [4] * HALF + [4 * (RING - HALF)]],
         compiler_params=pltpu.CompilerParams(vmem_limit_bytes=20 * 2**20),
         cost_estimate=pl.CostEstimate(flops=536_870_912, bytes_accessed=7_000_000, transcendentals=0),
     )(rows, grad_hidden, mine, other)
 
 
-def shift(a, by):
-    return lax.ppermute(a, "z", [(i, (i + by) % RING) for i in range(RING)])
+def onward(a):
+    up = [(z, (z + 1) % RING) for z in range(RING)]
+    down = [(RING + z, RING + (z - 1) % RING) for z in range(RING)]
+    return lax.ppermute(a, ("core", "z"), up + down)
 
 
 def swap(a, axis):
@@ -162,41 +168,72 @@
     return sum(a.astype(F32) for a in arrays)
 
 
+def pack_kernel(*refs):
+    sources, out_ref, sem = refs[:-2], refs[-2], refs[-1]
+    copies = [
+        pltpu.make_async_copy(ref.at[1], out_ref.at[pl.ds(4 * i, 4)], sem.at[i])
+        for i, ref in enumerate(sources)
+    ]
+    for copy in copies:
+        copy.start()
+    for copy in copies:
+        copy.wait()
+
+
 def gather_tokens(pair):
-    parts = [pair] * RING
-    up, down = pair, pair
-    for step in range(1, RING // 2 + 1):
-        got_up = shift(up, 1)
-        if step < RING // 2:
-            got_down = shift(down, -1)
-            up = held_until(got_up, down)
-            down = held_until(got_down, up)
-            parts[step] = down
-        else:
-            up = got_up
-        parts[-step] = up
-    return parts
-
-
-def step_kernel(got_ref, own_ref, after_ref, out_ref):
-    out_ref[...] = total(got_ref[...], own_ref[...]).astype(BF16)
-
-
-def add_step(got, own, after):
-    block = pl.BlockSpec(memory_space=pltpu.VMEM)
-    return pl.pallas_call(
-        step_kernel,
-        in_specs=[block, block, pl.BlockSpec(memory_space=pl.ANY)],
-        out_specs=block,
-        out_shape=jax.ShapeDtypeStruct(own.shape, BF16),
-        compiler_params=pltpu.CompilerParams(vmem_limit_bytes=2 * 2**20),
-        cost_estimate=pl.CostEstimate(flops=100_000, bytes_accessed=400_000, transcendentals=0),
-    )(got, own, after)
-
-
-def last_kernel(up_ref, down_ref, own_ref, keep_ref, give_ref):
-    summed = total(up_ref[...], down_ref[...], own_ref[...])
-    keep_ref[...] = summed[:2]
+    rounds = [jnp.stack([pair, swap(pair, "core")])]
+    for _ in range(RING // 2):
+        rounds.append(onward(rounds[-1]))
+    passed = rounds[1 : RING // 2]
+    anywhere = pl.BlockSpec(memory_space=pl.ANY)
+    others = pl.pallas_call(
+        pack_kernel,
+        in_specs=[anywhere] * len(passed),
+        out_specs=anywhere,
+        out_shape=jax.ShapeDtypeStruct((4 * len(passed),) + pair.shape[1:], BF16),
+        scratch_shapes=[pltpu.SemaphoreType.DMA((len(passed),))],
+        compiler_params=pltpu.CompilerParams(vmem_limit_bytes=2**20),
+        cost_estimate=pl.CostEstimate(flops=0, bytes_accessed=1_800_000, transcendentals=0),
+    )(*passed)
+    return rounds, swap(others, "core")
+
+
+def first_kernel(came_ref, own_ref, other_ref, out_ref):
+    out_ref[0] = total(came_ref[...], own_ref[...]).astype(BF16)
+    out_ref[1] = other_ref[...]
+
+
+def step_kernel(came_ref, own_ref, other_ref, out_ref):
+    out_ref[0] = total(came_ref[0], own_ref[...]).astype(BF16)
+    out_ref[1] = total(came_ref[1], other_ref[...]).astype(BF16)
+
+
+def add_step(came, own, others, steps):
+    block = pl.BlockSpec(own.shape, lambda i: (0, 0, 0))
+    both = pl.BlockSpec((2,) + own.shape, lambda i: (0, 0, 0, 0))
+    return pl.pallas_call(
+        first_kernel if came.ndim == 3 else step_kernel,
+        grid=(1,),
+        in_specs=[
+            block if came.ndim == 3 else both,
+            block,
+            pl.BlockSpec(own.shape, lambda i: (steps - 1, 0, 0)),
+        ],
+        out_specs=both,
+        out_shape=jax.ShapeDtypeStruct((2,) + own.shape, BF16),
+        compiler_params=pltpu.CompilerParams(vmem_limit_bytes=4 * 2**20),
+        cost_estimate=pl.CostEstimate(flops=200_000, bytes_accessed=800_000, transcendentals=0),
+    )(came, own, others)
+
+
+def arrive_kernel(came_ref, own_ref, keep_ref, give_ref):
+    keep_ref[...] = total(came_ref[0], own_ref[...])
+    give_ref[...] = came_ref[1]
+
+
+def split_kernel(keep_ref, got_ref, mine_ref, give_ref):
+    summed = keep_ref[...] + got_ref[...].astype(F32)
+    mine_ref[...] = summed[:2]
     give_ref[...] = summed[2:].astype(BF16)
 
 
@@ -205,29 +242,25 @@
     out_ref[...] = jnp.concatenate([summed[0], summed[1]], axis=1)
 
 
+def small_call(kernel, args, outs):
+    return pl.pallas_call(
+        kernel,
+        out_shape=outs,
+        compiler_params=pltpu.CompilerParams(vmem_limit_bytes=4 * 2**20),
+        cost_estimate=pl.CostEstimate(flops=200_000, bytes_accessed=600_000, transcendentals=0),
+    )(*args)
+
+
 def reduce_terms(terms):
     n_tok = terms[0].shape[1]
-    half = RING // 2
-    up, down = terms[half], terms[half + 1]
-    for step in range(half - 1):
-        got_up, got_down = shift(up, 1), shift(down, -1)
-        up = add_step(got_up, terms[half - 1 - step], down)
-        down = add_step(got_down, terms[half + 2 + step], up) if step < half - 2 else got_down
-    keep, give = pl.pallas_call(
-        last_kernel,
-        out_shape=[
-            jax.ShapeDtypeStruct((2, n_tok, 128), F32),
-            jax.ShapeDtypeStruct((2, n_tok, 128), BF16),
-        ],
-        compiler_params=pltpu.CompilerParams(vmem_limit_bytes=4 * 2**20),
-        cost_estimate=pl.CostEstimate(flops=200_000, bytes_accessed=600_000, transcendentals=0),
-    )(shift(up, 1), down, terms[0])
-    return pl.pallas_call(
-        finish_kernel,
-        out_shape=jax.ShapeDtypeStruct((n_tok, 256), BF16),
-        compiler_params=pltpu.CompilerParams(vmem_limit_bytes=4 * 2**20),
-        cost_estimate=pl.CostEstimate(flops=100_000, bytes_accessed=300_000, transcendentals=0),
-    )(keep, swap(give, "yh"))
+    shape = lambda n, dtype: jax.ShapeDtypeStruct((n, n_tok, 128), dtype)
+    others = swap(terms[-1], "core")
+    sums = terms[RING // 2]
+    for steps in range(RING // 2 - 1, 0, -1):
+        sums = add_step(onward(sums), terms[steps], others, steps)
+    keep, give = small_call(arrive_kernel, (onward(sums), terms[0]), [shape(4, F32), shape(4, BF16)])
+    keep, give = small_call(split_kernel, (keep, swap(give, "core")), [shape(2, F32), shape(2, BF16)])
+    return small_call(finish_kernel, (keep, swap(give, "yh")), jax.ShapeDtypeStruct((n_tok, 256), BF16))
 
 
 def sum_kernel(grads_ref, out_ref):
@@ -261,9 +294,8 @@
     )(x, *after)
 
 
-def add_kernel(keep_ref, got_ref, both_ref, mark_ref):
+def add_kernel(keep_ref, got_ref, both_ref):
     both_ref[...] = total(keep_ref[...], got_ref[...]).astype(BF16)
-    mark_ref[...] = jnp.zeros_like(mark_ref)
 
 
 def add_halves(keep, got):
@@ -272,11 +304,8 @@
         add_kernel,
         grid=(keep.shape[0] // 2,),
         in_specs=[block, block],
-        out_specs=[block, pl.BlockSpec((8, 128), lambda i: (0, 0))],
-        out_shape=[
-            jax.ShapeDtypeStruct(keep.shape, BF16),
-            jax.ShapeDtypeStruct((8, 128), F32),
-        ],
+        out_specs=block,
+        out_shape=jax.ShapeDtypeStruct(keep.shape, BF16),
         compiler_params=pltpu.CompilerParams(vmem_limit_bytes=8 * 2**20),
         cost_estimate=pl.CostEstimate(flops=1_000_000, bytes_accessed=6_300_000, transcendentals=0),
     )(keep, got)
@@ -293,21 +322,22 @@
     return mine, other, rows.astype(jnp.int32)
 
 
-def places(rows):
-    ahead = (rows % 32 // 2 - lax.axis_index("z")) % RING
-    return ahead * 4 + (rows // 32 + lax.axis_index("yh")) % 2 * 2 + rows % 2
+def places(rows, sign):
+    way = sign * (1 - 2 * lax.axis_index("core"))
+    steps = way * (rows % 32 // 2 - lax.axis_index("z")) % RING
+    slot = jnp.where(steps < HALF, steps, RING + HALF - 1 - steps)
+    return slot * 4 + (rows // 32 + lax.axis_index("yh")) % 2 * 2 + rows % 2
 
 
 def shards(tokens, block_values, block_rows, grad_act):
     n_tok = tokens.shape[0]
     mine = tokens.reshape(n_tok, 2, 128).transpose(1, 0, 2)
     pair = jnp.concatenate([mine, swap(mine, "yh")])
-    parts = gather_tokens(pair)
-    mine, other, rows = gather_weights(block_values, block_rows, pair, parts[5])
-    rows = places(rows)
-    activated, grad_hidden, keep, give = hidden_call(rows, parts, mine, other, grad_act)
-    both, mark = add_halves(keep, swap(give, "core"))
-    terms = term_call(rows, held_until(grad_hidden, mark), mine, other)
+    rounds, rest = gather_tokens(pair)
+    mine, other, rows = gather_weights(block_values, block_rows, pair, rounds[5])
+    activated, grad_hidden, keep, give = hidden_call(places(rows, -1), (*rounds, rest), mine, other, grad_act)
+    terms = term_call(places(rows, 1), grad_hidden, mine, other)
+    both = add_halves(keep, swap(give, "core"))
     grads = sum_grads(lax.all_to_all(both, ("x", "yl"), 0, 0))
     return activated, reduce_terms(terms), grads
 

time: 204 us -> 224 us (1.098)
  waiting for transfers between devices: 41.3 us -> 125 us
  starting transfers between devices: 131 us -> 62.4 us
  Pallas kernels: 19.5 us -> 23.9 us
    ppermute x30 -> x16, waiting for transfers between devices: 29.6 us -> 115 us  [onward(): return lax.ppermute(a, ('core', 'z'), up + down)]
    ppermute x30 -> x16, starting transfers between devices: 109 us -> 31.9 us  [onward(): return lax.ppermute(a, ('core', 'z'), up + down)]
    ppermute x4 -> x8, starting transfers between devices: 9.97 us -> 18.4 us  [swap(): return lax.ppermute(a, axis, [(0, 1), (1, 0)])]
    pallas_call x15 -> x11, Pallas kernels: 1.13 us -> 6.24 us  [the longest x1 5.14 us: gather_tokens(): pl.pallas_call(pack_kernel, in_specs=[anywhere] * len(passed), out_specs=...]
    ppermute x4 -> x8, waiting for transfers between devices: 11.7 us -> 10 us  [swap(): return lax.ppermute(a, axis, [(0, 1), (1, 0)])]
    unnamed x19 -> x43, local copies, waits for them, and re-layouts: 5.74 us -> 6.4 us
  transfers between devices with their start and end apart: 36 -> 26, of which waited for: 21 -> 19; matrix products, arithmetic and copies ran while one was open for 1% -> 1% of each run, Pallas kernels for 3% -> 6%
where the time goes in v8:
time: 224 us; the launch traced here: 223 us
  waiting for transfers between devices  125 us (56%)
  starting transfers between devices  62.4 us (28%)
  Pallas kernels  23.9 us (11%)
  local copies, waits for them, and re-layouts  8.88 us (4%)
    ppermute x16, waiting for transfers between devices, onward(): return lax.ppermute(a, ('core', 'z'), up + down)  115 us
    ppermute x16, starting transfers between devices, onward(): return lax.ppermute(a, ('core', 'z'), up + down)  31.9 us
    ppermute x8, starting transfers between devices, swap(): return lax.ppermute(a, axis, [(0, 1), (1, 0)])  18.4 us
    ppermute x8, waiting for transfers between devices, swap(): return lax.ppermute(a, axis, [(0, 1), (1, 0)])  10 us
    pallas_call x1, Pallas kernels, hidden_call(): pl.pallas_call(hidden_kernel, grid_spec=pltpu.PrefetchScalarGridSpec(num_...  9.69 us
    all_to_all x1, starting transfers between devices, gather_weights(): lax.all_to_all(jnp.broadcast_to(sent, (8,) + sent.shape), ('x', 'yl'), 0, 0)  6.44 us
    unnamed x43, local copies, waits for them, and re-layouts  6.4 us
    all_to_all x1, starting transfers between devices, shards(): grads = sum_grads(lax.all_to_all(both, ('x', 'yl'), 0, 0))  5.7 us
  transfers between devices with their start and end apart: 26, of which 19 were waited for; matrix products, arithmetic and copies ran while one was open for 1% of the time, Pallas kernels for 6%

profile of v8, /device:TPU:24, one launch (start us, length us, event | category | flops | bytes accessed | tf_op | source)
XLA Modules:
  0.0 223.1 jit_solution(12356229326654341645)
XLA Ops:
  1.7 3.1 %collective-permute-start = (bf16[2,128,128]{2,1,0:T(8,128)(2,1)S(1)}, bf16[2,128,128]{2,1,0:T(8,128)(2,1)S(1)}, u32[]{:S(2)}, u32[]{:S(2)}) collective-permute-start(bf16[2,128,128]{2,1,0:T(8,128)(2,1)S(1)} %bitcast.20), channel_id=1, source_target_pairs={{0,16},{16,0},{1,17},{17,1},{2,18},{18,2},{3,19},{19,3},{4,20},{20... | collective-permute-start | bytes 196616 | tf_op jit(solution)/shard_map/ppermute | solution.py:164
  6.5 2.9 %collective-permute-done = bf16[2,128,128]{2,1,0:T(8,128)(2,1)S(1)} collective-permute-done((bf16[2,128,128]{2,1,0:T(8,128)(2,1)S(1)}, bf16[2,128,128]{2,1,0:T(8,128)(2,1)S(1)}, u32[]{:S(2)}, u32[]{:S(2)}) %collective-permute-start) | collective-permute-done | bytes 65568 | tf_op jit(solution)/shard_map/ppermute | solution.py:164
  9.4 1.6 broadcast_in_dim.7
  11.0 6.4 %all-to-all-start = ((bf16[8,1040,128]{2,1,0:T(8,128)(2,1)}), bf16[8,1040,128]{2,1,0:T(8,128)(2,1)S(1)}, u32[]{:S(2)}, u32[]{:S(2)}) async-start(bf16[8,1040,128]{2,1,0:T(8,128)(2,1)} %broadcast_in_dim.7), calls=%async_computation | async-start | bytes 4259840 | tf_op jit(solution)/shard_map/all_to_all | solution.py:318
  17.5 1.9 collective-permute-start.1
  20.7 3.1 %collective-permute-start.2 = (bf16[2,4,128,128]{3,2,1,0:T(8,128)(2,1)S(1)}, bf16[2,4,128,128]{3,2,1,0:T(8,128)(2,1)S(1)}, u32[]{:S(2)}, u32[]{:S(2)}) collective-permute-start(bf16[2,4,128,128]{3,2,1,0:T(8,128)(2,1)S(1)} %pad_maximum_fusion.refs_0_), channel_id=1, source_target_pairs={{0,1},{1,2},{2,3},{3,4},{4,5},{5,6},{6,7},{7,8},{8,9},{9,10},{10,1... | collective-permute-start | bytes 786440 | tf_op jit(solution)/shard_map/ppermute | solution.py:160
  23.9 11.9 %collective-permute-done.2.refs_0_.refs_1_ = bf16[2,4,128,128]{3,2,1,0:T(8,128)(2,1)S(1)} collective-permute-done((bf16[2,4,128,128]{3,2,1,0:T(8,128)(2,1)S(1)}, bf16[2,4,128,128]{3,2,1,0:T(8,128)(2,1)S(1)}, u32[]{:S(2)}, u32[]{:S(2)}) %collective-permute-start.2) | collective-permute-done | bytes 262176 | tf_op jit(solution)/shard_map/ppermute | solution.py:160
  35.8 1.9 collective-permute-start.3
  37.7 7.5 %collective-permute-done.3.refs_1_.refs_2_ = bf16[2,4,128,128]{3,2,1,0:T(8,128)(2,1)S(1)} collective-permute-done((bf16[2,4,128,128]{3,2,1,0:T(8,128)(2,1)S(1)}, bf16[2,4,128,128]{3,2,1,0:T(8,128)(2,1)S(1)}, u32[]{:S(2)}, u32[]{:S(2)}) %collective-permute-start.3) | collective-permute-done | bytes 262176 | tf_op jit(solution)/shard_map/ppermute | solution.py:160
  45.3 1.9 collective-permute-start.4
  47.2 7.5 %collective-permute-done.4.refs_2_.refs_3_ = bf16[2,4,128,128]{3,2,1,0:T(8,128)(2,1)S(1)} collective-permute-done((bf16[2,4,128,128]{3,2,1,0:T(8,128)(2,1)S(1)}, bf16[2,4,128,128]{3,2,1,0:T(8,128)(2,1)S(1)}, u32[]{:S(2)}, u32[]{:S(2)}) %collective-permute-start.4) | collective-permute-done | bytes 262176 | tf_op jit(solution)/shard_map/ppermute | solution.py:160
  54.7 1.9 collective-permute-start.5
  56.6 7.5 %collective-permute-done.5.refs_3_.refs_4_ = bf16[2,4,128,128]{3,2,1,0:T(8,128)(2,1)S(1)} collective-permute-done((bf16[2,4,128,128]{3,2,1,0:T(8,128)(2,1)S(1)}, bf16[2,4,128,128]{3,2,1,0:T(8,128)(2,1)S(1)}, u32[]{:S(2)}, u32[]{:S(2)}) %collective-permute-start.5) | collective-permute-done | bytes 262176 | tf_op jit(solution)/shard_map/ppermute | solution.py:160
  64.2 1.9 collective-permute-start.6
  66.8 6.8 %collective-permute-done.6.refs_1_.refs_4_.refs_5_ = bf16[2,4,128,128]{3,2,1,0:T(8,128)(2,1)S(1)} collective-permute-done((bf16[2,4,128,128]{3,2,1,0:T(8,128)(2,1)S(1)}, bf16[2,4,128,128]{3,2,1,0:T(8,128)(2,1)S(1)}, u32[]{:S(2)}, u32[]{:S(2)}) %collective-permute-start.6) | collective-permute-done | bytes 262176 | tf_op jit(solution)/shard_map/ppermute | solution.py:160
  73.7 2.0 collective-permute-start.7
  75.7 1.9 collective-permute-start.8
  77.6 7.5 %collective-permute-done.8.refs_5_.refs_6_ = bf16[2,4,128,128]{3,2,1,0:T(8,128)(2,1)S(1)} collective-permute-done((bf16[2,4,128,128]{3,2,1,0:T(8,128)(2,1)S(1)}, bf16[2,4,128,128]{3,2,1,0:T(8,128)(2,1)S(1)}, u32[]{:S(2)}, u32[]{:S(2)}) %collective-permute-start.8) | collective-permute-done | bytes 262176 | tf_op jit(solution)/shard_map/ppermute | solution.py:160
  85.2 1.9 collective-permute-start.9
  87.1 7.7 %collective-permute-done.9.refs_6_.refs_7_ = bf16[2,4,128,128]{3,2,1,0:T(8,128)(2,1)} collective-permute-done((bf16[2,4,128,128]{3,2,1,0:T(8,128)(2,1)S(1)}, bf16[2,4,128,128]{3,2,1,0:T(8,128)(2,1)}, u32[]{:S(2)}, u32[]{:S(2)}) %collective-permute-start.9) | collective-permute-done | bytes 262176 | tf_op jit(solution)/shard_map/ppermute | solution.py:160
  94.8 5.1 %shard_map.69 = bf16[28,128,128]{2,1,0:T(8,128)(2,1)} custom-call(bf16[2,4,128,128]{3,2,1,0:T(8,128)(2,1)S(1)} %collective-permute-done.2.refs_0_.refs_1_, bf16[2,4,128,128]{3,2,1,0:T(8,128)(2,1)S(1)} %collective-permute-done.3.refs_1_.refs_2_, bf16[2,4,128,128]{3,2,1,0:T(8,128)(2,1)S(1)} %collective-permute-done.4.refs_2_.refs_3_, ...), custom_call_target="tpu_custom_call" | custom-call | bytes 1800000 | tf_op jit(solution)/shard_map/pallas_call | solution.py:189
  99.9 1.9 collective-permute-start.11
  101.9 1.9 collective-permute-start.10
  104.6 7.0 %collective-permute-done.10.refs_8_ = bf16[2,4,128,128]{3,2,1,0:T(8,128)(2,1)} collective-permute-done((bf16[2,4,128,128]{3,2,1,0:T(8,128)(2,1)}, bf16[2,4,128,128]{3,2,1,0:T(8,128)(2,1)}, u32[]{:S(2)}, u32[]{:S(2)}) %collective-permute-start.10) | collective-permute-done | bytes 262176 | tf_op jit(solution)/shard_map/ppermute | solution.py:160
  114.5 9.7 %shard_map.70 = (bf16[128,1024]{1,0:T(8,128)(2,1)}, bf16[128,1024]{1,0:T(8,128)(2,1)S(1)}, bf16[8,8,128,128]{3,2,1,0:T(8,128)(2,1)S(1)}, bf16[8,8,128,128]{3,2,1,0:T(8,128)(2,1)S(1)}) custom-call(s32[16,8]{1,0:T(8,128)S(1)} %get-tuple-element.60.rows_ref, bf16[2,4,128,128]{3,2,1,0:T(8,128)(2,1)S(1)} %pad_maximum_fusion.refs_0_, ...), custom_call_target="tpu_custom_call" | custom-call | flops 1073741824 | bytes 11000000 | tf_op jit(solution)/shard_map/pallas_call | solution.py:114
  124.2 1.9 collective-permute-start.23
  126.1 4.8 %shard_map.71 = (bf16[4,128,128]{2,1,0:T(8,128)(2,1)S(1)}, bf16[4,128,128]{2,1,0:T(8,128)(2,1)S(1)}, bf16[4,128,128]{2,1,0:T(8,128)(2,1)S(1)}, bf16[4,128,128]{2...) custom-call(s32[16,8]{1,0:T(8,128)S(1)} %get-tuple-element.59.rows_r, ...), custom_call_target="tpu_custom_call" | custom-call | flops 536870912 | bytes 7000000 | tf_op jit(solution)/shard_map/pallas_call | solution.py:137
  131.0 2.4 %collective-permute-start.13 = (bf16[28,128,128]{2,1,0:T(8,128)(2,1)S(1)}, bf16[28,128,128]{2,1,0:T(8,128)(2,1)S(1)}, u32[]{:S(2)}, u32[]{:S(2)}) collective-permute-start(bf16[28,128,128]{2,1,0:T(8,128)(2,1)S(1)} %get-tuple-element.37), channel_id=1, source_target_pairs={{0,32},{32,0},{1,33},{33,1},{2,34},{34,2},{3,35},{35,3},{4,36},{36... | collective-permute-start | bytes 2752520 | tf_op jit(solution)/shard_map/ppermute | solution.py:164
  133.4 1.9 collective-permute-start.12
  135.4 6.1 %collective-permute-done.12.came_ref = bf16[4,128,128]{2,1,0:T(8,128)(2,1)S(1)} collective-permute-done((bf16[4,128,128]{2,1,0:T(8,128)(2,1)S(1)}, bf16[4,128,128]{2,1,0:T(8,128)(2,1)S(1)}, u32[]{:S(2)}, u32[]{:S(2)}) %collective-permute-start.12) | collective-permute-done | bytes 131104 | tf_op jit(solution)/shard_map/ppermute | solution.py:160
  141.6 1.9 collective-permute-start.14
  143.6 2.1 shard_map.82
  145.6 5.7 %all-to-all-start.1 = ((bf16[8,8,128,128]{3,2,1,0:T(8,128)(2,1)}), bf16[8,8,128,128]{3,2,1,0:T(8,128)(2,1)S(1)}, u32[]{:S(2)}, u32[]{:S(2)}) async-start(bf16[8,8,128,128]{3,2,1,0:T(8,128)(2,1)} %shard_map.82), calls=%async_computation.1 | async-start | bytes 4194304 | tf_op jit(solution)/shard_map/all_to_all | solution.py:341
  152.3 1.9 collective-permute-start.15
  154.3 7.5 %collective-permute-done.15.came_ref = bf16[2,4,128,128]{3,2,1,0:T(8,128)(2,1)S(1)} collective-permute-done((bf16[2,4,128,128]{3,2,1,0:T(8,128)(2,1)S(1)}, bf16[2,4,128,128]{3,2,1,0:T(8,128)(2,1)S(1)}, u32[]{:S(2)}, u32[]{:S(2)}) %collective-permute-start.15) | collective-permute-done | bytes 262176 | tf_op jit(solution)/shard_map/ppermute | solution.py:160
  162.8 1.9 collective-permute-start.16
  164.7 7.5 %collective-permute-done.16.came_ref = bf16[2,4,128,128]{3,2,1,0:T(8,128)(2,1)S(1)} collective-permute-done((bf16[2,4,128,128]{3,2,1,0:T(8,128)(2,1)S(1)}, bf16[2,4,128,128]{3,2,1,0:T(8,128)(2,1)S(1)}, u32[]{:S(2)}, u32[]{:S(2)}) %collective-permute-start.16) | collective-permute-done | bytes 262176 | tf_op jit(solution)/shard_map/ppermute | solution.py:160
  172.3 1.9 collective-permute-start.17
  174.3 7.5 %collective-permute-done.17.came_ref = bf16[2,4,128,128]{3,2,1,0:T(8,128)(2,1)S(1)} collective-permute-done((bf16[2,4,128,128]{3,2,1,0:T(8,128)(2,1)S(1)}, bf16[2,4,128,128]{3,2,1,0:T(8,128)(2,1)S(1)}, u32[]{:S(2)}, u32[]{:S(2)}) %collective-permute-start.17) | collective-permute-done | bytes 262176 | tf_op jit(solution)/shard_map/ppermute | solution.py:160
  181.9 1.9 collective-permute-start.18
  183.8 7.5 %collective-permute-done.18.came_ref = bf16[2,4,128,128]{3,2,1,0:T(8,128)(2,1)S(1)} collective-permute-done((bf16[2,4,128,128]{3,2,1,0:T(8,128)(2,1)S(1)}, bf16[2,4,128,128]{3,2,1,0:T(8,128)(2,1)S(1)}, u32[]{:S(2)}, u32[]{:S(2)}) %collective-permute-start.18) | collective-permute-done | bytes 262176 | tf_op jit(solution)/shard_map/ppermute | solution.py:160
  191.4 1.9 collective-permute-start.19
  193.4 7.5 %collective-permute-done.19.came_ref = bf16[2,4,128,128]{3,2,1,0:T(8,128)(2,1)S(1)} collective-permute-done((bf16[2,4,128,128]{3,2,1,0:T(8,128)(2,1)S(1)}, bf16[2,4,128,128]{3,2,1,0:T(8,128)(2,1)S(1)}, u32[]{:S(2)}, u32[]{:S(2)}) %collective-permute-start.19) | collective-permute-done | bytes 262176 | tf_op jit(solution)/shard_map/ppermute | solution.py:160
  201.0 1.9 collective-permute-start.20
  202.9 7.5 %collective-permute-done.20.came_ref = bf16[2,4,128,128]{3,2,1,0:T(8,128)(2,1)S(1)} collective-permute-done((bf16[2,4,128,128]{3,2,1,0:T(8,128)(2,1)S(1)}, bf16[2,4,128,128]{3,2,1,0:T(8,128)(2,1)S(1)}, u32[]{:S(2)}, u32[]{:S(2)}) %collective-permute-start.20) | collective-permute-done | bytes 262176 | tf_op jit(solution)/shard_map/ppermute | solution.py:160
  210.5 1.9 collective-permute-start.21
  213.8 3.2 %collective-permute-start.22 = (bf16[2,128,128]{2,1,0:T(8,128)(2,1)S(1)}, bf16[2,128,128]{2,1,0:T(8,128)(2,1)S(1)}, u32[]{:S(2)}, u32[]{:S(2)}) collective-permute-start(bf16[2,128,128]{2,1,0:T(8,128)(2,1)S(1)} %get-tuple-element.48), channel_id=1, source_target_pairs={{0,16},{16,0},{1,17},{17,1},{2,18},{18,2},{3,19},{19,3},{4,20},{20... | collective-permute-start | bytes 196616 | tf_op jit(solution)/shard_map/ppermute | solution.py:164
  216.9 4.5 %collective-permute-done.22.got_ref = bf16[2,128,128]{2,1,0:T(8,128)(2,1)S(1)} collective-permute-done((bf16[2,128,128]{2,1,0:T(8,128)(2,1)S(1)}, bf16[2,128,128]{2,1,0:T(8,128)(2,1)S(1)}, u32[]{:S(2)}, u32[]{:S(2)}) %collective-permute-start.22) | collective-permute-done | bytes 65568 | tf_op jit(solution)/shard_map/ppermute | solution.py:164
  (73 shorter events, 13.8 us)
Async XLA Ops:
  1.7 7.7 %collective-permute-start = (bf16[2,128,128]{2,1,0:T(8,128)(2,1)S(1)}, bf16[2,128,128]{2,1,0:T(8,128)(2,1)S(1)}, u32[]{:S(2)}, u32[]{:S(2)}) collective-permute-start(bf16[2,128,128]{2,1,0:T(8,128)(2,1)S(1)} %bitcast.20), channel_id=1, source_target_pairs={{0,16},{16,0},{1,17},{17,1},{2,18},{18,2},{3,19},{19,3},{4,20},{20... | collective-permute-start | bytes 196616 | tf_op jit(solution)/shard_map/ppermute | solution.py:164
  11.0 62.6 %all-to-all-start = ((bf16[8,1040,128]{2,1,0:T(8,128)(2,1)}), bf16[8,1040,128]{2,1,0:T(8,128)(2,1)S(1)}, u32[]{:S(2)}, u32[]{:S(2)}) async-start(bf16[8,1040,128]{2,1,0:T(8,128)(2,1)} %broadcast_in_dim.7), calls=%async_computation | async-start | bytes 4259840 | tf_op jit(solution)/shard_map/all_to_all | solution.py:318
  17.5 3.2 %collective-permute-start.1 = (bf16[4,128,128]{2,1,0:T(8,128)(2,1)S(1)}, bf16[4,128,128]{2,1,0:T(8,128)(2,1)S(1)}, u32[]{:S(2)}, u32[]{:S(2)}) collective-permute-start(bf16[4,128,128]{2,1,0:T(8,128)(2,1)S(1)} %get-tuple-element.58.refs_1_), channel_id=1, source_target_pairs={{0,32},{32,0},{1,33},{33,1},{2,34},{34,2},{3,35},{35,3},{4,36},{36... | collective-permute-start | bytes 393224 | tf_op jit(solution)/shard_map/ppermute | solution.py:164
  20.7 15.1 %collective-permute-start.2 = (bf16[2,4,128,128]{3,2,1,0:T(8,128)(2,1)S(1)}, bf16[2,4,128,128]{3,2,1,0:T(8,128)(2,1)S(1)}, u32[]{:S(2)}, u32[]{:S(2)}) collective-permute-start(bf16[2,4,128,128]{3,2,1,0:T(8,128)(2,1)S(1)} %pad_maximum_fusion.refs_0_), channel_id=1, source_target_pairs={{0,1},{1,2},{2,3},{3,4},{4,5},{5,6},{6,7},{7,8},{8,9},{9,10},{10,1... | collective-permute-start | bytes 786440 | tf_op jit(solution)/shard_map/ppermute | solution.py:160
  35.8 9.5 %collective-permute-start.3 = (bf16[2,4,128,128]{3,2,1,0:T(8,128)(2,1)S(1)}, bf16[2,4,128,128]{3,2,1,0:T(8,128)(2,1)S(1)}, u32[]{:S(2)}, u32[]{:S(2)}) collective-permute-start(bf16[2,4,128,128]{3,2,1,0:T(8,128)(2,1)S(1)} %collective-permute-done.2.refs_0_.refs_1_), channel_id=1, source_target_pairs={{0,1},{1,2},{2,3},{3,4},{4,5},{5,6},{6,7},{7,8},{8,9},{9,10},{10,1... | collective-permute-start | bytes 786440 | tf_op jit(solution)/shard_map/ppermute | solution.py:160
  45.3 9.5 %collective-permute-start.4 = (bf16[2,4,128,128]{3,2,1,0:T(8,128)(2,1)S(1)}, bf16[2,4,128,128]{3,2,1,0:T(8,128)(2,1)S(1)}, u32[]{:S(2)}, u32[]{:S(2)}) collective-permute-start(bf16[2,4,128,128]{3,2,1,0:T(8,128)(2,1)S(1)} %collective-permute-done.3.refs_1_.refs_2_), channel_id=1, source_target_pairs={{0,1},{1,2},{2,3},{3,4},{4,5},{5,6},{6,7},{7,8},{8,9},{9,10},{10,1... | collective-permute-start | bytes 786440 | tf_op jit(solution)/shard_map/ppermute | solution.py:160
  54.7 9.5 %collective-permute-start.5 = (bf16[2,4,128,128]{3,2,1,0:T(8,128)(2,1)S(1)}, bf16[2,4,128,128]{3,2,1,0:T(8,128)(2,1)S(1)}, u32[]{:S(2)}, u32[]{:S(2)}) collective-permute-start(bf16[2,4,128,128]{3,2,1,0:T(8,128)(2,1)S(1)} %collective-permute-done.4.refs_2_.refs_3_), channel_id=1, source_target_pairs={{0,1},{1,2},{2,3},{3,4},{4,5},{5,6},{6,7},{7,8},{8,9},{9,10},{10,1... | collective-permute-start | bytes 786440 | tf_op jit(solution)/shard_map/ppermute | solution.py:160
  64.2 9.5 %collective-permute-start.6 = (bf16[2,4,128,128]{3,2,1,0:T(8,128)(2,1)S(1)}, bf16[2,4,128,128]{3,2,1,0:T(8,128)(2,1)S(1)}, u32[]{:S(2)}, u32[]{:S(2)}) collective-permute-start(bf16[2,4,128,128]{3,2,1,0:T(8,128)(2,1)S(1)} %collective-permute-done.5.refs_3_.refs_4_), channel_id=1, source_target_pairs={{0,1},{1,2},{2,3},{3,4},{4,5},{5,6},{6,7},{7,8},{8,9},{9,10},{10,1... | collective-permute-start | bytes 786440 | tf_op jit(solution)/shard_map/ppermute | solution.py:160
  66.1 0.7 copy-start
  73.7 21.1 %copy-start.1 = (bf16[2,4,128,128]{3,2,1,0:T(8,128)(2,1)S(1)}, bf16[2,4,128,128]{3,2,1,0:T(8,128)(2,1)}, u32[]{:S(2)}) copy-start(bf16[2,4,128,128]{3,2,1,0:T(8,128)(2,1)} %copy-done) | copy-start | bytes 786436
  73.7 30.2 %collective-permute-start.7 = (bf16[8,1040,128]{2,1,0:T(8,128)(2,1)S(1)}, bf16[8,1040,128]{2,1,0:T(8,128)(2,1)}, u32[]{:S(2)}, u32[]{:S(2)}) collective-permute-start(bf16[8,1040,128]{2,1,0:T(8,128)(2,1)S(1)} %shard_map.68.refs_10_.mine), channel_id=1, source_target_pairs={{0,32},{32,0},{1,33},{33,1},{2,34},{34,2},{3,35},{35,3},{4,36},{36... | collective-permute-start | bytes 6389768 | tf_op jit(solution)/shard_map/ppermute | solution.py:164
  75.7 9.5 %collective-permute-start.8 = (bf16[2,4,128,128]{3,2,1,0:T(8,128)(2,1)S(1)}, bf16[2,4,128,128]{3,2,1,0:T(8,128)(2,1)S(1)}, u32[]{:S(2)}, u32[]{:S(2)}) collective-permute-start(bf16[2,4,128,128]{3,2,1,0:T(8,128)(2,1)S(1)} %collective-permute-done.6.refs_1_.refs_4_.refs_5_), channel_id=1, source_target_pairs={{0,1},{1,2},{2,3},{3,4},{4,5},{5,6},{6,7},{7,8},{8,9},{9,10},{10,1... | collective-permute-start | bytes 786440 | tf_op jit(solution)/shard_map/ppermute | solution.py:160
  85.2 14.7 %copy-start.3 = (bf16[2,4,128,128]{3,2,1,0:T(8,128)(2,1)}, bf16[2,4,128,128]{3,2,1,0:T(8,128)(2,1)S(1)}, u32[]{:S(2)}) copy-start(bf16[2,4,128,128]{3,2,1,0:T(8,128)(2,1)S(1)} %collective-permute-done.8.refs_5_.refs_6_) | copy-start | bytes 786436
  85.2 9.6 %collective-permute-start.9 = (bf16[2,4,128,128]{3,2,1,0:T(8,128)(2,1)S(1)}, bf16[2,4,128,128]{3,2,1,0:T(8,128)(2,1)}, u32[]{:S(2)}, u32[]{:S(2)}) collective-permute-start(bf16[2,4,128,128]{3,2,1,0:T(8,128)(2,1)S(1)} %collective-permute-done.8.refs_5_.refs_6_), channel_id=1, source_target_pairs={{0,1},{1,2},{2,3},{3,4},{4,5},{5,6},{6,7},{7,8},{8,9},{9,10},{10,1... | collective-permute-start | bytes 786440 | tf_op jit(solution)/shard_map/ppermute | solution.py:160
  99.9 11.7 %collective-permute-start.11 = (bf16[28,128,128]{2,1,0:T(8,128)(2,1)}, bf16[28,128,128]{2,1,0:T(8,128)(2,1)}, u32[]{:S(2)}, u32[]{:S(2)}) collective-permute-start(bf16[28,128,128]{2,1,0:T(8,128)(2,1)} %shard_map.69), channel_id=1, source_target_pairs={{0,32},{32,0},{1,33},{33,1},{2,34},{34,2},{3,35},{35,3},{4,36},{36... | collective-permute-start | bytes 2752520 | tf_op jit(solution)/shard_map/ppermute | solution.py:164
  101.9 9.8 %collective-permute-start.10 = (bf16[2,4,128,128]{3,2,1,0:T(8,128)(2,1)}, bf16[2,4,128,128]{3,2,1,0:T(8,128)(2,1)}, u32[]{:S(2)}, u32[]{:S(2)}) collective-permute-start(bf16[2,4,128,128]{3,2,1,0:T(8,128)(2,1)} %collective-permute-done.9.refs_6_.refs_7_), channel_id=1, source_target_pairs={{0,1},{1,2},{2,3},{3,4},{4,5},{5,6},{6,7},{7,8},{8,9},{9,10},{10,1... | collective-permute-start | bytes 786440 | tf_op jit(solution)/shard_map/ppermute | solution.py:160
  111.7 1.0 copy-start.2
  112.6 0.9 copy-start.4
  113.6 0.9 copy-start.5
  124.2 19.3 %collective-permute-start.23 = (bf16[8,8,128,128]{3,2,1,0:T(8,128)(2,1)S(1)}, bf16[8,8,128,128]{3,2,1,0:T(8,128)(2,1)S(1)}, u32[]{:S(2)}, u32[]{:S(2)}) collective-permute-start(bf16[8,8,128,128]{3,2,1,0:T(8,128)(2,1)S(1)} %get-tuple-element.50), channel_id=1, source_target_pairs={{0,32},{32,0},{1,33},{33,1},{2,34},{34,2},{3,35},{35,3},{4,36},{36... | collective-permute-start | bytes 6291464 | tf_op jit(solution)/shard_map/ppermute | solution.py:164
  131.0 12.5 %copy-start.6 = (bf16[4,128,128]{2,1,0:T(8,128)(2,1)}, bf16[4,128,128]{2,1,0:T(8,128)(2,1)S(1)}, u32[]{:S(2)}) copy-start(bf16[4,128,128]{2,1,0:T(8,128)(2,1)S(1)} %get-tuple-element.44.own_ref) | copy-start | bytes 393220
  131.0 12.5 %copy-start.8 = (bf16[4,128,128]{2,1,0:T(8,128)(2,1)}, bf16[4,128,128]{2,1,0:T(8,128)(2,1)S(1)}, u32[]{:S(2)}) copy-start(bf16[4,128,128]{2,1,0:T(8,128)(2,1)S(1)} %get-tuple-element.43.own_ref) | copy-start | bytes 393220
  131.0 12.5 %copy-start.10 = (bf16[4,128,128]{2,1,0:T(8,128)(2,1)}, bf16[4,128,128]{2,1,0:T(8,128)(2,1)S(1)}, u32[]{:S(2)}) copy-start(bf16[4,128,128]{2,1,0:T(8,128)(2,1)S(1)} %get-tuple-element.42.own_ref) | copy-start | bytes 393220
  131.0 12.5 %copy-start.12 = (bf16[4,128,128]{2,1,0:T(8,128)(2,1)}, bf16[4,128,128]{2,1,0:T(8,128)(2,1)S(1)}, u32[]{:S(2)}) copy-start(bf16[4,128,128]{2,1,0:T(8,128)(2,1)S(1)} %get-tuple-element.41.own_ref) | copy-start | bytes 393220
  131.0 12.5 %copy-start.14 = (bf16[4,128,128]{2,1,0:T(8,128)(2,1)}, bf16[4,128,128]{2,1,0:T(8,128)(2,1)S(1)}, u32[]{:S(2)}) copy-start(bf16[4,128,128]{2,1,0:T(8,128)(2,1)S(1)} %get-tuple-element.40.own_ref) | copy-start | bytes 393220
  131.0 12.5 %copy-start.16 = (bf16[4,128,128]{2,1,0:T(8,128)(2,1)}, bf16[4,128,128]{2,1,0:T(8,128)(2,1)S(1)}, u32[]{:S(2)}) copy-start(bf16[4,128,128]{2,1,0:T(8,128)(2,1)S(1)} %get-tuple-element.39.own_ref) | copy-start | bytes 393220
  131.0 12.5 %copy-start.18 = (bf16[4,128,128]{2,1,0:T(8,128)(2,1)}, bf16[4,128,128]{2,1,0:T(8,128)(2,1)S(1)}, u32[]{:S(2)}) copy-start(bf16[4,128,128]{2,1,0:T(8,128)(2,1)S(1)} %get-tuple-element.38.own_ref) | copy-start | bytes 393220
  131.0 10.5 %collective-permute-start.13 = (bf16[28,128,128]{2,1,0:T(8,128)(2,1)S(1)}, bf16[28,128,128]{2,1,0:T(8,128)(2,1)S(1)}, u32[]{:S(2)}, u32[]{:S(2)}) collective-permute-start(bf16[28,128,128]{2,1,0:T(8,128)(2,1)S(1)} %get-tuple-element.37), channel_id=1, source_target_pairs={{0,32},{32,0},{1,33},{33,1},{2,34},{34,2},{3,35},{35,3},{4,36},{36... | collective-permute-start | bytes 2752520 | tf_op jit(solution)/shard_map/ppermute | solution.py:164
  133.4 8.1 %collective-permute-start.12 = (bf16[4,128,128]{2,1,0:T(8,128)(2,1)S(1)}, bf16[4,128,128]{2,1,0:T(8,128)(2,1)S(1)}, u32[]{:S(2)}, u32[]{:S(2)}) collective-permute-start(bf16[4,128,128]{2,1,0:T(8,128)(2,1)S(1)} %get-tuple-element.35), channel_id=1, source_target_pairs={{0,1},{1,2},{2,3},{3,4},{4,5},{5,6},{6,7},{7,8},{8,9},{9,10},{10,1... | collective-permute-start | bytes 393224 | tf_op jit(solution)/shard_map/ppermute | solution.py:160
  141.6 9.8 %collective-permute-start.14 = (bf16[2,4,128,128]{3,2,1,0:T(8,128)(2,1)S(1)}, bf16[2,4,128,128]{3,2,1,0:T(8,128)(2,1)S(1)}, u32[]{:S(2)}, u32[]{:S(2)}) collective-permute-start(bf16[2,4,128,128]{3,2,1,0:T(8,128)(2,1)S(1)} %shard_map.72), channel_id=1, source_target_pairs={{0,1},{1,2},{2,3},{3,4},{4,5},{5,6},{6,7},{7,8},{8,9},{9,10},{10,1... | collective-permute-start | bytes 786440 | tf_op jit(solution)/shard_map/ppermute | solution.py:160
  145.6 76.5 %all-to-all-start.1 = ((bf16[8,8,128,128]{3,2,1,0:T(8,128)(2,1)}), bf16[8,8,128,128]{3,2,1,0:T(8,128)(2,1)S(1)}, u32[]{:S(2)}, u32[]{:S(2)}) async-start(bf16[8,8,128,128]{3,2,1,0:T(8,128)(2,1)} %shard_map.82), calls=%async_computation.1 | async-start | bytes 4194304 | tf_op jit(solution)/shard_map/all_to_all | solution.py:341
  151.3 20.9 %copy-start.15 = (bf16[4,128,128]{2,1,0:T(8,128)(2,1)S(1)}, bf16[4,128,128]{2,1,0:T(8,128)(2,1)}, u32[]{:S(2)}) copy-start(bf16[4,128,128]{2,1,0:T(8,128)(2,1)} %copy-done.14) | copy-start | bytes 393220
  151.3 0.9 copy-start.19
  152.3 29.5 %copy-start.13 = (bf16[4,128,128]{2,1,0:T(8,128)(2,1)S(1)}, bf16[4,128,128]{2,1,0:T(8,128)(2,1)}, u32[]{:S(2)}) copy-start(bf16[4,128,128]{2,1,0:T(8,128)(2,1)} %copy-done.12) | copy-start | bytes 393220
  152.3 9.5 %collective-permute-start.15 = (bf16[2,4,128,128]{3,2,1,0:T(8,128)(2,1)S(1)}, bf16[2,4,128,128]{3,2,1,0:T(8,128)(2,1)S(1)}, u32[]{:S(2)}, u32[]{:S(2)}) collective-permute-start(bf16[2,4,128,128]{3,2,1,0:T(8,128)(2,1)S(1)} %shard_map.73), channel_id=1, source_target_pairs={{0,1},{1,2},{2,3},{3,4},{4,5},{5,6},{6,7},{7,8},{8,9},{9,10},{10,1... | collective-permute-start | bytes 786440 | tf_op jit(solution)/shard_map/ppermute | solution.py:160
  161.8 0.9 copy-start.17
  162.7 28.6 %copy-start.11 = (bf16[4,128,128]{2,1,0:T(8,128)(2,1)S(1)}, bf16[4,128,128]{2,1,0:T(8,128)(2,1)}, u32[]{:S(2)}) copy-start(bf16[4,128,128]{2,1,0:T(8,128)(2,1)} %copy-done.10) | copy-start | bytes 393220
  162.8 9.5 %collective-permute-start.16 = (bf16[2,4,128,128]{3,2,1,0:T(8,128)(2,1)S(1)}, bf16[2,4,128,128]{3,2,1,0:T(8,128)(2,1)S(1)}, u32[]{:S(2)}, u32[]{:S(2)}) collective-permute-start(bf16[2,4,128,128]{3,2,1,0:T(8,128)(2,1)S(1)} %shard_map.74), channel_id=1, source_target_pairs={{0,1},{1,2},{2,3},{3,4},{4,5},{5,6},{6,7},{7,8},{8,9},{9,10},{10,1... | collective-permute-start | bytes 786440 | tf_op jit(solution)/shard_map/ppermute | solution.py:160
  172.3 28.6 %copy-start.9 = (bf16[4,128,128]{2,1,0:T(8,128)(2,1)S(1)}, bf16[4,128,128]{2,1,0:T(8,128)(2,1)}, u32[]{:S(2)}) copy-start(bf16[4,128,128]{2,1,0:T(8,128)(2,1)} %copy-done.8) | copy-start | bytes 393220
  172.3 9.5 %collective-permute-start.17 = (bf16[2,4,128,128]{3,2,1,0:T(8,128)(2,1)S(1)}, bf16[2,4,128,128]{3,2,1,0:T(8,128)(2,1)S(1)}, u32[]{:S(2)}, u32[]{:S(2)}) collective-permute-start(bf16[2,4,128,128]{3,2,1,0:T(8,128)(2,1)S(1)} %shard_map.75), channel_id=1, source_target_pairs={{0,1},{1,2},{2,3},{3,4},{4,5},{5,6},{6,7},{7,8},{8,9},{9,10},{10,1... | collective-permute-start | bytes 786440 | tf_op jit(solution)/shard_map/ppermute | solution.py:160
  181.8 28.6 %copy-start.7 = (bf16[4,128,128]{2,1,0:T(8,128)(2,1)S(1)}, bf16[4,128,128]{2,1,0:T(8,128)(2,1)}, u32[]{:S(2)}) copy-start(bf16[4,128,128]{2,1,0:T(8,128)(2,1)} %copy-done.6) | copy-start | bytes 393220
  181.9 9.5 %collective-permute-start.18 = (bf16[2,4,128,128]{3,2,1,0:T(8,128)(2,1)S(1)}, bf16[2,4,128,128]{3,2,1,0:T(8,128)(2,1)S(1)}, u32[]{:S(2)}, u32[]{:S(2)}) collective-permute-start(bf16[2,4,128,128]{3,2,1,0:T(8,128)(2,1)S(1)} %shard_map.76), channel_id=1, source_target_pairs={{0,1},{1,2},{2,3},{3,4},{4,5},{5,6},{6,7},{7,8},{8,9},{9,10},{10,1... | collective-permute-start | bytes 786440 | tf_op jit(solution)/shard_map/ppermute | solution.py:160
  191.4 9.5 %collective-permute-start.19 = (bf16[2,4,128,128]{3,2,1,0:T(8,128)(2,1)S(1)}, bf16[2,4,128,128]{3,2,1,0:T(8,128)(2,1)S(1)}, u32[]{:S(2)}, u32[]{:S(2)}) collective-permute-start(bf16[2,4,128,128]{3,2,1,0:T(8,128)(2,1)S(1)} %shard_map.77), channel_id=1, source_target_pairs={{0,1},{1,2},{2,3},{3,4},{4,5},{5,6},{6,7},{7,8},{8,9},{9,10},{10,1... | collective-permute-start | bytes 786440 | tf_op jit(solution)/shard_map/ppermute | solution.py:160
  201.0 9.5 %collective-permute-start.20 = (bf16[2,4,128,128]{3,2,1,0:T(8,128)(2,1)S(1)}, bf16[2,4,128,128]{3,2,1,0:T(8,128)(2,1)S(1)}, u32[]{:S(2)}, u32[]{:S(2)}) collective-permute-start(bf16[2,4,128,128]{3,2,1,0:T(8,128)(2,1)S(1)} %shard_map.78), channel_id=1, source_target_pairs={{0,1},{1,2},{2,3},{3,4},{4,5},{5,6},{6,7},{7,8},{8,9},{9,10},{10,1... | collective-permute-start | bytes 786440 | tf_op jit(solution)/shard_map/ppermute | solution.py:160
  210.5 3.2 %collective-permute-start.21 = (bf16[4,128,128]{2,1,0:T(8,128)(2,1)S(1)}, bf16[4,128,128]{2,1,0:T(8,128)(2,1)S(1)}, u32[]{:S(2)}, u32[]{:S(2)}) collective-permute-start(bf16[4,128,128]{2,1,0:T(8,128)(2,1)S(1)} %get-tuple-element.46), channel_id=1, source_target_pairs={{0,32},{32,0},{1,33},{33,1},{2,34},{34,2},{3,35},{35,3},{4,36},{36... | collective-permute-start | bytes 393224 | tf_op jit(solution)/shard_map/ppermute | solution.py:164
  213.8 7.7 %collective-permute-start.22 = (bf16[2,128,128]{2,1,0:T(8,128)(2,1)S(1)}, bf16[2,128,128]{2,1,0:T(8,128)(2,1)S(1)}, u32[]{:S(2)}, u32[]{:S(2)}) collective-permute-start(bf16[2,128,128]{2,1,0:T(8,128)(2,1)S(1)} %get-tuple-element.48), channel_id=1, source_target_pairs={{0,16},{16,0},{1,17},{17,1},{2,18},{18,2},{3,19},{19,3},{4,20},{20... | collective-permute-start | bytes 196616 | tf_op jit(solution)/shard_map/ppermute | solution.py:164

commit v9 on v3

--- a/solution.py
+++ b/solution.py
@@ -40,10 +40,10 @@
 
 
 def hidden_kernel(
-    rows_ref, core_ref, own, left, right, far_left, far_right, w_ref, gact_ref, act_ref, gh_ref, keep_ref, give_ref, tok, w_all, sem, w_sem
+    rows_ref, own, left, right, far_left, far_right, w_ref, gact_ref, act_ref, gh_ref, gv_ref, tok, w_all, sem, w_sem
 ):
     c = pl.program_id(0)
-    half = keep_ref.shape[0]
+    kept = gv_ref.shape[0]
 
     @pl.when(c == 0)
     def _():
@@ -58,10 +58,8 @@
             copy.wait()
 
     await_column(w_ref, w_all, w_sem, c)
-    core = core_ref[0]
-    slots = [2 * j + core for j in range(half)] + [2 * j + 1 - core for j in range(half)]
-    weights = jnp.concatenate([w_all[k, c] for k in slots], axis=0)
-    picked = jnp.concatenate([tok[rows_ref[k, c]] for k in slots], axis=1)
+    weights = jnp.concatenate([w_all[k, c] for k in range(kept)], axis=0)
+    picked = jnp.concatenate([tok[rows_ref[k, c]] for k in range(kept)], axis=1)
     hidden = jnp.dot(picked, weights, preferred_element_type=F32)
     value, slope = gelu_parts(hidden)
     act_ref[...] = value.astype(BF16)
@@ -70,9 +68,8 @@
     grads = lax.dot_general(
         grad_hidden, picked, (((0,), (0,)), ((), ())), preferred_element_type=F32
     ).astype(BF16)
-    for j in range(half):
-        keep_ref[j, 0] = grads[:, j * 128 : (j + 1) * 128]
-        give_ref[j, 0] = grads[:, (half + j) * 128 : (half + j + 1) * 128]
+    for k in range(kept):
+        gv_ref[k, 0] = grads[:, k * 128 : (k + 1) * 128]
 
 
 def term_kernel(rows_ref, gh_ref, w_ref, own, left, right, far_left, far_right, acc, w_all, w_sem):
@@ -98,21 +95,21 @@
             ref[...] = acc[start : start + size].astype(BF16)
 
 
-def hidden_call(rows, core, parts, weights, grad_act):
+def hidden_call(rows, parts, weights, grad_act):
     kept, cols = rows.shape
     n_tok = grad_act.shape[0]
     column = pl.BlockSpec((n_tok, 128), lambda c, *_: (0, c))
-    half = pl.BlockSpec((kept // 2, 1, 128, 128), lambda c, *_: (0, c, 0, 0))
+    all_slots = pl.BlockSpec((kept, 1, 128, 128), lambda c, *_: (0, c, 0, 0))
     wide = jax.ShapeDtypeStruct((n_tok, cols * 128), BF16)
-    grads = jax.ShapeDtypeStruct((kept // 2, cols, 128, 128), BF16)
+    grads = jax.ShapeDtypeStruct((kept, cols, 128, 128), BF16)
     return pl.pallas_call(
         hidden_kernel,
         grid_spec=pltpu.PrefetchScalarGridSpec(
-            num_scalar_prefetch=2,
+            num_scalar_prefetch=1,
             grid=(cols,),
             in_specs=[pl.BlockSpec(memory_space=pl.ANY)] * 5
             + [pl.BlockSpec(memory_space=pltpu.HBM), column],
-            out_specs=[column, column, half, half],
+            out_specs=[column, column, all_slots],
             scratch_shapes=[
                 pltpu.VMEM((64, n_tok, 128), BF16),
                 pltpu.VMEM((kept, cols, 128, 128), BF16),
@@ -120,10 +117,10 @@
                 pltpu.SemaphoreType.DMA((cols,)),
             ],
         ),
-        out_shape=[wide, wide, grads, grads],
+        out_shape=[wide, wide, grads],
         compiler_params=pltpu.CompilerParams(vmem_limit_bytes=18 * 2**20),
         cost_estimate=pl.CostEstimate(flops=1_073_741_824, bytes_accessed=11_000_000, transcendentals=131072),
-    )(rows, core, *parts, weights, grad_act)
+    )(rows, *parts, weights, grad_act)
 
 
 def term_call(rows, grad_hidden, weights):
@@ -166,47 +163,52 @@
     return own, left, right, shift(left[:8], 1), shift(right[8:], -1)
 
 
-def combine_kernel(own_ref, left_ref, right_ref, grads_ref, own_out, grads_out):
-    own_out[...] = total(own_ref[...], left_ref[...], right_ref[...]).astype(BF16)
-    for c in range(grads_ref.shape[1]):
-        summed = sum(grads_ref[i, c].astype(F32) for i in range(grads_ref.shape[0]))
-        grads_out[c] = summed.T.astype(BF16)
-
-
-def add_kernel(keep_ref, got_ref, after_ref, both_ref):
-    both_ref[...] = total(keep_ref[...], got_ref[...]).astype(BF16)
-
-
-def add_after(keep, got, after):
-    block = pl.BlockSpec((2,) + keep.shape[1:], lambda i: (i, 0, 0, 0))
-    return pl.pallas_call(
-        add_kernel,
-        grid=(keep.shape[0] // 2,),
-        in_specs=[block, block, pl.BlockSpec(memory_space=pl.ANY)],
-        out_specs=block,
-        out_shape=jax.ShapeDtypeStruct(keep.shape, BF16),
-        compiler_params=pltpu.CompilerParams(vmem_limit_bytes=8 * 2**20),
-        cost_estimate=pl.CostEstimate(flops=1_000_000, bytes_accessed=6_300_000, transcendentals=0),
-    )(keep, got, after)
-
-
-def reduce_all(keep, give, own, left, right, far_left, far_right):
-    from_right, from_left = shift(far_left, -1), shift(far_right, 1)
-    both = add_after(keep, lax.ppermute(give, "core", [(0, 1), (1, 0)]), own)
-    grads = lax.all_to_all(both, ("x", "yl"), 0, 0)
-    left = jnp.concatenate([total(left[:8], from_right).astype(BF16), left[8:]])
-    right = jnp.concatenate([right[:8], total(right[8:], from_left).astype(BF16)])
-    own, grads = pl.pallas_call(
-        combine_kernel,
-        out_shape=[
-            jax.ShapeDtypeStruct(own.shape, BF16),
-            jax.ShapeDtypeStruct(grads.shape[1:], BF16),
-        ],
-        compiler_params=pltpu.CompilerParams(vmem_limit_bytes=12 * 2**20),
-        cost_estimate=pl.CostEstimate(flops=2_000_000, bytes_accessed=4_500_000, transcendentals=0),
-    )(own, shift(left, -1), shift(right, 1), grads)
-    own = lax.all_to_all(own.reshape((8, 2) + own.shape[1:]), FAR, 0, 0)
-    return total(*own).astype(BF16), grads[:, None]
+def near_kernel(left_ref, right_ref, from_right, from_left, left_out, right_out):
+    left_out[...] = total(left_ref[...], from_right[...]).astype(BF16)
+    right_out[...] = total(right_ref[...], from_left[...]).astype(BF16)
+
+
+def add_near(left, right, from_right, from_left):
+    n, n_tok, _ = left.shape
+    first = pl.BlockSpec((n // 2, n_tok, 128), lambda i: (0, 0, 0))
+    second = pl.BlockSpec((n // 2, n_tok, 128), lambda i: (1, 0, 0))
+    return pl.pallas_call(
+        near_kernel,
+        grid=(1,),
+        in_specs=[first, second, first, first],
+        out_specs=[first, second],
+        out_shape=[jax.ShapeDtypeStruct(left.shape, BF16)] * 2,
+        input_output_aliases={0: 0, 1: 1},
+        compiler_params=pltpu.CompilerParams(vmem_limit_bytes=6 * 2**20),
+        cost_estimate=pl.CostEstimate(flops=500_000, bytes_accessed=1_500_000, transcendentals=0),
+    )(left, right, from_right, from_left)
+
+
+def own_kernel(own_ref, left_ref, right_ref, out_ref):
+    out_ref[...] = total(own_ref[...], left_ref[...], right_ref[...]).astype(BF16)
+
+
+def finish_kernel(far_ref, out_ref):
+    summed = sum(far_ref[i].astype(F32) for i in range(far_ref.shape[0])).astype(BF16)
+    out_ref[...] = jnp.concatenate([summed[0], summed[1]], axis=1)
+
+
+def small_call(kernel, args, out):
+    return pl.pallas_call(
+        kernel,
+        out_shape=out,
+        compiler_params=pltpu.CompilerParams(vmem_limit_bytes=6 * 2**20),
+        cost_estimate=pl.CostEstimate(flops=500_000, bytes_accessed=2_000_000, transcendentals=0),
+    )(*args)
+
+
+def reduce_terms(own, left, right, far_left, far_right):
+    n_tok = own.shape[1]
+    left, right = add_near(left, right, shift(far_left, -1), shift(far_right, 1))
+    out = jax.ShapeDtypeStruct(own.shape, BF16)
+    own = small_call(own_kernel, (own, shift(left, -1), shift(right, 1)), out)
+    far = lax.all_to_all(own.reshape((8, 2, n_tok, 128)), FAR, 0, 0)
+    return small_call(finish_kernel, (far,), jax.ShapeDtypeStruct((n_tok, 256), BF16))
 
 
 def shards(tokens, block_values, block_rows, grad_act):
@@ -218,11 +220,10 @@
     weights = lax.all_gather(sent, SEQ, axis=0)
     rows = weights[:, cols * 128, :cols].astype(jnp.int32)
     rows = (rows // 2 - lax.axis_index("zl")) % 4 * 16 + rows // 32 * 8 + rows % 32 // 8 * 2 + rows % 2
-    core = lax.axis_index("core").reshape(1)
-    activated, grad_hidden, keep, give = hidden_call(rows, core, parts, weights, grad_act)
-    terms = term_call(rows, grad_hidden, weights)
-    summed, grads = reduce_all(keep, give, *terms)
-    return activated, summed.transpose(1, 0, 2).reshape(n_tok, 256), grads
+    activated, grad_hidden, grads = hidden_call(rows, parts, weights, grad_act)
+    grads = lax.psum_scatter(grads, SEQ, scatter_dimension=0)
+    summed = reduce_terms(*term_call(rows, grad_hidden, weights))
+    return activated, summed, grads.transpose(0, 2, 1)[:, None]
 
 
 def solution(mesh):

time: 190 us -> 178 us (0.937)
  the two profiles are of different devices: /device:TPU:1 before, /device:TPU:24 now
where the time goes in v9:
time: 178 us; the launch traced here: 175 us
  blocking collectives  74.4 us (42%)
  waiting for transfers between devices  31.9 us (18%)
  starting transfers between devices  28.4 us (16%)
  between operations  14.2 us (8%)
  Pallas kernels  12.7 us (7%)
  local copies, waits for them, and re-layouts  10.1 us (6%)
  other arithmetic  3.15 us (2%)
    all_to_all x1, blocking collectives, gather_tokens(): own = lax.all_to_all(jnp.broadcast_to(mine, (8,) + mine.shape), FAR, 0, 0)  44.1 us
    all_to_all x1, blocking collectives, reduce_terms(): far = lax.all_to_all(own.reshape((8, 2, n_tok, 128)), FAR, 0, 0)  30.3 us
    ppermute x8, waiting for transfers between devices, shift(): return lax.ppermute(a, Z, [(i, (i + by) % 16) for i in range(16)])  29.2 us
    ppermute x8, starting transfers between devices, shift(): return lax.ppermute(a, Z, [(i, (i + by) % 16) for i in range(16)])  28.3 us
    unnamed x9, local copies, waits for them, and re-layouts  9.14 us
    pallas_call x1, Pallas kernels, hidden_call(): pl.pallas_call(hidden_kernel, grid_spec=pltpu.PrefetchScalarGridSpec(num_...  7.18 us
    pallas_call x1, Pallas kernels, term_call(): pl.pallas_call(term_kernel, grid_spec=pltpu.PrefetchScalarGridSpec(num_sc...  4.28 us
  transfers between devices with their start and end apart: 10, of which 8 were waited for; matrix products, arithmetic and copies ran while one was open for 1% of the time, Pallas kernels for 3%

profile of v9, /device:TPU:24, one launch (start us, length us, event | category | flops | bytes accessed | tf_op | source)
XLA Modules:
  0.0 174.8 jit_solution(6172995399109800295)
XLA Ops:
  7.2 0.0 all-gather.3.cloned.1.call-start
  7.2 0.7 convert_bitcast_fusion
  7.9 1.7 fusion.1
  9.6 0.0 all-gather.3.cloned.1.call-update
  9.6 0.0 reduce-scatter.2.cloned.1.call-start
  9.6 0.9 reshape.57
  10.5 0.1 broadcast_in_dim.7
  10.6 44.1 %all_to_all.10 = bf16[8,2,128,128]{3,2,1,0:T(8,128)(2,1)S(1)} all-to-all(bf16[8,2,128,128]{3,2,1,0:T(8,128)(2,1)S(1)} %broadcast_in_dim.7), channel_id=1, replica_groups=mesh['x'=4,'yl'=2,'core'=2,'yh'=2,'zh'=4,'zl'=4] {'yh','zh'}, dimensions={0} | all-to-all | bytes 1048576 | tf_op jit(solution)/shard_map/all_to_all | solution.py:160
  54.7 6.8 %collective-permute-start.1 = (bf16[16,128,128]{2,1,0:T(8,128)(2,1)S(1)}, bf16[16,128,128]{2,1,0:T(8,128)(2,1)S(1)}, u32[]{:S(2)}, u32[]{:S(2)}) collective-permute-start(bf16[16,128,128]{2,1,0:T(8,128)(2,1)S(1)} %bitcast.16), channel_id=1, source_target_pairs={{0,15},{1,0},{2,1},{3,2},{4,3},{5,4},{6,5},{7,6},{8,7},{9,8},{10,9... | collective-permute-start | bytes 1572872 | tf_op jit(solution)/shard_map/ppermute | solution.py:152
  61.5 3.4 %collective-permute-start = (bf16[16,128,128]{2,1,0:T(8,128)(2,1)S(1)}, bf16[16,128,128]{2,1,0:T(8,128)(2,1)S(1)}, u32[]{:S(2)}, u32[]{:S(2)}) collective-permute-start(bf16[16,128,128]{2,1,0:T(8,128)(2,1)S(1)} %bitcast.17), channel_id=1, source_target_pairs={{0,1},{1,2},{2,3},{3,4},{4,5},{5,6},{6,7},{7,8},{8,9},{9,10},{10,1... | collective-permute-start | bytes 1572872 | tf_op jit(solution)/shard_map/ppermute | solution.py:152
  64.9 8.0 %collective-permute-done.1.right = bf16[16,128,128]{2,1,0:T(8,128)(2,1)S(1)} collective-permute-done((bf16[16,128,128]{2,1,0:T(8,128)(2,1)S(1)}, bf16[16,128,128]{2,1,0:T(8,128)(2,1)S(1)}, u32[]{:S(2)}, u32[]{:S(2)}) %collective-permute-start.1) | collective-permute-done | bytes 524320 | tf_op jit(solution)/shard_map/ppermute | solution.py:152
  72.9 4.5 %collective-permute-start.3 = (bf16[8,128,128]{2,1,0:T(8,128)(2,1)S(1)}, bf16[8,128,128]{2,1,0:T(8,128)(2,1)S(1)}, u32[]{:S(2)}, u32[]{:S(2)}) collective-permute-start(bf16[8,128,128]{2,1,0:T(8,128)(2,1)S(1)} %slice.30), channel_id=1, source_target_pairs={{0,15},{1,0},{2,1},{3,2},{4,3},{5,4},{6,5},{7,6},{8,7},{9,8},{10,9... | collective-permute-start | bytes 786440 | tf_op jit(solution)/shard_map/ppermute | solution.py:152
  77.4 0.0 collective-permute-done.left
  77.4 1.9 %collective-permute-start.2 = (bf16[8,128,128]{2,1,0:T(8,128)(2,1)S(1)}, bf16[8,128,128]{2,1,0:T(8,128)(2,1)S(1)}, u32[]{:S(2)}, u32[]{:S(2)}) collective-permute-start(bf16[8,128,128]{2,1,0:T(8,128)(2,1)S(1)} %slice.29), channel_id=1, source_target_pairs={{0,1},{1,2},{2,3},{3,4},{4,5},{5,6},{6,7},{7,8},{8,9},{9,10},{10,1... | collective-permute-start | bytes 786440 | tf_op jit(solution)/shard_map/ppermute | solution.py:152
  79.3 0.0 all-gather.3.cloned.1.call-done
  79.3 0.8 slice_convert_fusion
  80.1 1.1 collective-permute-done.3.far_right
  81.2 5.6 %collective-permute-done.2.far_left = bf16[8,128,128]{2,1,0:T(8,128)(2,1)S(1)} collective-permute-done((bf16[8,128,128]{2,1,0:T(8,128)(2,1)S(1)}, bf16[8,128,128]{2,1,0:T(8,128)(2,1)S(1)}, u32[]{:S(2)}, u32[]{:S(2)}) %collective-permute-start.2) | collective-permute-done | bytes 262176 | tf_op jit(solution)/shard_map/ppermute | solution.py:152
  86.9 0.0 copy-start
  86.9 2.2 %copy-done = bf16[16640,128]{1,0:T(8,128)(2,1)S(1)} copy-done((bf16[16640,128]{1,0:T(8,128)(2,1)S(1)}, bf16[16640,128]{1,0:T(8,128)(2,1)}, u32[]{:S(2)}) %copy-start) | copy-done | bytes 4259864
  89.1 0.0 copy-start.3
  89.1 0.9 copy-done.3
  90.0 7.2 %shard_map.67 = (bf16[128,1024]{1,0:T(8,128)(2,1)}, bf16[128,1024]{1,0:T(8,128)(2,1)S(1)}, bf16[16,8,128,128]{3,2,1,0:T(8,128)(2,1)S(1)}) custom-call(s32[16,8]{1,0:T(8,128)S(1)} %fusion.7.rows_ref, bf16[16,128,128]{2,1,0:T(8,128)(2,1)S(1)} %bitcast.18, bf16[16,128,128]{2,1,0:T(8,128)(2,1)S(1)} %collective-permute-done.left, ...), custom_call_target="tpu_custom_call" | custom-call | flops 1073741824 | bytes 11000000 | tf_op jit(solution)/shard_map/pallas_call | solution.py:105
  97.2 0.0 copy-start.2
  97.2 2.0 %copy-done.2 = bf16[16,8,128,128]{3,2,1,0:T(8,128)(2,1)} copy-done((bf16[16,8,128,128]{3,2,1,0:T(8,128)(2,1)}, bf16[16,8,128,128]{3,2,1,0:T(8,128)(2,1)S(1)}, u32[]{:S(2)}) %copy-start.2) | copy-done | bytes 4194328
  99.2 0.0 reduce-scatter.2.cloned.1.call-update
  99.2 0.0 copy-start.1
  99.3 2.2 %copy-done.1 = bf16[16640,128]{1,0:T(8,128)(2,1)S(1)} copy-done((bf16[16640,128]{1,0:T(8,128)(2,1)S(1)}, bf16[16640,128]{1,0:T(8,128)(2,1)}, u32[]{:S(2)}) %copy-start.1) | copy-done | bytes 4259864
  101.4 4.3 %shard_map.68 = (bf16[16,128,128]{2,1,0:T(8,128)(2,1)S(1)}, bf16[16,128,128]{2,1,0:T(8,128)(2,1)S(1)}, bf16[16,128,128]{2,1,0:T(8,128)(2,1)S(1)}, bf16[8,128,128...) custom-call(s32[16,8]{1,0:T(8,128)S(1)} %fusion.7.rows_ref, bf16[128,1024]{1,0:T(8,128)(2,1)S(1)} %get-tuple-element.26.gh_ref, ...), custom_call_target="tpu_custom_call" | custom-call | flops 536870912 | bytes 7000000 | tf_op jit(solution)/shard_map/pallas_call | solution.py:129
  105.7 1.9 %collective-permute-start.4 = (bf16[8,128,128]{2,1,0:T(8,128)(2,1)S(1)}, bf16[8,128,128]{2,1,0:T(8,128)(2,1)S(1)}, u32[]{:S(2)}, u32[]{:S(2)}) collective-permute-start(bf16[8,128,128]{2,1,0:T(8,128)(2,1)S(1)} %get-tuple-element.30), channel_id=1, source_target_pairs={{0,15},{1,0},{2,1},{3,2},{4,3},{5,4},{6,5},{7,6},{8,7},{9,8},{10,9... | collective-permute-start | bytes 786440 | tf_op jit(solution)/shard_map/ppermute | solution.py:152
  107.7 3.9 %collective-permute-start.5 = (bf16[8,128,128]{2,1,0:T(8,128)(2,1)S(1)}, bf16[8,128,128]{2,1,0:T(8,128)(2,1)S(1)}, u32[]{:S(2)}, u32[]{:S(2)}) collective-permute-start(bf16[8,128,128]{2,1,0:T(8,128)(2,1)S(1)} %get-tuple-element.31), channel_id=1, source_target_pairs={{0,1},{1,2},{2,3},{3,4},{4,5},{5,6},{6,7},{7,8},{8,9},{9,10},{10,1... | collective-permute-start | bytes 786440 | tf_op jit(solution)/shard_map/ppermute | solution.py:152
  111.6 2.4 %collective-permute-done.4.from_right = bf16[8,128,128]{2,1,0:T(8,128)(2,1)S(1)} collective-permute-done((bf16[8,128,128]{2,1,0:T(8,128)(2,1)S(1)}, bf16[8,128,128]{2,1,0:T(8,128)(2,1)S(1)}, u32[]{:S(2)}, u32[]{:S(2)}) %collective-permute-start.4) | collective-permute-done | bytes 262176 | tf_op jit(solution)/shard_map/ppermute | solution.py:152
  114.0 3.1 %collective-permute-done.5.from_left = bf16[8,128,128]{2,1,0:T(8,128)(2,1)S(1)} collective-permute-done((bf16[8,128,128]{2,1,0:T(8,128)(2,1)S(1)}, bf16[8,128,128]{2,1,0:T(8,128)(2,1)S(1)}, u32[]{:S(2)}, u32[]{:S(2)}) %collective-permute-start.5) | collective-permute-done | bytes 262176 | tf_op jit(solution)/shard_map/ppermute | solution.py:152
  117.1 0.4 shard_map.69
  117.5 1.9 %collective-permute-start.6 = (bf16[16,128,128]{2,1,0:T(8,128)(2,1)S(1)}, bf16[16,128,128]{2,1,0:T(8,128)(2,1)S(1)}, u32[]{:S(2)}, u32[]{:S(2)}) collective-permute-start(bf16[16,128,128]{2,1,0:T(8,128)(2,1)S(1)} %get-tuple-element.32), channel_id=1, source_target_pairs={{0,15},{1,0},{2,1},{3,2},{4,3},{5,4},{6,5},{7,6},{8,7},{9,8},{10,9... | collective-permute-start | bytes 1572872 | tf_op jit(solution)/shard_map/ppermute | solution.py:152
  119.5 3.9 %collective-permute-start.7 = (bf16[16,128,128]{2,1,0:T(8,128)(2,1)S(1)}, bf16[16,128,128]{2,1,0:T(8,128)(2,1)S(1)}, u32[]{:S(2)}, u32[]{:S(2)}) collective-permute-start(bf16[16,128,128]{2,1,0:T(8,128)(2,1)S(1)} %get-tuple-element.33), channel_id=1, source_target_pairs={{0,1},{1,2},{2,3},{3,4},{4,5},{5,6},{6,7},{7,8},{8,9},{9,10},{10,1... | collective-permute-start | bytes 1572872 | tf_op jit(solution)/shard_map/ppermute | solution.py:152
  123.4 5.8 %collective-permute-done.6.left_ref = bf16[16,128,128]{2,1,0:T(8,128)(2,1)S(1)} collective-permute-done((bf16[16,128,128]{2,1,0:T(8,128)(2,1)S(1)}, bf16[16,128,128]{2,1,0:T(8,128)(2,1)S(1)}, u32[]{:S(2)}, u32[]{:S(2)}) %collective-permute-start.6) | collective-permute-done | bytes 524320 | tf_op jit(solution)/shard_map/ppermute | solution.py:152
  129.2 3.1 %collective-permute-done.7.right_ref = bf16[16,128,128]{2,1,0:T(8,128)(2,1)S(1)} collective-permute-done((bf16[16,128,128]{2,1,0:T(8,128)(2,1)S(1)}, bf16[16,128,128]{2,1,0:T(8,128)(2,1)S(1)}, u32[]{:S(2)}, u32[]{:S(2)}) %collective-permute-start.7) | collective-permute-done | bytes 524320 | tf_op jit(solution)/shard_map/ppermute | solution.py:152
  132.3 0.2 shard_map.70
  132.5 30.3 %all_to_all.11.far_ref = bf16[8,2,128,128]{3,2,1,0:T(8,128)(2,1)S(1)} all-to-all(bf16[8,2,128,128]{3,2,1,0:T(8,128)(2,1)S(1)} %bitcast.19), channel_id=1, replica_groups=mesh['x'=4,'yl'=2,'core'=2,'yh'=2,'zh'=4,'zl'=4] {'yh','zh'}, dimensions={0} | all-to-all | bytes 1048576 | tf_op jit(solution)/shard_map/all_to_all | solution.py:210
  162.8 0.7 shard_map.71
  163.5 2.6 %reduce-scatter.2.cloned.1.call-done = bf16[1,8,128,128]{3,2,1,0:T(8,128)(2,1)} async-done(((bf16[16,8,128,128]{3,2,1,0:T(8,128)(2,1)}), bf16[1,8,128,128]{3,2,1,0:T(8,128)(2,1)}) %reduce-scatter.2.cloned.1.call-update) | async-done | bytes 262160 | tf_op jit(solution)/shard_map/reduce_scatter | solution.py:224
  166.2 1.8 %copy.22 = bf16[8,1,128,128]{3,2,1,0:T(8,128)(2,1)} copy(bf16[8,1,128,128]{2,3,0,1:T(8,128)(2,1)} %bitcast.21) | data formatting | bytes 524288
  (4 shorter events, 0.1 us)
Async XLA Ops:
  7.2 72.2 %all-gather.3.cloned.1.call-start = ((), (), s32[]{:S(2)}) async-start(), calls=%async_computation.4 | async-start | bytes 4526080 | tf_op jit(solution)/shard_map/all_gather | solution.py:220
  9.6 156.6 %reduce-scatter.2.cloned.1.call-start = ((), (), s32[]{:S(2)}) async-start(), calls=%async_computation.3 | async-start | bytes 4456448 | tf_op jit(solution)/shard_map/reduce_scatter | solution.py:224
  54.7 18.2 %collective-permute-start.1 = (bf16[16,128,128]{2,1,0:T(8,128)(2,1)S(1)}, bf16[16,128,128]{2,1,0:T(8,128)(2,1)S(1)}, u32[]{:S(2)}, u32[]{:S(2)}) collective-permute-start(bf16[16,128,128]{2,1,0:T(8,128)(2,1)S(1)} %bitcast.16), channel_id=1, source_target_pairs={{0,15},{1,0},{2,1},{3,2},{4,3},{5,4},{6,5},{7,6},{8,7},{9,8},{10,9... | collective-permute-start | bytes 1572872 | tf_op jit(solution)/shard_map/ppermute | solution.py:152
  61.5 15.9 %collective-permute-start = (bf16[16,128,128]{2,1,0:T(8,128)(2,1)S(1)}, bf16[16,128,128]{2,1,0:T(8,128)(2,1)S(1)}, u32[]{:S(2)}, u32[]{:S(2)}) collective-permute-start(bf16[16,128,128]{2,1,0:T(8,128)(2,1)S(1)} %bitcast.17), channel_id=1, source_target_pairs={{0,1},{1,2},{2,3},{3,4},{4,5},{5,6},{6,7},{7,8},{8,9},{9,10},{10,1... | collective-permute-start | bytes 1572872 | tf_op jit(solution)/shard_map/ppermute | solution.py:152
  72.9 8.3 %collective-permute-start.3 = (bf16[8,128,128]{2,1,0:T(8,128)(2,1)S(1)}, bf16[8,128,128]{2,1,0:T(8,128)(2,1)S(1)}, u32[]{:S(2)}, u32[]{:S(2)}) collective-permute-start(bf16[8,128,128]{2,1,0:T(8,128)(2,1)S(1)} %slice.30), channel_id=1, source_target_pairs={{0,15},{1,0},{2,1},{3,2},{4,3},{5,4},{6,5},{7,6},{8,7},{9,8},{10,9... | collective-permute-start | bytes 786440 | tf_op jit(solution)/shard_map/ppermute | solution.py:152
  77.4 9.5 %collective-permute-start.2 = (bf16[8,128,128]{2,1,0:T(8,128)(2,1)S(1)}, bf16[8,128,128]{2,1,0:T(8,128)(2,1)S(1)}, u32[]{:S(2)}, u32[]{:S(2)}) collective-permute-start(bf16[8,128,128]{2,1,0:T(8,128)(2,1)S(1)} %slice.29), channel_id=1, source_target_pairs={{0,1},{1,2},{2,3},{3,4},{4,5},{5,6},{6,7},{7,8},{8,9},{9,10},{10,1... | collective-permute-start | bytes 786440 | tf_op jit(solution)/shard_map/ppermute | solution.py:152
  86.9 2.2 %copy-start = (bf16[16640,128]{1,0:T(8,128)(2,1)S(1)}, bf16[16640,128]{1,0:T(8,128)(2,1)}, u32[]{:S(2)}) copy-start(bf16[16640,128]{1,0:T(8,128)(2,1)} %all-gather.3.cloned.1.call-done) | copy-start | bytes 12779524
  89.1 0.9 copy-start.3
  97.2 2.0 %copy-start.2 = (bf16[16,8,128,128]{3,2,1,0:T(8,128)(2,1)}, bf16[16,8,128,128]{3,2,1,0:T(8,128)(2,1)S(1)}, u32[]{:S(2)}) copy-start(bf16[16,8,128,128]{3,2,1,0:T(8,128)(2,1)S(1)} %get-tuple-element.34) | copy-start | bytes 12582916
  99.2 2.2 %copy-start.1 = (bf16[16640,128]{1,0:T(8,128)(2,1)S(1)}, bf16[16640,128]{1,0:T(8,128)(2,1)}, u32[]{:S(2)}) copy-start(bf16[16640,128]{1,0:T(8,128)(2,1)} %all-gather.3.cloned.1.call-done) | copy-start | bytes 12779524
  105.7 8.3 %collective-permute-start.4 = (bf16[8,128,128]{2,1,0:T(8,128)(2,1)S(1)}, bf16[8,128,128]{2,1,0:T(8,128)(2,1)S(1)}, u32[]{:S(2)}, u32[]{:S(2)}) collective-permute-start(bf16[8,128,128]{2,1,0:T(8,128)(2,1)S(1)} %get-tuple-element.30), channel_id=1, source_target_pairs={{0,15},{1,0},{2,1},{3,2},{4,3},{5,4},{6,5},{7,6},{8,7},{9,8},{10,9... | collective-permute-start | bytes 786440 | tf_op jit(solution)/shard_map/ppermute | solution.py:152
  107.7 9.5 %collective-permute-start.5 = (bf16[8,128,128]{2,1,0:T(8,128)(2,1)S(1)}, bf16[8,128,128]{2,1,0:T(8,128)(2,1)S(1)}, u32[]{:S(2)}, u32[]{:S(2)}) collective-permute-start(bf16[8,128,128]{2,1,0:T(8,128)(2,1)S(1)} %get-tuple-element.31), channel_id=1, source_target_pairs={{0,1},{1,2},{2,3},{3,4},{4,5},{5,6},{6,7},{7,8},{8,9},{9,10},{10,1... | collective-permute-start | bytes 786440 | tf_op jit(solution)/shard_map/ppermute | solution.py:152
  117.5 11.7 %collective-permute-start.6 = (bf16[16,128,128]{2,1,0:T(8,128)(2,1)S(1)}, bf16[16,128,128]{2,1,0:T(8,128)(2,1)S(1)}, u32[]{:S(2)}, u32[]{:S(2)}) collective-permute-start(bf16[16,128,128]{2,1,0:T(8,128)(2,1)S(1)} %get-tuple-element.32), channel_id=1, source_target_pairs={{0,15},{1,0},{2,1},{3,2},{4,3},{5,4},{6,5},{7,6},{8,7},{9,8},{10,9... | collective-permute-start | bytes 1572872 | tf_op jit(solution)/shard_map/ppermute | solution.py:152
  119.5 12.9 %collective-permute-start.7 = (bf16[16,128,128]{2,1,0:T(8,128)(2,1)S(1)}, bf16[16,128,128]{2,1,0:T(8,128)(2,1)S(1)}, u32[]{:S(2)}, u32[]{:S(2)}) collective-permute-start(bf16[16,128,128]{2,1,0:T(8,128)(2,1)S(1)} %get-tuple-element.33), channel_id=1, source_target_pairs={{0,1},{1,2},{2,3},{3,4},{4,5},{5,6},{6,7},{7,8},{8,9},{9,10},{10,1... | collective-permute-start | bytes 1572872 | tf_op jit(solution)/shard_map/ppermute | solution.py:152
Sparse Core Ops, SparseCore 0:
  10.1 50.6 all-gather.2
  99.4 66.7 reduce-scatter.1

commit v10 on v9

--- a/solution.py
+++ b/solution.py
@@ -118,7 +118,7 @@
             ],
         ),
         out_shape=[wide, wide, grads],
-        compiler_params=pltpu.CompilerParams(vmem_limit_bytes=18 * 2**20),
+        compiler_params=pltpu.CompilerParams(vmem_limit_bytes=56 * 2**20),
         cost_estimate=pl.CostEstimate(flops=1_073_741_824, bytes_accessed=11_000_000, transcendentals=131072),
     )(rows, *parts, weights, grad_act)
 
@@ -143,7 +143,7 @@
             ],
         ),
         out_shape=[jax.ShapeDtypeStruct((n, n_tok, 128), BF16) for _, n in PARTS],
-        compiler_params=pltpu.CompilerParams(vmem_limit_bytes=20 * 2**20),
+        compiler_params=pltpu.CompilerParams(vmem_limit_bytes=56 * 2**20),
         cost_estimate=pl.CostEstimate(flops=536_870_912, bytes_accessed=7_000_000, transcendentals=0),
     )(rows, grad_hidden, weights)
 
@@ -161,6 +161,11 @@
     own = own.reshape((16,) + mine.shape[1:])
     left, right = shift(own, 1), shift(own, -1)
     return own, left, right, shift(left[:8], 1), shift(right[8:], -1)
+
+
+def turn_kernel(grads_ref, out_ref):
+    for c in range(grads_ref.shape[0]):
+        out_ref[c] = grads_ref[c].T
 
 
 def near_kernel(left_ref, right_ref, from_right, from_left, left_out, right_out):
@@ -223,7 +228,8 @@
     activated, grad_hidden, grads = hidden_call(rows, parts, weights, grad_act)
     grads = lax.psum_scatter(grads, SEQ, scatter_dimension=0)
     summed = reduce_terms(*term_call(rows, grad_hidden, weights))
-    return activated, summed, grads.transpose(0, 2, 1)[:, None]
+    grads = small_call(turn_kernel, (grads,), jax.ShapeDtypeStruct(grads.shape, BF16))
+    return activated, summed, grads[:, None]
 
 
 def solution(mesh):

time: 178 us -> 185 us (1.039)
  the two profiles are of different devices: /device:TPU:24 before, /device:TPU:36 now
where the time goes in v10:
time: 185 us; the launch traced here: 183 us
  blocking collectives  88.1 us (48%)
  waiting for transfers between devices  26 us (14%)
  starting transfers between devices  23.5 us (13%)
  Pallas kernels  21.4 us (12%)
  between operations  14.2 us (8%)
  local copies, waits for them, and re-layouts  5.81 us (3%)
  other arithmetic  3.73 us (2%)
    all_to_all x1, blocking collectives, gather_tokens(): own = lax.all_to_all(jnp.broadcast_to(mine, (8,) + mine.shape), FAR, 0, 0)  51.2 us
    all_to_all x1, blocking collectives, reduce_terms(): far = lax.all_to_all(own.reshape((8, 2, n_tok, 128)), FAR, 0, 0)  36.9 us
    ppermute x8, waiting for transfers between devices, shift(): return lax.ppermute(a, Z, [(i, (i + by) % 16) for i in range(16)])  25.9 us
    ppermute x8, starting transfers between devices, shift(): return lax.ppermute(a, Z, [(i, (i + by) % 16) for i in range(16)])  23.4 us
    pallas_call x1, Pallas kernels, hidden_call(): pl.pallas_call(hidden_kernel, grid_spec=pltpu.PrefetchScalarGridSpec(num_...  11 us
    pallas_call x1, Pallas kernels, term_call(): pl.pallas_call(term_kernel, grid_spec=pltpu.PrefetchScalarGridSpec(num_sc...  8.35 us
    unnamed x18, local copies, waits for them, and re-layouts  4.8 us
  transfers between devices with their start and end apart: 10, of which 7 were waited for; matrix products, arithmetic and copies ran while one was open for 1% of the time, Pallas kernels for 5%

profile of v10, /device:TPU:36, one launch (start us, length us, event | category | flops | bytes accessed | tf_op | source)
XLA Modules:
  0.0 182.8 jit_solution(8514885064727869313)
XLA Ops:
  7.2 0.0 all-gather.3.cloned.1.call-start
  7.2 0.7 convert_bitcast_fusion
  7.9 1.7 fusion.1
  9.5 0.0 all-gather.3.cloned.1.call-update
  9.6 0.0 reduce-scatter.2.cloned.1.call-start
  9.6 0.9 reshape.57
  10.5 0.1 broadcast_in_dim.7
  10.6 51.2 %all_to_all.10 = bf16[8,2,128,128]{3,2,1,0:T(8,128)(2,1)S(1)} all-to-all(bf16[8,2,128,128]{3,2,1,0:T(8,128)(2,1)S(1)} %broadcast_in_dim.7), channel_id=1, replica_groups=mesh['x'=4,'yl'=2,'core'=2,'yh'=2,'zh'=4,'zl'=4] {'yh','zh'}, dimensions={0} | all-to-all | bytes 1048576 | tf_op jit(solution)/shard_map/all_to_all | solution.py:160
  61.8 0.0 copy-start.4
  61.8 1.9 %collective-permute-start.1 = (bf16[16,128,128]{2,1,0:T(8,128)(2,1)S(1)}, bf16[16,128,128]{2,1,0:T(8,128)(2,1)S(1)}, u32[]{:S(2)}, u32[]{:S(2)}) collective-permute-start(bf16[16,128,128]{2,1,0:T(8,128)(2,1)S(1)} %bitcast.17), channel_id=1, source_target_pairs={{0,15},{1,0},{2,1},{3,2},{4,3},{5,4},{6,5},{7,6},{8,7},{9,8},{10,9... | collective-permute-start | bytes 1572872 | tf_op jit(solution)/shard_map/ppermute | solution.py:152
  63.7 3.9 %collective-permute-start = (bf16[16,128,128]{2,1,0:T(8,128)(2,1)S(1)}, bf16[16,128,128]{2,1,0:T(8,128)(2,1)S(1)}, u32[]{:S(2)}, u32[]{:S(2)}) collective-permute-start(bf16[16,128,128]{2,1,0:T(8,128)(2,1)S(1)} %bitcast.18), channel_id=1, source_target_pairs={{0,1},{1,2},{2,3},{3,4},{4,5},{5,6},{6,7},{7,8},{8,9},{9,10},{10,1... | collective-permute-start | bytes 1572872 | tf_op jit(solution)/shard_map/ppermute | solution.py:152
  67.7 7.8 %collective-permute-done.1.right = bf16[16,128,128]{2,1,0:T(8,128)(2,1)S(1)} collective-permute-done((bf16[16,128,128]{2,1,0:T(8,128)(2,1)S(1)}, bf16[16,128,128]{2,1,0:T(8,128)(2,1)S(1)}, u32[]{:S(2)}, u32[]{:S(2)}) %collective-permute-start.1) | collective-permute-done | bytes 524320 | tf_op jit(solution)/shard_map/ppermute | solution.py:152
  75.5 0.0 copy-start.5
  75.5 2.2 %collective-permute-start.3 = (bf16[8,128,128]{2,1,0:T(8,128)(2,1)S(1)}, bf16[8,128,128]{2,1,0:T(8,128)(2,1)S(1)}, u32[]{:S(2)}, u32[]{:S(2)}) collective-permute-start(bf16[8,128,128]{2,1,0:T(8,128)(2,1)S(1)} %slice.30), channel_id=1, source_target_pairs={{0,15},{1,0},{2,1},{3,2},{4,3},{5,4},{6,5},{7,6},{8,7},{9,8},{10,9... | collective-permute-start | bytes 786440 | tf_op jit(solution)/shard_map/ppermute | solution.py:152
  77.7 0.0 collective-permute-done.left
  77.7 0.0 copy-start.6
  77.8 3.6 %collective-permute-start.2 = (bf16[8,128,128]{2,1,0:T(8,128)(2,1)S(1)}, bf16[8,128,128]{2,1,0:T(8,128)(2,1)S(1)}, u32[]{:S(2)}, u32[]{:S(2)}) collective-permute-start(bf16[8,128,128]{2,1,0:T(8,128)(2,1)S(1)} %slice.29), channel_id=1, source_target_pairs={{0,1},{1,2},{2,3},{3,4},{4,5},{5,6},{6,7},{7,8},{8,9},{9,10},{10,1... | collective-permute-start | bytes 786440 | tf_op jit(solution)/shard_map/ppermute | solution.py:152
  81.4 0.0 all-gather.3.cloned.1.call-done
  81.5 0.8 slice_convert_fusion
  82.2 0.6 fusion.7.rows_ref
  82.9 0.9 collective-permute-done.3.far_right
  83.8 2.3 %collective-permute-done.2.far_left = bf16[8,128,128]{2,1,0:T(8,128)(2,1)S(1)} collective-permute-done((bf16[8,128,128]{2,1,0:T(8,128)(2,1)S(1)}, bf16[8,128,128]{2,1,0:T(8,128)(2,1)S(1)}, u32[]{:S(2)}, u32[]{:S(2)}) %collective-permute-start.2) | collective-permute-done | bytes 262176 | tf_op jit(solution)/shard_map/ppermute | solution.py:152
  86.1 0.0 copy-done.4
  86.1 0.0 copy-done.5
  86.1 0.0 copy-done.6
  86.1 0.0 copy-done.7
  86.1 0.0 copy-start.8
  86.1 0.7 copy-done.8
  86.8 11.0 %shard_map.67 = (bf16[128,1024]{1,0:T(8,128)(2,1)}, bf16[128,1024]{1,0:T(8,128)(2,1)}, bf16[16,8,128,128]{3,2,1,0:T(8,128)(2,1)}) custom-call(s32[16,8]{1,0:T(8,128)} %fusion.7.rows_ref, bf16[16,128,128]{2,1,0:T(8,128)(2,1)} %bitcast.19, bf16[16,128,128]{2,1,0:T(8,128)(2,1)} %copy-done.6, bf16[16,128,128]{2,1,0:T(8,128)(2,1)} %copy-done.5, ...), custom_call_target="tpu_custom_call" | custom-call | flops 1073741824 | bytes 11000000 | tf_op jit(solution)/shard_map/pallas_call | solution.py:105
  97.8 0.0 reduce-scatter.2.cloned.1.call-update
  97.8 8.3 %shard_map.68 = (bf16[16,128,128]{2,1,0:T(8,128)(2,1)}, bf16[16,128,128]{2,1,0:T(8,128)(2,1)}, bf16[16,128,128]{2,1,0:T(8,128)(2,1)}, bf16[8,128,128]{2,1,0:T(8,128)(2,1)}, bf16[8,128,128]{2,1,0:T(8,128)(2,1)}) custom-call(s32[16,8]{1,0:T(8,128)} %fusion.7.rows_ref, bf16[128,1024]{1,0:T(8,128)(2,1)} %get-tuple-element.26.gh_ref, bf16[16,1040,128]{2,1,0:T(8,128)(2,1)} %bitcast.16), custom_call_target="tpu_custom_call" | custom-call | flops 536870912 | bytes 7000000 | tf_op jit(solution)/shard_map/pallas_call | solution.py:129
  106.2 3.2 %collective-permute-start.4 = (bf16[8,128,128]{2,1,0:T(8,128)(2,1)}, bf16[8,128,128]{2,1,0:T(8,128)(2,1)S(1)}, u32[]{:S(2)}, u32[]{:S(2)}) collective-permute-start(bf16[8,128,128]{2,1,0:T(8,128)(2,1)} %get-tuple-element.30), channel_id=1, source_target_pairs={{0,15},{1,0},{2,1},{3,2},{4,3},{5,4},{6,5},{7,6},{8,7},{9,8},{10,9... | collective-permute-start | bytes 786440 | tf_op jit(solution)/shard_map/ppermute | solution.py:152
  109.3 2.7 %collective-permute-start.5 = (bf16[8,128,128]{2,1,0:T(8,128)(2,1)}, bf16[8,128,128]{2,1,0:T(8,128)(2,1)S(1)}, u32[]{:S(2)}, u32[]{:S(2)}) collective-permute-start(bf16[8,128,128]{2,1,0:T(8,128)(2,1)} %get-tuple-element.31), channel_id=1, source_target_pairs={{0,1},{1,2},{2,3},{3,4},{4,5},{5,6},{6,7},{7,8},{8,9},{9,10},{10,1... | collective-permute-start | bytes 786440 | tf_op jit(solution)/shard_map/ppermute | solution.py:152
  112.0 2.6 %collective-permute-done.4.from_right = bf16[8,128,128]{2,1,0:T(8,128)(2,1)S(1)} collective-permute-done((bf16[8,128,128]{2,1,0:T(8,128)(2,1)}, bf16[8,128,128]{2,1,0:T(8,128)(2,1)S(1)}, u32[]{:S(2)}, u32[]{:S(2)}) %collective-permute-start.4) | collective-permute-done | bytes 262176 | tf_op jit(solution)/shard_map/ppermute | solution.py:152
  114.6 3.2 %collective-permute-done.5.from_left = bf16[8,128,128]{2,1,0:T(8,128)(2,1)S(1)} collective-permute-done((bf16[8,128,128]{2,1,0:T(8,128)(2,1)}, bf16[8,128,128]{2,1,0:T(8,128)(2,1)S(1)}, u32[]{:S(2)}, u32[]{:S(2)}) %collective-permute-start.5) | collective-permute-done | bytes 262176 | tf_op jit(solution)/shard_map/ppermute | solution.py:152
  117.8 1.0 copy-done
  118.9 1.0 copy-done.1
  119.9 0.4 shard_map.69
  120.3 4.0 %collective-permute-start.6 = (bf16[16,128,128]{2,1,0:T(8,128)(2,1)S(1)}, bf16[16,128,128]{2,1,0:T(8,128)(2,1)S(1)}, u32[]{:S(2)}, u32[]{:S(2)}) collective-permute-start(bf16[16,128,128]{2,1,0:T(8,128)(2,1)S(1)} %get-tuple-element.32), channel_id=1, source_target_pairs={{0,15},{1,0},{2,1},{3,2},{4,3},{5,4},{6,5},{7,6},{8,7},{9,8},{10,9... | collective-permute-start | bytes 1572872 | tf_op jit(solution)/shard_map/ppermute | solution.py:152
  124.3 1.9 %collective-permute-start.7 = (bf16[16,128,128]{2,1,0:T(8,128)(2,1)S(1)}, bf16[16,128,128]{2,1,0:T(8,128)(2,1)S(1)}, u32[]{:S(2)}, u32[]{:S(2)}) collective-permute-start(bf16[16,128,128]{2,1,0:T(8,128)(2,1)S(1)} %get-tuple-element.33), channel_id=1, source_target_pairs={{0,1},{1,2},{2,3},{3,4},{4,5},{5,6},{6,7},{7,8},{8,9},{9,10},{10,1... | collective-permute-start | bytes 1572872 | tf_op jit(solution)/shard_map/ppermute | solution.py:152
  126.2 5.1 %collective-permute-done.6.left_ref = bf16[16,128,128]{2,1,0:T(8,128)(2,1)S(1)} collective-permute-done((bf16[16,128,128]{2,1,0:T(8,128)(2,1)S(1)}, bf16[16,128,128]{2,1,0:T(8,128)(2,1)S(1)}, u32[]{:S(2)}, u32[]{:S(2)}) %collective-permute-start.6) | collective-permute-done | bytes 524320 | tf_op jit(solution)/shard_map/ppermute | solution.py:152
  131.4 4.0 %collective-permute-done.7.right_ref = bf16[16,128,128]{2,1,0:T(8,128)(2,1)S(1)} collective-permute-done((bf16[16,128,128]{2,1,0:T(8,128)(2,1)S(1)}, bf16[16,128,128]{2,1,0:T(8,128)(2,1)S(1)}, u32[]{:S(2)}, u32[]{:S(2)}) %collective-permute-start.7) | collective-permute-done | bytes 524320 | tf_op jit(solution)/shard_map/ppermute | solution.py:152
  135.4 1.0 copy-done.2
  136.4 0.2 shard_map.70
  136.6 36.9 %all_to_all.11.far_ref = bf16[8,2,128,128]{3,2,1,0:T(8,128)(2,1)S(1)} all-to-all(bf16[8,2,128,128]{3,2,1,0:T(8,128)(2,1)S(1)} %bitcast.12), channel_id=1, replica_groups=mesh['x'=4,'yl'=2,'core'=2,'yh'=2,'zh'=4,'zl'=4] {'yh','zh'}, dimensions={0} | all-to-all | bytes 1048576 | tf_op jit(solution)/shard_map/all_to_all | solution.py:215
  173.5 0.7 shard_map.71
  174.2 0.9 copy-done.3
  175.2 0.8 shard_map.72
  (9 shorter events, 0.1 us)
Async XLA Ops:
  7.2 74.3 %all-gather.3.cloned.1.call-start = ((), (), s32[]{:S(2)}) async-start(), calls=%async_computation.4 | async-start | bytes 4526080 | tf_op jit(solution)/shard_map/all_gather | solution.py:225
  9.6 164.6 %reduce-scatter.2.cloned.1.call-start = ((), (), s32[]{:S(2)}) async-start(), calls=%async_computation.3 | async-start | bytes 4456448 | tf_op jit(solution)/shard_map/reduce_scatter | solution.py:229
  61.8 24.2 %copy-start.4 = (bf16[8,2,128,128]{3,2,1,0:T(8,128)(2,1)}, bf16[8,2,128,128]{3,2,1,0:T(8,128)(2,1)S(1)}, u32[]{:S(2)}) copy-start(bf16[8,2,128,128]{3,2,1,0:T(8,128)(2,1)S(1)} %all_to_all.10) | copy-start | bytes 1572868
  61.8 13.7 %collective-permute-start.1 = (bf16[16,128,128]{2,1,0:T(8,128)(2,1)S(1)}, bf16[16,128,128]{2,1,0:T(8,128)(2,1)S(1)}, u32[]{:S(2)}, u32[]{:S(2)}) collective-permute-start(bf16[16,128,128]{2,1,0:T(8,128)(2,1)S(1)} %bitcast.17), channel_id=1, source_target_pairs={{0,15},{1,0},{2,1},{3,2},{4,3},{5,4},{6,5},{7,6},{8,7},{9,8},{10,9... | collective-permute-start | bytes 1572872 | tf_op jit(solution)/shard_map/ppermute | solution.py:152
  63.7 14.0 %collective-permute-start = (bf16[16,128,128]{2,1,0:T(8,128)(2,1)S(1)}, bf16[16,128,128]{2,1,0:T(8,128)(2,1)S(1)}, u32[]{:S(2)}, u32[]{:S(2)}) collective-permute-start(bf16[16,128,128]{2,1,0:T(8,128)(2,1)S(1)} %bitcast.18), channel_id=1, source_target_pairs={{0,1},{1,2},{2,3},{3,4},{4,5},{5,6},{6,7},{7,8},{8,9},{9,10},{10,1... | collective-permute-start | bytes 1572872 | tf_op jit(solution)/shard_map/ppermute | solution.py:152
  75.5 10.6 %copy-start.5 = (bf16[16,128,128]{2,1,0:T(8,128)(2,1)}, bf16[16,128,128]{2,1,0:T(8,128)(2,1)S(1)}, u32[]{:S(2)}) copy-start(bf16[16,128,128]{2,1,0:T(8,128)(2,1)S(1)} %collective-permute-done.1.right) | copy-start | bytes 1572868
  75.5 8.3 %collective-permute-start.3 = (bf16[8,128,128]{2,1,0:T(8,128)(2,1)S(1)}, bf16[8,128,128]{2,1,0:T(8,128)(2,1)S(1)}, u32[]{:S(2)}, u32[]{:S(2)}) collective-permute-start(bf16[8,128,128]{2,1,0:T(8,128)(2,1)S(1)} %slice.30), channel_id=1, source_target_pairs={{0,15},{1,0},{2,1},{3,2},{4,3},{5,4},{6,5},{7,6},{8,7},{9,8},{10,9... | collective-permute-start | bytes 786440 | tf_op jit(solution)/shard_map/ppermute | solution.py:152
  77.7 8.3 %copy-start.6 = (bf16[16,128,128]{2,1,0:T(8,128)(2,1)}, bf16[16,128,128]{2,1,0:T(8,128)(2,1)S(1)}, u32[]{:S(2)}) copy-start(bf16[16,128,128]{2,1,0:T(8,128)(2,1)S(1)} %collective-permute-done.left) | copy-start | bytes 1572868
  77.8 8.3 %collective-permute-start.2 = (bf16[8,128,128]{2,1,0:T(8,128)(2,1)S(1)}, bf16[8,128,128]{2,1,0:T(8,128)(2,1)S(1)}, u32[]{:S(2)}, u32[]{:S(2)}) collective-permute-start(bf16[8,128,128]{2,1,0:T(8,128)(2,1)S(1)} %slice.29), channel_id=1, source_target_pairs={{0,1},{1,2},{2,3},{3,4},{4,5},{5,6},{6,7},{7,8},{8,9},{9,10},{10,1... | collective-permute-start | bytes 786440 | tf_op jit(solution)/shard_map/ppermute | solution.py:152
  83.8 2.3 %copy-start.7 = (bf16[8,128,128]{2,1,0:T(8,128)(2,1)}, bf16[8,128,128]{2,1,0:T(8,128)(2,1)S(1)}, u32[]{:S(2)}) copy-start(bf16[8,128,128]{2,1,0:T(8,128)(2,1)S(1)} %collective-permute-done.3.far_right) | copy-start | bytes 786436
  86.1 0.7 copy-start.8
  106.2 8.5 %collective-permute-start.4 = (bf16[8,128,128]{2,1,0:T(8,128)(2,1)}, bf16[8,128,128]{2,1,0:T(8,128)(2,1)S(1)}, u32[]{:S(2)}, u32[]{:S(2)}) collective-permute-start(bf16[8,128,128]{2,1,0:T(8,128)(2,1)} %get-tuple-element.30), channel_id=1, source_target_pairs={{0,15},{1,0},{2,1},{3,2},{4,3},{5,4},{6,5},{7,6},{8,7},{9,8},{10,9... | collective-permute-start | bytes 786440 | tf_op jit(solution)/shard_map/ppermute | solution.py:152
  109.3 8.5 %collective-permute-start.5 = (bf16[8,128,128]{2,1,0:T(8,128)(2,1)}, bf16[8,128,128]{2,1,0:T(8,128)(2,1)S(1)}, u32[]{:S(2)}, u32[]{:S(2)}) collective-permute-start(bf16[8,128,128]{2,1,0:T(8,128)(2,1)} %get-tuple-element.31), channel_id=1, source_target_pairs={{0,1},{1,2},{2,3},{3,4},{4,5},{5,6},{6,7},{7,8},{8,9},{9,10},{10,1... | collective-permute-start | bytes 786440 | tf_op jit(solution)/shard_map/ppermute | solution.py:152
  117.8 1.1 copy-start
  118.9 1.0 copy-start.1
  120.3 11.1 %collective-permute-start.6 = (bf16[16,128,128]{2,1,0:T(8,128)(2,1)S(1)}, bf16[16,128,128]{2,1,0:T(8,128)(2,1)S(1)}, u32[]{:S(2)}, u32[]{:S(2)}) collective-permute-start(bf16[16,128,128]{2,1,0:T(8,128)(2,1)S(1)} %get-tuple-element.32), channel_id=1, source_target_pairs={{0,15},{1,0},{2,1},{3,2},{4,3},{5,4},{6,5},{7,6},{8,7},{9,8},{10,9... | collective-permute-start | bytes 1572872 | tf_op jit(solution)/shard_map/ppermute | solution.py:152
  124.3 11.1 %collective-permute-start.7 = (bf16[16,128,128]{2,1,0:T(8,128)(2,1)S(1)}, bf16[16,128,128]{2,1,0:T(8,128)(2,1)S(1)}, u32[]{:S(2)}, u32[]{:S(2)}) collective-permute-start(bf16[16,128,128]{2,1,0:T(8,128)(2,1)S(1)} %get-tuple-element.33), channel_id=1, source_target_pairs={{0,1},{1,2},{2,3},{3,4},{4,5},{5,6},{6,7},{7,8},{8,9},{9,10},{10,1... | collective-permute-start | bytes 1572872 | tf_op jit(solution)/shard_map/ppermute | solution.py:152
  135.4 1.0 copy-start.2
  174.2 1.0 copy-start.3
Sparse Core Ops, SparseCore 0:
  10.1 49.5 all-gather.2
  97.9 61.7 reduce-scatter.1

commit v11 on v10

--- a/solution.py
+++ b/solution.py
@@ -11,7 +11,7 @@
 AXES = ("x", "yl", "core", "yh", "zh", "zl")
 SIZES = (4, 2, 2, 2, 4, 4)
 SEQ = ("x", "yl", "core")
-FAR = ("yh", "zh")
+FAR = ("zh", "yh")
 MP = ("yh", "zh", "zl")
 Z = ("zh", "zl")
 BF16, F32 = jnp.bfloat16, jnp.float32
@@ -118,7 +118,7 @@
             ],
         ),
         out_shape=[wide, wide, grads],
-        compiler_params=pltpu.CompilerParams(vmem_limit_bytes=56 * 2**20),
+        compiler_params=pltpu.CompilerParams(vmem_limit_bytes=18 * 2**20),
         cost_estimate=pl.CostEstimate(flops=1_073_741_824, bytes_accessed=11_000_000, transcendentals=131072),
     )(rows, *parts, weights, grad_act)
 
@@ -143,7 +143,7 @@
             ],
         ),
         out_shape=[jax.ShapeDtypeStruct((n, n_tok, 128), BF16) for _, n in PARTS],
-        compiler_params=pltpu.CompilerParams(vmem_limit_bytes=56 * 2**20),
+        compiler_params=pltpu.CompilerParams(vmem_limit_bytes=20 * 2**20),
         cost_estimate=pl.CostEstimate(flops=536_870_912, bytes_accessed=7_000_000, transcendentals=0),
     )(rows, grad_hidden, weights)
 
@@ -156,9 +156,8 @@
     return sum(a.astype(F32) for a in arrays)
 
 
-def gather_tokens(mine):
-    own = lax.all_to_all(jnp.broadcast_to(mine, (8,) + mine.shape), FAR, 0, 0)
-    own = own.reshape((16,) + mine.shape[1:])
+def gather_tokens(copies):
+    own = lax.all_to_all(copies, FAR, 0, 0).reshape((16,) + copies.shape[2:])
     left, right = shift(own, 1), shift(own, -1)
     return own, left, right, shift(left[:8], 1), shift(right[8:], -1)
 
@@ -166,6 +165,22 @@
 def turn_kernel(grads_ref, out_ref):
     for c in range(grads_ref.shape[0]):
         out_ref[c] = grads_ref[c].T
+
+
+def order_kernel(*refs):
+    pass
+
+
+def held_until(x, after):
+    anywhere = pl.BlockSpec(memory_space=pl.ANY)
+    return pl.pallas_call(
+        order_kernel,
+        in_specs=[anywhere, anywhere],
+        out_specs=anywhere,
+        out_shape=jax.ShapeDtypeStruct(x.shape, x.dtype),
+        input_output_aliases={0: 0},
+        compiler_params=pltpu.CompilerParams(vmem_limit_bytes=2**20),
+    )(x, after)
 
 
 def near_kernel(left_ref, right_ref, from_right, from_left, left_out, right_out):
@@ -219,12 +234,15 @@
 def shards(tokens, block_values, block_rows, grad_act):
     n_tok = tokens.shape[0]
     cols = block_values.shape[0]
-    parts = gather_tokens(tokens.reshape(n_tok, 2, 128).transpose(1, 0, 2))
+    mine = tokens.reshape(n_tok, 2, 128).transpose(1, 0, 2)
+    copies = jnp.broadcast_to(mine, (8,) + mine.shape)
+    parts = gather_tokens(copies)
     row_tile = jnp.zeros((16, 128), BF16).at[0, :cols].set(block_rows[:, 0].astype(BF16))
+    row_tile = held_until(row_tile, copies)
     sent = jnp.concatenate([block_values.reshape(cols * 128, 128), row_tile])
     weights = lax.all_gather(sent, SEQ, axis=0)
     rows = weights[:, cols * 128, :cols].astype(jnp.int32)
-    rows = (rows // 2 - lax.axis_index("zl")) % 4 * 16 + rows // 32 * 8 + rows % 32 // 8 * 2 + rows % 2
+    rows = (rows // 2 - lax.axis_index("zl")) % 4 * 16 + rows % 32 // 8 * 4 + rows // 32 * 2 + rows % 2
     activated, grad_hidden, grads = hidden_call(rows, parts, weights, grad_act)
     grads = lax.psum_scatter(grads, SEQ, scatter_dimension=0)
     summed = reduce_terms(*term_call(rows, grad_hidden, weights))

time: 185 us -> 178 us (0.962)
  the two profiles are of different devices: /device:TPU:36 before, /device:TPU:1 now
where the time goes in v11:
time: 178 us
  blocking collectives  85.4 us (48%)
  waiting for transfers between devices  28.2 us (16%)
  starting transfers between devices  25.7 us (14%)
  between operations  14.2 us (8%)
  Pallas kernels  13.6 us (8%)
  local copies, waits for them, and re-layouts  7.57 us (4%)
  other arithmetic  3.19 us (2%)
    all_to_all x1, blocking collectives, gather_tokens(): own = lax.all_to_all(copies, FAR, 0, 0).reshape((16,) + copies.shape[2:])  46.8 us
    all_to_all x1, blocking collectives, reduce_terms(): far = lax.all_to_all(own.reshape((8, 2, n_tok, 128)), FAR, 0, 0)  38.6 us
    ppermute x8, waiting for transfers between devices, shift(): return lax.ppermute(a, Z, [(i, (i + by) % 16) for i in range(16)])  27 us
    ppermute x8, starting transfers between devices, shift(): return lax.ppermute(a, Z, [(i, (i + by) % 16) for i in range(16)])  25.6 us
    unnamed x12, local copies, waits for them, and re-layouts  7.43 us
    pallas_call x1, Pallas kernels, hidden_call(): pl.pallas_call(hidden_kernel, grid_spec=pltpu.PrefetchScalarGridSpec(num_...  7.18 us
    pallas_call x1, Pallas kernels, term_call(): pl.pallas_call(term_kernel, grid_spec=pltpu.PrefetchScalarGridSpec(num_sc...  4.27 us
  transfers between devices with their start and end apart: 10, of which 8 were waited for; matrix products, arithmetic and copies ran while one was open for 0% of the time, Pallas kernels for 3%

profile of v11, /device:TPU:1, one launch (start us, length us, event | category | flops | bytes accessed | tf_op | source)
XLA Modules:
  0.0 177.8 jit_solution(15871003290399520511)
XLA Ops:
  7.2 0.0 copy-start
  7.2 0.0 copy-start.4
  7.2 0.0 all-gather.3.cloned.1.call-start
  7.2 0.7 convert_bitcast_fusion
  7.9 0.1 copy-done
  8.0 0.1 broadcast_in_dim.7.refs_1_
  8.1 1.7 pad_maximum_fusion
  9.8 0.0 all-gather.3.cloned.1.call-update
  9.9 0.0 reduce-scatter.2.cloned.1.call-start
  9.9 46.8 %all_to_all.10 = bf16[8,2,128,128]{3,2,1,0:T(8,128)(2,1)S(1)} all-to-all(bf16[8,2,128,128]{3,2,1,0:T(8,128)(2,1)S(1)} %broadcast_in_dim.7.refs_1_), channel_id=1, replica_groups=mesh['x'=4,'yl'=2,'core'=2,'yh'=2,'zh'=4,'zl'=4] {'zh','yh'}, dimensions={0} | all-to-all | bytes 1048576 | tf_op jit(solution)/shard_map/all_to_all | solution.py:160
  56.7 5.9 %collective-permute-start.1 = (bf16[16,128,128]{2,1,0:T(8,128)(2,1)S(1)}, bf16[16,128,128]{2,1,0:T(8,128)(2,1)S(1)}, u32[]{:S(2)}, u32[]{:S(2)}) collective-permute-start(bf16[16,128,128]{2,1,0:T(8,128)(2,1)S(1)} %bitcast.21), channel_id=1, source_target_pairs={{0,15},{1,0},{2,1},{3,2},{4,3},{5,4},{6,5},{7,6},{8,7},{9,8},{10,9... | collective-permute-start | bytes 1572872 | tf_op jit(solution)/shard_map/ppermute | solution.py:152
  62.6 1.9 %collective-permute-start = (bf16[16,128,128]{2,1,0:T(8,128)(2,1)S(1)}, bf16[16,128,128]{2,1,0:T(8,128)(2,1)S(1)}, u32[]{:S(2)}, u32[]{:S(2)}) collective-permute-start(bf16[16,128,128]{2,1,0:T(8,128)(2,1)S(1)} %bitcast.22), channel_id=1, source_target_pairs={{0,1},{1,2},{2,3},{3,4},{4,5},{5,6},{6,7},{7,8},{8,9},{9,10},{10,1... | collective-permute-start | bytes 1572872 | tf_op jit(solution)/shard_map/ppermute | solution.py:152
  64.5 7.6 %collective-permute-done.1.right = bf16[16,128,128]{2,1,0:T(8,128)(2,1)S(1)} collective-permute-done((bf16[16,128,128]{2,1,0:T(8,128)(2,1)S(1)}, bf16[16,128,128]{2,1,0:T(8,128)(2,1)S(1)}, u32[]{:S(2)}, u32[]{:S(2)}) %collective-permute-start.1) | collective-permute-done | bytes 524320 | tf_op jit(solution)/shard_map/ppermute | solution.py:152
  72.1 5.3 %collective-permute-start.3 = (bf16[8,128,128]{2,1,0:T(8,128)(2,1)S(1)}, bf16[8,128,128]{2,1,0:T(8,128)(2,1)S(1)}, u32[]{:S(2)}, u32[]{:S(2)}) collective-permute-start(bf16[8,128,128]{2,1,0:T(8,128)(2,1)S(1)} %slice.30), channel_id=1, source_target_pairs={{0,15},{1,0},{2,1},{3,2},{4,3},{5,4},{6,5},{7,6},{8,7},{9,8},{10,9... | collective-permute-start | bytes 786440 | tf_op jit(solution)/shard_map/ppermute | solution.py:152
  77.5 0.0 collective-permute-done.left
  77.5 1.9 %collective-permute-start.2 = (bf16[8,128,128]{2,1,0:T(8,128)(2,1)S(1)}, bf16[8,128,128]{2,1,0:T(8,128)(2,1)S(1)}, u32[]{:S(2)}, u32[]{:S(2)}) collective-permute-start(bf16[8,128,128]{2,1,0:T(8,128)(2,1)S(1)} %slice.29), channel_id=1, source_target_pairs={{0,1},{1,2},{2,3},{3,4},{4,5},{5,6},{6,7},{7,8},{8,9},{9,10},{10,1... | collective-permute-start | bytes 786440 | tf_op jit(solution)/shard_map/ppermute | solution.py:152
  79.4 0.0 all-gather.3.cloned.1.call-done
  79.5 0.8 slice_convert_fusion
  80.3 0.5 collective-permute-done.3.far_right
  80.8 5.1 %collective-permute-done.2.far_left = bf16[8,128,128]{2,1,0:T(8,128)(2,1)S(1)} collective-permute-done((bf16[8,128,128]{2,1,0:T(8,128)(2,1)S(1)}, bf16[8,128,128]{2,1,0:T(8,128)(2,1)S(1)}, u32[]{:S(2)}, u32[]{:S(2)}) %collective-permute-start.2) | collective-permute-done | bytes 262176 | tf_op jit(solution)/shard_map/ppermute | solution.py:152
  85.8 0.0 copy-done.4
  85.8 0.0 copy-start.1
  85.8 2.2 %copy-done.1 = bf16[16640,128]{1,0:T(8,128)(2,1)S(1)} copy-done((bf16[16640,128]{1,0:T(8,128)(2,1)S(1)}, bf16[16640,128]{1,0:T(8,128)(2,1)}, u32[]{:S(2)}) %copy-start.1) | copy-done | bytes 4259864
  88.0 7.2 %shard_map.68 = (bf16[128,1024]{1,0:T(8,128)(2,1)}, bf16[128,1024]{1,0:T(8,128)(2,1)S(1)}, bf16[16,8,128,128]{3,2,1,0:T(8,128)(2,1)S(1)}) custom-call(s32[16,8]{1,0:T(8,128)S(1)} %fusion.5.rows_ref, bf16[16,128,128]{2,1,0:T(8,128)(2,1)S(1)} %bitcast.23, bf16[16,128,128]{2,1,0:T(8,128)(2,1)S(1)} %collective-permute-done.left, ...), custom_call_target="tpu_custom_call" | custom-call | flops 1073741824 | bytes 11000000 | tf_op jit(solution)/shard_map/pallas_call | solution.py:105
  95.2 0.0 copy-start.3
  95.2 2.0 %copy-done.3 = bf16[16,8,128,128]{3,2,1,0:T(8,128)(2,1)} copy-done((bf16[16,8,128,128]{3,2,1,0:T(8,128)(2,1)}, bf16[16,8,128,128]{3,2,1,0:T(8,128)(2,1)S(1)}, u32[]{:S(2)}) %copy-start.3) | copy-done | bytes 4194328
  97.2 0.0 reduce-scatter.2.cloned.1.call-update
  97.3 0.0 copy-start.2
  97.3 2.2 %copy-done.2 = bf16[16640,128]{1,0:T(8,128)(2,1)S(1)} copy-done((bf16[16640,128]{1,0:T(8,128)(2,1)S(1)}, bf16[16640,128]{1,0:T(8,128)(2,1)}, u32[]{:S(2)}) %copy-start.2) | copy-done | bytes 4259864
  99.5 4.3 %shard_map.69 = (bf16[16,128,128]{2,1,0:T(8,128)(2,1)S(1)}, bf16[16,128,128]{2,1,0:T(8,128)(2,1)S(1)}, bf16[16,128,128]{2,1,0:T(8,128)(2,1)S(1)}, bf16[8,128,128...) custom-call(s32[16,8]{1,0:T(8,128)S(1)} %fusion.5.rows_ref, bf16[128,1024]{1,0:T(8,128)(2,1)S(1)} %get-tuple-element.26.gh_ref, ...), custom_call_target="tpu_custom_call" | custom-call | flops 536870912 | bytes 7000000 | tf_op jit(solution)/shard_map/pallas_call | solution.py:129
  103.7 1.9 %collective-permute-start.4 = (bf16[8,128,128]{2,1,0:T(8,128)(2,1)S(1)}, bf16[8,128,128]{2,1,0:T(8,128)(2,1)S(1)}, u32[]{:S(2)}, u32[]{:S(2)}) collective-permute-start(bf16[8,128,128]{2,1,0:T(8,128)(2,1)S(1)} %get-tuple-element.30), channel_id=1, source_target_pairs={{0,15},{1,0},{2,1},{3,2},{4,3},{5,4},{6,5},{7,6},{8,7},{9,8},{10,9... | collective-permute-start | bytes 786440 | tf_op jit(solution)/shard_map/ppermute | solution.py:152
  105.7 3.4 %collective-permute-start.5 = (bf16[8,128,128]{2,1,0:T(8,128)(2,1)S(1)}, bf16[8,128,128]{2,1,0:T(8,128)(2,1)S(1)}, u32[]{:S(2)}, u32[]{:S(2)}) collective-permute-start(bf16[8,128,128]{2,1,0:T(8,128)(2,1)S(1)} %get-tuple-element.31), channel_id=1, source_target_pairs={{0,1},{1,2},{2,3},{3,4},{4,5},{5,6},{6,7},{7,8},{8,9},{9,10},{10,1... | collective-permute-start | bytes 786440 | tf_op jit(solution)/shard_map/ppermute | solution.py:152
  109.0 1.8 %collective-permute-done.4.from_right = bf16[8,128,128]{2,1,0:T(8,128)(2,1)S(1)} collective-permute-done((bf16[8,128,128]{2,1,0:T(8,128)(2,1)S(1)}, bf16[8,128,128]{2,1,0:T(8,128)(2,1)S(1)}, u32[]{:S(2)}, u32[]{:S(2)}) %collective-permute-start.4) | collective-permute-done | bytes 262176 | tf_op jit(solution)/shard_map/ppermute | solution.py:152
  110.9 3.5 %collective-permute-done.5.from_left = bf16[8,128,128]{2,1,0:T(8,128)(2,1)S(1)} collective-permute-done((bf16[8,128,128]{2,1,0:T(8,128)(2,1)S(1)}, bf16[8,128,128]{2,1,0:T(8,128)(2,1)S(1)}, u32[]{:S(2)}, u32[]{:S(2)}) %collective-permute-start.5) | collective-permute-done | bytes 262176 | tf_op jit(solution)/shard_map/ppermute | solution.py:152
  114.4 0.4 shard_map.70
  114.8 1.9 %collective-permute-start.6 = (bf16[16,128,128]{2,1,0:T(8,128)(2,1)S(1)}, bf16[16,128,128]{2,1,0:T(8,128)(2,1)S(1)}, u32[]{:S(2)}, u32[]{:S(2)}) collective-permute-start(bf16[16,128,128]{2,1,0:T(8,128)(2,1)S(1)} %get-tuple-element.32), channel_id=1, source_target_pairs={{0,15},{1,0},{2,1},{3,2},{4,3},{5,4},{6,5},{7,6},{8,7},{9,8},{10,9... | collective-permute-start | bytes 1572872 | tf_op jit(solution)/shard_map/ppermute | solution.py:152
  116.7 3.4 %collective-permute-start.7 = (bf16[16,128,128]{2,1,0:T(8,128)(2,1)S(1)}, bf16[16,128,128]{2,1,0:T(8,128)(2,1)S(1)}, u32[]{:S(2)}, u32[]{:S(2)}) collective-permute-start(bf16[16,128,128]{2,1,0:T(8,128)(2,1)S(1)} %get-tuple-element.33), channel_id=1, source_target_pairs={{0,1},{1,2},{2,3},{3,4},{4,5},{5,6},{6,7},{7,8},{8,9},{9,10},{10,1... | collective-permute-start | bytes 1572872 | tf_op jit(solution)/shard_map/ppermute | solution.py:152
  120.1 5.4 %collective-permute-done.6.left_ref = bf16[16,128,128]{2,1,0:T(8,128)(2,1)S(1)} collective-permute-done((bf16[16,128,128]{2,1,0:T(8,128)(2,1)S(1)}, bf16[16,128,128]{2,1,0:T(8,128)(2,1)S(1)}, u32[]{:S(2)}, u32[]{:S(2)}) %collective-permute-start.6) | collective-permute-done | bytes 524320 | tf_op jit(solution)/shard_map/ppermute | solution.py:152
  125.4 3.1 %collective-permute-done.7.right_ref = bf16[16,128,128]{2,1,0:T(8,128)(2,1)S(1)} collective-permute-done((bf16[16,128,128]{2,1,0:T(8,128)(2,1)S(1)}, bf16[16,128,128]{2,1,0:T(8,128)(2,1)S(1)}, u32[]{:S(2)}, u32[]{:S(2)}) %collective-permute-start.7) | collective-permute-done | bytes 524320 | tf_op jit(solution)/shard_map/ppermute | solution.py:152
  128.6 0.2 shard_map.71
  128.8 38.6 %all_to_all.11.far_ref = bf16[8,2,128,128]{3,2,1,0:T(8,128)(2,1)S(1)} all-to-all(bf16[8,2,128,128]{3,2,1,0:T(8,128)(2,1)S(1)} %bitcast.24), channel_id=1, replica_groups=mesh['x'=4,'yl'=2,'core'=2,'yh'=2,'zh'=4,'zl'=4] {'zh','yh'}, dimensions={0} | all-to-all | bytes 1048576 | tf_op jit(solution)/shard_map/all_to_all | solution.py:230
  167.4 0.7 shard_map.72
  168.1 1.1 reduce-scatter.2.cloned.1.call-done
  169.2 0.0 copy-start.5
  169.2 0.9 copy-done.5
  170.1 0.8 shard_map.73
  (6 shorter events, 0.1 us)
Async XLA Ops:
  7.2 0.8 copy-start
  7.2 78.7 %copy-start.4 = (bf16[128,1024]{1,0:T(8,128)(2,1)S(1)}, bf16[128,1024]{1,0:T(8,128)(2,1)}, u32[]{:S(2)}) copy-start(bf16[128,1024]{1,0:T(8,128)(2,1)} %gact_ref.1) | copy-start | bytes 786436
  7.2 72.3 %all-gather.3.cloned.1.call-start = ((), (), s32[]{:S(2)}) async-start(), calls=%async_computation.4 | async-start | bytes 4526080 | tf_op jit(solution)/shard_map/all_gather | solution.py:243
  9.9 159.3 %reduce-scatter.2.cloned.1.call-start = ((), (), s32[]{:S(2)}) async-start(), calls=%async_computation.3 | async-start | bytes 4456448 | tf_op jit(solution)/shard_map/reduce_scatter | solution.py:247
  56.7 15.5 %collective-permute-start.1 = (bf16[16,128,128]{2,1,0:T(8,128)(2,1)S(1)}, bf16[16,128,128]{2,1,0:T(8,128)(2,1)S(1)}, u32[]{:S(2)}, u32[]{:S(2)}) collective-permute-start(bf16[16,128,128]{2,1,0:T(8,128)(2,1)S(1)} %bitcast.21), channel_id=1, source_target_pairs={{0,15},{1,0},{2,1},{3,2},{4,3},{5,4},{6,5},{7,6},{8,7},{9,8},{10,9... | collective-permute-start | bytes 1572872 | tf_op jit(solution)/shard_map/ppermute | solution.py:152
  62.6 14.9 %collective-permute-start = (bf16[16,128,128]{2,1,0:T(8,128)(2,1)S(1)}, bf16[16,128,128]{2,1,0:T(8,128)(2,1)S(1)}, u32[]{:S(2)}, u32[]{:S(2)}) collective-permute-start(bf16[16,128,128]{2,1,0:T(8,128)(2,1)S(1)} %bitcast.22), channel_id=1, source_target_pairs={{0,1},{1,2},{2,3},{3,4},{4,5},{5,6},{6,7},{7,8},{8,9},{9,10},{10,1... | collective-permute-start | bytes 1572872 | tf_op jit(solution)/shard_map/ppermute | solution.py:152
  72.1 8.6 %collective-permute-start.3 = (bf16[8,128,128]{2,1,0:T(8,128)(2,1)S(1)}, bf16[8,128,128]{2,1,0:T(8,128)(2,1)S(1)}, u32[]{:S(2)}, u32[]{:S(2)}) collective-permute-start(bf16[8,128,128]{2,1,0:T(8,128)(2,1)S(1)} %slice.30), channel_id=1, source_target_pairs={{0,15},{1,0},{2,1},{3,2},{4,3},{5,4},{6,5},{7,6},{8,7},{9,8},{10,9... | collective-permute-start | bytes 786440 | tf_op jit(solution)/shard_map/ppermute | solution.py:152
  77.5 8.3 %collective-permute-start.2 = (bf16[8,128,128]{2,1,0:T(8,128)(2,1)S(1)}, bf16[8,128,128]{2,1,0:T(8,128)(2,1)S(1)}, u32[]{:S(2)}, u32[]{:S(2)}) collective-permute-start(bf16[8,128,128]{2,1,0:T(8,128)(2,1)S(1)} %slice.29), channel_id=1, source_target_pairs={{0,1},{1,2},{2,3},{3,4},{4,5},{5,6},{6,7},{7,8},{8,9},{9,10},{10,1... | collective-permute-start | bytes 786440 | tf_op jit(solution)/shard_map/ppermute | solution.py:152
  85.8 2.2 %copy-start.1 = (bf16[16640,128]{1,0:T(8,128)(2,1)S(1)}, bf16[16640,128]{1,0:T(8,128)(2,1)}, u32[]{:S(2)}) copy-start(bf16[16640,128]{1,0:T(8,128)(2,1)} %all-gather.3.cloned.1.call-done) | copy-start | bytes 12779524
  95.2 2.0 %copy-start.3 = (bf16[16,8,128,128]{3,2,1,0:T(8,128)(2,1)}, bf16[16,8,128,128]{3,2,1,0:T(8,128)(2,1)S(1)}, u32[]{:S(2)}) copy-start(bf16[16,8,128,128]{3,2,1,0:T(8,128)(2,1)S(1)} %get-tuple-element.34) | copy-start | bytes 12582916
  97.3 2.2 %copy-start.2 = (bf16[16640,128]{1,0:T(8,128)(2,1)S(1)}, bf16[16640,128]{1,0:T(8,128)(2,1)}, u32[]{:S(2)}) copy-start(bf16[16640,128]{1,0:T(8,128)(2,1)} %all-gather.3.cloned.1.call-done) | copy-start | bytes 12779524
  103.7 7.1 %collective-permute-start.4 = (bf16[8,128,128]{2,1,0:T(8,128)(2,1)S(1)}, bf16[8,128,128]{2,1,0:T(8,128)(2,1)S(1)}, u32[]{:S(2)}, u32[]{:S(2)}) collective-permute-start(bf16[8,128,128]{2,1,0:T(8,128)(2,1)S(1)} %get-tuple-element.30), channel_id=1, source_target_pairs={{0,15},{1,0},{2,1},{3,2},{4,3},{5,4},{6,5},{7,6},{8,7},{9,8},{10,9... | collective-permute-start | bytes 786440 | tf_op jit(solution)/shard_map/ppermute | solution.py:152
  105.7 8.7 %collective-permute-start.5 = (bf16[8,128,128]{2,1,0:T(8,128)(2,1)S(1)}, bf16[8,128,128]{2,1,0:T(8,128)(2,1)S(1)}, u32[]{:S(2)}, u32[]{:S(2)}) collective-permute-start(bf16[8,128,128]{2,1,0:T(8,128)(2,1)S(1)} %get-tuple-element.31), channel_id=1, source_target_pairs={{0,1},{1,2},{2,3},{3,4},{4,5},{5,6},{6,7},{7,8},{8,9},{9,10},{10,1... | collective-permute-start | bytes 786440 | tf_op jit(solution)/shard_map/ppermute | solution.py:152
  114.8 10.7 %collective-permute-start.6 = (bf16[16,128,128]{2,1,0:T(8,128)(2,1)S(1)}, bf16[16,128,128]{2,1,0:T(8,128)(2,1)S(1)}, u32[]{:S(2)}, u32[]{:S(2)}) collective-permute-start(bf16[16,128,128]{2,1,0:T(8,128)(2,1)S(1)} %get-tuple-element.32), channel_id=1, source_target_pairs={{0,15},{1,0},{2,1},{3,2},{4,3},{5,4},{6,5},{7,6},{8,7},{9,8},{10,9... | collective-permute-start | bytes 1572872 | tf_op jit(solution)/shard_map/ppermute | solution.py:152
  116.7 11.9 %collective-permute-start.7 = (bf16[16,128,128]{2,1,0:T(8,128)(2,1)S(1)}, bf16[16,128,128]{2,1,0:T(8,128)(2,1)S(1)}, u32[]{:S(2)}, u32[]{:S(2)}) collective-permute-start(bf16[16,128,128]{2,1,0:T(8,128)(2,1)S(1)} %get-tuple-element.33), channel_id=1, source_target_pairs={{0,1},{1,2},{2,3},{3,4},{4,5},{5,6},{6,7},{7,8},{8,9},{9,10},{10,1... | collective-permute-start | bytes 1572872 | tf_op jit(solution)/shard_map/ppermute | solution.py:152
  169.2 0.9 copy-start.5
Sparse Core Ops, SparseCore 0:
  10.2 53.2 all-gather.2
  97.4 71.7 reduce-scatter.1
